TPU v7x, 32 devices: a whole 2x2x4 slice. The times are simulated.
32 devices in a mesh: group: 4 (over y, x), expert: 8 (over z, core).
Axes of the slice: x: 2, y: 2, z: 4, core: 2. Of those that a mesh axis runs over, the one named last changes fastest.
Arguments:
- tokens: bfloat16 [128, 7168], P(('group', 'expert')), may hold values from -6 to 6
- expert_ids: int32 [128, 8], P(('group', 'expert')), may hold values from 0 to 31, all different within a row; in each aligned block of 4 rows (0 to 3, 4 to 7, ...) at most 2 rows name the same one
- gate_weights: bfloat16 [128, 8], P(('group', 'expert')), may hold values from 0.049804688 to 0.5
- w_gate: bfloat16 [32, 7168, 2048], P(('group', 'expert')), may hold values from -0.0625 to 0.0625
- w_up: bfloat16 [32, 7168, 2048], P(('group', 'expert')), may hold values from -0.0625 to 0.0625
- w_down: bfloat16 [32, 2048, 7168], P(('group', 'expert')), may hold values from -0.125 to 0.125
Outputs:
- mixed: bfloat16 [128, 7168], P(('group', 'expert'))
Inputs may be any that keep to these rules, and one draw needn't show every extreme that they name: `expert_ids`: each row names 8 different experts. Among the 4 rows of one device no expert is named by more than 2 rows, and in some device some expert is named by exactly 2 rows.
All inputs are finite; a program needn't handle non-finite values.
Results may differ from a plain program's by a relative error of at most 0.014.
Values may be sent and summed in bfloat16 or wider, within the bound.
No kernel may reach another device: no remote copies, remote signals or barrier semaphores. Data moves between devices by JAX's collectives and lax.ppermute only.
A program may use at most 128 MiB of HBM per device.

v0:
```python
import jax
import jax.numpy as jnp
from jax import lax
from jax.sharding import PartitionSpec as P

EXP_GRP = 8
CAP = 2


def route_tables(expert_ids, gate_weights, experts, capacity):
    count = expert_ids.shape[0]
    labels = jnp.arange(experts, dtype=jnp.int32)
    match = expert_ids[:, :, None] == labels[None, None, :]
    named = jnp.any(match, axis=1).astype(jnp.float32)
    weight = jnp.sum(
        jnp.where(match, gate_weights.astype(jnp.float32)[:, :, None], jnp.float32(0.0)), axis=1
    )
    earlier = (jnp.arange(count)[:, None] > jnp.arange(count)[None, :]).astype(jnp.float32)
    rank = jnp.dot(earlier, named, precision=lax.Precision.HIGHEST)
    places = jnp.arange(capacity, dtype=jnp.float32)
    select = named[:, :, None] * (rank[:, :, None] == places[None, None, :]).astype(jnp.float32)
    return (select, select * weight[:, :, None])


def hidden_rows(flat, gate_block, up_block):
    gate_val = jnp.dot(flat, gate_block, preferred_element_type=jnp.float32)
    up_val = jnp.dot(flat, up_block, preferred_element_type=jnp.float32)
    return (jax.nn.silu(gate_val) * up_val).astype(jnp.bfloat16)


def expert_rows(flat, gate_block, up_block, down_block):
    hidden = hidden_rows(flat, gate_block, up_block)
    return jnp.dot(hidden, down_block, preferred_element_type=jnp.float32).astype(jnp.bfloat16)


def fold_blocks(returned, split):
    shape = returned.shape
    sectioned = returned.reshape(shape[0], shape[1] // split, split, shape[2], shape[3])
    return jnp.sum(sectioned, axis=2, dtype=jnp.float32).astype(jnp.bfloat16)


def weigh_slots(mixing, expert_out):
    return jnp.einsum(
        "rec,ecd->rd", mixing, expert_out.astype(jnp.float32), precision=lax.Precision.HIGHEST
    ).astype(jnp.bfloat16)


def on_device(tokens, expert_ids, gate_weights, w_gate, w_up, w_down):
    groups = lax.axis_size("group")
    members = lax.axis_size("expert")
    split = members // EXP_GRP
    experts = groups * EXP_GRP
    width = tokens.shape[1]
    select, mixing = route_tables(expert_ids, gate_weights, experts, CAP)
    outbound = jnp.einsum(
        "rec,rd->ecd", select, tokens.astype(jnp.float32), precision=lax.Precision.HIGHEST
    ).astype(jnp.bfloat16)
    boxes = outbound.reshape(groups, EXP_GRP, CAP, width)
    copies = jnp.repeat(boxes, split, axis=1)
    arrived = lax.all_to_all(
        lax.all_to_all(copies, "group", split_axis=0, concat_axis=0, tiled=True),
        "expert",
        split_axis=1,
        concat_axis=1,
        tiled=True,
    )
    flat = arrived.reshape(-1, width)
    partial_value = expert_rows(flat, w_gate[0], w_up[0], w_down[0])
    partial_value = partial_value.reshape(arrived.shape)
    returned = lax.all_to_all(
        lax.all_to_all(partial_value, "group", split_axis=0, concat_axis=0, tiled=True),
        "expert",
        split_axis=1,
        concat_axis=1,
        tiled=True,
    )
    expert_out = fold_blocks(returned, split)
    mixed = weigh_slots(mixing, expert_out.reshape(experts, CAP, width))
    return mixed


def solution(mesh):
    in_specs = (
        P(("group", "expert"), None),
        P(("group", "expert"), None),
        P(("group", "expert"), None),
        P(("group", "expert"), None, None),
        P(("group", "expert"), None, None),
        P(("group", "expert"), None, None),
    )
    out_specs = P(("group", "expert"), None)
    return jax.shard_map(
        on_device, mesh=mesh, in_specs=in_specs, out_specs=out_specs, check_vma=False
    )
```

profile of v0, /device:TPU:0, one launch (start us, length us, event | category | flops | bytes accessed | tf_op | source)
XLA Modules:
  0.0 129.6 jit_solution(9724075752782917632)
XLA Ops:
  0.0 0.0 copy-start
  0.0 0.8 fusion.28
  0.8 0.1 fusion.37
  0.9 0.0 copy-done
  0.9 1.0 fusion.9
  1.9 0.9 copy.19
  2.8 17.7 %all_to_all.20 = bf16[4,8,2,7168]{3,2,1,0:T(2,128)(2,1)S(1)} all-to-all(bf16[4,8,2,7168]{3,2,1,0:T(2,128)(2,1)S(1)} %copy.19), channel_id=1, replica_groups=mesh['group'=4,'expert'=8] {'group'}, dimensions={0} | all-to-all | bytes 1835008 | tf_op jit(solution)/shard_map/all_to_all | solution.py:61
  20.5 0.6 copy.20
  21.2 28.5 %all_to_all.21 = bf16[4,8,2,7168]{3,2,0,1:T(2,128)(2,1)S(1)} all-to-all(bf16[4,8,2,7168]{3,2,0,1:T(2,128)(2,1)S(1)} %copy.20), channel_id=1, replica_groups=mesh['group'=4,'expert'=8] {'expert'}, dimensions={1} | all-to-all | bytes 1835008 | tf_op jit(solution)/shard_map/all_to_all | solution.py:60
  49.6 0.6 copy.21
  50.3 0.3 reshape.20
  50.6 0.0 copy-start.1
  50.6 12.1 %fusion.4 = f32[64,2048]{1,0:T(8,128)S(1)} fusion(bf16[64,7168]{1,0:T(8,128)(2,1)S(1)} %reshape.20, bf16[1,7168,2048]{2,1,0:T(8,128)(2,1)} %param.9), kind=kOutput, calls=%fused_computation.4 | convolution fusion | flops 1879048192 | bytes 30801920 | tf_op jit(solution)/shard_map/dot_general | solution.py:26
  62.7 0.0 copy-start.3
  62.7 0.0 copy-start.2
  62.7 20.9 %fusion.6 = bf16[64,7168]{1,0:T(8,128)(2,1)S(1)} fusion(bf16[1,2048,7168]{2,1,0:T(8,128)(2,1)} %param.11, bf16[64,7168]{1,0:T(8,128)(2,1)S(1)} %reshape.20, bf16[1,7168,2048]{2,1,0:T(8,128)(2,1)} %param.10, f32[64,2048]{1,0:T(8,128)S(1)} %fusion.4), kind=kOutput, calls=%fused_computation.6 | convolution fusion | flops 3759341568 | bytes 61079552 | tf_op jit(solution)/shard_map/dot_general | solution.py:33
  83.6 0.3 reshape.21
  84.0 15.2 %all_to_all.22 = bf16[4,8,2,7168]{3,2,1,0:T(2,128)(2,1)S(1)} all-to-all(bf16[4,8,2,7168]{3,2,1,0:T(2,128)(2,1)S(1)} %reshape.21), channel_id=1, replica_groups=mesh['group'=4,'expert'=8] {'group'}, dimensions={0} | all-to-all | bytes 1835008 | tf_op jit(solution)/shard_map/all_to_all | solution.py:71
  99.2 1.6 %copy.22 = bf16[4,8,2,7168]{3,2,0,1:T(2,128)(2,1)} copy(bf16[4,8,2,7168]{3,2,1,0:T(2,128)(2,1)S(1)} %all_to_all.22) | data formatting | bytes 1835008 | tf_op jit(solution)/shard_map/all_to_all | solution.py:71
  100.8 3.6 %all-to-all-start.3 = ((bf16[4,8,2,7168]{3,2,0,1:T(2,128)(2,1)}), bf16[4,8,2,7168]{3,2,0,1:T(2,128)(2,1)S(1)}, u32[]{:S(2)}, u32[]{:S(2)}) async-start(bf16[4,8,2,7168]{3,2,0,1:T(2,128)(2,1)} %copy.22), calls=%async_computation.3 | async-start | bytes 1835008 | tf_op jit(solution)/shard_map/all_to_all | solution.py:70
  104.4 0.0 copy-done.3
  104.4 0.0 copy-done.2
  104.4 0.1 select_reduce_fusion
  104.5 23.6 %all-to-all-done.3 = bf16[4,8,2,7168]{3,2,0,1:T(2,128)(2,1)S(1)} async-done(((bf16[4,8,2,7168]{3,2,0,1:T(2,128)(2,1)}), bf16[4,8,2,7168]{3,2,0,1:T(2,128)(2,1)S(1)}, u32[]{:S(2)}, u32[]{:S(2)}) %all-to-all-start.3) | async-done | bytes 917536 | tf_op jit(solution)/shard_map/all_to_all | solution.py:70
  128.1 1.5 %fusion.10 = bf16[4,7168]{1,0:T(4,128)(2,1)} fusion(bf16[4,8,2,7168]{3,2,0,1:T(2,128)(2,1)S(1)} %all-to-all-done.3, f32[4,32]{1,0:T(4,128)S(1)} %select_reduce_fusion, f32[4,32]{1,0:T(4,128)S(1)} %convert_element_type.33, f32[4,32]{1,0:T(4,128)S(1)} %fusion.37), kind=kOutput, calls=%fused_computation.10 | convolution fusion | flops 22049536 | bytes 976384 | tf_op jit(solution)/shard_map/rec,ecd->rd/dot_general | solution.py:43
  129.6 0.0 copy-done.1
  (2 shorter events, 0.0 us)
Async XLA Ops:
  0.0 0.9 copy-start
  50.6 79.0 %copy-start.1 = (bf16[4,7168]{1,0:T(4,128)(2,1)S(1)}, bf16[4,7168]{1,0:T(4,128)(2,1)}, u32[]{:S(2)}) copy-start(bf16[4,7168]{1,0:T(4,128)(2,1)} %param.6) | copy-start | bytes 172036
  62.7 41.7 %copy-start.3 = (bf16[4,8]{1,0:T(4,128)(2,1)S(1)}, bf16[4,8]{1,0:T(4,128)(2,1)}, u32[]{:S(2)}) copy-start(bf16[4,8]{1,0:T(4,128)(2,1)} %param.8) | copy-start | bytes 196
  62.7 41.7 %copy-start.2 = (s32[4,8]{1,0:T(4,128)S(1)}, s32[4,8]{1,0:T(4,128)}, u32[]{:S(2)}) copy-start(s32[4,8]{1,0:T(4,128)} %param.7) | copy-start | bytes 388
  100.8 27.3 %all-to-all-start.3 = ((bf16[4,8,2,7168]{3,2,0,1:T(2,128)(2,1)}), bf16[4,8,2,7168]{3,2,0,1:T(2,128)(2,1)S(1)}, u32[]{:S(2)}, u32[]{:S(2)}) async-start(bf16[4,8,2,7168]{3,2,0,1:T(2,128)(2,1)} %copy.22), calls=%async_computation.3 | async-start | bytes 1835008 | tf_op jit(solution)/shard_map/all_to_all | solution.py:70
where the time goes:
time: 130 us
  blocking collectives  61.4 us (47%)
  matrix products  35.5 us (27%)
  waiting for transfers between devices  23.6 us (18%)
  local copies, waits for them, and re-layouts  4.56 us (4%)
  starting transfers between devices  3.55 us (3%)
    all_to_all x1, blocking collectives, on_device(): lax.all_to_all(lax.all_to_all(copies, 'group', split_axis=0, concat_axis=...  28.5 us
    all_to_all x1, waiting for transfers between devices, on_device(): lax.all_to_all(lax.all_to_all(partial_value, 'group', split_axis=0, conca...  23.6 us
    dot_general x1, matrix products, expert_rows(): jnp.dot(hidden, down_block, preferred_element_type=jnp.float32)  20.9 us
    all_to_all x1, blocking collectives, on_device(): lax.all_to_all(copies, 'group', split_axis=0, concat_axis=0, tiled=True)  17.7 us
    all_to_all x1, blocking collectives, on_device(): lax.all_to_all(partial_value, 'group', split_axis=0, concat_axis=0, tiled...  15.2 us
    dot_general x1, matrix products, hidden_rows(): gate_val = jnp.dot(flat, gate_block, preferred_element_type=jnp.float32)  12.1 us
    all_to_all x1, starting transfers between devices, on_device(): lax.all_to_all(lax.all_to_all(partial_value, 'group', split_axis=0, conca...  3.55 us
  transfers between devices with their start and end apart: 1, of which 1 were waited for; matrix products, arithmetic and copies ran while one was open for 0% of the time, Pallas kernels for 0%

commit v1 on v0

v1 whole, which is shorter than its diff:
```python
import jax
import jax.numpy as jnp
from jax import lax
from jax.sharding import PartitionSpec as P

EXP_GRP = 8
AXES = ("group", "expert")


def on_device(tokens, expert_ids, gate_weights, w_gate, w_up, w_down):
    groups = lax.axis_size("group")
    members = lax.axis_size("expert")
    split = members // EXP_GRP
    experts = groups * EXP_GRP
    width = tokens.shape[1]
    me = lax.axis_index("group") * EXP_GRP + lax.axis_index("expert") // split
    labels = jnp.arange(experts, dtype=jnp.int32)
    match = expert_ids[:, :, None] == labels[None, None, :]
    weight = jnp.sum(
        jnp.where(match, gate_weights.astype(jnp.float32)[:, :, None], jnp.float32(0.0)), axis=1
    ).astype(jnp.bfloat16)
    pad = -(-experts // 128) * 128 - experts
    packed = jnp.concatenate([tokens, jnp.pad(weight, ((0, 0), (0, pad)))], axis=1)
    everyone = lax.all_gather(packed, AXES, axis=0, tiled=True)
    rows = everyone[:, :width]
    mine = labels == me
    scale = jnp.sum(
        jnp.where(mine[None, :], everyone[:, width : width + experts].astype(jnp.float32), 0.0),
        axis=1,
        keepdims=True,
    )
    gate_val = jnp.dot(rows, w_gate[0], preferred_element_type=jnp.float32)
    up_val = jnp.dot(rows, w_up[0], preferred_element_type=jnp.float32)
    hidden = (jax.nn.silu(gate_val) * up_val).astype(jnp.bfloat16)
    part = jnp.dot(hidden, w_down[0], preferred_element_type=jnp.float32)
    part = (part * scale).astype(jnp.bfloat16)
    return lax.psum_scatter(part, AXES, scatter_dimension=0, tiled=True)


def solution(mesh):
    in_specs = (
        P(AXES, None),
        P(AXES, None),
        P(AXES, None),
        P(AXES, None, None),
        P(AXES, None, None),
        P(AXES, None, None),
    )
    out_specs = P(AXES, None)
    return jax.shard_map(
        on_device, mesh=mesh, in_specs=in_specs, out_specs=out_specs, check_vma=False
    )
```

time: 130 us -> 246 us (1.89)
  waiting for transfers between devices: 23.6 us -> 191 us
  blocking collectives: 61.4 us -> 0 us
  between operations: 0.11 us -> 13.4 us
  starting transfers between devices: 3.55 us -> 0.04 us
    unnamed x0 -> x3, waiting for transfers between devices: none -> 132 us
    all_to_all x3 -> x0, blocking collectives: 61.4 us -> none  [the longest x1 28.5 us: on_device(): lax.all_to_all(lax.all_to_all(copies, 'group', split_axis=0, concat_axis=...]
    all_gather x0 -> x1, waiting for transfers between devices: none -> 59.4 us  [on_device(): everyone = lax.all_gather(packed, AXES, axis=0, tiled=True)]
    all_to_all x1 -> x0, waiting for transfers between devices: 23.6 us -> none  [on_device(): lax.all_to_all(lax.all_to_all(partial_value, 'group', split_axis=0, conca...]
    unnamed x8 -> x2, local copies, waits for them, and re-layouts: 0.02 us -> 4.51 us
    all_to_all x1 -> x0, starting transfers between devices: 3.55 us -> none  [on_device(): lax.all_to_all(lax.all_to_all(partial_value, 'group', split_axis=0, conca...]
    all_to_all x3 -> x0, local copies, waits for them, and re-layouts: 2.9 us -> none  [the longest x1 1.64 us: on_device(): lax.all_to_all(partial_value, 'group', split_axis=0, concat_axis=0, tiled...]
    dot_general x5 -> x2, matrix products: 35.5 us -> 33.2 us  [the longest x1 21.8 us: on_device(): part = jnp.dot(hidden, w_down[0], preferred_element_type=jnp.float32)]
  transfers between devices with their start and end apart: 1 -> 2, of which waited for: 1 -> 2; matrix products, arithmetic and copies ran while one was open for 0% -> 0% of each run, Pallas kernels for 0% -> 0%
where the time goes in v1:
time: 246 us
  waiting for transfers between devices  191 us (78%)
  matrix products  33.2 us (13%)
  between operations  13.4 us (5%)
  local copies, waits for them, and re-layouts  4.51 us (2%)
  other arithmetic  3.02 us (1%)
    unnamed x3, waiting for transfers between devices  132 us
    all_gather x1, waiting for transfers between devices, on_device(): everyone = lax.all_gather(packed, AXES, axis=0, tiled=True)  59.4 us
    dot_general x1, matrix products, on_device(): part = jnp.dot(hidden, w_down[0], preferred_element_type=jnp.float32)  21.8 us
    dot_general x1, matrix products, on_device(): gate_val = jnp.dot(rows, w_gate[0], preferred_element_type=jnp.float32)  11.4 us
  transfers between devices with their start and end apart: 2, of which 2 were waited for; matrix products, arithmetic and copies ran while one was open for 0% of the time, Pallas kernels for 0%

profile of v1, /device:TPU:0, one launch (start us, length us, event | category | flops | bytes accessed | tf_op | source)
XLA Modules:
  0.0 245.6 jit_solution(16644952933307224313)
XLA Ops:
  6.5 0.0 all-gather.3.cloned.1.call-start
  6.5 0.7 convert_element_type.17
  7.2 0.8 select_reduce_fusion.1
  8.0 1.5 fusion.31
  9.4 0.0 all-gather.3.cloned.1.call-update
  9.5 0.0 all-reduce.4.cloned.1.call-start
  9.5 59.4 %all-gather.3.cloned.1.call-done = bf16[32,4,7296]{2,1,0:T(4,128)(2,1)} async-done(((bf16[1,4,7296]{2,1,0:T(4,128)(2,1)}), bf16[32,4,7296]{2,1,0:T(4,128)(2,1)}) %all-gather.3.cloned.1.call-update) | async-done | bytes 1867792 | tf_op jit(solution)/shard_map/all_gather | solution.py:24
  69.0 3.0 %reshape.8 = bf16[128,7296]{1,0:T(8,128)(2,1)S(1)} reshape(bf16[32,4,7296]{2,1,0:T(4,128)(2,1)} %all-gather.3.cloned.1.call-done) | data formatting | bytes 3735552
  71.9 0.1 select_reduce_fusion
  72.1 11.4 %fusion.4 = f32[128,2048]{1,0:T(8,128)S(1)} fusion(bf16[1,7168,2048]{2,1,0:T(8,128)(2,1)} %param.9, bf16[128,7296]{1,0:T(8,128)(2,1)S(1)} %reshape.8), kind=kOutput, calls=%fused_computation.4 | convolution fusion | flops 3758096384 | bytes 32243712 | tf_op jit(solution)/shard_map/dot_general | solution.py:32
  83.5 21.8 %fusion.9 = bf16[128,7168]{1,0:T(8,128)(2,1)} fusion(bf16[1,2048,7168]{2,1,0:T(8,128)(2,1)} %param.11, bf16[1,7168,2048]{2,1,0:T(8,128)(2,1)} %param.10, f32[128]{0:T(128)S(1)} %select_reduce_fusion, bf16[128,7296]{1,0:T(8,128)(2,1)S(1)} %reshape.8, f32[128,2048]{1,0:T(8,128)S(1)} %fusion.4), kind=kOutput, calls=%fused_computation.7 | convolution fusion | flops 7519600640 | bytes 63439360 | tf_op jit(solution)/shard_map/dot_general | solution.py:35
  105.3 0.0 all-reduce.4.cloned.1.call-update
  105.3 132.0 %all-reduce.4.cloned.1.call-done = bf16[128,7168]{1,0:T(8,128)(2,1)} async-done(((bf16[128,7168]{1,0:T(8,128)(2,1)}), bf16[128,7168]{1,0:T(8,128)(2,1)}) %all-reduce.4.cloned.1.call-update) | async-done | bytes 1835024
  237.3 1.6 constant_dynamic-slice_fusion
  (1 shorter events, 0.0 us)
Async XLA Ops:
  6.5 62.4 %all-gather.3.cloned.1.call-start = ((), (), s32[]{:S(2)}) async-start(), calls=%async_computation | async-start | bytes 1926144 | tf_op jit(solution)/shard_map/all_gather | solution.py:24
  9.5 227.8 %all-reduce.4.cloned.1.call-start = ((), (), s32[]{:S(2)}) async-start(), calls=%async_computation.1 | async-start | bytes 3670016
Sparse Core Ops, SparseCore 0:
  10.2 58.7 all-gather.2
  105.4 131.8 all-reduce.3

commit v2 on v1

v2 whole, which is shorter than its diff:
```python
import functools

import jax
import jax.numpy as jnp
from jax import lax
from jax.experimental import pallas as pl
from jax.experimental.pallas import tpu as pltpu
from jax.sharding import PartitionSpec as P

EXP_GRP = 8
AXES = ("group", "expert")
CHUNKS = 2
LIMIT = 24 * 1024 * 1024


def block_of(total, most):
    size = most
    while total % size:
        size -= 128
    return size


def shifted(value, axis, size, shift, unit=1):
    count = size // unit
    pairs = []
    for i in range(size):
        slot, low = i // unit, i % unit
        pairs.append((i, ((slot + shift) % count) * unit + low))
    return lax.ppermute(value, axis, pairs)


def other_core(value, size):
    return lax.ppermute(value, "expert", [(i, i ^ 1) for i in range(size)])


def gather(value, groups, members):
    lines = members // 2
    column = jnp.concatenate(
        [value] + [shifted(value, "expert", members, s, 2) for s in range(1, lines)], axis=0
    )
    planes = [column] + [shifted(column, "group", groups, s) for s in range(1, groups)]
    return planes + [other_core(p, members) for p in planes]


def gate_up_kernel(parts, has_acc, last, *refs):
    x_refs = refs[:parts]
    gate_ref, up_ref = refs[parts : parts + 2]
    rest = refs[parts + 2 :]
    if has_acc:
        gate_in, up_in = rest[:2]
        rest = rest[2:]
    if last:
        hidden_ref, gate_acc, up_acc = rest
    else:
        gate_acc, up_acc = rest
    step = pl.program_id(0)
    x = jnp.concatenate([r[...] for r in x_refs], axis=0)
    gate = jnp.dot(x, gate_ref[0], preferred_element_type=jnp.float32)
    up = jnp.dot(x, up_ref[0], preferred_element_type=jnp.float32)

    @pl.when(step == 0)
    def _():
        if has_acc:
            gate_acc[...] = gate_in[...] + gate
            up_acc[...] = up_in[...] + up
        else:
            gate_acc[...] = gate
            up_acc[...] = up

    @pl.when(step > 0)
    def _():
        gate_acc[...] += gate
        up_acc[...] += up

    if last:

        @pl.when(step == pl.num_programs(0) - 1)
        def _():
            hidden_ref[...] = (jax.nn.silu(gate_acc[...]) * up_acc[...]).astype(jnp.bfloat16)


def gate_up(parts, w_gate, w_up, start, acc, last, width):
    rows = sum(p.shape[0] for p in parts)
    units = w_gate.shape[2]
    block = block_of(width, 512)
    first = start // block
    steps = width // block
    weight_spec = pl.BlockSpec((1, block, units), lambda i: (0, first + i, 0))
    whole = pl.BlockSpec((rows, units), lambda i: (0, 0))
    in_specs = [pl.BlockSpec((p.shape[0], block), lambda i: (0, i)) for p in parts]
    in_specs += [weight_spec, weight_spec]
    args = list(parts) + [w_gate, w_up]
    if acc is not None:
        in_specs += [whole, whole]
        args += list(acc)
    total = jax.ShapeDtypeStruct((rows, units), jnp.float32)
    if last:
        out_shape = jax.ShapeDtypeStruct((rows, units), jnp.bfloat16)
        out_specs = whole
        scratch = [pltpu.VMEM((rows, units), jnp.float32)] * 2
    else:
        out_shape = (total, total)
        out_specs = (whole, whole)
        scratch = []
    return pl.pallas_call(
        functools.partial(gate_up_kernel, len(parts), acc is not None, last),
        grid=(steps,),
        in_specs=in_specs,
        out_specs=out_specs,
        out_shape=out_shape,
        scratch_shapes=scratch,
        compiler_params=pltpu.CompilerParams(vmem_limit_bytes=LIMIT),
        cost_estimate=pl.CostEstimate(
            flops=4 * rows * width * units,
            bytes_accessed=4 * width * units,
            transcendentals=0,
        ),
    )(*args)


def down_kernel(hidden_ref, down_ref, me_ref, *refs):
    route_refs, (own_ref, far_ref) = refs[:-2], refs[-2:]
    route = jnp.concatenate([r[...] for r in route_refs], axis=0).astype(jnp.float32)
    lane = lax.broadcasted_iota(jnp.int32, route.shape, 1)
    scale = jnp.sum(jnp.where(lane == me_ref[0], route, 0.0), axis=1, keepdims=True)
    part = jnp.dot(hidden_ref[...], down_ref[0], preferred_element_type=jnp.float32)
    part = (part * scale).astype(jnp.bfloat16)
    half = part.shape[0] // 2
    own_ref[...] = part[:half]
    far_ref[...] = part[half:]


def down(hidden, w_down, routes, me, start, width):
    rows, units = hidden.shape
    block = block_of(width, 512)
    first = start // block
    half = jax.ShapeDtypeStruct((rows // 2, width), jnp.bfloat16)
    half_spec = pl.BlockSpec((rows // 2, block), lambda i: (0, i))
    return pl.pallas_call(
        down_kernel,
        grid=(width // block,),
        in_specs=[
            pl.BlockSpec((rows, units), lambda i: (0, 0)),
            pl.BlockSpec((1, units, block), lambda i: (0, 0, first + i)),
            pl.BlockSpec(memory_space=pltpu.SMEM),
        ]
        + [pl.BlockSpec(r.shape, lambda i: (0, 0)) for r in routes],
        out_specs=(half_spec, half_spec),
        out_shape=(half, half),
        compiler_params=pltpu.CompilerParams(vmem_limit_bytes=LIMIT),
        cost_estimate=pl.CostEstimate(
            flops=2 * rows * width * units,
            bytes_accessed=2 * width * units,
            transcendentals=0,
        ),
    )(hidden, w_down, me, *routes)


def add_kernel(count, *refs):
    ins, outs = refs[:count], refs[count:]
    total = ins[0][...].astype(jnp.float32)
    for ref in ins[1:]:
        total = total + ref[...].astype(jnp.float32)
    total = total.astype(jnp.bfloat16)
    size = total.shape[0] // len(outs)
    for i, ref in enumerate(outs):
        ref[...] = total[i * size : (i + 1) * size]


def add_split(values, pieces):
    rows, width = values[0].shape
    block = block_of(width, 1792)
    out = jax.ShapeDtypeStruct((rows // pieces, width), jnp.bfloat16)
    return pl.pallas_call(
        functools.partial(add_kernel, len(values)),
        grid=(width // block,),
        in_specs=[pl.BlockSpec((rows, block), lambda i: (0, i))] * len(values),
        out_specs=(pl.BlockSpec((rows // pieces, block), lambda i: (0, i)),) * pieces,
        out_shape=(out,) * pieces,
        compiler_params=pltpu.CompilerParams(vmem_limit_bytes=LIMIT),
        cost_estimate=pl.CostEstimate(
            flops=len(values) * rows * width,
            bytes_accessed=2 * (len(values) + 1) * rows * width,
            transcendentals=0,
        ),
    )(*values)


def give_back(own, far, groups, members):
    lines = members // 2
    planes = add_split([own, other_core(far, members)], groups)
    planes = [planes[0]] + [shifted(planes[s], "group", groups, -s) for s in range(1, groups)]
    column = add_split(planes, lines)
    column = [column[0]] + [
        shifted(column[s], "expert", members, -s, 2) for s in range(1, lines)
    ]
    total = column[0].astype(jnp.float32)
    for value in column[1:]:
        total = total + value.astype(jnp.float32)
    return total.astype(jnp.bfloat16)


def on_device(tokens, expert_ids, gate_weights, w_gate, w_up, w_down):
    groups = lax.axis_size("group")
    members = lax.axis_size("expert")
    split = members // EXP_GRP
    experts = groups * EXP_GRP
    width = tokens.shape[1] // CHUNKS
    me = lax.axis_index("group") * EXP_GRP + lax.axis_index("expert") // split
    labels = jnp.arange(-(-experts // 128) * 128, dtype=jnp.int32)
    match = expert_ids[:, :, None] == labels[None, None, :]
    route = jnp.sum(
        jnp.where(match, gate_weights.astype(jnp.float32)[:, :, None], jnp.float32(0.0)), axis=1
    ).astype(jnp.bfloat16)
    acc = None
    for c in range(CHUNKS):
        last = c == CHUNKS - 1
        chunk = tokens[:, c * width : (c + 1) * width]
        if last:
            chunk = jnp.concatenate([chunk, route], axis=1)
        parts = gather(chunk, groups, members)
        if last:
            routes = [p[:, width:] for p in parts]
        acc = gate_up(parts, w_gate, w_up, c * width, acc, last, width)
    hidden = acc
    me = me.astype(jnp.int32).reshape(1)
    outs = []
    for c in range(CHUNKS):
        own, far = down(hidden, w_down, routes, me, c * width, width)
        outs.append(give_back(own, far, groups, members))
    return jnp.concatenate(outs, axis=1)


def solution(mesh):
    in_specs = (
        P(AXES, None),
        P(AXES, None),
        P(AXES, None),
        P(AXES, None, None),
        P(AXES, None, None),
        P(AXES, None, None),
    )
    out_specs = P(AXES, None)
    return jax.shard_map(
        on_device, mesh=mesh, in_specs=in_specs, out_specs=out_specs, check_vma=False
    )
```

time: 246 us -> 99.6 us (0.40)
  waiting for transfers between devices: 191 us -> 13.1 us
  Pallas kernels: 0 us -> 36.9 us
  starting transfers between devices: 0.04 us -> 36.6 us
  matrix products: 33.2 us -> 0 us
  between operations: 13.4 us -> 0.2 us
  local copies, waits for them, and re-layouts: 4.51 us -> 10.1 us
    unnamed x3 -> x0, waiting for transfers between devices: 132 us -> none
    all_gather x1 -> x0, waiting for transfers between devices: 59.4 us -> none  [on_device(): everyone = lax.all_gather(packed, AXES, axis=0, tiled=True)]
    pallas_call x0 -> x8, Pallas kernels: none -> 36.9 us  [the longest x2 27.3 us: gate_up(): pl.pallas_call(functools.partial(gate_up_kernel, len(parts), acc is not N...]
    ppermute x0 -> x34, starting transfers between devices: none -> 36.6 us  [the longest x24 34.3 us: shifted(): return lax.ppermute(value, axis, pairs)]
    dot_general x2 -> x0, matrix products: 33.2 us -> none  [the longest x1 21.8 us: on_device(): part = jnp.dot(hidden, w_down[0], preferred_element_type=jnp.float32)]
    ppermute x0 -> x34, waiting for transfers between devices: none -> 13.1 us  [the longest x24 12.8 us: shifted(): return lax.ppermute(value, axis, pairs)]
    unnamed x2, local copies, waits for them, and re-layouts: 4.51 us -> 9.35 us
  transfers between devices with their start and end apart: 2 -> 34, of which waited for: 2 -> 10; matrix products, arithmetic and copies ran while one was open for 0% -> 2% of each run, Pallas kernels for 0% -> 18%
where the time goes in v2:
time: 99.6 us; the launch traced here: 99.3 us
  Pallas kernels  36.9 us (37%)
  starting transfers between devices  36.6 us (37%)
  waiting for transfers between devices  13.1 us (13%)
  local copies, waits for them, and re-layouts  10.1 us (10%)
  other arithmetic  2.34 us (2%)
    ppermute x24, starting transfers between devices, shifted(): return lax.ppermute(value, axis, pairs)  34.3 us
    pallas_call x2, Pallas kernels, gate_up(): pl.pallas_call(functools.partial(gate_up_kernel, len(parts), acc is not N...  27.3 us
    ppermute x24, waiting for transfers between devices, shifted(): return lax.ppermute(value, axis, pairs)  12.8 us
    unnamed x2, local copies, waits for them, and re-layouts  9.35 us
    pallas_call x2, Pallas kernels, down(): pl.pallas_call(down_kernel, grid=(width // block,), in_specs=[pl.BlockSpe...  8.79 us
    ppermute x10, starting transfers between devices, other_core(): return lax.ppermute(value, 'expert', [(i, i ^ 1) for i in range(size)])  2.32 us
  transfers between devices with their start and end apart: 34, of which 10 were waited for; matrix products, arithmetic and copies ran while one was open for 2% of the time, Pallas kernels for 18%

profile of v2, /device:TPU:0, one launch (start us, length us, event | category | flops | bytes accessed | tf_op | source)
XLA Modules:
  0.0 99.3 jit_solution(4381659382847658865)
XLA Ops:
  0.0 0.8 fusion
  0.8 3.1 %collective-permute-start.10 = (bf16[4,3584]{1,0:T(4,128)(2,1)S(1)}, bf16[4,3584]{1,0:T(4,128)(2,1)S(1)}, u32[]{:S(2)}, u32[]{:S(2)}) collective-permute-start(bf16[4,3584]{1,0:T(4,128)(2,1)S(1)} %get-tuple-element.49), channel_id=1, source_target_pairs={{0,2},{1,3},{2,4},{3,5},{4,6},{5,7},{6,0},{7,1},{8,10},{9,11},{10,... | collective-permute-start | bytes 86024 | tf_op jit(solution)/shard_map/ppermute | solution.py:29
  3.9 2.6 %collective-permute-start.11 = (bf16[4,3584]{1,0:T(4,128)(2,1)S(1)}, bf16[4,3584]{1,0:T(4,128)(2,1)S(1)}, u32[]{:S(2)}, u32[]{:S(2)}) collective-permute-start(bf16[4,3584]{1,0:T(4,128)(2,1)S(1)} %get-tuple-element.49), channel_id=1, source_target_pairs={{0,4},{1,5},{2,6},{3,7},{4,0},{5,1},{6,2},{7,3},{8,12},{9,13},{10,... | collective-permute-start | bytes 86024 | tf_op jit(solution)/shard_map/ppermute | solution.py:29
  6.5 1.3 %collective-permute-start.12 = (bf16[4,3584]{1,0:T(4,128)(2,1)S(1)}, bf16[4,3584]{1,0:T(4,128)(2,1)S(1)}, u32[]{:S(2)}, u32[]{:S(2)}) collective-permute-start(bf16[4,3584]{1,0:T(4,128)(2,1)S(1)} %get-tuple-element.49), channel_id=1, source_target_pairs={{0,6},{1,7},{2,0},{3,1},{4,2},{5,3},{6,4},{7,5},{8,14},{9,15},{10,... | collective-permute-start | bytes 86024 | tf_op jit(solution)/shard_map/ppermute | solution.py:29
  7.8 0.7 convert_element_type.36
  8.5 0.8 select_reduce_fusion
  9.3 0.7 collective-permute-start
  10.0 0.3 collective-permute-start.1
  10.3 2.8 %collective-permute-start.2 = (bf16[4,3712]{1,0:T(4,128)(2,1)S(1)}, bf16[4,3712]{1,0:T(4,128)(2,1)S(1)}, u32[]{:S(2)}, u32[]{:S(2)}) collective-permute-start(bf16[4,3712]{1,0:T(4,128)(2,1)S(1)} %pad_maximum_fusion.3), channel_id=1, source_target_pairs={{0,6},{1,7},{2,0},{3,1},{4,2},{5,3},{6,4},{7,5},{8,14},{9,15},{10,... | collective-permute-start | bytes 89096 | tf_op jit(solution)/shard_map/ppermute | solution.py:29
  13.2 1.5 %collective-permute-start.13 = (bf16[16,3584]{1,0:T(8,128)(2,1)S(1)}, bf16[16,3584]{1,0:T(8,128)(2,1)S(1)}, u32[]{:S(2)}, u32[]{:S(2)}) collective-permute-start(bf16[16,3584]{1,0:T(8,128)(2,1)S(1)} %pad_maximum_fusion.1.refs_0_), channel_id=1, source_target_pairs={{0,8},{8,16},{16,24},{24,0},{1,9},{9,17},{17,25},{25,1},{2,10},{10... | collective-permute-start | bytes 344072 | tf_op jit(solution)/shard_map/ppermute | solution.py:29
  14.8 1.5 %collective-permute-start.14 = (bf16[16,3584]{1,0:T(8,128)(2,1)S(1)}, bf16[16,3584]{1,0:T(8,128)(2,1)S(1)}, u32[]{:S(2)}, u32[]{:S(2)}) collective-permute-start(bf16[16,3584]{1,0:T(8,128)(2,1)S(1)} %pad_maximum_fusion.1.refs_0_), channel_id=1, source_target_pairs={{0,16},{8,24},{16,0},{24,8},{1,17},{9,25},{17,1},{25,9},{2,18},{10... | collective-permute-start | bytes 344072 | tf_op jit(solution)/shard_map/ppermute | solution.py:29
  16.4 0.8 collective-permute-start.3
  17.2 1.5 %collective-permute-start.4 = (bf16[16,3712]{1,0:T(8,128)(2,1)S(1)}, bf16[16,3712]{1,0:T(8,128)(2,1)S(1)}, u32[]{:S(2)}, u32[]{:S(2)}) collective-permute-start(bf16[16,3712]{1,0:T(8,128)(2,1)S(1)} %pad_maximum_fusion.refs_0_), channel_id=1, source_target_pairs={{0,16},{8,24},{16,0},{24,8},{1,17},{9,25},{17,1},{25,9},{2,18},{10... | collective-permute-start | bytes 356360 | tf_op jit(solution)/shard_map/ppermute | solution.py:29
  18.8 1.4 %collective-permute-start.5 = (bf16[16,3712]{1,0:T(8,128)(2,1)S(1)}, bf16[16,3712]{1,0:T(8,128)(2,1)S(1)}, u32[]{:S(2)}, u32[]{:S(2)}) collective-permute-start(bf16[16,3712]{1,0:T(8,128)(2,1)S(1)} %pad_maximum_fusion.refs_0_), channel_id=1, source_target_pairs={{0,24},{8,0},{16,8},{24,16},{1,25},{9,1},{17,9},{25,17},{2,26},{10... | collective-permute-start | bytes 356360 | tf_op jit(solution)/shard_map/ppermute | solution.py:29
  20.3 0.6 collective-permute-start.15
  20.9 3.1 %collective-permute-done.14.refs_2_ = bf16[16,3584]{1,0:T(8,128)(2,1)S(1)} collective-permute-done((bf16[16,3584]{1,0:T(8,128)(2,1)S(1)}, bf16[16,3584]{1,0:T(8,128)(2,1)S(1)}, u32[]{:S(2)}, u32[]{:S(2)}) %collective-permute-start.14) | collective-permute-done | bytes 114720 | tf_op jit(solution)/shard_map/ppermute | solution.py:29
  24.0 1.7 %collective-permute-done.15.refs_3_ = bf16[16,3584]{1,0:T(8,128)(2,1)S(1)} collective-permute-done((bf16[16,3584]{1,0:T(8,128)(2,1)S(1)}, bf16[16,3584]{1,0:T(8,128)(2,1)S(1)}, u32[]{:S(2)}, u32[]{:S(2)}) %collective-permute-start.15) | collective-permute-done | bytes 114720 | tf_op jit(solution)/shard_map/ppermute | solution.py:29
  25.7 0.5 collective-permute-start.17
  26.2 0.4 collective-permute-start.19
  27.0 0.3 collective-permute-start.8
  27.3 0.2 collective-permute-start.9
  27.5 0.2 collective-permute-done.19.refs_7_
  27.7 13.0 %shard_map.64 = (f32[128,2048]{1,0:T(8,128)S(1)}, f32[128,2048]{1,0:T(8,128)S(1)}) custom-call(bf16[16,3584]{1,0:T(8,128)(2,1)S(1)} %pad_maximum_fusion.1.refs_0_, bf16[16,3584]{1,0:T(8,128)(2,1)S(1)} %collective-permute-done.13.refs_1_, bf16[16,3584]{1,0:T(8,128)(2,1)S(1)} %collective-permute-done.14.refs_2_, ...), custom_call_target="tpu_custom_call" | custom-call | flops 3758096384 | bytes 29360128 | tf_op jit(solution)/shard_map/pallas_call | solution.py:105
  40.7 14.2 %shard_map.65.hidden_ref = bf16[128,2048]{1,0:T(8,128)(2,1)S(1)} custom-call(bf16[16,3712]{1,0:T(8,128)(2,1)S(1)} %pad_maximum_fusion.refs_0_, bf16[16,3712]{1,0:T(8,128)(2,1)S(1)} %collective-permute-done.3.refs_1_, bf16[16,3712]{1,0:T(8,128)(2,1)S(1)} %collective-permute-done.4.refs_2_, bf16[16,3712]{1,0:T(8,128)(2,1)S(1)} %collective-permute-done.5.refs_3_, ...), custom_call_target="tpu_custom_call" | custom-call | flops 3758096384 | bytes 29360128 | tf_op jit(solution)/shard_map/pallas_call | solution.py:105
  55.0 9.3 %copy-done = bf16[1,2048,7168]{2,1,0:T(8,128)(2,1)S(1)} copy-done((bf16[1,2048,7168]{2,1,0:T(8,128)(2,1)S(1)}, bf16[1,2048,7168]{2,1,0:T(8,128)(2,1)}, u32[]{:S(2)}) %copy-start) | copy-done | bytes 29360152
  64.3 4.4 %shard_map.66 = (bf16[64,3584]{1,0:T(8,128)(2,1)S(1)}, bf16[64,3584]{1,0:T(8,128)(2,1)S(1)}) custom-call(bf16[128,2048]{1,0:T(8,128)(2,1)S(1)} %shard_map.65.hidden_ref, bf16[1,2048,7168]{2,1,0:T(8,128)(2,1)S(1)} %copy-done, s32[1]{0:T(128)} %bitcast.me_ref, bf16[16,128]{1,0:T(8,128)(2,1)S(1)} %slice.40.refs_0_, bf16[16,128]{1,0:T(8,128)(2,1)S(1)} %slice.41.refs_1_, ...), custom_call_target="tpu_custom_call" | custom-call | flops 1879048192 | bytes 14680064 | tf_op jit(solution)/shard_map/pallas_call | solution.py:139
  68.7 0.4 collective-permute-start.20
  69.2 4.4 %shard_map.69 = (bf16[64,3584]{1,0:T(8,128)(2,1)S(1)}, bf16[64,3584]{1,0:T(8,128)(2,1)S(1)}) custom-call(bf16[128,2048]{1,0:T(8,128)(2,1)S(1)} %shard_map.65.hidden_ref, bf16[1,2048,7168]{2,1,0:T(8,128)(2,1)S(1)} %copy-done, s32[1]{0:T(128)} %bitcast.me_ref, bf16[16,128]{1,0:T(8,128)(2,1)S(1)} %slice.40.refs_0_, bf16[16,128]{1,0:T(8,128)(2,1)S(1)} %slice.41.refs_1_, ...), custom_call_target="tpu_custom_call" | custom-call | flops 1879048192 | bytes 14680064 | tf_op jit(solution)/shard_map/pallas_call | solution.py:139
  73.6 0.2 collective-permute-start.27
  73.8 0.3 shard_map.67
  74.1 2.2 %collective-permute-start.21 = (bf16[16,3584]{1,0:T(8,128)(2,1)S(1)}, bf16[16,3584]{1,0:T(8,128)(2,1)S(1)}, u32[]{:S(2)}, u32[]{:S(2)}) collective-permute-start(bf16[16,3584]{1,0:T(8,128)(2,1)S(1)} %get-tuple-element.32), channel_id=1, source_target_pairs={{0,24},{8,0},{16,8},{24,16},{1,25},{9,1},{17,9},{25,17},{2,26},{10... | collective-permute-start | bytes 344072 | tf_op jit(solution)/shard_map/ppermute | solution.py:29
  76.3 0.8 collective-permute-start.22
  77.1 0.5 collective-permute-start.23
  77.7 0.3 shard_map.70
  77.9 2.5 %collective-permute-start.28 = (bf16[16,3584]{1,0:T(8,128)(2,1)S(1)}, bf16[16,3584]{1,0:T(8,128)(2,1)S(1)}, u32[]{:S(2)}, u32[]{:S(2)}) collective-permute-start(bf16[16,3584]{1,0:T(8,128)(2,1)S(1)} %get-tuple-element.42), channel_id=1, source_target_pairs={{0,24},{8,0},{16,8},{24,16},{1,25},{9,1},{17,9},{25,17},{2,26},{10... | collective-permute-start | bytes 344072 | tf_op jit(solution)/shard_map/ppermute | solution.py:29
  80.4 1.2 %collective-permute-start.29 = (bf16[16,3584]{1,0:T(8,128)(2,1)S(1)}, bf16[16,3584]{1,0:T(8,128)(2,1)S(1)}, u32[]{:S(2)}, u32[]{:S(2)}) collective-permute-start(bf16[16,3584]{1,0:T(8,128)(2,1)S(1)} %get-tuple-element.43), channel_id=1, source_target_pairs={{0,16},{8,24},{16,0},{24,8},{1,17},{9,25},{17,1},{25,9},{2,18},{10... | collective-permute-start | bytes 344072 | tf_op jit(solution)/shard_map/ppermute | solution.py:29
  81.6 1.0 collective-permute-start.30
  82.6 2.2 %collective-permute-done.22.refs_2_ = bf16[16,3584]{1,0:T(8,128)(2,1)S(1)} collective-permute-done((bf16[16,3584]{1,0:T(8,128)(2,1)S(1)}, bf16[16,3584]{1,0:T(8,128)(2,1)S(1)}, u32[]{:S(2)}, u32[]{:S(2)}) %collective-permute-start.22) | collective-permute-done | bytes 114720 | tf_op jit(solution)/shard_map/ppermute | solution.py:29
  84.8 0.2 shard_map.68
  85.0 2.8 %collective-permute-start.24 = (bf16[4,3584]{1,0:T(4,128)(2,1)S(1)}, bf16[4,3584]{1,0:T(4,128)(2,1)S(1)}, u32[]{:S(2)}, u32[]{:S(2)}) collective-permute-start(bf16[4,3584]{1,0:T(4,128)(2,1)S(1)} %get-tuple-element.36), channel_id=1, source_target_pairs={{0,6},{1,7},{2,0},{3,1},{4,2},{5,3},{6,4},{7,5},{8,14},{9,15},{10,... | collective-permute-start | bytes 86024 | tf_op jit(solution)/shard_map/ppermute | solution.py:29
  87.8 0.9 collective-permute-start.26
  88.8 0.2 shard_map.71
  89.0 2.9 %collective-permute-start.31 = (bf16[4,3584]{1,0:T(4,128)(2,1)S(1)}, bf16[4,3584]{1,0:T(4,128)(2,1)S(1)}, u32[]{:S(2)}, u32[]{:S(2)}) collective-permute-start(bf16[4,3584]{1,0:T(4,128)(2,1)S(1)} %get-tuple-element.46), channel_id=1, source_target_pairs={{0,6},{1,7},{2,0},{3,1},{4,2},{5,3},{6,4},{7,5},{8,14},{9,15},{10,... | collective-permute-start | bytes 86024 | tf_op jit(solution)/shard_map/ppermute | solution.py:29
  91.9 1.1 %collective-permute-start.32 = (bf16[4,3584]{1,0:T(4,128)(2,1)S(1)}, bf16[4,3584]{1,0:T(4,128)(2,1)S(1)}, u32[]{:S(2)}, u32[]{:S(2)}) collective-permute-start(bf16[4,3584]{1,0:T(4,128)(2,1)S(1)} %get-tuple-element.47), channel_id=1, source_target_pairs={{0,4},{1,5},{2,6},{3,7},{4,0},{5,1},{6,2},{7,3},{8,12},{9,13},{10,... | collective-permute-start | bytes 86024 | tf_op jit(solution)/shard_map/ppermute | solution.py:29
  93.0 0.7 collective-permute-done.26
  93.8 2.8 %collective-permute-done.32 = bf16[4,3584]{1,0:T(4,128)(2,1)S(1)} collective-permute-done((bf16[4,3584]{1,0:T(4,128)(2,1)S(1)}, bf16[4,3584]{1,0:T(4,128)(2,1)S(1)}, u32[]{:S(2)}, u32[]{:S(2)}) %collective-permute-start.32) | collective-permute-done | bytes 28704 | tf_op jit(solution)/shard_map/ppermute | solution.py:29
  96.6 2.0 %collective-permute-done.33 = bf16[4,3584]{1,0:T(4,128)(2,1)S(1)} collective-permute-done((bf16[4,3584]{1,0:T(4,128)(2,1)S(1)}, bf16[4,3584]{1,0:T(4,128)(2,1)S(1)}, u32[]{:S(2)}, u32[]{:S(2)}) %collective-permute-start.33) | collective-permute-done | bytes 28704 | tf_op jit(solution)/shard_map/ppermute | solution.py:29
  98.7 0.7 pad_maximum_fusion.2
  (47 shorter events, 0.9 us)
Async XLA Ops:
  0.8 9.6 %collective-permute-start.10 = (bf16[4,3584]{1,0:T(4,128)(2,1)S(1)}, bf16[4,3584]{1,0:T(4,128)(2,1)S(1)}, u32[]{:S(2)}, u32[]{:S(2)}) collective-permute-start(bf16[4,3584]{1,0:T(4,128)(2,1)S(1)} %get-tuple-element.49), channel_id=1, source_target_pairs={{0,2},{1,3},{2,4},{3,5},{4,6},{5,7},{6,0},{7,1},{8,10},{9,11},{10,... | collective-permute-start | bytes 86024 | tf_op jit(solution)/shard_map/ppermute | solution.py:29
  3.9 9.3 %collective-permute-start.11 = (bf16[4,3584]{1,0:T(4,128)(2,1)S(1)}, bf16[4,3584]{1,0:T(4,128)(2,1)S(1)}, u32[]{:S(2)}, u32[]{:S(2)}) collective-permute-start(bf16[4,3584]{1,0:T(4,128)(2,1)S(1)} %get-tuple-element.49), channel_id=1, source_target_pairs={{0,4},{1,5},{2,6},{3,7},{4,0},{5,1},{6,2},{7,3},{8,12},{9,13},{10,... | collective-permute-start | bytes 86024 | tf_op jit(solution)/shard_map/ppermute | solution.py:29
  6.5 6.7 %collective-permute-start.12 = (bf16[4,3584]{1,0:T(4,128)(2,1)S(1)}, bf16[4,3584]{1,0:T(4,128)(2,1)S(1)}, u32[]{:S(2)}, u32[]{:S(2)}) collective-permute-start(bf16[4,3584]{1,0:T(4,128)(2,1)S(1)} %get-tuple-element.49), channel_id=1, source_target_pairs={{0,6},{1,7},{2,0},{3,1},{4,2},{5,3},{6,4},{7,5},{8,14},{9,15},{10,... | collective-permute-start | bytes 86024 | tf_op jit(solution)/shard_map/ppermute | solution.py:29
  9.3 7.0 %collective-permute-start = (bf16[4,3712]{1,0:T(4,128)(2,1)S(1)}, bf16[4,3712]{1,0:T(4,128)(2,1)S(1)}, u32[]{:S(2)}, u32[]{:S(2)}) collective-permute-start(bf16[4,3712]{1,0:T(4,128)(2,1)S(1)} %pad_maximum_fusion.3), channel_id=1, source_target_pairs={{0,2},{1,3},{2,4},{3,5},{4,6},{5,7},{6,0},{7,1},{8,10},{9,11},{10,... | collective-permute-start | bytes 89096 | tf_op jit(solution)/shard_map/ppermute | solution.py:29
  10.0 6.3 %collective-permute-start.1 = (bf16[4,3712]{1,0:T(4,128)(2,1)S(1)}, bf16[4,3712]{1,0:T(4,128)(2,1)S(1)}, u32[]{:S(2)}, u32[]{:S(2)}) collective-permute-start(bf16[4,3712]{1,0:T(4,128)(2,1)S(1)} %pad_maximum_fusion.3), channel_id=1, source_target_pairs={{0,4},{1,5},{2,6},{3,7},{4,0},{5,1},{6,2},{7,3},{8,12},{9,13},{10,... | collective-permute-start | bytes 89096 | tf_op jit(solution)/shard_map/ppermute | solution.py:29
  10.3 6.0 %collective-permute-start.2 = (bf16[4,3712]{1,0:T(4,128)(2,1)S(1)}, bf16[4,3712]{1,0:T(4,128)(2,1)S(1)}, u32[]{:S(2)}, u32[]{:S(2)}) collective-permute-start(bf16[4,3712]{1,0:T(4,128)(2,1)S(1)} %pad_maximum_fusion.3), channel_id=1, source_target_pairs={{0,6},{1,7},{2,0},{3,1},{4,2},{5,3},{6,4},{7,5},{8,14},{9,15},{10,... | collective-permute-start | bytes 89096 | tf_op jit(solution)/shard_map/ppermute | solution.py:29
  13.2 7.0 %collective-permute-start.13 = (bf16[16,3584]{1,0:T(8,128)(2,1)S(1)}, bf16[16,3584]{1,0:T(8,128)(2,1)S(1)}, u32[]{:S(2)}, u32[]{:S(2)}) collective-permute-start(bf16[16,3584]{1,0:T(8,128)(2,1)S(1)} %pad_maximum_fusion.1.refs_0_), channel_id=1, source_target_pairs={{0,8},{8,16},{16,24},{24,0},{1,9},{9,17},{17,25},{25,1},{2,10},{10... | collective-permute-start | bytes 344072 | tf_op jit(solution)/shard_map/ppermute | solution.py:29
  14.8 9.2 %collective-permute-start.14 = (bf16[16,3584]{1,0:T(8,128)(2,1)S(1)}, bf16[16,3584]{1,0:T(8,128)(2,1)S(1)}, u32[]{:S(2)}, u32[]{:S(2)}) collective-permute-start(bf16[16,3584]{1,0:T(8,128)(2,1)S(1)} %pad_maximum_fusion.1.refs_0_), channel_id=1, source_target_pairs={{0,16},{8,24},{16,0},{24,8},{1,17},{9,25},{17,1},{25,9},{2,18},{10... | collective-permute-start | bytes 344072 | tf_op jit(solution)/shard_map/ppermute | solution.py:29
  16.4 9.2 %collective-permute-start.3 = (bf16[16,3712]{1,0:T(8,128)(2,1)S(1)}, bf16[16,3712]{1,0:T(8,128)(2,1)S(1)}, u32[]{:S(2)}, u32[]{:S(2)}) collective-permute-start(bf16[16,3712]{1,0:T(8,128)(2,1)S(1)} %pad_maximum_fusion.refs_0_), channel_id=1, source_target_pairs={{0,8},{8,16},{16,24},{24,0},{1,9},{9,17},{17,25},{25,1},{2,10},{10... | collective-permute-start | bytes 356360 | tf_op jit(solution)/shard_map/ppermute | solution.py:29
  17.2 8.9 %collective-permute-start.4 = (bf16[16,3712]{1,0:T(8,128)(2,1)S(1)}, bf16[16,3712]{1,0:T(8,128)(2,1)S(1)}, u32[]{:S(2)}, u32[]{:S(2)}) collective-permute-start(bf16[16,3712]{1,0:T(8,128)(2,1)S(1)} %pad_maximum_fusion.refs_0_), channel_id=1, source_target_pairs={{0,16},{8,24},{16,0},{24,8},{1,17},{9,25},{17,1},{25,9},{2,18},{10... | collective-permute-start | bytes 356360 | tf_op jit(solution)/shard_map/ppermute | solution.py:29
  18.8 7.5 %collective-permute-start.5 = (bf16[16,3712]{1,0:T(8,128)(2,1)S(1)}, bf16[16,3712]{1,0:T(8,128)(2,1)S(1)}, u32[]{:S(2)}, u32[]{:S(2)}) collective-permute-start(bf16[16,3712]{1,0:T(8,128)(2,1)S(1)} %pad_maximum_fusion.refs_0_), channel_id=1, source_target_pairs={{0,24},{8,0},{16,8},{24,16},{1,25},{9,1},{17,9},{25,17},{2,26},{10... | collective-permute-start | bytes 356360 | tf_op jit(solution)/shard_map/ppermute | solution.py:29
  20.3 5.4 %collective-permute-start.15 = (bf16[16,3584]{1,0:T(8,128)(2,1)S(1)}, bf16[16,3584]{1,0:T(8,128)(2,1)S(1)}, u32[]{:S(2)}, u32[]{:S(2)}) collective-permute-start(bf16[16,3584]{1,0:T(8,128)(2,1)S(1)} %pad_maximum_fusion.1.refs_0_), channel_id=1, source_target_pairs={{0,24},{8,0},{16,8},{24,16},{1,25},{9,1},{17,9},{25,17},{2,26},{10... | collective-permute-start | bytes 344072 | tf_op jit(solution)/shard_map/ppermute | solution.py:29
  24.0 2.7 %collective-permute-start.6 = (bf16[16,3712]{1,0:T(8,128)(2,1)S(1)}, bf16[16,3712]{1,0:T(8,128)(2,1)S(1)}, u32[]{:S(2)}, u32[]{:S(2)}) collective-permute-start(bf16[16,3712]{1,0:T(8,128)(2,1)S(1)} %pad_maximum_fusion.refs_0_), channel_id=1, source_target_pairs={{0,1},{1,0},{2,3},{3,2},{4,5},{5,4},{6,7},{7,6},{8,9},{9,8},{10,11... | collective-permute-start | bytes 356360 | tf_op jit(solution)/shard_map/ppermute | solution.py:33
  25.6 1.3 %collective-permute-start.16 = (bf16[16,3584]{1,0:T(8,128)(2,1)S(1)}, bf16[16,3584]{1,0:T(8,128)(2,1)S(1)}, u32[]{:S(2)}, u32[]{:S(2)}) collective-permute-start(bf16[16,3584]{1,0:T(8,128)(2,1)S(1)} %pad_maximum_fusion.1.refs_0_), channel_id=1, source_target_pairs={{0,1},{1,0},{2,3},{3,2},{4,5},{5,4},{6,7},{7,6},{8,9},{9,8},{10,11... | collective-permute-start | bytes 344072 | tf_op jit(solution)/shard_map/ppermute | solution.py:33
  25.7 1.6 %collective-permute-start.17 = (bf16[16,3584]{1,0:T(8,128)(2,1)S(1)}, bf16[16,3584]{1,0:T(8,128)(2,1)S(1)}, u32[]{:S(2)}, u32[]{:S(2)}) collective-permute-start(bf16[16,3584]{1,0:T(8,128)(2,1)S(1)} %collective-permute-done.13.refs_1_), channel_id=1, source_target_pairs={{0,1},{1,0},{2,3},{3,2},{4,5},{5,4},{6,7},{7,6},{8,9},{9,8},{10,11... | collective-permute-start | bytes 344072 | tf_op jit(solution)/shard_map/ppermute | solution.py:33
  26.2 1.3 %collective-permute-start.18 = (bf16[16,3584]{1,0:T(8,128)(2,1)S(1)}, bf16[16,3584]{1,0:T(8,128)(2,1)S(1)}, u32[]{:S(2)}, u32[]{:S(2)}) collective-permute-start(bf16[16,3584]{1,0:T(8,128)(2,1)S(1)} %collective-permute-done.14.refs_2_), channel_id=1, source_target_pairs={{0,1},{1,0},{2,3},{3,2},{4,5},{5,4},{6,7},{7,6},{8,9},{9,8},{10,11... | collective-permute-start | bytes 344072 | tf_op jit(solution)/shard_map/ppermute | solution.py:33
  26.2 1.4 %collective-permute-start.19 = (bf16[16,3584]{1,0:T(8,128)(2,1)S(1)}, bf16[16,3584]{1,0:T(8,128)(2,1)S(1)}, u32[]{:S(2)}, u32[]{:S(2)}) collective-permute-start(bf16[16,3584]{1,0:T(8,128)(2,1)S(1)} %collective-permute-done.15.refs_3_), channel_id=1, source_target_pairs={{0,1},{1,0},{2,3},{3,2},{4,5},{5,4},{6,7},{7,6},{8,9},{9,8},{10,11... | collective-permute-start | bytes 344072 | tf_op jit(solution)/shard_map/ppermute | solution.py:33
  26.7 14.0 %collective-permute-start.7 = (bf16[16,3712]{1,0:T(8,128)(2,1)S(1)}, bf16[16,3712]{1,0:T(8,128)(2,1)S(1)}, u32[]{:S(2)}, u32[]{:S(2)}) collective-permute-start(bf16[16,3712]{1,0:T(8,128)(2,1)S(1)} %collective-permute-done.3.refs_1_), channel_id=1, source_target_pairs={{0,1},{1,0},{2,3},{3,2},{4,5},{5,4},{6,7},{7,6},{8,9},{9,8},{10,11... | collective-permute-start | bytes 356360 | tf_op jit(solution)/shard_map/ppermute | solution.py:33
  27.0 13.7 %collective-permute-start.8 = (bf16[16,3712]{1,0:T(8,128)(2,1)S(1)}, bf16[16,3712]{1,0:T(8,128)(2,1)S(1)}, u32[]{:S(2)}, u32[]{:S(2)}) collective-permute-start(bf16[16,3712]{1,0:T(8,128)(2,1)S(1)} %collective-permute-done.4.refs_2_), channel_id=1, source_target_pairs={{0,1},{1,0},{2,3},{3,2},{4,5},{5,4},{6,7},{7,6},{8,9},{9,8},{10,11... | collective-permute-start | bytes 356360 | tf_op jit(solution)/shard_map/ppermute | solution.py:33
  27.3 13.4 %collective-permute-start.9 = (bf16[16,3712]{1,0:T(8,128)(2,1)S(1)}, bf16[16,3712]{1,0:T(8,128)(2,1)S(1)}, u32[]{:S(2)}, u32[]{:S(2)}) collective-permute-start(bf16[16,3712]{1,0:T(8,128)(2,1)S(1)} %collective-permute-done.5.refs_3_), channel_id=1, source_target_pairs={{0,1},{1,0},{2,3},{3,2},{4,5},{5,4},{6,7},{7,6},{8,9},{9,8},{10,11... | collective-permute-start | bytes 356360 | tf_op jit(solution)/shard_map/ppermute | solution.py:33
  55.0 9.4 %copy-start = (bf16[1,2048,7168]{2,1,0:T(8,128)(2,1)S(1)}, bf16[1,2048,7168]{2,1,0:T(8,128)(2,1)}, u32[]{:S(2)}) copy-start(bf16[1,2048,7168]{2,1,0:T(8,128)(2,1)} %down_ref.3) | copy-start | bytes 88080384
  68.7 5.1 %collective-permute-start.20 = (bf16[64,3584]{1,0:T(8,128)(2,1)S(1)}, bf16[64,3584]{1,0:T(8,128)(2,1)S(1)}, u32[]{:S(2)}, u32[]{:S(2)}) collective-permute-start(bf16[64,3584]{1,0:T(8,128)(2,1)S(1)} %get-tuple-element.30), channel_id=1, source_target_pairs={{0,1},{1,0},{2,3},{3,2},{4,5},{5,4},{6,7},{7,6},{8,9},{9,8},{10,11... | collective-permute-start | bytes 1376264 | tf_op jit(solution)/shard_map/ppermute | solution.py:33
  73.6 4.1 %collective-permute-start.27 = (bf16[64,3584]{1,0:T(8,128)(2,1)S(1)}, bf16[64,3584]{1,0:T(8,128)(2,1)S(1)}, u32[]{:S(2)}, u32[]{:S(2)}) collective-permute-start(bf16[64,3584]{1,0:T(8,128)(2,1)S(1)} %get-tuple-element.40), channel_id=1, source_target_pairs={{0,1},{1,0},{2,3},{3,2},{4,5},{5,4},{6,7},{7,6},{8,9},{9,8},{10,11... | collective-permute-start | bytes 1376264 | tf_op jit(solution)/shard_map/ppermute | solution.py:33
  74.1 7.5 %collective-permute-start.21 = (bf16[16,3584]{1,0:T(8,128)(2,1)S(1)}, bf16[16,3584]{1,0:T(8,128)(2,1)S(1)}, u32[]{:S(2)}, u32[]{:S(2)}) collective-permute-start(bf16[16,3584]{1,0:T(8,128)(2,1)S(1)} %get-tuple-element.32), channel_id=1, source_target_pairs={{0,24},{8,0},{16,8},{24,16},{1,25},{9,1},{17,9},{25,17},{2,26},{10... | collective-permute-start | bytes 344072 | tf_op jit(solution)/shard_map/ppermute | solution.py:29
  76.3 8.5 %collective-permute-start.22 = (bf16[16,3584]{1,0:T(8,128)(2,1)S(1)}, bf16[16,3584]{1,0:T(8,128)(2,1)S(1)}, u32[]{:S(2)}, u32[]{:S(2)}) collective-permute-start(bf16[16,3584]{1,0:T(8,128)(2,1)S(1)} %get-tuple-element.33), channel_id=1, source_target_pairs={{0,16},{8,24},{16,0},{24,8},{1,17},{9,25},{17,1},{25,9},{2,18},{10... | collective-permute-start | bytes 344072 | tf_op jit(solution)/shard_map/ppermute | solution.py:29
  77.1 7.7 %collective-permute-start.23 = (bf16[16,3584]{1,0:T(8,128)(2,1)S(1)}, bf16[16,3584]{1,0:T(8,128)(2,1)S(1)}, u32[]{:S(2)}, u32[]{:S(2)}) collective-permute-start(bf16[16,3584]{1,0:T(8,128)(2,1)S(1)} %get-tuple-element.34), channel_id=1, source_target_pairs={{0,8},{8,16},{16,24},{24,0},{1,9},{9,17},{17,25},{25,1},{2,10},{10... | collective-permute-start | bytes 344072 | tf_op jit(solution)/shard_map/ppermute | solution.py:29
  77.9 9.9 %collective-permute-start.28 = (bf16[16,3584]{1,0:T(8,128)(2,1)S(1)}, bf16[16,3584]{1,0:T(8,128)(2,1)S(1)}, u32[]{:S(2)}, u32[]{:S(2)}) collective-permute-start(bf16[16,3584]{1,0:T(8,128)(2,1)S(1)} %get-tuple-element.42), channel_id=1, source_target_pairs={{0,24},{8,0},{16,8},{24,16},{1,25},{9,1},{17,9},{25,17},{2,26},{10... | collective-permute-start | bytes 344072 | tf_op jit(solution)/shard_map/ppermute | solution.py:29
  80.4 8.4 %collective-permute-start.29 = (bf16[16,3584]{1,0:T(8,128)(2,1)S(1)}, bf16[16,3584]{1,0:T(8,128)(2,1)S(1)}, u32[]{:S(2)}, u32[]{:S(2)}) collective-permute-start(bf16[16,3584]{1,0:T(8,128)(2,1)S(1)} %get-tuple-element.43), channel_id=1, source_target_pairs={{0,16},{8,24},{16,0},{24,8},{1,17},{9,25},{17,1},{25,9},{2,18},{10... | collective-permute-start | bytes 344072 | tf_op jit(solution)/shard_map/ppermute | solution.py:29
  81.6 7.2 %collective-permute-start.30 = (bf16[16,3584]{1,0:T(8,128)(2,1)S(1)}, bf16[16,3584]{1,0:T(8,128)(2,1)S(1)}, u32[]{:S(2)}, u32[]{:S(2)}) collective-permute-start(bf16[16,3584]{1,0:T(8,128)(2,1)S(1)} %get-tuple-element.44), channel_id=1, source_target_pairs={{0,8},{8,16},{16,24},{24,0},{1,9},{9,17},{17,25},{25,1},{2,10},{10... | collective-permute-start | bytes 344072 | tf_op jit(solution)/shard_map/ppermute | solution.py:29
  85.0 8.0 %collective-permute-start.24 = (bf16[4,3584]{1,0:T(4,128)(2,1)S(1)}, bf16[4,3584]{1,0:T(4,128)(2,1)S(1)}, u32[]{:S(2)}, u32[]{:S(2)}) collective-permute-start(bf16[4,3584]{1,0:T(4,128)(2,1)S(1)} %get-tuple-element.36), channel_id=1, source_target_pairs={{0,6},{1,7},{2,0},{3,1},{4,2},{5,3},{6,4},{7,5},{8,14},{9,15},{10,... | collective-permute-start | bytes 86024 | tf_op jit(solution)/shard_map/ppermute | solution.py:29
  87.8 5.2 %collective-permute-start.25 = (bf16[4,3584]{1,0:T(4,128)(2,1)S(1)}, bf16[4,3584]{1,0:T(4,128)(2,1)S(1)}, u32[]{:S(2)}, u32[]{:S(2)}) collective-permute-start(bf16[4,3584]{1,0:T(4,128)(2,1)S(1)} %get-tuple-element.37), channel_id=1, source_target_pairs={{0,4},{1,5},{2,6},{3,7},{4,0},{5,1},{6,2},{7,3},{8,12},{9,13},{10,... | collective-permute-start | bytes 86024 | tf_op jit(solution)/shard_map/ppermute | solution.py:29
  87.8 6.0 %collective-permute-start.26 = (bf16[4,3584]{1,0:T(4,128)(2,1)S(1)}, bf16[4,3584]{1,0:T(4,128)(2,1)S(1)}, u32[]{:S(2)}, u32[]{:S(2)}) collective-permute-start(bf16[4,3584]{1,0:T(4,128)(2,1)S(1)} %get-tuple-element.38), channel_id=1, source_target_pairs={{0,2},{1,3},{2,4},{3,5},{4,6},{5,7},{6,0},{7,1},{8,10},{9,11},{10,... | collective-permute-start | bytes 86024 | tf_op jit(solution)/shard_map/ppermute | solution.py:29
  89.0 4.8 %collective-permute-start.31 = (bf16[4,3584]{1,0:T(4,128)(2,1)S(1)}, bf16[4,3584]{1,0:T(4,128)(2,1)S(1)}, u32[]{:S(2)}, u32[]{:S(2)}) collective-permute-start(bf16[4,3584]{1,0:T(4,128)(2,1)S(1)} %get-tuple-element.46), channel_id=1, source_target_pairs={{0,6},{1,7},{2,0},{3,1},{4,2},{5,3},{6,4},{7,5},{8,14},{9,15},{10,... | collective-permute-start | bytes 86024 | tf_op jit(solution)/shard_map/ppermute | solution.py:29
  91.9 4.8 %collective-permute-start.32 = (bf16[4,3584]{1,0:T(4,128)(2,1)S(1)}, bf16[4,3584]{1,0:T(4,128)(2,1)S(1)}, u32[]{:S(2)}, u32[]{:S(2)}) collective-permute-start(bf16[4,3584]{1,0:T(4,128)(2,1)S(1)} %get-tuple-element.47), channel_id=1, source_target_pairs={{0,4},{1,5},{2,6},{3,7},{4,0},{5,1},{6,2},{7,3},{8,12},{9,13},{10,... | collective-permute-start | bytes 86024 | tf_op jit(solution)/shard_map/ppermute | solution.py:29
  93.0 5.7 %collective-permute-start.33 = (bf16[4,3584]{1,0:T(4,128)(2,1)S(1)}, bf16[4,3584]{1,0:T(4,128)(2,1)S(1)}, u32[]{:S(2)}, u32[]{:S(2)}) collective-permute-start(bf16[4,3584]{1,0:T(4,128)(2,1)S(1)} %get-tuple-element.48), channel_id=1, source_target_pairs={{0,2},{1,3},{2,4},{3,5},{4,6},{5,7},{6,0},{7,1},{8,10},{9,11},{10,... | collective-permute-start | bytes 86024 | tf_op jit(solution)/shard_map/ppermute | solution.py:29

commit v3 on v1

v3 whole, which is shorter than its diff:
```python
import functools

import jax
import jax.numpy as jnp
from jax import lax
from jax.experimental import pallas as pl
from jax.experimental.pallas import tpu as pltpu
from jax.sharding import PartitionSpec as P

EXP_GRP = 8
CAP = 2
LANES = 128
AXES = ("group", "expert")
VMEM = pltpu.VMEM
UNIT_BLOCK = 256
DOWN_BLOCK = 512
UP_RING = 2
DOWN_RING = 3


def in_vmem(value):
    return pltpu.with_memory_space_constraint(value, VMEM)


def in_hbm(value):
    return pltpu.with_memory_space_constraint(value, pltpu.HBM)


def whole_vmem(count):
    return [pl.BlockSpec(memory_space=VMEM)] * count


def shifted(value, axis, size, shift, unit=1):
    count = size // unit
    pairs = []
    for i in range(size):
        slot, low = i // unit, i % unit
        pairs.append((i, ((slot + shift) % count) * unit + low))
    return lax.ppermute(value, axis, pairs)


def other_core(value, size):
    return lax.ppermute(value, "expert", [(i, i ^ 1) for i in range(size)])


def pack_kernel(tokens_ref, ids_ref, weights_ref, out_ref):
    width = tokens_ref.shape[1]
    out_ref[:, :width] = tokens_ref[...]
    ids = ids_ref[...]
    weights = weights_ref[...].astype(jnp.float32)
    label = lax.broadcasted_iota(jnp.int32, (ids.shape[0], LANES), 1)
    route = jnp.zeros((ids.shape[0], LANES), jnp.float32)
    for k in range(ids.shape[1]):
        route += jnp.where(ids[:, k : k + 1] == label, weights[:, k : k + 1], 0.0)
    out_ref[:, width:] = route.astype(out_ref.dtype)


def pack(tokens, expert_ids, gate_weights):
    rows, width = tokens.shape
    return pl.pallas_call(
        pack_kernel,
        in_specs=whole_vmem(3),
        out_specs=whole_vmem(1)[0],
        out_shape=VMEM((rows, width + LANES), tokens.dtype),
        compiler_params=pltpu.CompilerParams(vmem_limit_bytes=2 * 1024 * 1024),
    )(tokens, expert_ids, gate_weights)


def fetch_kernel(jobs, sources, *refs):
    src_refs = refs[:sources]
    out_refs = refs[sources + 1 : sources + 1 + len(jobs)]
    mark_ref, sems = refs[-2:]
    copies = []
    for n, (source, first, columns) in enumerate(jobs):
        rows = src_refs[source].shape[1]
        size = rows // 4
        for i in range(4):
            copies.append(
                pltpu.make_async_copy(
                    src_refs[source].at[0, pl.ds(i * size, size), pl.ds(first, columns)],
                    out_refs[n].at[pl.ds(i * size, size), :],
                    sems.at[n * 4 + i],
                )
            )
    for copy in copies:
        copy.start()
    mark_ref[...] = jnp.zeros_like(mark_ref)
    for copy in copies:
        copy.wait()


def fetch(jobs, weights, after):
    rows = weights[0].shape[1]
    shapes = [VMEM((rows, columns), weights[0].dtype) for _, _, columns in jobs]
    amount = sum(2 * rows * columns for _, _, columns in jobs)
    hbm = pl.BlockSpec(memory_space=pltpu.HBM)
    *out, mark = pl.pallas_call(
        functools.partial(fetch_kernel, jobs, len(weights)),
        in_specs=[hbm] * len(weights) + [pl.BlockSpec(memory_space=pl.ANY)],
        out_specs=whole_vmem(len(jobs) + 1),
        out_shape=shapes + [jax.ShapeDtypeStruct((8, LANES), jnp.float32)],
        scratch_shapes=[pltpu.SemaphoreType.DMA((4 * len(jobs),))],
        compiler_params=pltpu.CompilerParams(vmem_limit_bytes=1024 * 1024),
        cost_estimate=pl.CostEstimate(flops=0, bytes_accessed=amount, transcendentals=0),
    )(*[in_hbm(w) for w in weights], after)
    return out, mark


def join_kernel(count, *refs):
    rows = refs[0].shape[0]
    out_ref = refs[-1]
    out_ref[...] = jnp.concatenate(
        [r[...].astype(jnp.float32) for r in refs[:count]], axis=0
    ).astype(out_ref.dtype)


def join(values, after):
    rows, width = values[0].shape
    return pl.pallas_call(
        functools.partial(join_kernel, len(values)),
        in_specs=whole_vmem(len(values)) + [pl.BlockSpec(memory_space=pl.ANY)],
        out_specs=whole_vmem(1)[0],
        out_shape=VMEM((rows * len(values), width), values[0].dtype),
        compiler_params=pltpu.CompilerParams(vmem_limit_bytes=8 * 1024 * 1024),
    )(*[in_vmem(v) for v in values], after)


def expert_kernel(plan, share, *refs):
    parts, gate_at, up_at, streamed = plan
    x_refs, rest = refs[:parts], refs[parts:]
    held, rest = rest[: 1 + len(set(r for r, _ in gate_at + up_at if r is not None))], rest
    count = len(held) - 1
    w_refs = rest[:count]
    up_hbm, down_hbm, me_ref, own_ref, far_ref = rest[count : count + 5]
    flat, hidden, mix, up_ring, down_ring, up_sem, down_sem = rest[count + 5 :]
    width, units = flat.shape[1], hidden.shape[1]
    blocks = units // UNIT_BLOCK
    downs = width // DOWN_BLOCK

    def up_copy(n):
        first = streamed[n] * UNIT_BLOCK
        return pltpu.make_async_copy(
            up_hbm.at[0, :, pl.ds(first, UNIT_BLOCK)], up_ring.at[n % UP_RING], up_sem.at[n % UP_RING]
        )

    def down_copy(d, slot):
        first = d * DOWN_BLOCK
        if not isinstance(d, int):
            first = pl.multiple_of(first, DOWN_BLOCK)
        return pltpu.make_async_copy(
            down_hbm.at[0, :, pl.ds(first, DOWN_BLOCK)], down_ring.at[slot], down_sem.at[slot]
        )

    for n in range(min(UP_RING, len(streamed))):
        up_copy(n).start()
    for d in range(min(DOWN_RING, downs)):
        down_copy(d, d).start()

    route = jnp.concatenate([r[:, width:] for r in x_refs], axis=0)
    rows = route.shape[0]
    slots = flat.shape[0]
    lane = lax.broadcasted_iota(jnp.int32, (8, LANES), 1)
    pick = jnp.where(lane == me_ref[0], 1.0, 0.0).astype(jnp.bfloat16)
    weight = lax.dot_general(
        pick, route, (((1,), (1,)), ((), ())), preferred_element_type=jnp.float32
    )
    named = jnp.where(weight > 0.0, 1.0, 0.0)
    source = lax.broadcasted_iota(jnp.int32, (rows, rows), 0)
    target = lax.broadcasted_iota(jnp.int32, (rows, rows), 1)
    before = (source // share == target // share) & (source < target)
    rank = jnp.dot(
        named.astype(jnp.bfloat16),
        jnp.where(before, 1.0, 0.0).astype(jnp.bfloat16),
        preferred_element_type=jnp.float32,
    )
    token = lax.broadcasted_iota(jnp.int32, (1, rows), 1)
    slot = (token // share) * CAP + rank[:1].astype(jnp.int32)
    place = lax.broadcasted_iota(jnp.int32, (slots, rows), 0)
    chosen = (place == slot) & (named[:1] > 0.0)
    select = jnp.where(chosen, 1.0, 0.0).astype(jnp.bfloat16)
    mix[...] = jnp.transpose(jnp.where(chosen, weight[:1], 0.0)).astype(jnp.bfloat16)

    @pl.loop(0, downs)
    def _(d):
        columns = pl.ds(pl.multiple_of(d * DOWN_BLOCK, DOWN_BLOCK), DOWN_BLOCK)
        x = jnp.concatenate([r[:, columns] for r in x_refs], axis=0)
        flat[:, columns] = jnp.dot(
            select, x, preferred_element_type=jnp.float32
        ).astype(jnp.bfloat16)

    stream_of = {b: n for n, b in enumerate(streamed)}
    fixed = [b for b in range(blocks) if b not in stream_of]
    order = []
    waiting = list(streamed)
    for b in fixed:
        order.append(b)
        take = -(-len(waiting) // (len(fixed) - len(order) + sum(o in stream_of for o in order) + 1))
        order += waiting[:take]
        waiting = waiting[take:]
    order += waiting
    for b in order:
        where, first = gate_at[b]
        gate = jnp.dot(
            flat[...], w_refs[where][:, first : first + UNIT_BLOCK],
            preferred_element_type=jnp.float32,
        )
        if b in stream_of:
            n = stream_of[b]
            up_copy(n).wait()
            up = jnp.dot(
                flat[...], up_ring[n % UP_RING], preferred_element_type=jnp.float32
            )
            if n + UP_RING < len(streamed):
                up_copy(n + UP_RING).start()
        else:
            where, first = up_at[b]
            up = jnp.dot(
                flat[...], w_refs[where][:, first : first + UNIT_BLOCK],
                preferred_element_type=jnp.float32,
            )
        hidden[:, b * UNIT_BLOCK : (b + 1) * UNIT_BLOCK] = (jax.nn.silu(gate) * up).astype(
            jnp.bfloat16
        )

    @pl.loop(0, downs)
    def _(d):
        slot_of = lax.rem(d, DOWN_RING)
        columns = pl.ds(pl.multiple_of(d * DOWN_BLOCK, DOWN_BLOCK), DOWN_BLOCK)
        down_copy(d, slot_of).wait()
        part = jnp.dot(hidden[...], down_ring[slot_of], preferred_element_type=jnp.float32)

        @pl.when(d + DOWN_RING < downs)
        def _():
            down_copy(d + DOWN_RING, slot_of).start()

        spread = jnp.dot(
            mix[...], part.astype(jnp.bfloat16), preferred_element_type=jnp.float32
        ).astype(jnp.bfloat16)
        own_ref[:, columns] = spread[: rows // 2]
        far_ref[:, columns] = spread[rows // 2 :]


def hold_kernel(*refs):
    pass


def hold(values, after):
    out = pl.pallas_call(
        hold_kernel,
        in_specs=[pl.BlockSpec(memory_space=pl.ANY)] * (len(values) + 1),
        out_specs=[pl.BlockSpec(memory_space=pl.ANY)] * len(values),
        out_shape=[jax.ShapeDtypeStruct(v.shape, v.dtype) for v in values],
        input_output_aliases={i: i for i in range(len(values))},
    )(*values, after)
    return list(out)


def run_expert(parts, held, gate_at, up_at, streamed, w_up, w_down, me, share):
    rows = sum(p.shape[0] for p in parts)
    depth, units = w_up.shape[1], w_up.shape[2]
    slots = rows // share * CAP
    half = VMEM((rows // 2, depth), jnp.bfloat16)
    hbm = pl.BlockSpec(memory_space=pltpu.HBM)
    ring = max(1, min(UP_RING, len(streamed)))
    scratch = 2 * (
        slots * (depth + units) + rows * max(slots, LANES)
        + ring * depth * UNIT_BLOCK + DOWN_RING * units * DOWN_BLOCK
    )
    work = 4 * 1024 * 1024 + 10 * rows * rows
    return pl.pallas_call(
        functools.partial(expert_kernel, (len(parts), gate_at, up_at, streamed), share),
        in_specs=whole_vmem(len(parts) + len(held))
        + [hbm, hbm, pl.BlockSpec(memory_space=pltpu.SMEM)],
        out_specs=whole_vmem(2),
        out_shape=(half, half),
        scratch_shapes=[
            VMEM((slots, depth), jnp.bfloat16),
            VMEM((slots, units), jnp.bfloat16),
            VMEM((rows, slots), jnp.bfloat16),
            VMEM((ring, depth, UNIT_BLOCK), jnp.bfloat16),
            VMEM((DOWN_RING, units, DOWN_BLOCK), jnp.bfloat16),
            pltpu.SemaphoreType.DMA((ring,)),
            pltpu.SemaphoreType.DMA((DOWN_RING,)),
        ],
        compiler_params=pltpu.CompilerParams(vmem_limit_bytes=scratch + work),
        cost_estimate=pl.CostEstimate(
            flops=6 * slots * depth * units, bytes_accessed=4 * depth * units, transcendentals=0
        ),
    )(*[in_vmem(p) for p in parts], *[in_vmem(w) for w in held], in_hbm(w_up), in_hbm(w_down), me)


def add_kernel(count, *refs):
    ins, outs = refs[:count], refs[count:]
    total = ins[0][...].astype(jnp.float32)
    for ref in ins[1:]:
        total = total + ref[...].astype(jnp.float32)
    total = total.astype(jnp.bfloat16)
    size = total.shape[0] // len(outs)
    for i, ref in enumerate(outs):
        ref[...] = total[i * size : (i + 1) * size]


def add_split(values, pieces):
    rows, width = values[0].shape
    block = 1792
    out = jax.ShapeDtypeStruct((rows // pieces, width), jnp.bfloat16)
    return pl.pallas_call(
        functools.partial(add_kernel, len(values)),
        grid=(width // block,),
        in_specs=[pl.BlockSpec((rows, block), lambda i: (0, i))] * len(values),
        out_specs=(pl.BlockSpec((rows // pieces, block), lambda i: (0, i)),) * pieces,
        out_shape=(out,) * pieces,
        compiler_params=pltpu.CompilerParams(vmem_limit_bytes=24 * 1024 * 1024),
    )(*values)


def give_back(own, far, groups, members):
    lines = members // 2
    planes = add_split([own, other_core(far, members)], groups)
    planes = [planes[0]] + [shifted(planes[s], "group", groups, -s) for s in range(1, groups)]
    column = add_split(planes, lines)
    column = [column[0]] + [
        shifted(column[s], "expert", members, -s, 2) for s in range(1, lines)
    ]
    total = column[0].astype(jnp.float32)
    for value in column[1:]:
        total = total + value.astype(jnp.float32)
    return total.astype(jnp.bfloat16)


def on_device(tokens, expert_ids, gate_weights, w_gate, w_up, w_down):
    groups = lax.axis_size("group")
    members = lax.axis_size("expert")
    split = members // EXP_GRP
    lines = members // 2
    me = lax.axis_index("group") * EXP_GRP + lax.axis_index("expert") // split
    me = me.astype(jnp.int32).reshape(1)
    units = w_gate.shape[2]
    blocks = units // UNIT_BLOCK
    early = -(-blocks // 2)
    ups = max(1, 3 * blocks // 8)

    packed = pack(tokens, expert_ids, gate_weights)
    line = [packed] + [shifted(packed, "expert", members, s, 2) for s in range(1, lines)]
    held, mark = fetch([(0, 0, early * UNIT_BLOCK)], [w_gate], packed)
    column = join(line, mark)
    planes = [column] + [shifted(column, "group", groups, s) for s in range(1, groups)]
    jobs, sources = [], []
    if early < blocks:
        jobs.append((0, early * UNIT_BLOCK, (blocks - early) * UNIT_BLOCK))
        sources.append(w_gate)
    jobs.append((len(sources), 0, ups * UNIT_BLOCK))
    sources.append(w_up)
    more, mark = fetch(jobs, sources, column)
    held = held + more
    gate_at = [
        (0, b * UNIT_BLOCK) if b < early else (1, (b - early) * UNIT_BLOCK) for b in range(blocks)
    ]
    up_at = [
        (len(held) - 1, b * UNIT_BLOCK) if b < ups else (None, None) for b in range(blocks)
    ]
    planes = [column] + hold(planes[1:], mark)
    parts = planes + [other_core(p, members) for p in planes]
    own, far = run_expert(
        parts, held, gate_at, up_at, list(range(ups, blocks)), w_up, w_down, me, tokens.shape[0]
    )
    return give_back(own, far, groups, members)


def solution(mesh):
    in_specs = (
        P(AXES, None),
        P(AXES, None),
        P(AXES, None),
        P(AXES, None, None),
        P(AXES, None, None),
        P(AXES, None, None),
    )
    out_specs = P(AXES, None)
    return jax.shard_map(
        on_device, mesh=mesh, in_specs=in_specs, out_specs=out_specs, check_vma=False
    )
```

time: 246 us -> 115 us (0.47)
  waiting for transfers between devices: 191 us -> 20.6 us
  Pallas kernels: 0 us -> 38.8 us
  matrix products: 33.2 us -> 0 us
  local copies, waits for them, and re-layouts: 4.51 us -> 35.2 us
  starting transfers between devices: 0.04 us -> 19 us
  between operations: 13.4 us -> 0.13 us
    unnamed x3 -> x0, waiting for transfers between devices: 132 us -> none
    all_gather x1 -> x0, waiting for transfers between devices: 59.4 us -> none  [on_device(): everyone = lax.all_gather(packed, AXES, axis=0, tiled=True)]
    pallas_call x0 -> x8, Pallas kernels: none -> 38.8 us  [the longest x1 24 us: run_expert(): pl.pallas_call(functools.partial(expert_kernel, (len(parts), gate_at, up_...]
    dot_general x2 -> x0, matrix products: 33.2 us -> none  [the longest x1 21.8 us: on_device(): part = jnp.dot(hidden, w_down[0], preferred_element_type=jnp.float32)]
    unnamed x2 -> x32, local copies, waits for them, and re-layouts: 4.51 us -> 35.2 us
    ppermute x0 -> x17, waiting for transfers between devices: none -> 20.6 us  [the longest x12 16.9 us: shifted(): return lax.ppermute(value, axis, pairs)]
    ppermute x0 -> x17, starting transfers between devices: none -> 19 us  [the longest x12 17.6 us: shifted(): return lax.ppermute(value, axis, pairs)]
  transfers between devices with their start and end apart: 2 -> 17, of which waited for: 2 -> 9; matrix products, arithmetic and copies ran while one was open for 0% -> 0% of each run, Pallas kernels for 0% -> 12%
where the time goes in v3:
time: 115 us; the launch traced here: 114 us
  Pallas kernels  38.8 us (34%)
  local copies, waits for them, and re-layouts  35.2 us (31%)
  waiting for transfers between devices  20.6 us (18%)
  starting transfers between devices  19 us (17%)
    unnamed x32, local copies, waits for them, and re-layouts  35.2 us
    pallas_call x1, Pallas kernels, run_expert(): pl.pallas_call(functools.partial(expert_kernel, (len(parts), gate_at, up_...  24 us
    ppermute x12, starting transfers between devices, shifted(): return lax.ppermute(value, axis, pairs)  17.6 us
    ppermute x12, waiting for transfers between devices, shifted(): return lax.ppermute(value, axis, pairs)  16.9 us
    pallas_call x2, Pallas kernels, fetch(): pl.pallas_call(functools.partial(fetch_kernel, jobs, len(weights)), in_sp...  13.8 us
    ppermute x5, waiting for transfers between devices, other_core(): return lax.ppermute(value, 'expert', [(i, i ^ 1) for i in range(size)])  3.67 us
  transfers between devices with their start and end apart: 17, of which 9 were waited for; matrix products, arithmetic and copies ran while one was open for 0% of the time, Pallas kernels for 12%

profile of v3, /device:TPU:0, one launch (start us, length us, event | category | flops | bytes accessed | tf_op | source)
XLA Modules:
  0.0 114.4 jit_solution(11837457027833794853)
XLA Ops:
  0.0 0.8 copy-done.12
  0.8 0.7 copy-done.14
  1.5 0.7 copy-done.15
  2.2 0.1 shard_map.64.refs_1_.refs_0_
  2.3 5.1 %collective-permute-start.2 = (bf16[4,7296]{1,0:T(4,128)(2,1)S(1)}, bf16[4,7296]{1,0:T(4,128)(2,1)S(1)}, u32[]{:S(2)}, u32[]{:S(2)}) collective-permute-start(bf16[4,7296]{1,0:T(4,128)(2,1)S(1)} %shard_map.64.refs_1_.refs_0_), channel_id=1, source_target_pairs={{0,6},{1,7},{2,0},{3,1},{4,2},{5,3},{6,4},{7,5},{8,14},{9,15},{10,... | collective-permute-start | bytes 175112 | tf_op jit(solution)/shard_map/ppermute | solution.py:39
  7.4 0.0 collective-permute-start.1
  7.4 1.0 collective-permute-start
  8.4 5.3 %shard_map.65 = (bf16[7168,1024]{1,0:T(8,128)(2,1)S(1)}, f32[8,128]{1,0:T(8,128)S(1)}) custom-call(bf16[1,7168,2048]{2,1,0:T(8,128)(2,1)} %refs_0_.3, bf16[4,7296]{1,0:T(4,128)(2,1)S(1)} %shard_map.64.refs_1_.refs_0_), custom_call_target="tpu_custom_call" | custom-call | bytes 14680064 | tf_op jit(solution)/shard_map/pallas_call | solution.py:97
  13.7 5.2 %copy-done = bf16[7168,1024]{1,0:T(8,128)(2,1)} copy-done((bf16[7168,1024]{1,0:T(8,128)(2,1)}, bf16[7168,1024]{1,0:T(8,128)(2,1)S(1)}, u32[]{:S(2)}) %copy-start) | copy-done | bytes 14680088
  18.9 0.1 shard_map.66.refs_2_.refs_0_
  19.0 2.5 %collective-permute-start.5 = (bf16[16,7296]{1,0:T(8,128)(2,1)S(1)}, bf16[16,7296]{1,0:T(8,128)(2,1)S(1)}, u32[]{:S(2)}, u32[]{:S(2)}) collective-permute-start(bf16[16,7296]{1,0:T(8,128)(2,1)S(1)} %shard_map.66.refs_2_.refs_0_), channel_id=1, source_target_pairs={{0,24},{8,0},{16,8},{24,16},{1,25},{9,1},{17,9},{25,17},{2,26},{10... | collective-permute-start | bytes 700424 | tf_op jit(solution)/shard_map/ppermute | solution.py:39
  21.5 0.5 collective-permute-start.4
  22.0 0.6 collective-permute-start.3
  22.6 8.5 %shard_map.67 = (bf16[7168,1024]{1,0:T(8,128)(2,1)S(1)}, bf16[7168,768]{1,0:T(8,128)(2,1)S(1)}, f32[8,128]{1,0:T(8,128)S(1)}) custom-call(bf16[1,7168,2048]{2,1,0:T(8,128)(2,1)} %refs_0_.3, bf16[1,7168,2048]{2,1,0:T(8,128)(2,1)} %refs_11_.1, bf16[16,7296]{1,0:T(8,128)(2,1)S(1)} %shard_map.66.refs_2_.refs_0_), custom_call_target="tpu_custom_call" | custom-call | bytes 25690112 | tf_op jit(solution)/shard_map/pallas_call | solution.py:97
  31.1 5.1 %copy-done.2 = bf16[7168,1024]{1,0:T(8,128)(2,1)} copy-done((bf16[7168,1024]{1,0:T(8,128)(2,1)}, bf16[7168,1024]{1,0:T(8,128)(2,1)S(1)}, u32[]{:S(2)}) %copy-start.2) | copy-done | bytes 14680088
  36.2 4.0 %copy-done.4 = bf16[7168,768]{1,0:T(8,128)(2,1)} copy-done((bf16[7168,768]{1,0:T(8,128)(2,1)}, bf16[7168,768]{1,0:T(8,128)(2,1)S(1)}, u32[]{:S(2)}) %copy-start.4) | copy-done | bytes 11010072
  40.2 0.6 copy-done.13
  40.8 0.7 copy-done.6
  41.5 0.1 copy-done.8
  41.6 0.1 copy-done.10
  41.7 0.5 collective-permute-start.7
  42.2 0.0 collective-permute-start.8
  42.2 0.5 collective-permute-start.9
  42.7 0.8 collective-permute-done.7.refs_5_
  43.5 0.4 collective-permute-done.8.refs_6_
  43.9 0.3 collective-permute-done.9.refs_7_
  44.2 5.2 %copy-done.1 = bf16[7168,1024]{1,0:T(8,128)(2,1)S(1)} copy-done((bf16[7168,1024]{1,0:T(8,128)(2,1)S(1)}, bf16[7168,1024]{1,0:T(8,128)(2,1)}, u32[]{:S(2)}) %copy-start.1) | copy-done | bytes 14680088
  49.4 5.2 %copy-done.3 = bf16[7168,1024]{1,0:T(8,128)(2,1)S(1)} copy-done((bf16[7168,1024]{1,0:T(8,128)(2,1)S(1)}, bf16[7168,1024]{1,0:T(8,128)(2,1)}, u32[]{:S(2)}) %copy-start.3) | copy-done | bytes 14680088
  54.6 4.1 %copy-done.5 = bf16[7168,768]{1,0:T(8,128)(2,1)S(1)} copy-done((bf16[7168,768]{1,0:T(8,128)(2,1)S(1)}, bf16[7168,768]{1,0:T(8,128)(2,1)}, u32[]{:S(2)}) %copy-start.5) | copy-done | bytes 11010072
  58.7 0.9 copy-done.7
  59.6 0.9 copy-done.9
  60.6 0.9 copy-done.11
  61.5 24.0 %shard_map.69 = (bf16[64,7168]{1,0:T(8,128)(2,1)S(1)}, bf16[64,7168]{1,0:T(8,128)(2,1)S(1)}) custom-call(bf16[16,7296]{1,0:T(8,128)(2,1)S(1)} %shard_map.66.refs_2_.refs_0_, bf16[16,7296]{1,0:T(8,128)(2,1)S(1)} %copy-done.11, bf16[16,7296]{1,0:T(8,128)(2,1)S(1)} %copy-done.9, bf16[16,7296]{1,0:T(8,128)(2,1)S(1)} %copy-done.7, ...), custom_call_target="tpu_custom_call" | custom-call | flops 5637144576 | bytes 58720256 | tf_op jit(solution)/shard_map/pallas_call | solution.py:270
  85.5 0.4 collective-permute-start.10
  85.9 2.1 %collective-permute-done.10.refs_1_ = bf16[64,7168]{1,0:T(8,128)(2,1)S(1)} collective-permute-done((bf16[64,7168]{1,0:T(8,128)(2,1)S(1)}, bf16[64,7168]{1,0:T(8,128)(2,1)S(1)}, u32[]{:S(2)}, u32[]{:S(2)}) %collective-permute-start.10) | collective-permute-done | bytes 917536 | tf_op jit(solution)/shard_map/ppermute | solution.py:43
  88.0 0.5 shard_map.70
  88.6 2.4 %collective-permute-start.11 = (bf16[16,7168]{1,0:T(8,128)(2,1)S(1)}, bf16[16,7168]{1,0:T(8,128)(2,1)S(1)}, u32[]{:S(2)}, u32[]{:S(2)}) collective-permute-start(bf16[16,7168]{1,0:T(8,128)(2,1)S(1)} %get-tuple-element.34), channel_id=1, source_target_pairs={{0,24},{8,0},{16,8},{24,16},{1,25},{9,1},{17,9},{25,17},{2,26},{10... | collective-permute-start | bytes 688136 | tf_op jit(solution)/shard_map/ppermute | solution.py:39
  91.0 1.5 %collective-permute-start.12 = (bf16[16,7168]{1,0:T(8,128)(2,1)S(1)}, bf16[16,7168]{1,0:T(8,128)(2,1)S(1)}, u32[]{:S(2)}, u32[]{:S(2)}) collective-permute-start(bf16[16,7168]{1,0:T(8,128)(2,1)S(1)} %get-tuple-element.35), channel_id=1, source_target_pairs={{0,16},{8,24},{16,0},{24,8},{1,17},{9,25},{17,1},{25,9},{2,18},{10... | collective-permute-start | bytes 688136 | tf_op jit(solution)/shard_map/ppermute | solution.py:39
  92.5 4.9 %collective-permute-done.11.refs_1_ = bf16[16,7168]{1,0:T(8,128)(2,1)S(1)} collective-permute-done((bf16[16,7168]{1,0:T(8,128)(2,1)S(1)}, bf16[16,7168]{1,0:T(8,128)(2,1)S(1)}, u32[]{:S(2)}, u32[]{:S(2)}) %collective-permute-start.11) | collective-permute-done | bytes 229408 | tf_op jit(solution)/shard_map/ppermute | solution.py:39
  97.4 6.1 %collective-permute-done.12.refs_2_ = bf16[16,7168]{1,0:T(8,128)(2,1)S(1)} collective-permute-done((bf16[16,7168]{1,0:T(8,128)(2,1)S(1)}, bf16[16,7168]{1,0:T(8,128)(2,1)S(1)}, u32[]{:S(2)}, u32[]{:S(2)}) %collective-permute-start.12) | collective-permute-done | bytes 229408 | tf_op jit(solution)/shard_map/ppermute | solution.py:39
  103.4 0.3 shard_map.71
  103.8 2.9 %collective-permute-start.14 = (bf16[4,7168]{1,0:T(4,128)(2,1)S(1)}, bf16[4,7168]{1,0:T(4,128)(2,1)S(1)}, u32[]{:S(2)}, u32[]{:S(2)}) collective-permute-start(bf16[4,7168]{1,0:T(4,128)(2,1)S(1)} %get-tuple-element.38), channel_id=1, source_target_pairs={{0,6},{1,7},{2,0},{3,1},{4,2},{5,3},{6,4},{7,5},{8,14},{9,15},{10,... | collective-permute-start | bytes 172040 | tf_op jit(solution)/shard_map/ppermute | solution.py:39
  106.6 1.1 collective-permute-start.15
  107.7 0.0 collective-permute-start.16
  107.8 0.9 collective-permute-done.14
  108.6 3.7 %collective-permute-done.15 = bf16[4,7168]{1,0:T(4,128)(2,1)S(1)} collective-permute-done((bf16[4,7168]{1,0:T(4,128)(2,1)S(1)}, bf16[4,7168]{1,0:T(4,128)(2,1)S(1)}, u32[]{:S(2)}, u32[]{:S(2)}) %collective-permute-start.15) | collective-permute-done | bytes 57376 | tf_op jit(solution)/shard_map/ppermute | solution.py:39
  112.4 1.4 %collective-permute-done.16 = bf16[4,7168]{1,0:T(4,128)(2,1)S(1)} collective-permute-done((bf16[4,7168]{1,0:T(4,128)(2,1)S(1)}, bf16[4,7168]{1,0:T(4,128)(2,1)S(1)}, u32[]{:S(2)}, u32[]{:S(2)}) %collective-permute-start.16) | collective-permute-done | bytes 57376 | tf_op jit(solution)/shard_map/ppermute | solution.py:39
  113.7 0.7 add_convert_fusion
  (27 shorter events, 0.1 us)
Async XLA Ops:
  0.0 0.8 copy-start.12
  0.8 0.7 copy-start.14
  1.5 0.7 copy-start.15
  2.3 16.6 %collective-permute-start.2 = (bf16[4,7296]{1,0:T(4,128)(2,1)S(1)}, bf16[4,7296]{1,0:T(4,128)(2,1)S(1)}, u32[]{:S(2)}, u32[]{:S(2)}) collective-permute-start(bf16[4,7296]{1,0:T(4,128)(2,1)S(1)} %shard_map.64.refs_1_.refs_0_), channel_id=1, source_target_pairs={{0,6},{1,7},{2,0},{3,1},{4,2},{5,3},{6,4},{7,5},{8,14},{9,15},{10,... | collective-permute-start | bytes 175112 | tf_op jit(solution)/shard_map/ppermute | solution.py:39
  7.4 11.5 %collective-permute-start.1 = (bf16[4,7296]{1,0:T(4,128)(2,1)S(1)}, bf16[4,7296]{1,0:T(4,128)(2,1)S(1)}, u32[]{:S(2)}, u32[]{:S(2)}) collective-permute-start(bf16[4,7296]{1,0:T(4,128)(2,1)S(1)} %shard_map.64.refs_1_.refs_0_), channel_id=1, source_target_pairs={{0,4},{1,5},{2,6},{3,7},{4,0},{5,1},{6,2},{7,3},{8,12},{9,13},{10,... | collective-permute-start | bytes 175112 | tf_op jit(solution)/shard_map/ppermute | solution.py:39
  7.4 11.5 %collective-permute-start = (bf16[4,7296]{1,0:T(4,128)(2,1)S(1)}, bf16[4,7296]{1,0:T(4,128)(2,1)S(1)}, u32[]{:S(2)}, u32[]{:S(2)}) collective-permute-start(bf16[4,7296]{1,0:T(4,128)(2,1)S(1)} %shard_map.64.refs_1_.refs_0_), channel_id=1, source_target_pairs={{0,2},{1,3},{2,4},{3,5},{4,6},{5,7},{6,0},{7,1},{8,10},{9,11},{10,... | collective-permute-start | bytes 175112 | tf_op jit(solution)/shard_map/ppermute | solution.py:39
  13.7 5.2 %copy-start = (bf16[7168,1024]{1,0:T(8,128)(2,1)}, bf16[7168,1024]{1,0:T(8,128)(2,1)S(1)}, u32[]{:S(2)}) copy-start(bf16[7168,1024]{1,0:T(8,128)(2,1)S(1)} %get-tuple-element.28.refs_8_) | copy-start | bytes 44040196
  19.0 21.8 %collective-permute-start.5 = (bf16[16,7296]{1,0:T(8,128)(2,1)S(1)}, bf16[16,7296]{1,0:T(8,128)(2,1)S(1)}, u32[]{:S(2)}, u32[]{:S(2)}) collective-permute-start(bf16[16,7296]{1,0:T(8,128)(2,1)S(1)} %shard_map.66.refs_2_.refs_0_), channel_id=1, source_target_pairs={{0,24},{8,0},{16,8},{24,16},{1,25},{9,1},{17,9},{25,17},{2,26},{10... | collective-permute-start | bytes 700424 | tf_op jit(solution)/shard_map/ppermute | solution.py:39
  21.5 19.3 %collective-permute-start.4 = (bf16[16,7296]{1,0:T(8,128)(2,1)S(1)}, bf16[16,7296]{1,0:T(8,128)(2,1)S(1)}, u32[]{:S(2)}, u32[]{:S(2)}) collective-permute-start(bf16[16,7296]{1,0:T(8,128)(2,1)S(1)} %shard_map.66.refs_2_.refs_0_), channel_id=1, source_target_pairs={{0,16},{8,24},{16,0},{24,8},{1,17},{9,25},{17,1},{25,9},{2,18},{10... | collective-permute-start | bytes 700424 | tf_op jit(solution)/shard_map/ppermute | solution.py:39
  22.0 18.9 %collective-permute-start.3 = (bf16[16,7296]{1,0:T(8,128)(2,1)S(1)}, bf16[16,7296]{1,0:T(8,128)(2,1)S(1)}, u32[]{:S(2)}, u32[]{:S(2)}) collective-permute-start(bf16[16,7296]{1,0:T(8,128)(2,1)S(1)} %shard_map.66.refs_2_.refs_0_), channel_id=1, source_target_pairs={{0,8},{8,16},{16,24},{24,0},{1,9},{9,17},{17,25},{25,1},{2,10},{10... | collective-permute-start | bytes 700424 | tf_op jit(solution)/shard_map/ppermute | solution.py:39
  22.6 20.1 %collective-permute-start.6 = (bf16[16,7296]{1,0:T(8,128)(2,1)S(1)}, bf16[16,7296]{1,0:T(8,128)(2,1)S(1)}, u32[]{:S(2)}, u32[]{:S(2)}) collective-permute-start(bf16[16,7296]{1,0:T(8,128)(2,1)S(1)} %shard_map.66.refs_2_.refs_0_), channel_id=1, source_target_pairs={{0,1},{1,0},{2,3},{3,2},{4,5},{5,4},{6,7},{7,6},{8,9},{9,8},{10,11... | collective-permute-start | bytes 700424 | tf_op jit(solution)/shard_map/ppermute | solution.py:43
  31.1 5.1 %copy-start.2 = (bf16[7168,1024]{1,0:T(8,128)(2,1)}, bf16[7168,1024]{1,0:T(8,128)(2,1)S(1)}, u32[]{:S(2)}) copy-start(bf16[7168,1024]{1,0:T(8,128)(2,1)S(1)} %get-tuple-element.29.refs_9_) | copy-start | bytes 44040196
  36.2 4.0 %copy-start.4 = (bf16[7168,768]{1,0:T(8,128)(2,1)}, bf16[7168,768]{1,0:T(8,128)(2,1)S(1)}, u32[]{:S(2)}) copy-start(bf16[7168,768]{1,0:T(8,128)(2,1)S(1)} %get-tuple-element.30.refs_10_) | copy-start | bytes 33030148
  40.2 0.6 copy-start.13
  40.8 0.7 copy-start.6
  40.8 0.8 copy-start.8
  40.8 0.8 copy-start.10
  41.7 1.8 %collective-permute-start.7 = (bf16[16,7296]{1,0:T(8,128)(2,1)}, bf16[16,7296]{1,0:T(8,128)(2,1)S(1)}, u32[]{:S(2)}, u32[]{:S(2)}) collective-permute-start(bf16[16,7296]{1,0:T(8,128)(2,1)} %get-tuple-element.25.refs_1_), channel_id=1, source_target_pairs={{0,1},{1,0},{2,3},{3,2},{4,5},{5,4},{6,7},{7,6},{8,9},{9,8},{10,11... | collective-permute-start | bytes 700424 | tf_op jit(solution)/shard_map/ppermute | solution.py:43
  42.2 1.7 %collective-permute-start.8 = (bf16[16,7296]{1,0:T(8,128)(2,1)}, bf16[16,7296]{1,0:T(8,128)(2,1)S(1)}, u32[]{:S(2)}, u32[]{:S(2)}) collective-permute-start(bf16[16,7296]{1,0:T(8,128)(2,1)} %get-tuple-element.26.refs_2_), channel_id=1, source_target_pairs={{0,1},{1,0},{2,3},{3,2},{4,5},{5,4},{6,7},{7,6},{8,9},{9,8},{10,11... | collective-permute-start | bytes 700424 | tf_op jit(solution)/shard_map/ppermute | solution.py:43
  42.2 2.0 %collective-permute-start.9 = (bf16[16,7296]{1,0:T(8,128)(2,1)}, bf16[16,7296]{1,0:T(8,128)(2,1)S(1)}, u32[]{:S(2)}, u32[]{:S(2)}) collective-permute-start(bf16[16,7296]{1,0:T(8,128)(2,1)} %get-tuple-element.27.refs_3_), channel_id=1, source_target_pairs={{0,1},{1,0},{2,3},{3,2},{4,5},{5,4},{6,7},{7,6},{8,9},{9,8},{10,11... | collective-permute-start | bytes 700424 | tf_op jit(solution)/shard_map/ppermute | solution.py:43
  44.2 5.2 %copy-start.1 = (bf16[7168,1024]{1,0:T(8,128)(2,1)S(1)}, bf16[7168,1024]{1,0:T(8,128)(2,1)}, u32[]{:S(2)}) copy-start(bf16[7168,1024]{1,0:T(8,128)(2,1)} %copy-done) | copy-start | bytes 44040196
  49.4 5.2 %copy-start.3 = (bf16[7168,1024]{1,0:T(8,128)(2,1)S(1)}, bf16[7168,1024]{1,0:T(8,128)(2,1)}, u32[]{:S(2)}) copy-start(bf16[7168,1024]{1,0:T(8,128)(2,1)} %copy-done.2) | copy-start | bytes 44040196
  54.5 4.1 %copy-start.5 = (bf16[7168,768]{1,0:T(8,128)(2,1)S(1)}, bf16[7168,768]{1,0:T(8,128)(2,1)}, u32[]{:S(2)}) copy-start(bf16[7168,768]{1,0:T(8,128)(2,1)} %copy-done.4) | copy-start | bytes 33030148
  58.7 0.9 copy-start.7
  59.6 0.9 copy-start.9
  60.6 0.9 copy-start.11
  85.5 2.5 %collective-permute-start.10 = (bf16[64,7168]{1,0:T(8,128)(2,1)S(1)}, bf16[64,7168]{1,0:T(8,128)(2,1)S(1)}, u32[]{:S(2)}, u32[]{:S(2)}) collective-permute-start(bf16[64,7168]{1,0:T(8,128)(2,1)S(1)} %get-tuple-element.32), channel_id=1, source_target_pairs={{0,1},{1,0},{2,3},{3,2},{4,5},{5,4},{6,7},{7,6},{8,9},{9,8},{10,11... | collective-permute-start | bytes 2752520 | tf_op jit(solution)/shard_map/ppermute | solution.py:43
  88.6 8.8 %collective-permute-start.11 = (bf16[16,7168]{1,0:T(8,128)(2,1)S(1)}, bf16[16,7168]{1,0:T(8,128)(2,1)S(1)}, u32[]{:S(2)}, u32[]{:S(2)}) collective-permute-start(bf16[16,7168]{1,0:T(8,128)(2,1)S(1)} %get-tuple-element.34), channel_id=1, source_target_pairs={{0,24},{8,0},{16,8},{24,16},{1,25},{9,1},{17,9},{25,17},{2,26},{10... | collective-permute-start | bytes 688136 | tf_op jit(solution)/shard_map/ppermute | solution.py:39
  91.0 12.5 %collective-permute-start.12 = (bf16[16,7168]{1,0:T(8,128)(2,1)S(1)}, bf16[16,7168]{1,0:T(8,128)(2,1)S(1)}, u32[]{:S(2)}, u32[]{:S(2)}) collective-permute-start(bf16[16,7168]{1,0:T(8,128)(2,1)S(1)} %get-tuple-element.35), channel_id=1, source_target_pairs={{0,16},{8,24},{16,0},{24,8},{1,17},{9,25},{17,1},{25,9},{2,18},{10... | collective-permute-start | bytes 688136 | tf_op jit(solution)/shard_map/ppermute | solution.py:39
  92.5 11.0 %collective-permute-start.13 = (bf16[16,7168]{1,0:T(8,128)(2,1)S(1)}, bf16[16,7168]{1,0:T(8,128)(2,1)S(1)}, u32[]{:S(2)}, u32[]{:S(2)}) collective-permute-start(bf16[16,7168]{1,0:T(8,128)(2,1)S(1)} %get-tuple-element.36), channel_id=1, source_target_pairs={{0,8},{8,16},{16,24},{24,0},{1,9},{9,17},{17,25},{25,1},{2,10},{10... | collective-permute-start | bytes 688136 | tf_op jit(solution)/shard_map/ppermute | solution.py:39
  103.8 4.9 %collective-permute-start.14 = (bf16[4,7168]{1,0:T(4,128)(2,1)S(1)}, bf16[4,7168]{1,0:T(4,128)(2,1)S(1)}, u32[]{:S(2)}, u32[]{:S(2)}) collective-permute-start(bf16[4,7168]{1,0:T(4,128)(2,1)S(1)} %get-tuple-element.38), channel_id=1, source_target_pairs={{0,6},{1,7},{2,0},{3,1},{4,2},{5,3},{6,4},{7,5},{8,14},{9,15},{10,... | collective-permute-start | bytes 172040 | tf_op jit(solution)/shard_map/ppermute | solution.py:39
  106.6 5.7 %collective-permute-start.15 = (bf16[4,7168]{1,0:T(4,128)(2,1)S(1)}, bf16[4,7168]{1,0:T(4,128)(2,1)S(1)}, u32[]{:S(2)}, u32[]{:S(2)}) collective-permute-start(bf16[4,7168]{1,0:T(4,128)(2,1)S(1)} %get-tuple-element.39), channel_id=1, source_target_pairs={{0,4},{1,5},{2,6},{3,7},{4,0},{5,1},{6,2},{7,3},{8,12},{9,13},{10,... | collective-permute-start | bytes 172040 | tf_op jit(solution)/shard_map/ppermute | solution.py:39
  107.7 6.0 %collective-permute-start.16 = (bf16[4,7168]{1,0:T(4,128)(2,1)S(1)}, bf16[4,7168]{1,0:T(4,128)(2,1)S(1)}, u32[]{:S(2)}, u32[]{:S(2)}) collective-permute-start(bf16[4,7168]{1,0:T(4,128)(2,1)S(1)} %get-tuple-element.40), channel_id=1, source_target_pairs={{0,2},{1,3},{2,4},{3,5},{4,6},{5,7},{6,0},{7,1},{8,10},{9,11},{10,... | collective-permute-start | bytes 172040 | tf_op jit(solution)/shard_map/ppermute | solution.py:39

commit v4 on v1

v4 whole, which is shorter than its diff:
```python
import functools

import jax
import jax.numpy as jnp
from jax import lax
from jax.experimental import pallas as pl
from jax.experimental.pallas import tpu as pltpu
from jax.sharding import PartitionSpec as P

EXP_GRP = 8
LANES = 128
AXES = ("group", "expert")
VMEM = pltpu.VMEM
UNIT_BLOCK = 256
DOWN_BLOCK = 512
UP_RING = 2
DOWN_RING = 3
EARLY_DOWN = 2


def in_vmem(value):
    return pltpu.with_memory_space_constraint(value, VMEM)


def in_hbm(value):
    return pltpu.with_memory_space_constraint(value, pltpu.HBM)


def whole_vmem(count):
    return [pl.BlockSpec(memory_space=VMEM)] * count


def swap(value, axis, size, mask):
    return lax.ppermute(value, axis, [(i, i ^ mask) for i in range(size)])


def limit(amount):
    return pltpu.CompilerParams(vmem_limit_bytes=int(amount))


def cost(flops, amount):
    return pl.CostEstimate(flops=flops, bytes_accessed=amount, transcendentals=0)


def pack_kernel(tokens_ref, ids_ref, weights_ref, out_ref):
    width = tokens_ref.shape[1]
    out_ref[:, :width] = tokens_ref[...]
    ids = ids_ref[...]
    weights = weights_ref[...].astype(jnp.float32)
    label = lax.broadcasted_iota(jnp.int32, (ids.shape[0], LANES), 1)
    route = jnp.zeros((ids.shape[0], LANES), jnp.float32)
    for k in range(ids.shape[1]):
        route += jnp.where(ids[:, k : k + 1] == label, weights[:, k : k + 1], 0.0)
    out_ref[:, width:] = route.astype(out_ref.dtype)


def pack(tokens, expert_ids, gate_weights):
    rows, width = tokens.shape
    args = (tokens, expert_ids, gate_weights)
    return pl.pallas_call(
        pack_kernel,
        grid=(1,),
        in_specs=[pl.BlockSpec(a.shape, lambda i: (0, 0)) for a in args],
        out_specs=whole_vmem(1)[0],
        out_shape=VMEM((rows, width + LANES), tokens.dtype),
        compiler_params=limit(2 * 1024 * 1024),
    )(*[in_hbm(a) for a in args])


def fetch_kernel(jobs, *refs):
    src_refs = refs[: len(jobs)]
    out_refs = refs[len(jobs) + 1 : 2 * len(jobs) + 1]
    mark_ref, sems = refs[-2:]
    copies = []
    for n, (_, first, columns) in enumerate(jobs):
        size = src_refs[n].shape[1] // 4
        for i in range(4):
            copies.append(
                pltpu.make_async_copy(
                    src_refs[n].at[0, pl.ds(i * size, size), pl.ds(first, columns)],
                    out_refs[n].at[pl.ds(i * size, size), :],
                    sems.at[n * 4 + i],
                )
            )
    for copy in copies:
        copy.start()
    mark_ref[...] = jnp.zeros_like(mark_ref)
    for copy in copies:
        copy.wait()


def fetch(jobs, after):
    if not jobs:
        return [], None
    rows = jobs[0][0].shape[1]
    hbm = pl.BlockSpec(memory_space=pltpu.HBM)
    *out, mark = pl.pallas_call(
        functools.partial(fetch_kernel, jobs),
        in_specs=[hbm] * len(jobs) + [pl.BlockSpec(memory_space=pl.ANY)],
        out_specs=whole_vmem(len(jobs) + 1),
        out_shape=[VMEM((rows, columns), w.dtype) for w, _, columns in jobs]
        + [VMEM((8, LANES), jnp.float32)],
        scratch_shapes=[pltpu.SemaphoreType.DMA((4 * len(jobs),))],
        compiler_params=limit(256 * 1024),
        cost_estimate=cost(0, sum(2 * rows * columns for _, _, columns in jobs)),
    )(*[in_hbm(w) for w, _, _ in jobs], after)
    return out, mark


def join_kernel(cuts, first_ref, second_ref, after_ref, *out_refs):
    for (start, size), out_ref in zip(cuts, out_refs):
        columns = slice(start, start + size)
        halves = [r[:, columns].astype(jnp.float32) for r in (first_ref, second_ref)]
        out_ref[...] = jnp.concatenate(halves, axis=0).astype(out_ref.dtype)


def join(first, second, after, cuts=None):
    rows, width = first.shape
    cuts = cuts or [(0, width)]
    after = first if after is None else after
    return pl.pallas_call(
        functools.partial(join_kernel, cuts),
        in_specs=whole_vmem(2) + [pl.BlockSpec(memory_space=pl.ANY)],
        out_specs=whole_vmem(len(cuts)),
        out_shape=[VMEM((2 * rows, size), first.dtype) for _, size in cuts],
        compiler_params=limit(1024 * 1024 + 16 * rows * width),
    )(in_vmem(first), in_vmem(second), after)


def hold_kernel(*refs):
    pass


def hold(values, after):
    if after is None:
        return values
    return pl.pallas_call(
        hold_kernel,
        in_specs=[pl.BlockSpec(memory_space=pl.ANY)] * (len(values) + 1),
        out_specs=[pl.BlockSpec(memory_space=pl.ANY)] * len(values),
        out_shape=[jax.ShapeDtypeStruct(v.shape, v.dtype) for v in values],
        input_output_aliases={i: i for i in range(len(values))},
        compiler_params=limit(256 * 1024),
    )(*values, after)


def down_copier(down_hbm, ring, sems, start):
    def copy(d, slot):
        first = start + d * DOWN_BLOCK
        if not isinstance(d, int):
            first = pl.multiple_of(first, DOWN_BLOCK)
        return pltpu.make_async_copy(
            down_hbm.at[0, :, pl.ds(first, DOWN_BLOCK)], ring.at[slot], sems.at[slot]
        )

    return copy


def down_block(hidden_ref, weight, scale, own_ref, far_ref, columns):
    part = jnp.dot(hidden_ref[...], weight, preferred_element_type=jnp.float32)
    part = (part * scale).astype(jnp.bfloat16)
    half = part.shape[0] // 2
    own_ref[:, columns] = part[:half]
    far_ref[:, columns] = part[half:]


def down_loop(hidden_ref, ring, copy, scale_ref, own_ref, far_ref, first, downs):
    @pl.loop(first, downs)
    def _(d):
        slot = lax.rem(d, DOWN_RING)
        columns = pl.ds(pl.multiple_of(d * DOWN_BLOCK, DOWN_BLOCK), DOWN_BLOCK)
        copy(d, slot).wait()
        down_block(hidden_ref, ring[slot], scale_ref[:, :1], own_ref, far_ref, columns)

        @pl.when(d + DOWN_RING < downs)
        def _():
            copy(d + DOWN_RING, slot).start()


def expert_kernel(gate_at, up_at, streamed, held, *refs):
    a_refs, b_refs, refs = refs[:4], refs[4:8], refs[8:]
    w_refs, refs = refs[:held], refs[held:]
    up_hbm, down_hbm, me_ref, own_ref, far_ref, hidden, scale_ref, early_ref = refs[:8]
    x, up_ring, down_ring, up_sem, down_sem, early_sem = refs[8:]
    depth = x.shape[1]
    units = hidden.shape[1]
    width = own_ref.shape[1]
    blocks = units // UNIT_BLOCK
    downs = width // DOWN_BLOCK

    def up_copy(n):
        return pltpu.make_async_copy(
            up_hbm.at[0, :, pl.ds(streamed[n] * UNIT_BLOCK, UNIT_BLOCK)],
            up_ring.at[n % UP_RING],
            up_sem.at[n % UP_RING],
        )

    down_copy = down_copier(down_hbm, down_ring, down_sem, 0)
    early_copy = pltpu.make_async_copy(
        down_hbm.at[0, :, pl.ds(width, early_ref.shape[1])], early_ref, early_sem
    )
    later = {}
    for n in range(min(DOWN_RING, downs)):
        later.setdefault(min(blocks - 1, 2 + n), []).append(down_copy(n, n))
    later.setdefault(min(blocks - 1, 5), []).append(early_copy)

    for n in range(min(UP_RING, len(streamed))):
        up_copy(n).start()

    plane = a_refs[0].shape[0] // 2
    route = []
    for n, (a_ref, b_ref) in enumerate(zip(a_refs, b_refs)):
        core, pair = n // 2, n % 2
        for j in range(2):
            rows = slice(j * plane, (j + 1) * plane)
            at = core * 4 * plane + (2 * pair + j) * plane
            x[at : at + plane, :width] = a_ref[rows, :]
            at = core * 4 * plane + (2 * j + pair) * plane
            x[at : at + plane, width:] = b_ref[rows, :width]
            route.append((at, b_ref[rows, width:]))
    route = jnp.concatenate([r for _, r in sorted(route, key=lambda p: p[0])], axis=0)
    route = route.astype(jnp.float32)
    lane = lax.broadcasted_iota(jnp.int32, route.shape, 1)
    scale = jnp.sum(jnp.where(lane == me_ref[0], route, 0.0), axis=1, keepdims=True)
    scale_ref[...] = jnp.broadcast_to(scale, scale_ref.shape)

    def times(ref):
        return jnp.dot(x[...], ref[...], preferred_element_type=jnp.float32)

    for b in range(blocks):
        where, first = gate_at[b]
        gate = times(w_refs[where].at[:, first : first + UNIT_BLOCK])
        if up_at[b] is None:
            n = streamed.index(b)
            up_copy(n).wait()
            up = times(up_ring.at[n % UP_RING])
            if n + UP_RING < len(streamed):
                up_copy(n + UP_RING).start()
        else:
            where, first = up_at[b]
            up = times(w_refs[where].at[:, first : first + UNIT_BLOCK])
        for copy in later.get(b, []):
            copy.start()
        hidden[:, b * UNIT_BLOCK : (b + 1) * UNIT_BLOCK] = (jax.nn.silu(gate) * up).astype(
            jnp.bfloat16
        )
    down_loop(hidden, down_ring, down_copy, scale_ref, own_ref, far_ref, 0, downs)
    early_copy.wait()


def run_expert(a_parts, b_parts, held, gate_at, up_at, streamed, w_up, w_down, me):
    rows = sum(p.shape[0] for p in a_parts)
    depth, units = w_up.shape[1], w_up.shape[2]
    width = depth // 2
    half = VMEM((rows // 2, width), jnp.bfloat16)
    hbm = pl.BlockSpec(memory_space=pltpu.HBM)
    ring = max(1, min(UP_RING, len(streamed)))
    scratch = 2 * (rows * depth + ring * depth * UNIT_BLOCK + DOWN_RING * units * DOWN_BLOCK)
    work = 2816 * 1024 + 12 * rows * UNIT_BLOCK + 4 * rows * DOWN_BLOCK
    args = [in_vmem(v) for v in [*a_parts, *b_parts, *held]]
    return pl.pallas_call(
        functools.partial(expert_kernel, gate_at, up_at, streamed, len(held)),
        in_specs=whole_vmem(len(args)) + [hbm, hbm, pl.BlockSpec(memory_space=pltpu.SMEM)],
        out_specs=whole_vmem(5),
        out_shape=(
            half,
            half,
            VMEM((rows, units), jnp.bfloat16),
            VMEM((rows, LANES), jnp.float32),
            VMEM((units, EARLY_DOWN * DOWN_BLOCK), jnp.bfloat16),
        ),
        scratch_shapes=[
            VMEM((rows, depth), jnp.bfloat16),
            VMEM((ring, depth, UNIT_BLOCK), jnp.bfloat16),
            VMEM((DOWN_RING, units, DOWN_BLOCK), jnp.bfloat16),
            pltpu.SemaphoreType.DMA((ring,)),
            pltpu.SemaphoreType.DMA((DOWN_RING,)),
            pltpu.SemaphoreType.DMA,
        ],
        compiler_params=limit(scratch + work),
        cost_estimate=cost(5 * rows * depth * units, 4 * depth * units),
    )(*args, in_hbm(w_up), in_hbm(w_down), me)


def rest_kernel(hidden, scale_ref, early_ref, down_hbm, own_ref, far_ref, ring, sems):
    width = own_ref.shape[1]
    downs = width // DOWN_BLOCK
    copy = down_copier(down_hbm, ring, sems, width)
    for d in range(EARLY_DOWN, min(EARLY_DOWN + DOWN_RING, downs)):
        copy(d, d % DOWN_RING).start()
    for d in range(EARLY_DOWN):
        columns = slice(d * DOWN_BLOCK, (d + 1) * DOWN_BLOCK)
        down_block(hidden, early_ref[:, columns], scale_ref[:, :1], own_ref, far_ref, columns)
    down_loop(hidden, ring, copy, scale_ref, own_ref, far_ref, EARLY_DOWN, downs)


def run_rest(hidden, scale, early, w_down):
    rows, units = hidden.shape
    width = w_down.shape[2] // 2
    half = VMEM((rows // 2, width), jnp.bfloat16)
    scratch = 2 * DOWN_RING * units * DOWN_BLOCK
    work = 2 * 1024 * 1024 + 12 * rows * DOWN_BLOCK
    return pl.pallas_call(
        rest_kernel,
        in_specs=whole_vmem(3) + [pl.BlockSpec(memory_space=pltpu.HBM)],
        out_specs=whole_vmem(2),
        out_shape=(half, half),
        scratch_shapes=[
            VMEM((DOWN_RING, units, DOWN_BLOCK), jnp.bfloat16),
            pltpu.SemaphoreType.DMA((DOWN_RING,)),
        ],
        compiler_params=limit(scratch + work),
        cost_estimate=cost(2 * rows * width * units, 2 * width * units),
    )(in_vmem(hidden), in_vmem(scale), in_vmem(early), in_hbm(w_down))


def fold_kernel(picks, first_ref, second_ref, *out_refs):
    total = first_ref[...].astype(jnp.float32) + second_ref[...].astype(jnp.float32)
    for pick, out_ref in zip(picks, out_refs):
        pieces = [total[start : start + size] for start, size in pick]
        value = pieces[0] if len(pieces) == 1 else jnp.concatenate(pieces, axis=0)
        out_ref[...] = value.astype(out_ref.dtype)


def fold(first, second, picks):
    rows, width = first.shape
    return pl.pallas_call(
        functools.partial(fold_kernel, picks),
        in_specs=whole_vmem(2),
        out_specs=whole_vmem(len(picks)),
        out_shape=[VMEM((sum(n for _, n in pick), width), first.dtype) for pick in picks],
        compiler_params=limit(1024 * 1024 + 10 * rows * width),
    )(in_vmem(first), in_vmem(second))


def give_back(own, far, masks, groups, members):
    plane = own.shape[0] // 4
    keeps = [j for j in range(4) if not j & masks[0]]
    sends = [j for j in range(4) if j & masks[0]]
    picks = [[(j * plane, plane) for j in js] for js in (keeps, sends)]
    keep, send = fold(own, swap(far, "expert", members, 1), picks)
    for axis, size, mask in [
        ("group", groups, masks[0]),
        ("group", groups, masks[1]),
        *[("expert", members, 2 << k) for k in range((members // 2).bit_length() - 2)],
    ]:
        half = keep.shape[0] // 2
        keep, send = fold(keep, swap(send, axis, size, mask), [[(0, half)], [(half, half)]])
    got = swap(send, "expert", members, members // 2)
    return (keep.astype(jnp.float32) + got.astype(jnp.float32)).astype(jnp.bfloat16)


def on_device(tokens, expert_ids, gate_weights, w_gate, w_up, w_down):
    groups = lax.axis_size("group")
    members = lax.axis_size("expert")
    split = members // EXP_GRP
    me = lax.axis_index("group") * EXP_GRP + lax.axis_index("expert") // split
    me = me.astype(jnp.int32).reshape(1)
    width = tokens.shape[1] // 2
    blocks = w_gate.shape[2] // UNIT_BLOCK
    ups = max(1, blocks // 8)
    group = -(-blocks // 4)

    jobs, gate_at, count = [], [], 0
    for n in range(4):
        inside = list(range(n * group, min(blocks, (n + 1) * group)))
        job = []
        if inside:
            job.append((w_gate, inside[0] * UNIT_BLOCK, len(inside) * UNIT_BLOCK))
            gate_at += [(count, i * UNIT_BLOCK) for i in range(len(inside))]
            count += 1
        jobs.append(job)
    jobs[3].append((w_up, 0, ups * UNIT_BLOCK))
    up_at = [(count, b * UNIT_BLOCK) if b < ups else None for b in range(blocks)]
    streamed = list(range(ups, blocks))

    value = pack(tokens, expert_ids, gate_weights)
    held = []
    steps = [2 << k for k in reversed(range((members // 2).bit_length() - 1))]
    for n, mask in enumerate(steps):
        got = swap(value, "expert", members, mask)
        more, mark = fetch(jobs[n] if n < 2 else [], value)
        held += more
        if n < len(steps) - 1:
            (value,) = join(value, got, mark)
    a, b = join(value, got, mark, [(0, width), (width, width + LANES)])

    a_got, b_got = swap(a, "group", groups, 1), swap(b, "group", groups, 2)
    more, mark = fetch(jobs[2], a)
    held += more
    (a,) = join(a, a_got, mark)
    (b,) = join(b, b_got, mark)
    a_got, b_got = swap(a, "group", groups, 2), swap(b, "group", groups, 1)
    a_core, b_core = swap(a, "expert", members, 1), swap(b, "expert", members, 1)
    more, mark = fetch(jobs[3], a)
    held += more
    a_got, b_got = hold([a_got, b_got], mark)
    a_parts = [a, a_got, a_core, swap(a_got, "expert", members, 1)]
    b_parts = [b, b_got, b_core, swap(b_got, "expert", members, 1)]

    own, far, hidden, scale, early = run_expert(
        a_parts, b_parts, held, gate_at, up_at, streamed, w_up, w_down, me
    )
    left = give_back(own, far, (1, 2), groups, members)
    own, far = run_rest(hidden, scale, early, w_down)
    right = give_back(own, far, (2, 1), groups, members)
    return jnp.concatenate([left, right], axis=1)


def solution(mesh):
    in_specs = (
        P(AXES, None),
        P(AXES, None),
        P(AXES, None),
        P(AXES, None, None),
        P(AXES, None, None),
        P(AXES, None, None),
    )
    out_specs = P(AXES, None)
    return jax.shard_map(
        on_device, mesh=mesh, in_specs=in_specs, out_specs=out_specs, check_vma=False
    )
```

time: 246 us -> 106 us (0.43)
  waiting for transfers between devices: 191 us -> 15.9 us
  Pallas kernels: 0 us -> 40.6 us
  matrix products: 33.2 us -> 0 us
  local copies, waits for them, and re-layouts: 4.51 us -> 27.9 us
  starting transfers between devices: 0.04 us -> 20.6 us
  between operations: 13.4 us -> 0.17 us
    unnamed x3 -> x0, waiting for transfers between devices: 132 us -> none
    all_gather x1 -> x0, waiting for transfers between devices: 59.4 us -> none  [on_device(): everyone = lax.all_gather(packed, AXES, axis=0, tiled=True)]
    pallas_call x0 -> x20, Pallas kernels: none -> 40.6 us  [the longest x1 20.3 us: run_expert(): pl.pallas_call(functools.partial(expert_kernel, gate_at, up_at, streamed,...]
    dot_general x2 -> x0, matrix products: 33.2 us -> none  [the longest x1 21.8 us: on_device(): part = jnp.dot(hidden, w_down[0], preferred_element_type=jnp.float32)]
    unnamed x2 -> x20, local copies, waits for them, and re-layouts: 4.51 us -> 27.9 us
    ppermute x0 -> x20, starting transfers between devices: none -> 20.6 us  [swap(): return lax.ppermute(value, axis, [(i, i ^ mask) for i in range(size)])]
    ppermute x0 -> x20, waiting for transfers between devices: none -> 15.9 us  [swap(): return lax.ppermute(value, axis, [(i, i ^ mask) for i in range(size)])]
  transfers between devices with their start and end apart: 2 -> 20, of which waited for: 2 -> 9; matrix products, arithmetic and copies ran while one was open for 0% -> 0% of each run, Pallas kernels for 0% -> 18%
where the time goes in v4:
time: 106 us
  Pallas kernels  40.6 us (38%)
  local copies, waits for them, and re-layouts  27.9 us (26%)
  starting transfers between devices  20.6 us (19%)
  waiting for transfers between devices  15.9 us (15%)
    unnamed x20, local copies, waits for them, and re-layouts  27.9 us
    ppermute x20, starting transfers between devices, swap(): return lax.ppermute(value, axis, [(i, i ^ mask) for i in range(size)])  20.6 us
    pallas_call x1, Pallas kernels, run_expert(): pl.pallas_call(functools.partial(expert_kernel, gate_at, up_at, streamed,...  20.3 us
    ppermute x20, waiting for transfers between devices, swap(): return lax.ppermute(value, axis, [(i, i ^ mask) for i in range(size)])  15.9 us
    pallas_call x4, Pallas kernels, fetch(): pl.pallas_call(functools.partial(fetch_kernel, jobs), in_specs=[hbm] * le...  14.1 us
    pallas_call x1, Pallas kernels, run_rest(): pl.pallas_call(rest_kernel, in_specs=whole_vmem(3) + [pl.BlockSpec(memory...  4.81 us
  transfers between devices with their start and end apart: 20, of which 9 were waited for; matrix products, arithmetic and copies ran while one was open for 0% of the time, Pallas kernels for 18%

profile of v4, /device:TPU:0, one launch (start us, length us, event | category | flops | bytes accessed | tf_op | source)
XLA Modules:
  0.0 105.9 jit_solution(780748447216928749)
XLA Ops:
  0.0 0.9 shard_map.64.refs_1_.first_ref
  0.9 4.1 %collective-permute-start = (bf16[4,7296]{1,0:T(4,128)(2,1)S(1)}, bf16[4,7296]{1,0:T(4,128)(2,1)S(1)}, u32[]{:S(2)}, u32[]{:S(2)}) collective-permute-start(bf16[4,7296]{1,0:T(4,128)(2,1)S(1)} %shard_map.64.refs_1_.first_ref), channel_id=1, source_target_pairs={{0,4},{1,5},{2,6},{3,7},{4,0},{5,1},{6,2},{7,3},{8,12},{9,13},{10,... | collective-permute-start | bytes 175112 | tf_op jit(solution)/shard_map/ppermute | solution.py:34
  5.0 3.2 %shard_map.65 = (bf16[7168,512]{1,0:T(8,128)(2,1)S(1)}, f32[8,128]{1,0:T(8,128)S(1)}) custom-call(bf16[1,7168,2048]{2,1,0:T(8,128)(2,1)} %refs_0_.7, bf16[4,7296]{1,0:T(4,128)(2,1)S(1)} %shard_map.64.refs_1_.first_ref), custom_call_target="tpu_custom_call" | custom-call | bytes 7340032 | tf_op jit(solution)/shard_map/pallas_call | solution.py:97
  8.3 2.9 %copy-done = bf16[7168,512]{1,0:T(8,128)(2,1)} copy-done((bf16[7168,512]{1,0:T(8,128)(2,1)}, bf16[7168,512]{1,0:T(8,128)(2,1)S(1)}, u32[]{:S(2)}) %copy-start) | copy-done | bytes 7340056
  11.2 1.6 %collective-permute-start.1 = (bf16[8,7296]{1,0:T(8,128)(2,1)S(1)}, bf16[8,7296]{1,0:T(8,128)(2,1)S(1)}, u32[]{:S(2)}, u32[]{:S(2)}) collective-permute-start(bf16[8,7296]{1,0:T(8,128)(2,1)S(1)} %shard_map.66.refs_1_.first_ref), channel_id=1, source_target_pairs={{0,2},{1,3},{2,0},{3,1},{4,6},{5,7},{6,4},{7,5},{8,10},{9,11},{10,... | collective-permute-start | bytes 350216 | tf_op jit(solution)/shard_map/ppermute | solution.py:34
  12.8 3.2 %shard_map.67 = (bf16[7168,512]{1,0:T(8,128)(2,1)S(1)}, f32[8,128]{1,0:T(8,128)S(1)}) custom-call(bf16[1,7168,2048]{2,1,0:T(8,128)(2,1)} %refs_0_.7, bf16[8,7296]{1,0:T(8,128)(2,1)S(1)} %shard_map.66.refs_1_.first_ref), custom_call_target="tpu_custom_call" | custom-call | bytes 7340032 | tf_op jit(solution)/shard_map/pallas_call | solution.py:97
  16.1 3.0 %copy-done.2 = bf16[7168,512]{1,0:T(8,128)(2,1)} copy-done((bf16[7168,512]{1,0:T(8,128)(2,1)}, bf16[7168,512]{1,0:T(8,128)(2,1)S(1)}, u32[]{:S(2)}) %copy-start.2) | copy-done | bytes 7340056
  19.1 1.6 %collective-permute-start.4 = (bf16[16,3712]{1,0:T(8,128)(2,1)S(1)}, bf16[16,3712]{1,0:T(8,128)(2,1)S(1)}, u32[]{:S(2)}, u32[]{:S(2)}) collective-permute-start(bf16[16,3712]{1,0:T(8,128)(2,1)S(1)} %get-tuple-element.45.first_ref), channel_id=1, source_target_pairs={{0,16},{8,24},{16,0},{24,8},{1,17},{9,25},{17,1},{25,9},{2,18},{10... | collective-permute-start | bytes 356360 | tf_op jit(solution)/shard_map/ppermute | solution.py:34
  20.7 1.5 %collective-permute-start.2 = (bf16[16,3584]{1,0:T(8,128)(2,1)S(1)}, bf16[16,3584]{1,0:T(8,128)(2,1)S(1)}, u32[]{:S(2)}, u32[]{:S(2)}) collective-permute-start(bf16[16,3584]{1,0:T(8,128)(2,1)S(1)} %get-tuple-element.43.refs_1_.first_ref), channel_id=1, source_target_pairs={{0,8},{8,0},{16,24},{24,16},{1,9},{9,1},{17,25},{25,17},{2,10},{10... | collective-permute-start | bytes 344072 | tf_op jit(solution)/shard_map/ppermute | solution.py:34
  22.2 3.2 %shard_map.69 = (bf16[7168,512]{1,0:T(8,128)(2,1)S(1)}, f32[8,128]{1,0:T(8,128)S(1)}) custom-call(bf16[1,7168,2048]{2,1,0:T(8,128)(2,1)} %refs_0_.7, bf16[16,3584]{1,0:T(8,128)(2,1)S(1)} %get-tuple-element.43.refs_1_.first_ref), custom_call_target="tpu_custom_call" | custom-call | bytes 7340032 | tf_op jit(solution)/shard_map/pallas_call | solution.py:97
  25.4 2.9 %copy-done.4 = bf16[7168,512]{1,0:T(8,128)(2,1)} copy-done((bf16[7168,512]{1,0:T(8,128)(2,1)}, bf16[7168,512]{1,0:T(8,128)(2,1)S(1)}, u32[]{:S(2)}) %copy-start.4) | copy-done | bytes 7340056
  28.4 0.6 collective-permute-start.5
  29.0 0.6 collective-permute-start.3
  29.6 4.4 %shard_map.72 = (bf16[7168,512]{1,0:T(8,128)(2,1)S(1)}, bf16[7168,256]{1,0:T(8,128)(2,1)S(1)}, f32[8,128]{1,0:T(8,128)S(1)}) custom-call(bf16[1,7168,2048]{2,1,0:T(8,128)(2,1)} %refs_0_.7, bf16[1,7168,2048]{2,1,0:T(8,128)(2,1)} %refs_13_.1, bf16[32,3584]{1,0:T(8,128)(2,1)S(1)} %shard_map.70.refs_2_.refs_0_), custom_call_target="tpu_custom_call" | custom-call | bytes 11010048 | tf_op jit(solution)/shard_map/pallas_call | solution.py:97
  34.0 3.0 %copy-done.6 = bf16[7168,512]{1,0:T(8,128)(2,1)} copy-done((bf16[7168,512]{1,0:T(8,128)(2,1)}, bf16[7168,512]{1,0:T(8,128)(2,1)S(1)}, u32[]{:S(2)}) %copy-start.6) | copy-done | bytes 7340056
  37.0 1.8 %copy-done.8 = bf16[7168,256]{1,0:T(8,128)(2,1)} copy-done((bf16[7168,256]{1,0:T(8,128)(2,1)}, bf16[7168,256]{1,0:T(8,128)(2,1)S(1)}, u32[]{:S(2)}) %copy-start.8) | copy-done | bytes 3670040
  38.7 0.5 collective-permute-start.9
  39.2 0.1 collective-permute-start.6
  39.3 0.4 collective-permute-start.7
  39.7 1.1 %collective-permute-done.6.refs_2_ = bf16[32,3584]{1,0:T(8,128)(2,1)S(1)} collective-permute-done((bf16[32,3584]{1,0:T(8,128)(2,1)S(1)}, bf16[32,3584]{1,0:T(8,128)(2,1)S(1)}, u32[]{:S(2)}, u32[]{:S(2)}) %collective-permute-start.6) | collective-permute-done | bytes 229408 | tf_op jit(solution)/shard_map/ppermute | solution.py:34
  40.9 0.3 collective-permute-done.7.refs_3_
  41.2 3.1 %copy-done.1 = bf16[7168,512]{1,0:T(8,128)(2,1)S(1)} copy-done((bf16[7168,512]{1,0:T(8,128)(2,1)S(1)}, bf16[7168,512]{1,0:T(8,128)(2,1)}, u32[]{:S(2)}) %copy-start.1) | copy-done | bytes 7340056
  44.3 3.1 %copy-done.3 = bf16[7168,512]{1,0:T(8,128)(2,1)S(1)} copy-done((bf16[7168,512]{1,0:T(8,128)(2,1)S(1)}, bf16[7168,512]{1,0:T(8,128)(2,1)}, u32[]{:S(2)}) %copy-start.3) | copy-done | bytes 7340056
  47.4 3.1 %copy-done.5 = bf16[7168,512]{1,0:T(8,128)(2,1)S(1)} copy-done((bf16[7168,512]{1,0:T(8,128)(2,1)S(1)}, bf16[7168,512]{1,0:T(8,128)(2,1)}, u32[]{:S(2)}) %copy-start.5) | copy-done | bytes 7340056
  50.5 3.1 %copy-done.7 = bf16[7168,512]{1,0:T(8,128)(2,1)S(1)} copy-done((bf16[7168,512]{1,0:T(8,128)(2,1)S(1)}, bf16[7168,512]{1,0:T(8,128)(2,1)}, u32[]{:S(2)}) %copy-start.7) | copy-done | bytes 7340056
  53.6 2.0 %copy-done.9 = bf16[7168,256]{1,0:T(8,128)(2,1)S(1)} copy-done((bf16[7168,256]{1,0:T(8,128)(2,1)S(1)}, bf16[7168,256]{1,0:T(8,128)(2,1)}, u32[]{:S(2)}) %copy-start.9) | copy-done | bytes 3670040
  55.6 20.3 %shard_map.74 = (bf16[64,3584]{1,0:T(8,128)(2,1)S(1)}, bf16[64,3584]{1,0:T(8,128)(2,1)S(1)}, bf16[128,2048]{1,0:T(8,128)(2,1)S(1)}, f32[128,128]{1,0:T(8,128)S(1)}, bf16[2048,1024]{1,0:T(8,128)(2,1)S(1)}) custom-call(bf16[32,3584]{1,0:T(8,128)(2,1)S(1)} %shard_map.70.refs_2_.refs_0_, bf16[32,3584]{1,0:T(8,128)(2,1)S(1)} %get-tuple-element.47.refs_1_, ...), custom_call_target="tpu_custom_call" | custom-call | flops 9395240960 | bytes 58720256 | tf_op jit(solution)/shard_map/pallas_call | solution.py:261
  75.9 0.2 collective-permute-start.10
  76.2 4.8 %shard_map.79 = (bf16[64,3584]{1,0:T(8,128)(2,1)S(1)}, bf16[64,3584]{1,0:T(8,128)(2,1)S(1)}) custom-call(bf16[128,2048]{1,0:T(8,128)(2,1)S(1)} %get-tuple-element.64.hidden, f32[128,128]{1,0:T(8,128)S(1)} %get-tuple-element.65.scale_ref, bf16[2048,1024]{1,0:T(8,128)(2,1)S(1)} %get-tuple-element.66.early_ref, bf16[1,2048,7168]{2,1,0:T(8,128)(2,1)} %down_hbm.1), custom_call_target="tpu_custom_call" | custom-call | flops 1879048192 | bytes 14680064 | tf_op jit(solution)/shard_map/pallas_call | solution.py:303
  81.0 0.4 collective-permute-start.15
  81.4 0.1 shard_map.75
  81.5 1.6 %collective-permute-start.11 = (bf16[32,3584]{1,0:T(8,128)(2,1)S(1)}, bf16[32,3584]{1,0:T(8,128)(2,1)S(1)}, u32[]{:S(2)}, u32[]{:S(2)}) collective-permute-start(bf16[32,3584]{1,0:T(8,128)(2,1)S(1)} %get-tuple-element.57), channel_id=1, source_target_pairs={{0,8},{8,0},{16,24},{24,16},{1,9},{9,1},{17,25},{25,17},{2,10},{10... | collective-permute-start | bytes 688136 | tf_op jit(solution)/shard_map/ppermute | solution.py:34
  83.1 0.1 shard_map.80
  83.2 1.6 %collective-permute-start.16 = (bf16[32,3584]{1,0:T(8,128)(2,1)S(1)}, bf16[32,3584]{1,0:T(8,128)(2,1)S(1)}, u32[]{:S(2)}, u32[]{:S(2)}) collective-permute-start(bf16[32,3584]{1,0:T(8,128)(2,1)S(1)} %get-tuple-element.70), channel_id=1, source_target_pairs={{0,16},{8,24},{16,0},{24,8},{1,17},{9,25},{17,1},{25,9},{2,18},{10... | collective-permute-start | bytes 688136 | tf_op jit(solution)/shard_map/ppermute | solution.py:34
  84.8 4.5 %collective-permute-done.11.second_ref = bf16[32,3584]{1,0:T(8,128)(2,1)S(1)} collective-permute-done((bf16[32,3584]{1,0:T(8,128)(2,1)S(1)}, bf16[32,3584]{1,0:T(8,128)(2,1)S(1)}, u32[]{:S(2)}, u32[]{:S(2)}) %collective-permute-start.11) | collective-permute-done | bytes 229408 | tf_op jit(solution)/shard_map/ppermute | solution.py:34
  89.3 1.6 %collective-permute-start.12 = (bf16[16,3584]{1,0:T(8,128)(2,1)S(1)}, bf16[16,3584]{1,0:T(8,128)(2,1)S(1)}, u32[]{:S(2)}, u32[]{:S(2)}) collective-permute-start(bf16[16,3584]{1,0:T(8,128)(2,1)S(1)} %get-tuple-element.59), channel_id=1, source_target_pairs={{0,16},{8,24},{16,0},{24,8},{1,17},{9,25},{17,1},{25,9},{2,18},{10... | collective-permute-start | bytes 344072 | tf_op jit(solution)/shard_map/ppermute | solution.py:34
  91.0 1.6 %collective-permute-start.17 = (bf16[16,3584]{1,0:T(8,128)(2,1)S(1)}, bf16[16,3584]{1,0:T(8,128)(2,1)S(1)}, u32[]{:S(2)}, u32[]{:S(2)}) collective-permute-start(bf16[16,3584]{1,0:T(8,128)(2,1)S(1)} %get-tuple-element.72), channel_id=1, source_target_pairs={{0,8},{8,0},{16,24},{24,16},{1,9},{9,1},{17,25},{25,17},{2,10},{10... | collective-permute-start | bytes 344072 | tf_op jit(solution)/shard_map/ppermute | solution.py:34
  92.5 1.6 %collective-permute-done.12.second_ref = bf16[16,3584]{1,0:T(8,128)(2,1)S(1)} collective-permute-done((bf16[16,3584]{1,0:T(8,128)(2,1)S(1)}, bf16[16,3584]{1,0:T(8,128)(2,1)S(1)}, u32[]{:S(2)}, u32[]{:S(2)}) %collective-permute-start.12) | collective-permute-done | bytes 114720 | tf_op jit(solution)/shard_map/ppermute | solution.py:34
  94.2 0.5 collective-permute-start.13
  94.7 1.1 %collective-permute-done.17.second_ref = bf16[16,3584]{1,0:T(8,128)(2,1)S(1)} collective-permute-done((bf16[16,3584]{1,0:T(8,128)(2,1)S(1)}, bf16[16,3584]{1,0:T(8,128)(2,1)S(1)}, u32[]{:S(2)}, u32[]{:S(2)}) %collective-permute-start.17) | collective-permute-done | bytes 114720 | tf_op jit(solution)/shard_map/ppermute | solution.py:34
  95.9 0.5 collective-permute-start.18
  96.4 2.0 %collective-permute-done.13.second_ref = bf16[8,3584]{1,0:T(8,128)(2,1)S(1)} collective-permute-done((bf16[8,3584]{1,0:T(8,128)(2,1)S(1)}, bf16[8,3584]{1,0:T(8,128)(2,1)S(1)}, u32[]{:S(2)}, u32[]{:S(2)}) %collective-permute-start.13) | collective-permute-done | bytes 57376 | tf_op jit(solution)/shard_map/ppermute | solution.py:34
  98.5 0.4 collective-permute-start.14
  98.9 1.5 %collective-permute-done.18.second_ref = bf16[8,3584]{1,0:T(8,128)(2,1)S(1)} collective-permute-done((bf16[8,3584]{1,0:T(8,128)(2,1)S(1)}, bf16[8,3584]{1,0:T(8,128)(2,1)S(1)}, u32[]{:S(2)}, u32[]{:S(2)}) %collective-permute-start.18) | collective-permute-done | bytes 57376 | tf_op jit(solution)/shard_map/ppermute | solution.py:34
  100.4 1.2 %collective-permute-start.19 = (bf16[4,3584]{1,0:T(4,128)(2,1)S(1)}, bf16[4,3584]{1,0:T(4,128)(2,1)S(1)}, u32[]{:S(2)}, u32[]{:S(2)}) collective-permute-start(bf16[4,3584]{1,0:T(4,128)(2,1)S(1)} %get-tuple-element.76), channel_id=1, source_target_pairs={{0,4},{1,5},{2,6},{3,7},{4,0},{5,1},{6,2},{7,3},{8,12},{9,13},{10,... | collective-permute-start | bytes 86024 | tf_op jit(solution)/shard_map/ppermute | solution.py:34
  101.6 2.1 %collective-permute-done.14 = bf16[4,3584]{1,0:T(4,128)(2,1)S(1)} collective-permute-done((bf16[4,3584]{1,0:T(4,128)(2,1)S(1)}, bf16[4,3584]{1,0:T(4,128)(2,1)S(1)}, u32[]{:S(2)}, u32[]{:S(2)}) %collective-permute-start.14) | collective-permute-done | bytes 28704 | tf_op jit(solution)/shard_map/ppermute | solution.py:34
  103.6 1.6 %collective-permute-done.19 = bf16[4,3584]{1,0:T(4,128)(2,1)S(1)} collective-permute-done((bf16[4,3584]{1,0:T(4,128)(2,1)S(1)}, bf16[4,3584]{1,0:T(4,128)(2,1)S(1)}, u32[]{:S(2)}, u32[]{:S(2)}) %collective-permute-start.19) | collective-permute-done | bytes 28704 | tf_op jit(solution)/shard_map/ppermute | solution.py:34
  105.2 0.7 pad_maximum_fusion
  (35 shorter events, 0.4 us)
Async XLA Ops:
  0.9 10.2 %collective-permute-start = (bf16[4,7296]{1,0:T(4,128)(2,1)S(1)}, bf16[4,7296]{1,0:T(4,128)(2,1)S(1)}, u32[]{:S(2)}, u32[]{:S(2)}) collective-permute-start(bf16[4,7296]{1,0:T(4,128)(2,1)S(1)} %shard_map.64.refs_1_.first_ref), channel_id=1, source_target_pairs={{0,4},{1,5},{2,6},{3,7},{4,0},{5,1},{6,2},{7,3},{8,12},{9,13},{10,... | collective-permute-start | bytes 175112 | tf_op jit(solution)/shard_map/ppermute | solution.py:34
  8.3 2.9 %copy-start = (bf16[7168,512]{1,0:T(8,128)(2,1)}, bf16[7168,512]{1,0:T(8,128)(2,1)S(1)}, u32[]{:S(2)}) copy-start(bf16[7168,512]{1,0:T(8,128)(2,1)S(1)} %get-tuple-element.49.refs_8_) | copy-start | bytes 22020100
  11.2 7.9 %collective-permute-start.1 = (bf16[8,7296]{1,0:T(8,128)(2,1)S(1)}, bf16[8,7296]{1,0:T(8,128)(2,1)S(1)}, u32[]{:S(2)}, u32[]{:S(2)}) collective-permute-start(bf16[8,7296]{1,0:T(8,128)(2,1)S(1)} %shard_map.66.refs_1_.first_ref), channel_id=1, source_target_pairs={{0,2},{1,3},{2,0},{3,1},{4,6},{5,7},{6,4},{7,5},{8,10},{9,11},{10,... | collective-permute-start | bytes 350216 | tf_op jit(solution)/shard_map/ppermute | solution.py:34
  16.1 3.0 %copy-start.2 = (bf16[7168,512]{1,0:T(8,128)(2,1)}, bf16[7168,512]{1,0:T(8,128)(2,1)S(1)}, u32[]{:S(2)}) copy-start(bf16[7168,512]{1,0:T(8,128)(2,1)S(1)} %get-tuple-element.50.refs_9_) | copy-start | bytes 22020100
  19.1 9.3 %collective-permute-start.4 = (bf16[16,3712]{1,0:T(8,128)(2,1)S(1)}, bf16[16,3712]{1,0:T(8,128)(2,1)S(1)}, u32[]{:S(2)}, u32[]{:S(2)}) collective-permute-start(bf16[16,3712]{1,0:T(8,128)(2,1)S(1)} %get-tuple-element.45.first_ref), channel_id=1, source_target_pairs={{0,16},{8,24},{16,0},{24,8},{1,17},{9,25},{17,1},{25,9},{2,18},{10... | collective-permute-start | bytes 356360 | tf_op jit(solution)/shard_map/ppermute | solution.py:34
  20.7 8.3 %collective-permute-start.2 = (bf16[16,3584]{1,0:T(8,128)(2,1)S(1)}, bf16[16,3584]{1,0:T(8,128)(2,1)S(1)}, u32[]{:S(2)}, u32[]{:S(2)}) collective-permute-start(bf16[16,3584]{1,0:T(8,128)(2,1)S(1)} %get-tuple-element.43.refs_1_.first_ref), channel_id=1, source_target_pairs={{0,8},{8,0},{16,24},{24,16},{1,9},{9,1},{17,25},{25,17},{2,10},{10... | collective-permute-start | bytes 344072 | tf_op jit(solution)/shard_map/ppermute | solution.py:34
  25.4 2.9 %copy-start.4 = (bf16[7168,512]{1,0:T(8,128)(2,1)}, bf16[7168,512]{1,0:T(8,128)(2,1)S(1)}, u32[]{:S(2)}) copy-start(bf16[7168,512]{1,0:T(8,128)(2,1)S(1)} %get-tuple-element.51.refs_10_) | copy-start | bytes 22020100
  28.4 10.3 %collective-permute-start.5 = (bf16[32,3712]{1,0:T(8,128)(2,1)S(1)}, bf16[32,3712]{1,0:T(8,128)(2,1)S(1)}, u32[]{:S(2)}, u32[]{:S(2)}) collective-permute-start(bf16[32,3712]{1,0:T(8,128)(2,1)S(1)} %shard_map.71.refs_4_), channel_id=1, source_target_pairs={{0,8},{8,0},{16,24},{24,16},{1,9},{9,1},{17,25},{25,17},{2,10},{10... | collective-permute-start | bytes 712712 | tf_op jit(solution)/shard_map/ppermute | solution.py:34
  29.0 9.7 %collective-permute-start.3 = (bf16[32,3584]{1,0:T(8,128)(2,1)S(1)}, bf16[32,3584]{1,0:T(8,128)(2,1)S(1)}, u32[]{:S(2)}, u32[]{:S(2)}) collective-permute-start(bf16[32,3584]{1,0:T(8,128)(2,1)S(1)} %shard_map.70.refs_2_.refs_0_), channel_id=1, source_target_pairs={{0,16},{8,24},{16,0},{24,8},{1,17},{9,25},{17,1},{25,9},{2,18},{10... | collective-permute-start | bytes 688136 | tf_op jit(solution)/shard_map/ppermute | solution.py:34
  34.0 3.0 %copy-start.6 = (bf16[7168,512]{1,0:T(8,128)(2,1)}, bf16[7168,512]{1,0:T(8,128)(2,1)S(1)}, u32[]{:S(2)}) copy-start(bf16[7168,512]{1,0:T(8,128)(2,1)S(1)} %get-tuple-element.52.refs_11_) | copy-start | bytes 22020100
  36.9 1.8 %copy-start.8 = (bf16[7168,256]{1,0:T(8,128)(2,1)}, bf16[7168,256]{1,0:T(8,128)(2,1)S(1)}, u32[]{:S(2)}) copy-start(bf16[7168,256]{1,0:T(8,128)(2,1)S(1)} %get-tuple-element.53.refs_12_) | copy-start | bytes 11010052
  38.7 2.2 %collective-permute-start.8 = (bf16[32,3712]{1,0:T(8,128)(2,1)S(1)}, bf16[32,3712]{1,0:T(8,128)(2,1)S(1)}, u32[]{:S(2)}, u32[]{:S(2)}) collective-permute-start(bf16[32,3712]{1,0:T(8,128)(2,1)S(1)} %shard_map.71.refs_4_), channel_id=1, source_target_pairs={{0,1},{1,0},{2,3},{3,2},{4,5},{5,4},{6,7},{7,6},{8,9},{9,8},{10,11... | collective-permute-start | bytes 712712 | tf_op jit(solution)/shard_map/ppermute | solution.py:34
  38.7 2.5 %collective-permute-start.9 = (bf16[32,3712]{1,0:T(8,128)(2,1)S(1)}, bf16[32,3712]{1,0:T(8,128)(2,1)S(1)}, u32[]{:S(2)}, u32[]{:S(2)}) collective-permute-start(bf16[32,3712]{1,0:T(8,128)(2,1)S(1)} %get-tuple-element.48.refs_5_), channel_id=1, source_target_pairs={{0,1},{1,0},{2,3},{3,2},{4,5},{5,4},{6,7},{7,6},{8,9},{9,8},{10,11... | collective-permute-start | bytes 712712 | tf_op jit(solution)/shard_map/ppermute | solution.py:34
  39.2 1.6 %collective-permute-start.6 = (bf16[32,3584]{1,0:T(8,128)(2,1)S(1)}, bf16[32,3584]{1,0:T(8,128)(2,1)S(1)}, u32[]{:S(2)}, u32[]{:S(2)}) collective-permute-start(bf16[32,3584]{1,0:T(8,128)(2,1)S(1)} %shard_map.70.refs_2_.refs_0_), channel_id=1, source_target_pairs={{0,1},{1,0},{2,3},{3,2},{4,5},{5,4},{6,7},{7,6},{8,9},{9,8},{10,11... | collective-permute-start | bytes 688136 | tf_op jit(solution)/shard_map/ppermute | solution.py:34
  39.3 1.9 %collective-permute-start.7 = (bf16[32,3584]{1,0:T(8,128)(2,1)S(1)}, bf16[32,3584]{1,0:T(8,128)(2,1)S(1)}, u32[]{:S(2)}, u32[]{:S(2)}) collective-permute-start(bf16[32,3584]{1,0:T(8,128)(2,1)S(1)} %get-tuple-element.47.refs_1_), channel_id=1, source_target_pairs={{0,1},{1,0},{2,3},{3,2},{4,5},{5,4},{6,7},{7,6},{8,9},{9,8},{10,11... | collective-permute-start | bytes 688136 | tf_op jit(solution)/shard_map/ppermute | solution.py:34
  41.2 3.1 %copy-start.1 = (bf16[7168,512]{1,0:T(8,128)(2,1)S(1)}, bf16[7168,512]{1,0:T(8,128)(2,1)}, u32[]{:S(2)}) copy-start(bf16[7168,512]{1,0:T(8,128)(2,1)} %copy-done) | copy-start | bytes 22020100
  44.3 3.1 %copy-start.3 = (bf16[7168,512]{1,0:T(8,128)(2,1)S(1)}, bf16[7168,512]{1,0:T(8,128)(2,1)}, u32[]{:S(2)}) copy-start(bf16[7168,512]{1,0:T(8,128)(2,1)} %copy-done.2) | copy-start | bytes 22020100
  47.4 3.1 %copy-start.5 = (bf16[7168,512]{1,0:T(8,128)(2,1)S(1)}, bf16[7168,512]{1,0:T(8,128)(2,1)}, u32[]{:S(2)}) copy-start(bf16[7168,512]{1,0:T(8,128)(2,1)} %copy-done.4) | copy-start | bytes 22020100
  50.5 3.1 %copy-start.7 = (bf16[7168,512]{1,0:T(8,128)(2,1)S(1)}, bf16[7168,512]{1,0:T(8,128)(2,1)}, u32[]{:S(2)}) copy-start(bf16[7168,512]{1,0:T(8,128)(2,1)} %copy-done.6) | copy-start | bytes 22020100
  53.6 2.0 %copy-start.9 = (bf16[7168,256]{1,0:T(8,128)(2,1)S(1)}, bf16[7168,256]{1,0:T(8,128)(2,1)}, u32[]{:S(2)}) copy-start(bf16[7168,256]{1,0:T(8,128)(2,1)} %copy-done.8) | copy-start | bytes 11010052
  75.9 5.5 %collective-permute-start.10 = (bf16[64,3584]{1,0:T(8,128)(2,1)S(1)}, bf16[64,3584]{1,0:T(8,128)(2,1)S(1)}, u32[]{:S(2)}, u32[]{:S(2)}) collective-permute-start(bf16[64,3584]{1,0:T(8,128)(2,1)S(1)} %get-tuple-element.55), channel_id=1, source_target_pairs={{0,1},{1,0},{2,3},{3,2},{4,5},{5,4},{6,7},{7,6},{8,9},{9,8},{10,11... | collective-permute-start | bytes 1376264 | tf_op jit(solution)/shard_map/ppermute | solution.py:34
  81.0 2.1 %collective-permute-start.15 = (bf16[64,3584]{1,0:T(8,128)(2,1)S(1)}, bf16[64,3584]{1,0:T(8,128)(2,1)S(1)}, u32[]{:S(2)}, u32[]{:S(2)}) collective-permute-start(bf16[64,3584]{1,0:T(8,128)(2,1)S(1)} %get-tuple-element.68), channel_id=1, source_target_pairs={{0,1},{1,0},{2,3},{3,2},{4,5},{5,4},{6,7},{7,6},{8,9},{9,8},{10,11... | collective-permute-start | bytes 1376264 | tf_op jit(solution)/shard_map/ppermute | solution.py:34
  81.5 7.7 %collective-permute-start.11 = (bf16[32,3584]{1,0:T(8,128)(2,1)S(1)}, bf16[32,3584]{1,0:T(8,128)(2,1)S(1)}, u32[]{:S(2)}, u32[]{:S(2)}) collective-permute-start(bf16[32,3584]{1,0:T(8,128)(2,1)S(1)} %get-tuple-element.57), channel_id=1, source_target_pairs={{0,8},{8,0},{16,24},{24,16},{1,9},{9,1},{17,25},{25,17},{2,10},{10... | collective-permute-start | bytes 688136 | tf_op jit(solution)/shard_map/ppermute | solution.py:34
  83.2 7.7 %collective-permute-start.16 = (bf16[32,3584]{1,0:T(8,128)(2,1)S(1)}, bf16[32,3584]{1,0:T(8,128)(2,1)S(1)}, u32[]{:S(2)}, u32[]{:S(2)}) collective-permute-start(bf16[32,3584]{1,0:T(8,128)(2,1)S(1)} %get-tuple-element.70), channel_id=1, source_target_pairs={{0,16},{8,24},{16,0},{24,8},{1,17},{9,25},{17,1},{25,9},{2,18},{10... | collective-permute-start | bytes 688136 | tf_op jit(solution)/shard_map/ppermute | solution.py:34
  89.3 4.9 %collective-permute-start.12 = (bf16[16,3584]{1,0:T(8,128)(2,1)S(1)}, bf16[16,3584]{1,0:T(8,128)(2,1)S(1)}, u32[]{:S(2)}, u32[]{:S(2)}) collective-permute-start(bf16[16,3584]{1,0:T(8,128)(2,1)S(1)} %get-tuple-element.59), channel_id=1, source_target_pairs={{0,16},{8,24},{16,0},{24,8},{1,17},{9,25},{17,1},{25,9},{2,18},{10... | collective-permute-start | bytes 344072 | tf_op jit(solution)/shard_map/ppermute | solution.py:34
  91.0 4.9 %collective-permute-start.17 = (bf16[16,3584]{1,0:T(8,128)(2,1)S(1)}, bf16[16,3584]{1,0:T(8,128)(2,1)S(1)}, u32[]{:S(2)}, u32[]{:S(2)}) collective-permute-start(bf16[16,3584]{1,0:T(8,128)(2,1)S(1)} %get-tuple-element.72), channel_id=1, source_target_pairs={{0,8},{8,0},{16,24},{24,16},{1,9},{9,1},{17,25},{25,17},{2,10},{10... | collective-permute-start | bytes 344072 | tf_op jit(solution)/shard_map/ppermute | solution.py:34
  94.2 4.2 %collective-permute-start.13 = (bf16[8,3584]{1,0:T(8,128)(2,1)S(1)}, bf16[8,3584]{1,0:T(8,128)(2,1)S(1)}, u32[]{:S(2)}, u32[]{:S(2)}) collective-permute-start(bf16[8,3584]{1,0:T(8,128)(2,1)S(1)} %get-tuple-element.61), channel_id=1, source_target_pairs={{0,2},{1,3},{2,0},{3,1},{4,6},{5,7},{6,4},{7,5},{8,10},{9,11},{10,... | collective-permute-start | bytes 172040 | tf_op jit(solution)/shard_map/ppermute | solution.py:34
  95.9 4.5 %collective-permute-start.18 = (bf16[8,3584]{1,0:T(8,128)(2,1)S(1)}, bf16[8,3584]{1,0:T(8,128)(2,1)S(1)}, u32[]{:S(2)}, u32[]{:S(2)}) collective-permute-start(bf16[8,3584]{1,0:T(8,128)(2,1)S(1)} %get-tuple-element.74), channel_id=1, source_target_pairs={{0,2},{1,3},{2,0},{3,1},{4,6},{5,7},{6,4},{7,5},{8,10},{9,11},{10,... | collective-permute-start | bytes 172040 | tf_op jit(solution)/shard_map/ppermute | solution.py:34
  98.5 5.1 %collective-permute-start.14 = (bf16[4,3584]{1,0:T(4,128)(2,1)S(1)}, bf16[4,3584]{1,0:T(4,128)(2,1)S(1)}, u32[]{:S(2)}, u32[]{:S(2)}) collective-permute-start(bf16[4,3584]{1,0:T(4,128)(2,1)S(1)} %get-tuple-element.63), channel_id=1, source_target_pairs={{0,4},{1,5},{2,6},{3,7},{4,0},{5,1},{6,2},{7,3},{8,12},{9,13},{10,... | collective-permute-start | bytes 86024 | tf_op jit(solution)/shard_map/ppermute | solution.py:34
  100.4 4.8 %collective-permute-start.19 = (bf16[4,3584]{1,0:T(4,128)(2,1)S(1)}, bf16[4,3584]{1,0:T(4,128)(2,1)S(1)}, u32[]{:S(2)}, u32[]{:S(2)}) collective-permute-start(bf16[4,3584]{1,0:T(4,128)(2,1)S(1)} %get-tuple-element.76), channel_id=1, source_target_pairs={{0,4},{1,5},{2,6},{3,7},{4,0},{5,1},{6,2},{7,3},{8,12},{9,13},{10,... | collective-permute-start | bytes 86024 | tf_op jit(solution)/shard_map/ppermute | solution.py:34

commit v5 on v1

v5 whole, which is shorter than its diff:
```python
import functools

import jax
import jax.numpy as jnp
from jax import lax
from jax.experimental import pallas as pl
from jax.experimental.pallas import tpu as pltpu
from jax.sharding import PartitionSpec as P

EXP_GRP = 8
LANES = 128
AXES = ("group", "expert")
VMEM = pltpu.VMEM
UNIT_BLOCK = 256
DOWN_BLOCK = 512
UP_RING = 3
DOWN_RING = 3
DEPTH_CUT = 1024


def in_vmem(value):
    return pltpu.with_memory_space_constraint(value, VMEM)


def in_hbm(value):
    return pltpu.with_memory_space_constraint(value, pltpu.HBM)


def whole_vmem(count):
    return [pl.BlockSpec(memory_space=VMEM)] * count


def swap(value, axis, size, mask):
    return lax.ppermute(value, axis, [(i, i ^ mask) for i in range(size)])


def swap_group(value, groups, members, masks):
    pairs = []
    for g in range(groups):
        for e in range(members):
            pairs.append((g * members + e, (g ^ masks[e % 2]) * members + e))
    return lax.ppermute(value, AXES, pairs)


def limit(amount):
    return pltpu.CompilerParams(vmem_limit_bytes=int(amount))


def cost(flops, amount):
    return pl.CostEstimate(flops=flops, bytes_accessed=amount, transcendentals=0)


def pack_kernel(me_ref, tokens_ref, ids_ref, weights_ref, out_ref):
    width = tokens_ref.shape[1]
    out_ref[:, :width] = tokens_ref[...]
    ids = ids_ref[...]
    weights = weights_ref[...].astype(jnp.float32)
    label = lax.broadcasted_iota(jnp.int32, (ids.shape[0], LANES), 1)
    route = jnp.zeros((ids.shape[0], LANES), jnp.float32)
    for k in range(ids.shape[1]):
        route += jnp.where(ids[:, k : k + 1] == label, weights[:, k : k + 1], 0.0)
    out_ref[:, width:] = route.astype(out_ref.dtype)


def pack(me, tokens, expert_ids, gate_weights):
    rows, width = tokens.shape
    args = (tokens, expert_ids, gate_weights)
    return pl.pallas_call(
        pack_kernel,
        grid=(1,),
        in_specs=[pl.BlockSpec(memory_space=pltpu.SMEM)]
        + [pl.BlockSpec(a.shape, lambda i: (0, 0)) for a in args],
        out_specs=whole_vmem(1)[0],
        out_shape=VMEM((rows, width + LANES), tokens.dtype),
        compiler_params=limit(2 * 1024 * 1024),
    )(me, *[in_hbm(a) for a in args])


def fetch_kernel(jobs, *refs):
    src_refs = refs[: len(jobs)]
    out_refs = refs[len(jobs) + 1 : 2 * len(jobs) + 1]
    mark_ref, sems = refs[-2:]
    copies = []
    for n, (_, first, columns) in enumerate(jobs):
        size = src_refs[n].shape[1] // 4
        for i in range(4):
            copies.append(
                pltpu.make_async_copy(
                    src_refs[n].at[0, pl.ds(i * size, size), pl.ds(first, columns)],
                    out_refs[n].at[pl.ds(i * size, size), :],
                    sems.at[n * 4 + i],
                )
            )
    for copy in copies:
        copy.start()
    mark_ref[...] = jnp.zeros_like(mark_ref)
    for copy in copies:
        copy.wait()


def fetch(jobs, after):
    if not jobs:
        return [], None
    rows = jobs[0][0].shape[1]
    hbm = pl.BlockSpec(memory_space=pltpu.HBM)
    *out, mark = pl.pallas_call(
        functools.partial(fetch_kernel, jobs),
        in_specs=[hbm] * len(jobs) + [pl.BlockSpec(memory_space=pl.ANY)],
        out_specs=whole_vmem(len(jobs) + 1),
        out_shape=[VMEM((rows, columns), w.dtype) for w, _, columns in jobs]
        + [VMEM((8, LANES), jnp.float32)],
        scratch_shapes=[pltpu.SemaphoreType.DMA((4 * len(jobs),))],
        compiler_params=limit(256 * 1024),
        cost_estimate=cost(0, sum(2 * rows * columns for _, _, columns in jobs)),
    )(*[in_hbm(w) for w, _, _ in jobs], after)
    return out, mark


def join_kernel(first_ref, second_ref, after_ref, out_ref):
    halves = [r[...].astype(jnp.float32) for r in (first_ref, second_ref)]
    out_ref[...] = jnp.concatenate(halves, axis=0).astype(out_ref.dtype)


def join(first, second, after):
    rows, width = first.shape
    after = first if after is None else after
    return pl.pallas_call(
        join_kernel,
        in_specs=whole_vmem(2) + [pl.BlockSpec(memory_space=pl.ANY)],
        out_specs=whole_vmem(1)[0],
        out_shape=VMEM((2 * rows, width), first.dtype),
        compiler_params=limit(1024 * 1024 + 16 * rows * width),
    )(in_vmem(first), in_vmem(second), after)


def hold_kernel(*refs):
    pass


def hold(value, after):
    if after is None:
        return value
    return pl.pallas_call(
        hold_kernel,
        in_specs=[pl.BlockSpec(memory_space=pl.ANY)] * 2,
        out_specs=pl.BlockSpec(memory_space=pl.ANY),
        out_shape=jax.ShapeDtypeStruct(value.shape, value.dtype),
        input_output_aliases={0: 0},
        compiler_params=limit(256 * 1024),
    )(value, after)


def times(left_ref, right_ref):
    depth = left_ref.shape[1]
    total = None
    for k in range(0, depth, DEPTH_CUT):
        inner = slice(k, min(depth, k + DEPTH_CUT))
        value = jnp.dot(left_ref[:, inner], right_ref[inner, :], preferred_element_type=jnp.float32)
        total = value if total is None else total + value
    return total


def expert_kernel(gate_at, up_at, streamed, held, *refs):
    x_refs, w_refs, refs = refs[:4], refs[4 : 4 + held], refs[4 + held :]
    up_hbm, down_hbm, me_ref, own_ref, far_ref = refs[:5]
    x, hidden, scale_ref, up_ring, down_ring, up_sem, down_sem = refs[5:]
    depth, units = x.shape[1], hidden.shape[1]
    blocks = units // UNIT_BLOCK
    downs = depth // DOWN_BLOCK

    def up_copy(n):
        return pltpu.make_async_copy(
            up_hbm.at[0, :, pl.ds(streamed[n] * UNIT_BLOCK, UNIT_BLOCK)],
            up_ring.at[n % UP_RING],
            up_sem.at[n % UP_RING],
        )

    def down_copy(d, slot):
        first = d * DOWN_BLOCK
        if not isinstance(d, int):
            first = pl.multiple_of(first, DOWN_BLOCK)
        return pltpu.make_async_copy(
            down_hbm.at[0, :, pl.ds(first, DOWN_BLOCK)], down_ring.at[slot], down_sem.at[slot]
        )

    later = {}
    for n in range(min(DOWN_RING, downs)):
        later.setdefault(min(blocks - 1, 2 + n), []).append(down_copy(n, n))
    for n in range(min(UP_RING, len(streamed))):
        up_copy(n).start()

    part = x_refs[0].shape[0]
    for n, x_ref in enumerate(x_refs):
        x[n * part : (n + 1) * part, :] = x_ref[:, :depth]
        route = x_ref[:, depth:].astype(jnp.float32)
        lane = lax.broadcasted_iota(jnp.int32, route.shape, 1)
        scale = jnp.sum(jnp.where(lane == me_ref[0], route, 0.0), axis=1, keepdims=True)
        scale_ref[n * part : (n + 1) * part, :] = jnp.broadcast_to(scale, route.shape)

    for b in range(blocks):
        where, first = gate_at[b]
        gate = times(x, w_refs[where].at[:, first : first + UNIT_BLOCK])
        if up_at[b] is None:
            n = streamed.index(b)
            up_copy(n).wait()
            up = times(x, up_ring.at[n % UP_RING])
            if n + UP_RING < len(streamed):
                up_copy(n + UP_RING).start()
        else:
            where, first = up_at[b]
            up = times(x, w_refs[where].at[:, first : first + UNIT_BLOCK])
        for copy in later.get(b, []):
            copy.start()
        hidden[:, b * UNIT_BLOCK : (b + 1) * UNIT_BLOCK] = (jax.nn.silu(gate) * up).astype(
            jnp.bfloat16
        )

    @pl.loop(0, downs)
    def _(d):
        slot = lax.rem(d, DOWN_RING)
        columns = pl.ds(pl.multiple_of(d * DOWN_BLOCK, DOWN_BLOCK), DOWN_BLOCK)
        down_copy(d, slot).wait()
        value = (times(hidden, down_ring.at[slot]) * scale_ref[:, :1]).astype(jnp.bfloat16)

        @pl.when(d + DOWN_RING < downs)
        def _():
            down_copy(d + DOWN_RING, slot).start()

        own_ref[:, columns] = value[: 2 * part]
        far_ref[:, columns] = value[2 * part :]


def run_expert(parts, held, gate_at, up_at, streamed, w_up, w_down, me):
    rows = sum(p.shape[0] for p in parts)
    depth, units = w_up.shape[1], w_up.shape[2]
    half = VMEM((rows // 2, depth), jnp.bfloat16)
    hbm = pl.BlockSpec(memory_space=pltpu.HBM)
    ring = max(1, min(UP_RING, len(streamed)))
    scratch = 2 * (
        rows * (depth + units + 2 * LANES)
        + ring * depth * UNIT_BLOCK
        + DOWN_RING * units * DOWN_BLOCK
    )
    work = 2560 * 1024 + 12 * rows * UNIT_BLOCK + 4 * rows * DOWN_BLOCK
    args = [in_vmem(v) for v in [*parts, *held]]
    return pl.pallas_call(
        functools.partial(expert_kernel, gate_at, up_at, streamed, len(held)),
        in_specs=whole_vmem(len(args)) + [hbm, hbm, pl.BlockSpec(memory_space=pltpu.SMEM)],
        out_specs=whole_vmem(2),
        out_shape=(half, half),
        scratch_shapes=[
            VMEM((rows, depth), jnp.bfloat16),
            VMEM((rows, units), jnp.bfloat16),
            VMEM((rows, LANES), jnp.float32),
            VMEM((ring, depth, UNIT_BLOCK), jnp.bfloat16),
            VMEM((DOWN_RING, units, DOWN_BLOCK), jnp.bfloat16),
            pltpu.SemaphoreType.DMA((ring,)),
            pltpu.SemaphoreType.DMA((DOWN_RING,)),
        ],
        compiler_params=limit(scratch + work),
        cost_estimate=cost(6 * rows * depth * units, 4 * depth * units),
    )(*args, in_hbm(w_up), in_hbm(w_down), me)


def fold_kernel(first_ref, second_ref, keep_ref, send_ref):
    total = first_ref[...].astype(jnp.float32) + second_ref[...].astype(jnp.float32)
    half = keep_ref.shape[0]
    keep_ref[...] = total[:half].astype(keep_ref.dtype)
    send_ref[...] = total[half:].astype(send_ref.dtype)


def fold(first, second):
    rows, width = first.shape
    return pl.pallas_call(
        fold_kernel,
        in_specs=whole_vmem(2),
        out_specs=whole_vmem(2),
        out_shape=[VMEM((rows // 2, width), first.dtype)] * 2,
        compiler_params=limit(1024 * 1024 + 10 * rows * width),
    )(in_vmem(first), in_vmem(second))


def give_back(own, far, groups, members):
    keep, send = fold(own, swap(far, "expert", members, 1))
    keep, send = fold(keep, swap_group(send, groups, members, (2, 1)))
    keep, send = fold(keep, swap_group(send, groups, members, (1, 2)))
    mask = 2
    while mask < members // 2:
        keep, send = fold(keep, swap(send, "expert", members, mask))
        mask *= 2
    got = swap(send, "expert", members, mask)
    return (keep.astype(jnp.float32) + got.astype(jnp.float32)).astype(jnp.bfloat16)


def on_device(tokens, expert_ids, gate_weights, w_gate, w_up, w_down):
    groups = lax.axis_size("group")
    members = lax.axis_size("expert")
    split = members // EXP_GRP
    me = lax.axis_index("group") * EXP_GRP + lax.axis_index("expert") // split
    me = me.astype(jnp.int32).reshape(1)
    blocks = w_gate.shape[2] // UNIT_BLOCK
    ups = max(1, blocks // 8)
    group = -(-blocks // 4)

    jobs, gate_at, count = [], [], 0
    for n in range(4):
        inside = list(range(n * group, min(blocks, (n + 1) * group)))
        job = []
        if inside:
            job.append((w_gate, inside[0] * UNIT_BLOCK, len(inside) * UNIT_BLOCK))
            gate_at += [(count, i * UNIT_BLOCK) for i in range(len(inside))]
            count += 1
        jobs.append(job)
    jobs[3].append((w_up, 0, ups * UNIT_BLOCK))
    up_at = [(count, b * UNIT_BLOCK) if b < ups else None for b in range(blocks)]
    streamed = list(range(ups, blocks))

    value = pack(me, tokens, expert_ids, gate_weights)
    held = []
    mask = members // 2
    number = 0
    while mask > 1:
        got = swap(value, "expert", members, mask)
        more, mark = fetch(jobs[number] if number < 2 else [], value)
        held += more
        value = join(value, got, mark)
        mask //= 2
        number += 1
    got = swap_group(value, groups, members, (1, 2))
    more, mark = fetch(jobs[2], value)
    held += more
    value = join(value, got, mark)
    got = swap_group(value, groups, members, (2, 1))
    core = swap(value, "expert", members, 1)
    more, mark = fetch(jobs[3], value)
    held += more
    got = hold(got, mark)
    parts = [value, got, core, swap(got, "expert", members, 1)]
    own, far = run_expert(parts, held, gate_at, up_at, streamed, w_up, w_down, me)
    return give_back(own, far, groups, members)


def solution(mesh):
    in_specs = (
        P(AXES, None),
        P(AXES, None),
        P(AXES, None),
        P(AXES, None, None),
        P(AXES, None, None),
        P(AXES, None, None),
    )
    out_specs = P(AXES, None)
    return jax.shard_map(
        on_device, mesh=mesh, in_specs=in_specs, out_specs=out_specs, check_vma=False
    )
```

time: 246 us -> 80.8 us (0.33)
  waiting for transfers between devices: 191 us -> 24.1 us
  Pallas kernels: 0 us -> 37.9 us
  matrix products: 33.2 us -> 0 us
  starting transfers between devices: 0.04 us -> 17.8 us
  between operations: 13.4 us -> 0.1 us
  local copies, waits for them, and re-layouts: 4.51 us -> 0 us
    unnamed x3 -> x0, waiting for transfers between devices: 132 us -> none
    all_gather x1 -> x0, waiting for transfers between devices: 59.4 us -> none  [on_device(): everyone = lax.all_gather(packed, AXES, axis=0, tiled=True)]
    pallas_call x0 -> x14, Pallas kernels: none -> 37.9 us  [the longest x1 22.5 us: run_expert(): pl.pallas_call(functools.partial(expert_kernel, gate_at, up_at, streamed,...]
    dot_general x2 -> x0, matrix products: 33.2 us -> none  [the longest x1 21.8 us: on_device(): part = jnp.dot(hidden, w_down[0], preferred_element_type=jnp.float32)]
    ppermute x0 -> x11, waiting for transfers between devices: none -> 24.1 us  [the longest x4 14.1 us: swap_group(): return lax.ppermute(value, AXES, pairs)]
    ppermute x0 -> x11, starting transfers between devices: none -> 17.8 us  [the longest x7 10.1 us: swap(): return lax.ppermute(value, axis, [(i, i ^ mask) for i in range(size)])]
    unnamed x2 -> x0, local copies, waits for them, and re-layouts: 4.51 us -> none
  transfers between devices with their start and end apart: 2 -> 11, of which waited for: 2 -> 8; matrix products, arithmetic and copies ran while one was open for 0% -> 0% of each run, Pallas kernels for 0% -> 17%
where the time goes in v5:
time: 80.8 us; the launch traced here: 80.6 us
  Pallas kernels  37.9 us (47%)
  waiting for transfers between devices  24.1 us (30%)
  starting transfers between devices  17.8 us (22%)
    pallas_call x1, Pallas kernels, run_expert(): pl.pallas_call(functools.partial(expert_kernel, gate_at, up_at, streamed,...  22.5 us
    ppermute x4, waiting for transfers between devices, swap_group(): return lax.ppermute(value, AXES, pairs)  14.1 us
    pallas_call x4, Pallas kernels, fetch(): pl.pallas_call(functools.partial(fetch_kernel, jobs), in_specs=[hbm] * le...  14 us
    ppermute x7, starting transfers between devices, swap(): return lax.ppermute(value, axis, [(i, i ^ mask) for i in range(size)])  10.1 us
    ppermute x7, waiting for transfers between devices, swap(): return lax.ppermute(value, axis, [(i, i ^ mask) for i in range(size)])  10 us
    ppermute x4, starting transfers between devices, swap_group(): return lax.ppermute(value, AXES, pairs)  7.73 us
  transfers between devices with their start and end apart: 11, of which 8 were waited for; matrix products, arithmetic and copies ran while one was open for 0% of the time, Pallas kernels for 17%

profile of v5, /device:TPU:0, one launch (start us, length us, event | category | flops | bytes accessed | tf_op | source)
XLA Modules:
  0.0 80.6 jit_solution(3959471896460279738)
XLA Ops:
  0.0 0.9 %shard_map.64.refs_1_.first_ref = bf16[4,7296]{1,0:T(4,128)(2,1)S(1)} custom-call(s32[1]{0:T(128)} %bitcast.me_ref.refs_11_, bf16[4,7168]{1,0:T(4,128)(2,1)} %tokens_ref.1, s32[4,8]{1,0:T(4,128)} %ids_ref.1, bf16[4,8]{1,0:T(4,128)(2,1)} %weights_ref.1), custom_call_target="tpu_custom_call" | custom-call | tf_op jit(solution)/shard_map/pallas_call | solution.py:68
  0.9 4.1 %collective-permute-start = (bf16[4,7296]{1,0:T(4,128)(2,1)S(1)}, bf16[4,7296]{1,0:T(4,128)(2,1)S(1)}, u32[]{:S(2)}, u32[]{:S(2)}) collective-permute-start(bf16[4,7296]{1,0:T(4,128)(2,1)S(1)} %shard_map.64.refs_1_.first_ref), channel_id=1, source_target_pairs={{0,4},{1,5},{2,6},{3,7},{4,0},{5,1},{6,2},{7,3},{8,12},{9,13},{10,... | collective-permute-start | bytes 175112 | tf_op jit(solution)/shard_map/ppermute | solution.py:34
  5.0 3.2 %shard_map.65 = (bf16[7168,512]{1,0:T(8,128)(2,1)S(1)}, f32[8,128]{1,0:T(8,128)S(1)}) custom-call(bf16[1,7168,2048]{2,1,0:T(8,128)(2,1)} %refs_0_.7, bf16[4,7296]{1,0:T(4,128)(2,1)S(1)} %shard_map.64.refs_1_.first_ref), custom_call_target="tpu_custom_call" | custom-call | bytes 7340032 | tf_op jit(solution)/shard_map/pallas_call | solution.py:106
  8.3 0.0 collective-permute-done.second_ref
  8.3 1.6 %collective-permute-start.1 = (bf16[8,7296]{1,0:T(8,128)(2,1)S(1)}, bf16[8,7296]{1,0:T(8,128)(2,1)S(1)}, u32[]{:S(2)}, u32[]{:S(2)}) collective-permute-start(bf16[8,7296]{1,0:T(8,128)(2,1)S(1)} %shard_map.66.refs_1_.first_ref), channel_id=1, source_target_pairs={{0,2},{1,3},{2,0},{3,1},{4,6},{5,7},{6,4},{7,5},{8,10},{9,11},{10,... | collective-permute-start | bytes 350216 | tf_op jit(solution)/shard_map/ppermute | solution.py:34
  10.0 3.2 %shard_map.67 = (bf16[7168,512]{1,0:T(8,128)(2,1)S(1)}, f32[8,128]{1,0:T(8,128)S(1)}) custom-call(bf16[1,7168,2048]{2,1,0:T(8,128)(2,1)} %refs_0_.7, bf16[8,7296]{1,0:T(8,128)(2,1)S(1)} %shard_map.66.refs_1_.first_ref), custom_call_target="tpu_custom_call" | custom-call | bytes 7340032 | tf_op jit(solution)/shard_map/pallas_call | solution.py:106
  13.2 0.0 collective-permute-done.1.second_ref
  13.2 1.9 %collective-permute-start.2 = (bf16[16,7296]{1,0:T(8,128)(2,1)S(1)}, bf16[16,7296]{1,0:T(8,128)(2,1)S(1)}, u32[]{:S(2)}, u32[]{:S(2)}) collective-permute-start(bf16[16,7296]{1,0:T(8,128)(2,1)S(1)} %shard_map.68.refs_1_.first_ref), channel_id=1, source_target_pairs={{0,8},{1,17},{2,10},{3,19},{4,12},{5,21},{6,14},{7,23},{8,0},{9,25... | collective-permute-start | bytes 700424 | tf_op jit(solution)/shard_map/ppermute | solution.py:42
  15.2 3.2 %shard_map.69 = (bf16[7168,512]{1,0:T(8,128)(2,1)S(1)}, f32[8,128]{1,0:T(8,128)S(1)}) custom-call(bf16[1,7168,2048]{2,1,0:T(8,128)(2,1)} %refs_0_.7, bf16[16,7296]{1,0:T(8,128)(2,1)S(1)} %shard_map.68.refs_1_.first_ref), custom_call_target="tpu_custom_call" | custom-call | bytes 7340032 | tf_op jit(solution)/shard_map/pallas_call | solution.py:106
  18.4 1.0 %collective-permute-done.2.second_ref = bf16[16,7296]{1,0:T(8,128)(2,1)S(1)} collective-permute-done((bf16[16,7296]{1,0:T(8,128)(2,1)S(1)}, bf16[16,7296]{1,0:T(8,128)(2,1)S(1)}, u32[]{:S(2)}, u32[]{:S(2)}) %collective-permute-start.2) | collective-permute-done | bytes 233504 | tf_op jit(solution)/shard_map/ppermute | solution.py:42
  19.4 1.9 %collective-permute-start.3 = (bf16[32,7296]{1,0:T(8,128)(2,1)S(1)}, bf16[32,7296]{1,0:T(8,128)(2,1)S(1)}, u32[]{:S(2)}, u32[]{:S(2)}) collective-permute-start(bf16[32,7296]{1,0:T(8,128)(2,1)S(1)} %shard_map.70.refs_2_.refs_0_), channel_id=1, source_target_pairs={{0,16},{1,9},{2,18},{3,11},{4,20},{5,13},{6,22},{7,15},{8,24},{9,1... | collective-permute-start | bytes 1400840 | tf_op jit(solution)/shard_map/ppermute | solution.py:42
  21.3 0.0 collective-permute-start.4
  21.4 4.3 %shard_map.71 = (bf16[7168,512]{1,0:T(8,128)(2,1)S(1)}, bf16[7168,256]{1,0:T(8,128)(2,1)S(1)}, f32[8,128]{1,0:T(8,128)S(1)}) custom-call(bf16[1,7168,2048]{2,1,0:T(8,128)(2,1)} %refs_0_.7, bf16[1,7168,2048]{2,1,0:T(8,128)(2,1)} %refs_9_.1, bf16[32,7296]{1,0:T(8,128)(2,1)S(1)} %shard_map.70.refs_2_.refs_0_), custom_call_target="tpu_custom_call" | custom-call | bytes 11010048 | tf_op jit(solution)/shard_map/pallas_call | solution.py:106
  25.7 2.3 %collective-permute-done.3.refs_0_ = bf16[32,7296]{1,0:T(8,128)(2,1)S(1)} collective-permute-done((bf16[32,7296]{1,0:T(8,128)(2,1)S(1)}, bf16[32,7296]{1,0:T(8,128)(2,1)S(1)}, u32[]{:S(2)}, u32[]{:S(2)}) %collective-permute-start.3) | collective-permute-done | bytes 466976 | tf_op jit(solution)/shard_map/ppermute | solution.py:42
  28.0 0.0 collective-permute-start.5
  28.0 0.0 collective-permute-done.4.refs_2_
  28.0 1.8 %collective-permute-done.5.refs_3_ = bf16[32,7296]{1,0:T(8,128)(2,1)S(1)} collective-permute-done((bf16[32,7296]{1,0:T(8,128)(2,1)S(1)}, bf16[32,7296]{1,0:T(8,128)(2,1)S(1)}, u32[]{:S(2)}, u32[]{:S(2)}) %collective-permute-start.5) | collective-permute-done | bytes 466976 | tf_op jit(solution)/shard_map/ppermute | solution.py:34
  29.9 22.5 %shard_map.73 = (bf16[64,7168]{1,0:T(8,128)(2,1)S(1)}, bf16[64,7168]{1,0:T(8,128)(2,1)S(1)}) custom-call(bf16[32,7296]{1,0:T(8,128)(2,1)S(1)} %shard_map.70.refs_2_.refs_0_, bf16[32,7296]{1,0:T(8,128)(2,1)S(1)} %shard_map.72.refs_1_, bf16[32,7296]{1,0:T(8,128)(2,1)S(1)} %collective-permute-done.4.refs_2_, ...), custom_call_target="tpu_custom_call" | custom-call | flops 11274289152 | bytes 58720256 | tf_op jit(solution)/shard_map/pallas_call | solution.py:246
  52.3 0.2 collective-permute-start.6
  52.5 2.3 %collective-permute-done.6.second_ref = bf16[64,7168]{1,0:T(8,128)(2,1)S(1)} collective-permute-done((bf16[64,7168]{1,0:T(8,128)(2,1)S(1)}, bf16[64,7168]{1,0:T(8,128)(2,1)S(1)}, u32[]{:S(2)}, u32[]{:S(2)}) %collective-permute-start.6) | collective-permute-done | bytes 917536 | tf_op jit(solution)/shard_map/ppermute | solution.py:34
  54.9 0.2 shard_map.74
  55.1 1.9 %collective-permute-start.7 = (bf16[32,7168]{1,0:T(8,128)(2,1)S(1)}, bf16[32,7168]{1,0:T(8,128)(2,1)S(1)}, u32[]{:S(2)}, u32[]{:S(2)}) collective-permute-start(bf16[32,7168]{1,0:T(8,128)(2,1)S(1)} %get-tuple-element.36), channel_id=1, source_target_pairs={{0,16},{1,9},{2,18},{3,11},{4,20},{5,13},{6,22},{7,15},{8,24},{9,1... | collective-permute-start | bytes 1376264 | tf_op jit(solution)/shard_map/ppermute | solution.py:42
  57.0 6.6 %collective-permute-done.7.second_ref = bf16[32,7168]{1,0:T(8,128)(2,1)S(1)} collective-permute-done((bf16[32,7168]{1,0:T(8,128)(2,1)S(1)}, bf16[32,7168]{1,0:T(8,128)(2,1)S(1)}, u32[]{:S(2)}, u32[]{:S(2)}) %collective-permute-start.7) | collective-permute-done | bytes 458784 | tf_op jit(solution)/shard_map/ppermute | solution.py:42
  63.6 0.1 shard_map.75
  63.7 1.9 %collective-permute-start.8 = (bf16[16,7168]{1,0:T(8,128)(2,1)S(1)}, bf16[16,7168]{1,0:T(8,128)(2,1)S(1)}, u32[]{:S(2)}, u32[]{:S(2)}) collective-permute-start(bf16[16,7168]{1,0:T(8,128)(2,1)S(1)} %get-tuple-element.38), channel_id=1, source_target_pairs={{0,8},{1,17},{2,10},{3,19},{4,12},{5,21},{6,14},{7,23},{8,0},{9,25... | collective-permute-start | bytes 688136 | tf_op jit(solution)/shard_map/ppermute | solution.py:42
  65.7 4.2 %collective-permute-done.8.second_ref = bf16[16,7168]{1,0:T(8,128)(2,1)S(1)} collective-permute-done((bf16[16,7168]{1,0:T(8,128)(2,1)S(1)}, bf16[16,7168]{1,0:T(8,128)(2,1)S(1)}, u32[]{:S(2)}, u32[]{:S(2)}) %collective-permute-start.8) | collective-permute-done | bytes 229408 | tf_op jit(solution)/shard_map/ppermute | solution.py:42
  69.8 0.1 shard_map.76
  69.9 1.6 %collective-permute-start.9 = (bf16[8,7168]{1,0:T(8,128)(2,1)S(1)}, bf16[8,7168]{1,0:T(8,128)(2,1)S(1)}, u32[]{:S(2)}, u32[]{:S(2)}) collective-permute-start(bf16[8,7168]{1,0:T(8,128)(2,1)S(1)} %get-tuple-element.40), channel_id=1, source_target_pairs={{0,2},{1,3},{2,0},{3,1},{4,6},{5,7},{6,4},{7,5},{8,10},{9,11},{10,... | collective-permute-start | bytes 344072 | tf_op jit(solution)/shard_map/ppermute | solution.py:34
  71.5 3.2 %collective-permute-done.9.second_ref = bf16[8,7168]{1,0:T(8,128)(2,1)S(1)} collective-permute-done((bf16[8,7168]{1,0:T(8,128)(2,1)S(1)}, bf16[8,7168]{1,0:T(8,128)(2,1)S(1)}, u32[]{:S(2)}, u32[]{:S(2)}) %collective-permute-start.9) | collective-permute-done | bytes 114720 | tf_op jit(solution)/shard_map/ppermute | solution.py:34
  74.8 2.5 %collective-permute-start.10 = (bf16[4,7168]{1,0:T(4,128)(2,1)S(1)}, bf16[4,7168]{1,0:T(4,128)(2,1)S(1)}, u32[]{:S(2)}, u32[]{:S(2)}) collective-permute-start(bf16[4,7168]{1,0:T(4,128)(2,1)S(1)} %get-tuple-element.42), channel_id=1, source_target_pairs={{0,4},{1,5},{2,6},{3,7},{4,0},{5,1},{6,2},{7,3},{8,12},{9,13},{10,... | collective-permute-start | bytes 172040 | tf_op jit(solution)/shard_map/ppermute | solution.py:34
  77.3 2.6 %collective-permute-done.10 = bf16[4,7168]{1,0:T(4,128)(2,1)S(1)} collective-permute-done((bf16[4,7168]{1,0:T(4,128)(2,1)S(1)}, bf16[4,7168]{1,0:T(4,128)(2,1)S(1)}, u32[]{:S(2)}, u32[]{:S(2)}) %collective-permute-start.10) | collective-permute-done | bytes 57376 | tf_op jit(solution)/shard_map/ppermute | solution.py:34
  79.9 0.7 add_convert_fusion
  (5 shorter events, 0.1 us)
Async XLA Ops:
  0.9 7.3 %collective-permute-start = (bf16[4,7296]{1,0:T(4,128)(2,1)S(1)}, bf16[4,7296]{1,0:T(4,128)(2,1)S(1)}, u32[]{:S(2)}, u32[]{:S(2)}) collective-permute-start(bf16[4,7296]{1,0:T(4,128)(2,1)S(1)} %shard_map.64.refs_1_.first_ref), channel_id=1, source_target_pairs={{0,4},{1,5},{2,6},{3,7},{4,0},{5,1},{6,2},{7,3},{8,12},{9,13},{10,... | collective-permute-start | bytes 175112 | tf_op jit(solution)/shard_map/ppermute | solution.py:34
  8.3 4.9 %collective-permute-start.1 = (bf16[8,7296]{1,0:T(8,128)(2,1)S(1)}, bf16[8,7296]{1,0:T(8,128)(2,1)S(1)}, u32[]{:S(2)}, u32[]{:S(2)}) collective-permute-start(bf16[8,7296]{1,0:T(8,128)(2,1)S(1)} %shard_map.66.refs_1_.first_ref), channel_id=1, source_target_pairs={{0,2},{1,3},{2,0},{3,1},{4,6},{5,7},{6,4},{7,5},{8,10},{9,11},{10,... | collective-permute-start | bytes 350216 | tf_op jit(solution)/shard_map/ppermute | solution.py:34
  13.2 6.1 %collective-permute-start.2 = (bf16[16,7296]{1,0:T(8,128)(2,1)S(1)}, bf16[16,7296]{1,0:T(8,128)(2,1)S(1)}, u32[]{:S(2)}, u32[]{:S(2)}) collective-permute-start(bf16[16,7296]{1,0:T(8,128)(2,1)S(1)} %shard_map.68.refs_1_.first_ref), channel_id=1, source_target_pairs={{0,8},{1,17},{2,10},{3,19},{4,12},{5,21},{6,14},{7,23},{8,0},{9,25... | collective-permute-start | bytes 700424 | tf_op jit(solution)/shard_map/ppermute | solution.py:42
  19.4 8.6 %collective-permute-start.3 = (bf16[32,7296]{1,0:T(8,128)(2,1)S(1)}, bf16[32,7296]{1,0:T(8,128)(2,1)S(1)}, u32[]{:S(2)}, u32[]{:S(2)}) collective-permute-start(bf16[32,7296]{1,0:T(8,128)(2,1)S(1)} %shard_map.70.refs_2_.refs_0_), channel_id=1, source_target_pairs={{0,16},{1,9},{2,18},{3,11},{4,20},{5,13},{6,22},{7,15},{8,24},{9,1... | collective-permute-start | bytes 1400840 | tf_op jit(solution)/shard_map/ppermute | solution.py:42
  21.3 6.7 %collective-permute-start.4 = (bf16[32,7296]{1,0:T(8,128)(2,1)S(1)}, bf16[32,7296]{1,0:T(8,128)(2,1)S(1)}, u32[]{:S(2)}, u32[]{:S(2)}) collective-permute-start(bf16[32,7296]{1,0:T(8,128)(2,1)S(1)} %shard_map.70.refs_2_.refs_0_), channel_id=1, source_target_pairs={{0,1},{1,0},{2,3},{3,2},{4,5},{5,4},{6,7},{7,6},{8,9},{9,8},{10,11... | collective-permute-start | bytes 1400840 | tf_op jit(solution)/shard_map/ppermute | solution.py:34
  28.0 1.8 %collective-permute-start.5 = (bf16[32,7296]{1,0:T(8,128)(2,1)S(1)}, bf16[32,7296]{1,0:T(8,128)(2,1)S(1)}, u32[]{:S(2)}, u32[]{:S(2)}) collective-permute-start(bf16[32,7296]{1,0:T(8,128)(2,1)S(1)} %shard_map.72.refs_1_), channel_id=1, source_target_pairs={{0,1},{1,0},{2,3},{3,2},{4,5},{5,4},{6,7},{7,6},{8,9},{9,8},{10,11... | collective-permute-start | bytes 1400840 | tf_op jit(solution)/shard_map/ppermute | solution.py:34
  52.3 2.5 %collective-permute-start.6 = (bf16[64,7168]{1,0:T(8,128)(2,1)S(1)}, bf16[64,7168]{1,0:T(8,128)(2,1)S(1)}, u32[]{:S(2)}, u32[]{:S(2)}) collective-permute-start(bf16[64,7168]{1,0:T(8,128)(2,1)S(1)} %get-tuple-element.34), channel_id=1, source_target_pairs={{0,1},{1,0},{2,3},{3,2},{4,5},{5,4},{6,7},{7,6},{8,9},{9,8},{10,11... | collective-permute-start | bytes 2752520 | tf_op jit(solution)/shard_map/ppermute | solution.py:34
  55.1 8.5 %collective-permute-start.7 = (bf16[32,7168]{1,0:T(8,128)(2,1)S(1)}, bf16[32,7168]{1,0:T(8,128)(2,1)S(1)}, u32[]{:S(2)}, u32[]{:S(2)}) collective-permute-start(bf16[32,7168]{1,0:T(8,128)(2,1)S(1)} %get-tuple-element.36), channel_id=1, source_target_pairs={{0,16},{1,9},{2,18},{3,11},{4,20},{5,13},{6,22},{7,15},{8,24},{9,1... | collective-permute-start | bytes 1376264 | tf_op jit(solution)/shard_map/ppermute | solution.py:42
  63.7 6.1 %collective-permute-start.8 = (bf16[16,7168]{1,0:T(8,128)(2,1)S(1)}, bf16[16,7168]{1,0:T(8,128)(2,1)S(1)}, u32[]{:S(2)}, u32[]{:S(2)}) collective-permute-start(bf16[16,7168]{1,0:T(8,128)(2,1)S(1)} %get-tuple-element.38), channel_id=1, source_target_pairs={{0,8},{1,17},{2,10},{3,19},{4,12},{5,21},{6,14},{7,23},{8,0},{9,25... | collective-permute-start | bytes 688136 | tf_op jit(solution)/shard_map/ppermute | solution.py:42
  69.9 4.9 %collective-permute-start.9 = (bf16[8,7168]{1,0:T(8,128)(2,1)S(1)}, bf16[8,7168]{1,0:T(8,128)(2,1)S(1)}, u32[]{:S(2)}, u32[]{:S(2)}) collective-permute-start(bf16[8,7168]{1,0:T(8,128)(2,1)S(1)} %get-tuple-element.40), channel_id=1, source_target_pairs={{0,2},{1,3},{2,0},{3,1},{4,6},{5,7},{6,4},{7,5},{8,10},{9,11},{10,... | collective-permute-start | bytes 344072 | tf_op jit(solution)/shard_map/ppermute | solution.py:34
  74.8 5.1 %collective-permute-start.10 = (bf16[4,7168]{1,0:T(4,128)(2,1)S(1)}, bf16[4,7168]{1,0:T(4,128)(2,1)S(1)}, u32[]{:S(2)}, u32[]{:S(2)}) collective-permute-start(bf16[4,7168]{1,0:T(4,128)(2,1)S(1)} %get-tuple-element.42), channel_id=1, source_target_pairs={{0,4},{1,5},{2,6},{3,7},{4,0},{5,1},{6,2},{7,3},{8,12},{9,13},{10,... | collective-permute-start | bytes 172040 | tf_op jit(solution)/shard_map/ppermute | solution.py:34

commit v6 on v5

v6 whole, which is shorter than its diff:
```python
import functools

import jax
import jax.numpy as jnp
from jax import lax
from jax.experimental import pallas as pl
from jax.experimental.pallas import tpu as pltpu
from jax.sharding import PartitionSpec as P

EXP_GRP = 8
LANES = 128
AXES = ("group", "expert")
VMEM = pltpu.VMEM
FIRST_BLOCK = 512
UNIT_BLOCK = 256
DOWN_BLOCK = 512
EARLY = 2
RING = 6
DOWN_RING = 4
FOLD_BLOCK = 1024
DEPTH_CUT = 1024


def in_vmem(value):
    return pltpu.with_memory_space_constraint(value, VMEM)


def in_hbm(value):
    return pltpu.with_memory_space_constraint(value, pltpu.HBM)


def whole_vmem(count):
    return [pl.BlockSpec(memory_space=VMEM)] * count


def swap(value, axis, size, mask):
    return lax.ppermute(value, axis, [(i, i ^ mask) for i in range(size)])


def swap_group(value, groups, members, masks):
    pairs = []
    for g in range(groups):
        for e in range(members):
            pairs.append((g * members + e, (g ^ masks[e % 2]) * members + e))
    return lax.ppermute(value, AXES, pairs)


def limit(amount):
    return pltpu.CompilerParams(vmem_limit_bytes=int(amount))


def cost(flops, amount):
    return pl.CostEstimate(flops=flops, bytes_accessed=amount, transcendentals=0)


def pack_kernel(me_ref, tokens_ref, ids_ref, weights_ref, out_ref):
    width = tokens_ref.shape[1]
    out_ref[:, :width] = tokens_ref[...]
    ids = ids_ref[...]
    weights = weights_ref[...].astype(jnp.float32)
    label = lax.broadcasted_iota(jnp.int32, (ids.shape[0], LANES), 1)
    route = jnp.zeros((ids.shape[0], LANES), jnp.float32)
    for k in range(ids.shape[1]):
        route += jnp.where(ids[:, k : k + 1] == label, weights[:, k : k + 1], 0.0)
    out_ref[:, width:] = route.astype(out_ref.dtype)


def pack(me, tokens, expert_ids, gate_weights):
    rows, width = tokens.shape
    args = (tokens, expert_ids, gate_weights)
    return pl.pallas_call(
        pack_kernel,
        grid=(1,),
        in_specs=[pl.BlockSpec(memory_space=pltpu.SMEM)]
        + [pl.BlockSpec(a.shape, lambda i: (0, 0)) for a in args],
        out_specs=whole_vmem(1)[0],
        out_shape=VMEM((rows, width + LANES), tokens.dtype),
        compiler_params=limit(2 * 1024 * 1024),
    )(me, *[in_hbm(a) for a in args])


def fetch_kernel(jobs, *refs):
    src_refs = refs[: len(jobs)]
    out_refs = refs[len(jobs) + 1 : 2 * len(jobs) + 1]
    mark_ref, sems = refs[-2:]
    copies = []
    for n, (_, first, columns) in enumerate(jobs):
        size = out_refs[n].shape[0] // 4
        for i in range(4):
            copies.append(
                pltpu.make_async_copy(
                    src_refs[n].at[0, pl.ds(i * size, size), pl.ds(first, columns)],
                    out_refs[n].at[pl.ds(i * size, size), :],
                    sems.at[n * 4 + i],
                )
            )
    for copy in copies:
        copy.start()
    mark_ref[...] = jnp.zeros_like(mark_ref)
    for copy in copies:
        copy.wait()


def fetch(jobs, rows, after):
    hbm = pl.BlockSpec(memory_space=pltpu.HBM)
    *out, mark = pl.pallas_call(
        functools.partial(fetch_kernel, jobs),
        in_specs=[hbm] * len(jobs) + [pl.BlockSpec(memory_space=pl.ANY)],
        out_specs=whole_vmem(len(jobs) + 1),
        out_shape=[VMEM((rows, columns), w.dtype) for w, _, columns in jobs]
        + [VMEM((8, LANES), jnp.float32)],
        scratch_shapes=[pltpu.SemaphoreType.DMA((4 * len(jobs),))],
        compiler_params=limit(256 * 1024),
        cost_estimate=cost(0, sum(2 * rows * columns for _, _, columns in jobs)),
    )(*[in_hbm(w) for w, _, _ in jobs], after)
    return out, mark


def join_kernel(start, *refs):
    *in_refs, after_ref, out_ref = refs
    columns = slice(start, start + out_ref.shape[1])
    pieces = [r[:, columns].astype(jnp.float32) for r in in_refs]
    out_ref[...] = jnp.concatenate(pieces, axis=0).astype(out_ref.dtype)


def join(values, after, start=0, width=None):
    rows = sum(v.shape[0] for v in values)
    width = width or values[0].shape[1]
    after = values[0] if after is None else after
    return pl.pallas_call(
        functools.partial(join_kernel, start),
        in_specs=whole_vmem(len(values)) + [pl.BlockSpec(memory_space=pl.ANY)],
        out_specs=whole_vmem(1)[0],
        out_shape=VMEM((rows, width), values[0].dtype),
        compiler_params=limit(1024 * 1024 + 8 * rows * width),
    )(*[in_vmem(v) for v in values], after)


def hold_kernel(*refs):
    pass


def hold(value, after):
    return pl.pallas_call(
        hold_kernel,
        in_specs=[pl.BlockSpec(memory_space=pl.ANY)] * 2,
        out_specs=pl.BlockSpec(memory_space=pl.ANY),
        out_shape=jax.ShapeDtypeStruct(value.shape, value.dtype),
        input_output_aliases={0: 0},
        compiler_params=limit(256 * 1024),
    )(value, after)


def times(left_ref, right_ref):
    depth = left_ref.shape[1]
    total = None
    for k in range(0, depth, DEPTH_CUT):
        inner = slice(k, min(depth, k + DEPTH_CUT))
        value = jnp.dot(left_ref[:, inner], right_ref[inner, :], preferred_element_type=jnp.float32)
        total = value if total is None else total + value
    return total


def first_kernel(held, streams, early, *refs):
    x_refs, refs = refs[:4], refs[4:]
    held_refs, refs = refs[:held], refs[held:]
    hbm, after_ref, gate_ref, up_ref = refs[:2], *refs[2:5]
    early_refs, refs = refs[5 : 5 + len(early)], refs[5 + len(early) :]
    x, slots, stream_sem, early_sem = refs
    depth = x.shape[1]
    block = held_refs[0].shape[1]
    count = gate_ref.shape[1] // block

    copies = [
        pltpu.make_async_copy(
            hbm[m].at[0, pl.ds(0, depth), pl.ds(b * block, block)], slots.at[n], stream_sem.at[n]
        )
        for n, (m, b) in enumerate(streams)
    ]
    later = [
        pltpu.make_async_copy(
            hbm[m].at[0, pl.ds(depth, ref.shape[0]), pl.ds(b * UNIT_BLOCK, UNIT_BLOCK)],
            ref,
            early_sem.at[n],
        )
        for n, ((m, b), ref) in enumerate(zip(early, early_refs))
    ]
    for copy in copies:
        copy.start()
    part = x_refs[0].shape[0]
    for n, x_ref in enumerate(x_refs):
        x[n * part : (n + 1) * part, :] = x_ref[...]
    for n in range(2 * count):
        if n < held:
            weight = held_refs[n]
        else:
            copies[n - held].wait()
            weight = slots.at[n - held]
        out_ref = gate_ref if n < count else up_ref
        at = n % count * block
        out_ref[:, at : at + block] = times(x, weight)
        if n == min(1, 2 * count - 1):
            for copy in later:
                copy.start()
    for copy in later:
        copy.wait()


def run_first(parts, held, w_gate, w_up, after):
    rows = sum(p.shape[0] for p in parts)
    depth = parts[0].shape[1]
    units = w_gate.shape[2]
    block = held[0].shape[1]
    count = units // block
    order = [(0, b) for b in range(count)] + [(1, b) for b in range(count)]
    streams = order[len(held) :]
    early = [(m, b) for b in range(min(EARLY, units // UNIT_BLOCK)) for m in range(2)]
    hbm = pl.BlockSpec(memory_space=pltpu.HBM)
    slots = max(1, len(streams))
    scratch = 2 * (rows * depth + slots * depth * block)
    args = [in_vmem(v) for v in [*parts, *held]]
    return pl.pallas_call(
        functools.partial(first_kernel, len(held), streams, early),
        in_specs=whole_vmem(len(args)) + [hbm, hbm, pl.BlockSpec(memory_space=pl.ANY)],
        out_specs=whole_vmem(2 + len(early)),
        out_shape=[VMEM((rows, units), jnp.float32)] * 2
        + [VMEM((w_gate.shape[1] - depth, UNIT_BLOCK), w_gate.dtype)] * len(early),
        scratch_shapes=[
            VMEM((rows, depth), jnp.bfloat16),
            VMEM((slots, depth, block), jnp.bfloat16),
            pltpu.SemaphoreType.DMA((slots,)),
            pltpu.SemaphoreType.DMA((len(early),)),
        ],
        compiler_params=limit(scratch + 4 * 1024 * 1024 + 16 * rows * block),
        cost_estimate=cost(4 * rows * depth * units, 2 * depth * units),
    )(*args, in_hbm(w_gate), in_hbm(w_up), after)


def second_kernel(start, early, streams, *refs):
    x_refs, refs = refs[:4], refs[4:]
    gate_ref, up_ref, refs = refs[0], refs[1], refs[2:]
    early_refs, refs = refs[: len(early)], refs[len(early) :]
    hbm, down_hbm, me_ref, own_ref, far_ref = refs[:2], *refs[2:6]
    x, hidden, scale_ref, ring, down_ring, sems, down_sem = refs[6:]
    depth, units = x.shape[1], hidden.shape[1]
    blocks = units // UNIT_BLOCK
    downs = down_hbm.shape[2] // DOWN_BLOCK

    def copy(n):
        m, b = streams[n]
        return pltpu.make_async_copy(
            hbm[m].at[0, pl.ds(start, depth), pl.ds(b * UNIT_BLOCK, UNIT_BLOCK)],
            ring.at[n % RING],
            sems.at[n % RING],
        )

    def down_copy(d, slot):
        first = d * DOWN_BLOCK
        if not isinstance(d, int):
            first = pl.multiple_of(first, DOWN_BLOCK)
        return pltpu.make_async_copy(
            down_hbm.at[0, :, pl.ds(first, DOWN_BLOCK)], down_ring.at[slot], down_sem.at[slot]
        )

    for n in range(min(RING, len(streams))):
        copy(n).start()
    later = {}
    for n in range(min(DOWN_RING, downs)):
        later.setdefault(min(blocks - 1, 3 + n), []).append(down_copy(n, n))

    part = x_refs[0].shape[0]
    for n, x_ref in enumerate(x_refs):
        x[n * part : (n + 1) * part, :] = x_ref[:, :depth]
        route = x_ref[:, depth:].astype(jnp.float32)
        lane = lax.broadcasted_iota(jnp.int32, route.shape, 1)
        scale = jnp.sum(jnp.where(lane == me_ref[0], route, 0.0), axis=1, keepdims=True)
        scale_ref[n * part : (n + 1) * part, :] = jnp.broadcast_to(scale, route.shape)

    def product(m, b):
        if (m, b) in early:
            return times(x, early_refs[early.index((m, b))])
        n = streams.index((m, b))
        copy(n).wait()
        value = times(x, ring.at[n % RING])
        if n + RING < len(streams):
            copy(n + RING).start()
        return value

    for b in range(blocks):
        columns = slice(b * UNIT_BLOCK, (b + 1) * UNIT_BLOCK)
        gate = gate_ref[:, columns] + product(0, b)
        up = up_ref[:, columns] + product(1, b)
        for piece in later.get(b, []):
            piece.start()
        hidden[:, columns] = (jax.nn.silu(gate) * up).astype(jnp.bfloat16)

    @pl.loop(0, downs)
    def _(d):
        slot = lax.rem(d, DOWN_RING)
        columns = pl.ds(pl.multiple_of(d * DOWN_BLOCK, DOWN_BLOCK), DOWN_BLOCK)
        down_copy(d, slot).wait()
        value = (times(hidden, down_ring.at[slot]) * scale_ref[:, :1]).astype(jnp.bfloat16)

        @pl.when(d + DOWN_RING < downs)
        def _():
            down_copy(d + DOWN_RING, slot).start()

        own_ref[:, columns] = value[: 2 * part]
        far_ref[:, columns] = value[2 * part :]


def run_second(parts, gate, up, early_values, w_gate, w_up, w_down, me):
    rows = sum(p.shape[0] for p in parts)
    units, width = w_down.shape[1], w_down.shape[2]
    depth = parts[0].shape[1] - LANES
    blocks = units // UNIT_BLOCK
    order = [(m, b) for b in range(blocks) for m in range(2)]
    early = order[: len(early_values)]
    streams = order[len(early_values) :]
    half = VMEM((rows // 2, width), jnp.bfloat16)
    hbm = pl.BlockSpec(memory_space=pltpu.HBM)
    ring = max(1, min(RING, len(streams)))
    scratch = 2 * (
        rows * (depth + units + 2 * LANES)
        + ring * depth * UNIT_BLOCK
        + DOWN_RING * units * DOWN_BLOCK
    )
    args = [in_vmem(v) for v in [*parts, gate, up, *early_values]]
    return pl.pallas_call(
        functools.partial(second_kernel, width - depth, early, streams),
        in_specs=whole_vmem(len(args)) + [hbm] * 3 + [pl.BlockSpec(memory_space=pltpu.SMEM)],
        out_specs=whole_vmem(2),
        out_shape=(half, half),
        scratch_shapes=[
            VMEM((rows, depth), jnp.bfloat16),
            VMEM((rows, units), jnp.bfloat16),
            VMEM((rows, LANES), jnp.float32),
            VMEM((ring, depth, UNIT_BLOCK), jnp.bfloat16),
            VMEM((DOWN_RING, units, DOWN_BLOCK), jnp.bfloat16),
            pltpu.SemaphoreType.DMA((ring,)),
            pltpu.SemaphoreType.DMA((DOWN_RING,)),
        ],
        compiler_params=limit(scratch + 4 * 1024 * 1024 + 16 * rows * DOWN_BLOCK),
        cost_estimate=cost(2 * rows * units * (2 * depth + width), 2 * depth * units),
    )(*args, in_hbm(w_gate), in_hbm(w_up), in_hbm(w_down), me)


def fold_kernel(count, *refs):
    in_refs, out_refs = refs[:count], refs[count:]
    size = out_refs[0].shape[0]
    for first in range(0, in_refs[0].shape[1], FOLD_BLOCK):
        columns = slice(first, first + FOLD_BLOCK)
        total = in_refs[0][:, columns].astype(jnp.float32)
        for ref in in_refs[1:]:
            total = total + ref[:, columns].astype(jnp.float32)
        for n, ref in enumerate(out_refs):
            ref[:, columns] = total[n * size : (n + 1) * size].astype(ref.dtype)


def fold(values, pieces):
    rows, width = values[0].shape
    return pl.pallas_call(
        functools.partial(fold_kernel, len(values)),
        in_specs=whole_vmem(len(values)),
        out_specs=whole_vmem(pieces),
        out_shape=[VMEM((rows // pieces, width), values[0].dtype)] * pieces,
        compiler_params=limit(1024 * 1024 + 12 * rows * FOLD_BLOCK),
    )(*[in_vmem(v) for v in values])


def line_steps(lines):
    steps = []
    while lines > 1:
        radix = min(4, lines)
        lines //= radix
        steps.append([2 * lines * m for m in range(1, radix)])
    return steps


def give_back(own, far, groups, members):
    values = [own, swap(far, "expert", members, 1)]
    for masks in [(2, 1), (1, 2)]:
        keep, send = fold(values, 2)
        values = [keep, swap_group(send, groups, members, masks)]
    for masks in reversed(line_steps(members // 2)):
        keep, *sends = fold(values, len(masks) + 1)
        values = [keep] + [swap(v, "expert", members, m) for v, m in zip(sends, masks)]
    total = values[0].astype(jnp.float32)
    for value in values[1:]:
        total = total + value.astype(jnp.float32)
    return total.astype(jnp.bfloat16)


def on_device(tokens, expert_ids, gate_weights, w_gate, w_up, w_down):
    groups = lax.axis_size("group")
    members = lax.axis_size("expert")
    split = members // EXP_GRP
    me = lax.axis_index("group") * EXP_GRP + lax.axis_index("expert") // split
    me = me.astype(jnp.int32).reshape(1)
    depth, units = w_gate.shape[1], w_gate.shape[2]
    first = depth // DOWN_BLOCK * 3 // 8 * DOWN_BLOCK
    block = min(FIRST_BLOCK, units)
    jobs = [(w, at, block) for w in (w_gate, w_up) for at in range(0, units, block)]
    one = max(1, len(jobs) * 3 // 8)
    two = one + max(1, len(jobs) // 4)

    value = pack(me, tokens, expert_ids, gate_weights)
    held, mark = fetch(jobs[:one], first, value)
    for masks in line_steps(members // 2):
        line = [value] + [swap(value, "expert", members, m) for m in masks]
        if masks[0] > 2:
            value = join(line, mark)
    a = join(line, mark, 0, first)
    b = join(line, a, first, depth - first + LANES)

    a_got = swap_group(a, groups, members, (1, 2))
    b_got = swap_group(b, groups, members, (1, 2))
    a = join([a, a_got], b)
    b = join([b, b_got], a)
    a_got = swap_group(a, groups, members, (2, 1))
    b_got = swap_group(b, groups, members, (2, 1))
    more, mark = fetch(jobs[one:two], first, a)
    a_got = hold(a_got, mark)
    parts = [a, a_got, swap(a, "expert", members, 1), swap(a_got, "expert", members, 1)]
    gate, up, *early = run_first(parts, held + more, w_gate, w_up, b)
    b_got = hold(b_got, gate)
    parts = [b, b_got, swap(b, "expert", members, 1), swap(b_got, "expert", members, 1)]
    own, far = run_second(parts, gate, up, early, w_gate, w_up, w_down, me)
    return give_back(own, far, groups, members)


def solution(mesh):
    in_specs = (
        P(AXES, None),
        P(AXES, None),
        P(AXES, None),
        P(AXES, None, None),
        P(AXES, None, None),
        P(AXES, None, None),
    )
    out_specs = P(AXES, None)
    return jax.shard_map(
        on_device, mesh=mesh, in_specs=in_specs, out_specs=out_specs, check_vma=False
    )
```

time: 80.8 us -> 81.8 us (1.012)
  starting transfers between devices: 17.8 us -> 20 us
  Pallas kernels: 37.9 us -> 36.4 us
    pallas_call x4 -> x2, Pallas kernels: 14 us -> 5.97 us  [fetch(): pl.pallas_call(functools.partial(fetch_kernel, jobs), in_specs=[hbm] * le...]
    pallas_call x8 -> x9, Pallas kernels: 23 us -> 29.5 us  [the longest x1 21.1 us: run_second(): pl.pallas_call(functools.partial(second_kernel, width - depth, early, str...]
    ppermute x7 -> x11, starting transfers between devices: 10.1 us -> 11.7 us  [swap(): return lax.ppermute(value, axis, [(i, i ^ mask) for i in range(size)])]
    ppermute x4 -> x6, waiting for transfers between devices: 14.1 us -> 15.2 us  [swap_group(): return lax.ppermute(value, AXES, pairs)]
    ppermute x7 -> x11, waiting for transfers between devices: 10 us -> 9.13 us  [swap(): return lax.ppermute(value, axis, [(i, i ^ mask) for i in range(size)])]
    ppermute x4 -> x6, starting transfers between devices: 7.73 us -> 8.33 us  [swap_group(): return lax.ppermute(value, AXES, pairs)]
  transfers between devices with their start and end apart: 11 -> 17, of which waited for: 8 -> 10; matrix products, arithmetic and copies ran while one was open for 0% -> 0% of each run, Pallas kernels for 17% -> 17%
where the time goes in v6:
time: 81.8 us; the launch traced here: 81.6 us
  Pallas kernels  36.4 us (44%)
  waiting for transfers between devices  24.4 us (30%)
  starting transfers between devices  20 us (24%)
    pallas_call x1, Pallas kernels, run_second(): pl.pallas_call(functools.partial(second_kernel, width - depth, early, str...  21.1 us
    ppermute x6, waiting for transfers between devices, swap_group(): return lax.ppermute(value, AXES, pairs)  15.2 us
    ppermute x11, starting transfers between devices, swap(): return lax.ppermute(value, axis, [(i, i ^ mask) for i in range(size)])  11.7 us
    ppermute x11, waiting for transfers between devices, swap(): return lax.ppermute(value, axis, [(i, i ^ mask) for i in range(size)])  9.13 us
    ppermute x6, starting transfers between devices, swap_group(): return lax.ppermute(value, AXES, pairs)  8.33 us
    pallas_call x1, Pallas kernels, run_first(): pl.pallas_call(functools.partial(first_kernel, len(held), streams, early)...  7.94 us
    pallas_call x2, Pallas kernels, fetch(): pl.pallas_call(functools.partial(fetch_kernel, jobs), in_specs=[hbm] * le...  5.97 us
  transfers between devices with their start and end apart: 17, of which 10 were waited for; matrix products, arithmetic and copies ran while one was open for 0% of the time, Pallas kernels for 17%

profile of v6, /device:TPU:0, one launch (start us, length us, event | category | flops | bytes accessed | tf_op | source)
XLA Modules:
  0.0 81.6 jit_solution(13141186361378401401)
XLA Ops:
  0.0 0.9 %shard_map.64.refs_3_.refs_0_ = bf16[4,7296]{1,0:T(4,128)(2,1)S(1)} custom-call(s32[1]{0:T(128)} %bitcast.me_ref.refs_13_, bf16[4,7168]{1,0:T(4,128)(2,1)} %tokens_ref.1, s32[4,8]{1,0:T(4,128)} %ids_ref.1, bf16[4,8]{1,0:T(4,128)(2,1)} %weights_ref.1), custom_call_target="tpu_custom_call" | custom-call | tf_op jit(solution)/shard_map/pallas_call | solution.py:71
  0.9 3.1 %collective-permute-start = (bf16[4,7296]{1,0:T(4,128)(2,1)S(1)}, bf16[4,7296]{1,0:T(4,128)(2,1)S(1)}, u32[]{:S(2)}, u32[]{:S(2)}) collective-permute-start(bf16[4,7296]{1,0:T(4,128)(2,1)S(1)} %shard_map.64.refs_3_.refs_0_), channel_id=1, source_target_pairs={{0,2},{1,3},{2,0},{3,1},{4,6},{5,7},{6,4},{7,5},{8,10},{9,11},{10,... | collective-permute-start | bytes 175112 | tf_op jit(solution)/shard_map/ppermute | solution.py:37
  4.0 2.6 %collective-permute-start.1 = (bf16[4,7296]{1,0:T(4,128)(2,1)S(1)}, bf16[4,7296]{1,0:T(4,128)(2,1)S(1)}, u32[]{:S(2)}, u32[]{:S(2)}) collective-permute-start(bf16[4,7296]{1,0:T(4,128)(2,1)S(1)} %shard_map.64.refs_3_.refs_0_), channel_id=1, source_target_pairs={{0,4},{1,5},{2,6},{3,7},{4,0},{5,1},{6,2},{7,3},{8,12},{9,13},{10,... | collective-permute-start | bytes 175112 | tf_op jit(solution)/shard_map/ppermute | solution.py:37
  6.6 0.0 collective-permute-start.2
  6.6 3.4 %shard_map.65 = (bf16[2560,512]{1,0:T(8,128)(2,1)S(1)}, bf16[2560,512]{1,0:T(8,128)(2,1)S(1)}, bf16[2560,512]{1,0:T(8,128)(2,1)S(1)}, f32[8,128]{1,0:T(8,128)S(1)}) custom-call(bf16[1,7168,2048]{2,1,0:T(8,128)(2,1)} %refs_10_.3, bf16[1,7168,2048]{2,1,0:T(8,128)(2,1)} %refs_10_.3, bf16[1,7168,2048]{2,1,0:T(8,128)(2,1)} %refs_10_.3, ...), custom_call_target="tpu_custom_call" | custom-call | bytes 7864320 | tf_op jit(solution)/shard_map/pallas_call | solution.py:106
  10.0 0.0 collective-permute-done.refs_1_
  10.0 0.2 collective-permute-done.1.refs_2_
  10.2 2.4 %collective-permute-done.2.refs_3_ = bf16[4,7296]{1,0:T(4,128)(2,1)S(1)} collective-permute-done((bf16[4,7296]{1,0:T(4,128)(2,1)S(1)}, bf16[4,7296]{1,0:T(4,128)(2,1)S(1)}, u32[]{:S(2)}, u32[]{:S(2)}) %collective-permute-start.2) | collective-permute-done | bytes 58400 | tf_op jit(solution)/shard_map/ppermute | solution.py:37
  12.6 1.6 %collective-permute-start.4 = (bf16[16,2560]{1,0:T(8,128)(2,1)S(1)}, bf16[16,2560]{1,0:T(8,128)(2,1)S(1)}, u32[]{:S(2)}, u32[]{:S(2)}) collective-permute-start(bf16[16,2560]{1,0:T(8,128)(2,1)S(1)} %shard_map.66.refs_4_.refs_0_), channel_id=1, source_target_pairs={{0,8},{1,17},{2,10},{3,19},{4,12},{5,21},{6,14},{7,23},{8,0},{9,25... | collective-permute-start | bytes 245768 | tf_op jit(solution)/shard_map/ppermute | solution.py:45
  14.2 3.2 %collective-permute-done.4.refs_1_ = bf16[16,2560]{1,0:T(8,128)(2,1)S(1)} collective-permute-done((bf16[16,2560]{1,0:T(8,128)(2,1)S(1)}, bf16[16,2560]{1,0:T(8,128)(2,1)S(1)}, u32[]{:S(2)}, u32[]{:S(2)}) %collective-permute-start.4) | collective-permute-done | bytes 81952 | tf_op jit(solution)/shard_map/ppermute | solution.py:45
  17.4 1.6 %collective-permute-start.6 = (bf16[32,2560]{1,0:T(8,128)(2,1)S(1)}, bf16[32,2560]{1,0:T(8,128)(2,1)S(1)}, u32[]{:S(2)}, u32[]{:S(2)}) collective-permute-start(bf16[32,2560]{1,0:T(8,128)(2,1)S(1)} %shard_map.68.refs_2_.refs_0_), channel_id=1, source_target_pairs={{0,16},{1,9},{2,18},{3,11},{4,20},{5,13},{6,22},{7,15},{8,24},{9,1... | collective-permute-start | bytes 491528 | tf_op jit(solution)/shard_map/ppermute | solution.py:45
  19.0 1.5 %collective-permute-start.3 = (bf16[16,4736]{1,0:T(8,128)(2,1)S(1)}, bf16[16,4736]{1,0:T(8,128)(2,1)S(1)}, u32[]{:S(2)}, u32[]{:S(2)}) collective-permute-start(bf16[16,4736]{1,0:T(8,128)(2,1)S(1)} %shard_map.67.refs_2_.refs_0_), channel_id=1, source_target_pairs={{0,8},{1,17},{2,10},{3,19},{4,12},{5,21},{6,14},{7,23},{8,0},{9,25... | collective-permute-start | bytes 454664 | tf_op jit(solution)/shard_map/ppermute | solution.py:45
  20.5 0.0 collective-permute-start.7
  20.5 2.6 %shard_map.70 = (bf16[2560,512]{1,0:T(8,128)(2,1)S(1)}, bf16[2560,512]{1,0:T(8,128)(2,1)S(1)}, f32[8,128]{1,0:T(8,128)S(1)}) custom-call(bf16[1,7168,2048]{2,1,0:T(8,128)(2,1)} %refs_10_.3, bf16[1,7168,2048]{2,1,0:T(8,128)(2,1)} %refs_11_.1, bf16[32,2560]{1,0:T(8,128)(2,1)S(1)} %shard_map.68.refs_2_.refs_0_), custom_call_target="tpu_custom_call" | custom-call | bytes 5242880 | tf_op jit(solution)/shard_map/pallas_call | solution.py:106
  23.1 0.0 collective-permute-done.6.refs_0_
  23.1 0.6 collective-permute-start.8
  23.7 0.5 collective-permute-done.3.refs_1_
  24.2 0.6 collective-permute-start.5
  24.8 0.0 collective-permute-start.9
  24.8 0.0 collective-permute-done.7.refs_2_
  24.8 0.0 collective-permute-done.8.refs_3_
  24.8 7.9 %shard_map.72 = (f32[128,2048]{1,0:T(8,128)S(1)}, f32[128,2048]{1,0:T(8,128)S(1)}, bf16[4608,256]{1,0:T(8,128)(2,1)S(1)}, bf16[4608,256]{1,0:T(8,128)(2,1)S(1)},...) custom-call(bf16[32,2560]{1,0:T(8,128)(2,1)S(1)} %shard_map.68.refs_2_.refs_0_, ...), custom_call_target="tpu_custom_call" | custom-call | flops 2684354560 | bytes 10485760 | tf_op jit(solution)/shard_map/pallas_call | solution.py:222
  32.8 0.0 collective-permute-done.5.refs_0_
  32.8 0.6 collective-permute-start.10
  33.4 0.0 collective-permute-done.9.refs_2_
  33.4 1.2 %collective-permute-done.10.refs_3_ = bf16[32,4736]{1,0:T(8,128)(2,1)S(1)} collective-permute-done((bf16[32,4736]{1,0:T(8,128)(2,1)S(1)}, bf16[32,4736]{1,0:T(8,128)(2,1)S(1)}, u32[]{:S(2)}, u32[]{:S(2)}) %collective-permute-start.10) | collective-permute-done | bytes 303136 | tf_op jit(solution)/shard_map/ppermute | solution.py:37
  34.6 21.1 %shard_map.74 = (bf16[64,7168]{1,0:T(8,128)(2,1)S(1)}, bf16[64,7168]{1,0:T(8,128)(2,1)S(1)}) custom-call(bf16[32,4736]{1,0:T(8,128)(2,1)S(1)} %shard_map.69.refs_11_.refs_0_, bf16[32,4736]{1,0:T(8,128)(2,1)S(1)} %shard_map.73.refs_1_, bf16[32,4736]{1,0:T(8,128)(2,1)S(1)} %collective-permute-done.9.refs_2_, ...), custom_call_target="tpu_custom_call" | custom-call | flops 8589934592 | bytes 18874368 | tf_op jit(solution)/shard_map/pallas_call | solution.py:329
  55.7 0.4 collective-permute-start.11
  56.1 2.1 %collective-permute-done.11.refs_1_ = bf16[64,7168]{1,0:T(8,128)(2,1)S(1)} collective-permute-done((bf16[64,7168]{1,0:T(8,128)(2,1)S(1)}, bf16[64,7168]{1,0:T(8,128)(2,1)S(1)}, u32[]{:S(2)}, u32[]{:S(2)}) %collective-permute-start.11) | collective-permute-done | bytes 917536 | tf_op jit(solution)/shard_map/ppermute | solution.py:37
  58.2 0.2 shard_map.75
  58.4 1.6 %collective-permute-start.12 = (bf16[32,7168]{1,0:T(8,128)(2,1)S(1)}, bf16[32,7168]{1,0:T(8,128)(2,1)S(1)}, u32[]{:S(2)}, u32[]{:S(2)}) collective-permute-start(bf16[32,7168]{1,0:T(8,128)(2,1)S(1)} %get-tuple-element.44), channel_id=1, source_target_pairs={{0,16},{1,9},{2,18},{3,11},{4,20},{5,13},{6,22},{7,15},{8,24},{9,1... | collective-permute-start | bytes 1376264 | tf_op jit(solution)/shard_map/ppermute | solution.py:45
  60.0 7.0 %collective-permute-done.12.refs_1_ = bf16[32,7168]{1,0:T(8,128)(2,1)S(1)} collective-permute-done((bf16[32,7168]{1,0:T(8,128)(2,1)S(1)}, bf16[32,7168]{1,0:T(8,128)(2,1)S(1)}, u32[]{:S(2)}, u32[]{:S(2)}) %collective-permute-start.12) | collective-permute-done | bytes 458784 | tf_op jit(solution)/shard_map/ppermute | solution.py:45
  67.0 0.1 shard_map.76
  67.1 1.6 %collective-permute-start.13 = (bf16[16,7168]{1,0:T(8,128)(2,1)S(1)}, bf16[16,7168]{1,0:T(8,128)(2,1)S(1)}, u32[]{:S(2)}, u32[]{:S(2)}) collective-permute-start(bf16[16,7168]{1,0:T(8,128)(2,1)S(1)} %get-tuple-element.46), channel_id=1, source_target_pairs={{0,8},{1,17},{2,10},{3,19},{4,12},{5,21},{6,14},{7,23},{8,0},{9,25... | collective-permute-start | bytes 688136 | tf_op jit(solution)/shard_map/ppermute | solution.py:45
  68.6 4.5 %collective-permute-done.13.refs_1_ = bf16[16,7168]{1,0:T(8,128)(2,1)S(1)} collective-permute-done((bf16[16,7168]{1,0:T(8,128)(2,1)S(1)}, bf16[16,7168]{1,0:T(8,128)(2,1)S(1)}, u32[]{:S(2)}, u32[]{:S(2)}) %collective-permute-start.13) | collective-permute-done | bytes 229408 | tf_op jit(solution)/shard_map/ppermute | solution.py:45
  73.2 0.1 shard_map.77
  73.2 0.1 collective-permute-start.14
  73.3 1.6 %collective-permute-start.15 = (bf16[4,7168]{1,0:T(4,128)(2,1)S(1)}, bf16[4,7168]{1,0:T(4,128)(2,1)S(1)}, u32[]{:S(2)}, u32[]{:S(2)}) collective-permute-start(bf16[4,7168]{1,0:T(4,128)(2,1)S(1)} %get-tuple-element.49), channel_id=1, source_target_pairs={{0,4},{1,5},{2,6},{3,7},{4,0},{5,1},{6,2},{7,3},{8,12},{9,13},{10,... | collective-permute-start | bytes 172040 | tf_op jit(solution)/shard_map/ppermute | solution.py:37
  74.9 2.8 %collective-permute-start.16 = (bf16[4,7168]{1,0:T(4,128)(2,1)S(1)}, bf16[4,7168]{1,0:T(4,128)(2,1)S(1)}, u32[]{:S(2)}, u32[]{:S(2)}) collective-permute-start(bf16[4,7168]{1,0:T(4,128)(2,1)S(1)} %get-tuple-element.50), channel_id=1, source_target_pairs={{0,6},{1,7},{2,4},{3,5},{4,2},{5,3},{6,0},{7,1},{8,14},{9,15},{10,... | collective-permute-start | bytes 172040 | tf_op jit(solution)/shard_map/ppermute | solution.py:37
  77.7 0.0 collective-permute-done.14
  77.7 1.2 %collective-permute-done.15 = bf16[4,7168]{1,0:T(4,128)(2,1)S(1)} collective-permute-done((bf16[4,7168]{1,0:T(4,128)(2,1)S(1)}, bf16[4,7168]{1,0:T(4,128)(2,1)S(1)}, u32[]{:S(2)}, u32[]{:S(2)}) %collective-permute-start.15) | collective-permute-done | bytes 57376 | tf_op jit(solution)/shard_map/ppermute | solution.py:37
  78.9 2.0 %collective-permute-done.16 = bf16[4,7168]{1,0:T(4,128)(2,1)S(1)} collective-permute-done((bf16[4,7168]{1,0:T(4,128)(2,1)S(1)}, bf16[4,7168]{1,0:T(4,128)(2,1)S(1)}, u32[]{:S(2)}, u32[]{:S(2)}) %collective-permute-start.16) | collective-permute-done | bytes 57376 | tf_op jit(solution)/shard_map/ppermute | solution.py:37
  80.9 0.7 add_convert_fusion
  (6 shorter events, 0.1 us)
Async XLA Ops:
  0.9 9.1 %collective-permute-start = (bf16[4,7296]{1,0:T(4,128)(2,1)S(1)}, bf16[4,7296]{1,0:T(4,128)(2,1)S(1)}, u32[]{:S(2)}, u32[]{:S(2)}) collective-permute-start(bf16[4,7296]{1,0:T(4,128)(2,1)S(1)} %shard_map.64.refs_3_.refs_0_), channel_id=1, source_target_pairs={{0,2},{1,3},{2,0},{3,1},{4,6},{5,7},{6,4},{7,5},{8,10},{9,11},{10,... | collective-permute-start | bytes 175112 | tf_op jit(solution)/shard_map/ppermute | solution.py:37
  4.0 6.2 %collective-permute-start.1 = (bf16[4,7296]{1,0:T(4,128)(2,1)S(1)}, bf16[4,7296]{1,0:T(4,128)(2,1)S(1)}, u32[]{:S(2)}, u32[]{:S(2)}) collective-permute-start(bf16[4,7296]{1,0:T(4,128)(2,1)S(1)} %shard_map.64.refs_3_.refs_0_), channel_id=1, source_target_pairs={{0,4},{1,5},{2,6},{3,7},{4,0},{5,1},{6,2},{7,3},{8,12},{9,13},{10,... | collective-permute-start | bytes 175112 | tf_op jit(solution)/shard_map/ppermute | solution.py:37
  6.6 6.0 %collective-permute-start.2 = (bf16[4,7296]{1,0:T(4,128)(2,1)S(1)}, bf16[4,7296]{1,0:T(4,128)(2,1)S(1)}, u32[]{:S(2)}, u32[]{:S(2)}) collective-permute-start(bf16[4,7296]{1,0:T(4,128)(2,1)S(1)} %shard_map.64.refs_3_.refs_0_), channel_id=1, source_target_pairs={{0,6},{1,7},{2,4},{3,5},{4,2},{5,3},{6,0},{7,1},{8,14},{9,15},{10,... | collective-permute-start | bytes 175112 | tf_op jit(solution)/shard_map/ppermute | solution.py:37
  12.6 4.8 %collective-permute-start.4 = (bf16[16,2560]{1,0:T(8,128)(2,1)S(1)}, bf16[16,2560]{1,0:T(8,128)(2,1)S(1)}, u32[]{:S(2)}, u32[]{:S(2)}) collective-permute-start(bf16[16,2560]{1,0:T(8,128)(2,1)S(1)} %shard_map.66.refs_4_.refs_0_), channel_id=1, source_target_pairs={{0,8},{1,17},{2,10},{3,19},{4,12},{5,21},{6,14},{7,23},{8,0},{9,25... | collective-permute-start | bytes 245768 | tf_op jit(solution)/shard_map/ppermute | solution.py:45
  17.4 5.7 %collective-permute-start.6 = (bf16[32,2560]{1,0:T(8,128)(2,1)S(1)}, bf16[32,2560]{1,0:T(8,128)(2,1)S(1)}, u32[]{:S(2)}, u32[]{:S(2)}) collective-permute-start(bf16[32,2560]{1,0:T(8,128)(2,1)S(1)} %shard_map.68.refs_2_.refs_0_), channel_id=1, source_target_pairs={{0,16},{1,9},{2,18},{3,11},{4,20},{5,13},{6,22},{7,15},{8,24},{9,1... | collective-permute-start | bytes 491528 | tf_op jit(solution)/shard_map/ppermute | solution.py:45
  19.0 5.2 %collective-permute-start.3 = (bf16[16,4736]{1,0:T(8,128)(2,1)S(1)}, bf16[16,4736]{1,0:T(8,128)(2,1)S(1)}, u32[]{:S(2)}, u32[]{:S(2)}) collective-permute-start(bf16[16,4736]{1,0:T(8,128)(2,1)S(1)} %shard_map.67.refs_2_.refs_0_), channel_id=1, source_target_pairs={{0,8},{1,17},{2,10},{3,19},{4,12},{5,21},{6,14},{7,23},{8,0},{9,25... | collective-permute-start | bytes 454664 | tf_op jit(solution)/shard_map/ppermute | solution.py:45
  20.5 4.3 %collective-permute-start.7 = (bf16[32,2560]{1,0:T(8,128)(2,1)S(1)}, bf16[32,2560]{1,0:T(8,128)(2,1)S(1)}, u32[]{:S(2)}, u32[]{:S(2)}) collective-permute-start(bf16[32,2560]{1,0:T(8,128)(2,1)S(1)} %shard_map.68.refs_2_.refs_0_), channel_id=1, source_target_pairs={{0,1},{1,0},{2,3},{3,2},{4,5},{5,4},{6,7},{7,6},{8,9},{9,8},{10,11... | collective-permute-start | bytes 491528 | tf_op jit(solution)/shard_map/ppermute | solution.py:37
  23.1 1.7 %collective-permute-start.8 = (bf16[32,2560]{1,0:T(8,128)(2,1)S(1)}, bf16[32,2560]{1,0:T(8,128)(2,1)S(1)}, u32[]{:S(2)}, u32[]{:S(2)}) collective-permute-start(bf16[32,2560]{1,0:T(8,128)(2,1)S(1)} %shard_map.71.refs_1_), channel_id=1, source_target_pairs={{0,1},{1,0},{2,3},{3,2},{4,5},{5,4},{6,7},{7,6},{8,9},{9,8},{10,11... | collective-permute-start | bytes 491528 | tf_op jit(solution)/shard_map/ppermute | solution.py:37
  24.2 8.5 %collective-permute-start.5 = (bf16[32,4736]{1,0:T(8,128)(2,1)S(1)}, bf16[32,4736]{1,0:T(8,128)(2,1)S(1)}, u32[]{:S(2)}, u32[]{:S(2)}) collective-permute-start(bf16[32,4736]{1,0:T(8,128)(2,1)S(1)} %shard_map.69.refs_11_.refs_0_), channel_id=1, source_target_pairs={{0,16},{1,9},{2,18},{3,11},{4,20},{5,13},{6,22},{7,15},{8,24},{9,1... | collective-permute-start | bytes 909320 | tf_op jit(solution)/shard_map/ppermute | solution.py:45
  24.8 8.5 %collective-permute-start.9 = (bf16[32,4736]{1,0:T(8,128)(2,1)S(1)}, bf16[32,4736]{1,0:T(8,128)(2,1)S(1)}, u32[]{:S(2)}, u32[]{:S(2)}) collective-permute-start(bf16[32,4736]{1,0:T(8,128)(2,1)S(1)} %shard_map.69.refs_11_.refs_0_), channel_id=1, source_target_pairs={{0,1},{1,0},{2,3},{3,2},{4,5},{5,4},{6,7},{7,6},{8,9},{9,8},{10,11... | collective-permute-start | bytes 909320 | tf_op jit(solution)/shard_map/ppermute | solution.py:37
  32.8 1.8 %collective-permute-start.10 = (bf16[32,4736]{1,0:T(8,128)(2,1)S(1)}, bf16[32,4736]{1,0:T(8,128)(2,1)S(1)}, u32[]{:S(2)}, u32[]{:S(2)}) collective-permute-start(bf16[32,4736]{1,0:T(8,128)(2,1)S(1)} %shard_map.73.refs_1_), channel_id=1, source_target_pairs={{0,1},{1,0},{2,3},{3,2},{4,5},{5,4},{6,7},{7,6},{8,9},{9,8},{10,11... | collective-permute-start | bytes 909320 | tf_op jit(solution)/shard_map/ppermute | solution.py:37
  55.7 2.5 %collective-permute-start.11 = (bf16[64,7168]{1,0:T(8,128)(2,1)S(1)}, bf16[64,7168]{1,0:T(8,128)(2,1)S(1)}, u32[]{:S(2)}, u32[]{:S(2)}) collective-permute-start(bf16[64,7168]{1,0:T(8,128)(2,1)S(1)} %get-tuple-element.42), channel_id=1, source_target_pairs={{0,1},{1,0},{2,3},{3,2},{4,5},{5,4},{6,7},{7,6},{8,9},{9,8},{10,11... | collective-permute-start | bytes 2752520 | tf_op jit(solution)/shard_map/ppermute | solution.py:37
  58.4 8.5 %collective-permute-start.12 = (bf16[32,7168]{1,0:T(8,128)(2,1)S(1)}, bf16[32,7168]{1,0:T(8,128)(2,1)S(1)}, u32[]{:S(2)}, u32[]{:S(2)}) collective-permute-start(bf16[32,7168]{1,0:T(8,128)(2,1)S(1)} %get-tuple-element.44), channel_id=1, source_target_pairs={{0,16},{1,9},{2,18},{3,11},{4,20},{5,13},{6,22},{7,15},{8,24},{9,1... | collective-permute-start | bytes 1376264 | tf_op jit(solution)/shard_map/ppermute | solution.py:45
  67.1 6.1 %collective-permute-start.13 = (bf16[16,7168]{1,0:T(8,128)(2,1)S(1)}, bf16[16,7168]{1,0:T(8,128)(2,1)S(1)}, u32[]{:S(2)}, u32[]{:S(2)}) collective-permute-start(bf16[16,7168]{1,0:T(8,128)(2,1)S(1)} %get-tuple-element.46), channel_id=1, source_target_pairs={{0,8},{1,17},{2,10},{3,19},{4,12},{5,21},{6,14},{7,23},{8,0},{9,25... | collective-permute-start | bytes 688136 | tf_op jit(solution)/shard_map/ppermute | solution.py:45
  73.2 4.5 %collective-permute-start.14 = (bf16[4,7168]{1,0:T(4,128)(2,1)S(1)}, bf16[4,7168]{1,0:T(4,128)(2,1)S(1)}, u32[]{:S(2)}, u32[]{:S(2)}) collective-permute-start(bf16[4,7168]{1,0:T(4,128)(2,1)S(1)} %get-tuple-element.48), channel_id=1, source_target_pairs={{0,2},{1,3},{2,0},{3,1},{4,6},{5,7},{6,4},{7,5},{8,10},{9,11},{10,... | collective-permute-start | bytes 172040 | tf_op jit(solution)/shard_map/ppermute | solution.py:37
  73.3 5.6 %collective-permute-start.15 = (bf16[4,7168]{1,0:T(4,128)(2,1)S(1)}, bf16[4,7168]{1,0:T(4,128)(2,1)S(1)}, u32[]{:S(2)}, u32[]{:S(2)}) collective-permute-start(bf16[4,7168]{1,0:T(4,128)(2,1)S(1)} %get-tuple-element.49), channel_id=1, source_target_pairs={{0,4},{1,5},{2,6},{3,7},{4,0},{5,1},{6,2},{7,3},{8,12},{9,13},{10,... | collective-permute-start | bytes 172040 | tf_op jit(solution)/shard_map/ppermute | solution.py:37
  74.9 6.0 %collective-permute-start.16 = (bf16[4,7168]{1,0:T(4,128)(2,1)S(1)}, bf16[4,7168]{1,0:T(4,128)(2,1)S(1)}, u32[]{:S(2)}, u32[]{:S(2)}) collective-permute-start(bf16[4,7168]{1,0:T(4,128)(2,1)S(1)} %get-tuple-element.50), channel_id=1, source_target_pairs={{0,6},{1,7},{2,4},{3,5},{4,2},{5,3},{6,0},{7,1},{8,14},{9,15},{10,... | collective-permute-start | bytes 172040 | tf_op jit(solution)/shard_map/ppermute | solution.py:37

commit v7 on v5

--- a/solution.py
+++ b/solution.py
@@ -13,8 +13,9 @@
 VMEM = pltpu.VMEM
 UNIT_BLOCK = 256
 DOWN_BLOCK = 512
-UP_RING = 3
-DOWN_RING = 3
+UP_RING = 2
+DOWN_RING = 5
+FOLD_BLOCK = 1024
 DEPTH_CUT = 1024
 
 
@@ -116,21 +117,24 @@
     return out, mark
 
 
-def join_kernel(first_ref, second_ref, after_ref, out_ref):
-    halves = [r[...].astype(jnp.float32) for r in (first_ref, second_ref)]
-    out_ref[...] = jnp.concatenate(halves, axis=0).astype(out_ref.dtype)
-
-
-def join(first, second, after):
-    rows, width = first.shape
-    after = first if after is None else after
-    return pl.pallas_call(
-        join_kernel,
-        in_specs=whole_vmem(2) + [pl.BlockSpec(memory_space=pl.ANY)],
+def join_kernel(start, *refs):
+    *in_refs, after_ref, out_ref = refs
+    columns = slice(start, start + out_ref.shape[1])
+    pieces = [r[:, columns].astype(jnp.float32) for r in in_refs]
+    out_ref[...] = jnp.concatenate(pieces, axis=0).astype(out_ref.dtype)
+
+
+def join(values, after, start=0, width=None):
+    rows = sum(v.shape[0] for v in values)
+    width = width or values[0].shape[1]
+    after = values[0] if after is None else after
+    return pl.pallas_call(
+        functools.partial(join_kernel, start),
+        in_specs=whole_vmem(len(values)) + [pl.BlockSpec(memory_space=pl.ANY)],
         out_specs=whole_vmem(1)[0],
-        out_shape=VMEM((2 * rows, width), first.dtype),
-        compiler_params=limit(1024 * 1024 + 16 * rows * width),
-    )(in_vmem(first), in_vmem(second), after)
+        out_shape=VMEM((rows, width), values[0].dtype),
+        compiler_params=limit(1024 * 1024 + 8 * rows * width),
+    )(*[in_vmem(v) for v in values], after)
 
 
 def hold_kernel(*refs):
@@ -185,7 +189,7 @@
 
     later = {}
     for n in range(min(DOWN_RING, downs)):
-        later.setdefault(min(blocks - 1, 2 + n), []).append(down_copy(n, n))
+        later.setdefault(min(blocks - 1, 1 + n), []).append(down_copy(n, n))
     for n in range(min(UP_RING, len(streamed))):
         up_copy(n).start()
 
@@ -262,34 +266,50 @@
     )(*args, in_hbm(w_up), in_hbm(w_down), me)
 
 
-def fold_kernel(first_ref, second_ref, keep_ref, send_ref):
-    total = first_ref[...].astype(jnp.float32) + second_ref[...].astype(jnp.float32)
-    half = keep_ref.shape[0]
-    keep_ref[...] = total[:half].astype(keep_ref.dtype)
-    send_ref[...] = total[half:].astype(send_ref.dtype)
-
-
-def fold(first, second):
-    rows, width = first.shape
-    return pl.pallas_call(
-        fold_kernel,
-        in_specs=whole_vmem(2),
-        out_specs=whole_vmem(2),
-        out_shape=[VMEM((rows // 2, width), first.dtype)] * 2,
-        compiler_params=limit(1024 * 1024 + 10 * rows * width),
-    )(in_vmem(first), in_vmem(second))
+def fold_kernel(count, *refs):
+    in_refs, out_refs = refs[:count], refs[count:]
+    size = out_refs[0].shape[0]
+    for first in range(0, in_refs[0].shape[1], FOLD_BLOCK):
+        columns = slice(first, first + FOLD_BLOCK)
+        total = in_refs[0][:, columns].astype(jnp.float32)
+        for ref in in_refs[1:]:
+            total = total + ref[:, columns].astype(jnp.float32)
+        for n, ref in enumerate(out_refs):
+            ref[:, columns] = total[n * size : (n + 1) * size].astype(ref.dtype)
+
+
+def fold(values, pieces):
+    rows, width = values[0].shape
+    return pl.pallas_call(
+        functools.partial(fold_kernel, len(values)),
+        in_specs=whole_vmem(len(values)),
+        out_specs=whole_vmem(pieces),
+        out_shape=[VMEM((rows // pieces, width), values[0].dtype)] * pieces,
+        compiler_params=limit(1024 * 1024 + 12 * rows * FOLD_BLOCK),
+    )(*[in_vmem(v) for v in values])
+
+
+def line_steps(lines):
+    steps = []
+    while lines > 1:
+        radix = min(4, lines)
+        lines //= radix
+        steps.append([2 * lines * m for m in range(1, radix)])
+    return steps
 
 
 def give_back(own, far, groups, members):
-    keep, send = fold(own, swap(far, "expert", members, 1))
-    keep, send = fold(keep, swap_group(send, groups, members, (2, 1)))
-    keep, send = fold(keep, swap_group(send, groups, members, (1, 2)))
-    mask = 2
-    while mask < members // 2:
-        keep, send = fold(keep, swap(send, "expert", members, mask))
-        mask *= 2
-    got = swap(send, "expert", members, mask)
-    return (keep.astype(jnp.float32) + got.astype(jnp.float32)).astype(jnp.bfloat16)
+    values = [own, swap(far, "expert", members, 1)]
+    for masks in [(2, 1), (1, 2)]:
+        keep, send = fold(values, 2)
+        values = [keep, swap_group(send, groups, members, masks)]
+    for masks in reversed(line_steps(members // 2)):
+        keep, *sends = fold(values, len(masks) + 1)
+        values = [keep] + [swap(v, "expert", members, m) for v, m in zip(sends, masks)]
+    total = values[0].astype(jnp.float32)
+    for value in values[1:]:
+        total = total + value.astype(jnp.float32)
+    return total.astype(jnp.bfloat16)
 
 
 def on_device(tokens, expert_ids, gate_weights, w_gate, w_up, w_down):
@@ -299,40 +319,36 @@
     me = lax.axis_index("group") * EXP_GRP + lax.axis_index("expert") // split
     me = me.astype(jnp.int32).reshape(1)
     blocks = w_gate.shape[2] // UNIT_BLOCK
-    ups = max(1, blocks // 8)
-    group = -(-blocks // 4)
-
-    jobs, gate_at, count = [], [], 0
-    for n in range(4):
-        inside = list(range(n * group, min(blocks, (n + 1) * group)))
+    ups = max(1, blocks // 4)
+    order = [(0, n) for n in range(blocks)] + [(1, n) for n in range(ups)]
+    cuts = [len(order) * 3 // 10, len(order) * 6 // 10, len(order)]
+    jobs, place = [], {}
+    for start, stop in zip([0] + cuts, cuts):
         job = []
-        if inside:
-            job.append((w_gate, inside[0] * UNIT_BLOCK, len(inside) * UNIT_BLOCK))
-            gate_at += [(count, i * UNIT_BLOCK) for i in range(len(inside))]
-            count += 1
+        for m in range(2):
+            inside = [n for k, n in order[start:stop] if k == m]
+            for i, n in enumerate(inside):
+                place[m, n] = (sum(map(len, jobs)) + len(job), i * UNIT_BLOCK)
+            if inside:
+                weight = (w_gate, w_up)[m]
+                job.append((weight, inside[0] * UNIT_BLOCK, len(inside) * UNIT_BLOCK))
         jobs.append(job)
-    jobs[3].append((w_up, 0, ups * UNIT_BLOCK))
-    up_at = [(count, b * UNIT_BLOCK) if b < ups else None for b in range(blocks)]
+    gate_at = [place[0, n] for n in range(blocks)]
+    up_at = [place.get((1, n)) for n in range(blocks)]
     streamed = list(range(ups, blocks))
 
     value = pack(me, tokens, expert_ids, gate_weights)
-    held = []
-    mask = members // 2
-    number = 0
-    while mask > 1:
-        got = swap(value, "expert", members, mask)
-        more, mark = fetch(jobs[number] if number < 2 else [], value)
-        held += more
-        value = join(value, got, mark)
-        mask //= 2
-        number += 1
+    held, mark = fetch(jobs[0], value)
+    for masks in line_steps(members // 2):
+        line = [value] + [swap(value, "expert", members, m) for m in masks]
+        value = join(line, mark)
     got = swap_group(value, groups, members, (1, 2))
-    more, mark = fetch(jobs[2], value)
+    more, mark = fetch(jobs[1], value)
     held += more
-    value = join(value, got, mark)
+    value = join([value, got], mark)
     got = swap_group(value, groups, members, (2, 1))
     core = swap(value, "expert", members, 1)
-    more, mark = fetch(jobs[3], value)
+    more, mark = fetch(jobs[2], value)
     held += more
     got = hold(got, mark)
     parts = [value, got, core, swap(got, "expert", members, 1)]

time: 80.8 us -> 79.4 us (0.983)
  waiting for transfers between devices: 24.1 us -> 23 us
    ppermute x4, waiting for transfers between devices: 14.1 us -> 13 us  [swap_group(): return lax.ppermute(value, AXES, pairs)]
    ppermute x4, starting transfers between devices: 7.73 us -> 6.62 us  [swap_group(): return lax.ppermute(value, AXES, pairs)]
    ppermute x7 -> x9, starting transfers between devices: 10.1 us -> 10.4 us  [swap(): return lax.ppermute(value, axis, [(i, i ^ mask) for i in range(size)])]
    pallas_call x4 -> x3, Pallas kernels: 14 us -> 14.1 us  [fetch(): pl.pallas_call(functools.partial(fetch_kernel, jobs), in_specs=[hbm] * le...]
    ppermute x7 -> x9, waiting for transfers between devices: 10 us -> 10.1 us  [swap(): return lax.ppermute(value, axis, [(i, i ^ mask) for i in range(size)])]
  transfers between devices with their start and end apart: 11 -> 13, of which waited for: 8 -> 9; matrix products, arithmetic and copies ran while one was open for 0% -> 0% of each run, Pallas kernels for 17% -> 18%
where the time goes in v7:
time: 79.4 us; the launch traced here: 79.3 us
  Pallas kernels  38.4 us (48%)
  waiting for transfers between devices  23 us (29%)
  starting transfers between devices  17 us (21%)
    pallas_call x1, Pallas kernels, run_expert(): pl.pallas_call(functools.partial(expert_kernel, gate_at, up_at, streamed,...  23 us
    pallas_call x3, Pallas kernels, fetch(): pl.pallas_call(functools.partial(fetch_kernel, jobs), in_specs=[hbm] * le...  14.1 us
    ppermute x4, waiting for transfers between devices, swap_group(): return lax.ppermute(value, AXES, pairs)  13 us
    ppermute x9, starting transfers between devices, swap(): return lax.ppermute(value, axis, [(i, i ^ mask) for i in range(size)])  10.4 us
    ppermute x9, waiting for transfers between devices, swap(): return lax.ppermute(value, axis, [(i, i ^ mask) for i in range(size)])  10.1 us
    ppermute x4, starting transfers between devices, swap_group(): return lax.ppermute(value, AXES, pairs)  6.62 us
  transfers between devices with their start and end apart: 13, of which 9 were waited for; matrix products, arithmetic and copies ran while one was open for 0% of the time, Pallas kernels for 18%

profile of v7, /device:TPU:0, one launch (start us, length us, event | category | flops | bytes accessed | tf_op | source)
XLA Modules:
  0.0 79.3 jit_solution(6847000161017580852)
XLA Ops:
  0.0 0.9 %shard_map.64.refs_1_.refs_0_ = bf16[4,7296]{1,0:T(4,128)(2,1)S(1)} custom-call(s32[1]{0:T(128)} %bitcast.me_ref.refs_10_, bf16[4,7168]{1,0:T(4,128)(2,1)} %tokens_ref.1, s32[4,8]{1,0:T(4,128)} %ids_ref.1, bf16[4,8]{1,0:T(4,128)(2,1)} %weights_ref.1), custom_call_target="tpu_custom_call" | custom-call | tf_op jit(solution)/shard_map/pallas_call | solution.py:69
  0.9 5.1 %collective-permute-start.2 = (bf16[4,7296]{1,0:T(4,128)(2,1)S(1)}, bf16[4,7296]{1,0:T(4,128)(2,1)S(1)}, u32[]{:S(2)}, u32[]{:S(2)}) collective-permute-start(bf16[4,7296]{1,0:T(4,128)(2,1)S(1)} %shard_map.64.refs_1_.refs_0_), channel_id=1, source_target_pairs={{0,6},{1,7},{2,4},{3,5},{4,2},{5,3},{6,0},{7,1},{8,14},{9,15},{10,... | collective-permute-start | bytes 175112 | tf_op jit(solution)/shard_map/ppermute | solution.py:35
  6.0 0.0 collective-permute-start.1
  6.1 0.6 collective-permute-start
  6.7 4.3 %shard_map.65 = (bf16[7168,768]{1,0:T(8,128)(2,1)S(1)}, f32[8,128]{1,0:T(8,128)S(1)}) custom-call(bf16[1,7168,2048]{2,1,0:T(8,128)(2,1)} %refs_0_.5, bf16[4,7296]{1,0:T(4,128)(2,1)S(1)} %shard_map.64.refs_1_.refs_0_), custom_call_target="tpu_custom_call" | custom-call | bytes 11010048 | tf_op jit(solution)/shard_map/pallas_call | solution.py:107
  11.0 0.0 collective-permute-done.2.refs_3_
  11.0 0.1 collective-permute-done.1.refs_2_
  11.1 0.0 collective-permute-done.refs_1_
  11.1 0.1 shard_map.66.refs_1_.refs_0_
  11.2 1.6 %collective-permute-start.3 = (bf16[16,7296]{1,0:T(8,128)(2,1)S(1)}, bf16[16,7296]{1,0:T(8,128)(2,1)S(1)}, u32[]{:S(2)}, u32[]{:S(2)}) collective-permute-start(bf16[16,7296]{1,0:T(8,128)(2,1)S(1)} %shard_map.66.refs_1_.refs_0_), channel_id=1, source_target_pairs={{0,8},{1,17},{2,10},{3,19},{4,12},{5,21},{6,14},{7,23},{8,0},{9,25... | collective-permute-start | bytes 700424 | tf_op jit(solution)/shard_map/ppermute | solution.py:43
  12.8 4.3 %shard_map.67 = (bf16[7168,768]{1,0:T(8,128)(2,1)S(1)}, f32[8,128]{1,0:T(8,128)S(1)}) custom-call(bf16[1,7168,2048]{2,1,0:T(8,128)(2,1)} %refs_0_.5, bf16[16,7296]{1,0:T(8,128)(2,1)S(1)} %shard_map.66.refs_1_.refs_0_), custom_call_target="tpu_custom_call" | custom-call | bytes 11010048 | tf_op jit(solution)/shard_map/pallas_call | solution.py:107
  17.1 0.2 collective-permute-done.3.refs_1_
  17.4 1.7 %collective-permute-start.4 = (bf16[32,7296]{1,0:T(8,128)(2,1)S(1)}, bf16[32,7296]{1,0:T(8,128)(2,1)S(1)}, u32[]{:S(2)}, u32[]{:S(2)}) collective-permute-start(bf16[32,7296]{1,0:T(8,128)(2,1)S(1)} %shard_map.68.refs_2_.refs_0_), channel_id=1, source_target_pairs={{0,16},{1,9},{2,18},{3,11},{4,20},{5,13},{6,22},{7,15},{8,24},{9,1... | collective-permute-start | bytes 1400840 | tf_op jit(solution)/shard_map/ppermute | solution.py:43
  19.0 0.0 collective-permute-start.5
  19.0 5.5 %shard_map.69 = (bf16[7168,512]{1,0:T(8,128)(2,1)S(1)}, bf16[7168,512]{1,0:T(8,128)(2,1)S(1)}, f32[8,128]{1,0:T(8,128)S(1)}) custom-call(bf16[1,7168,2048]{2,1,0:T(8,128)(2,1)} %refs_0_.5, bf16[1,7168,2048]{2,1,0:T(8,128)(2,1)} %refs_8_.1, bf16[32,7296]{1,0:T(8,128)(2,1)S(1)} %shard_map.68.refs_2_.refs_0_), custom_call_target="tpu_custom_call" | custom-call | bytes 14680064 | tf_op jit(solution)/shard_map/pallas_call | solution.py:107
  24.6 1.4 %collective-permute-done.4.refs_0_ = bf16[32,7296]{1,0:T(8,128)(2,1)S(1)} collective-permute-done((bf16[32,7296]{1,0:T(8,128)(2,1)S(1)}, bf16[32,7296]{1,0:T(8,128)(2,1)S(1)}, u32[]{:S(2)}, u32[]{:S(2)}) %collective-permute-start.4) | collective-permute-done | bytes 466976 | tf_op jit(solution)/shard_map/ppermute | solution.py:43
  26.0 0.0 collective-permute-start.6
  26.0 0.0 collective-permute-done.5.refs_2_
  26.0 1.8 %collective-permute-done.6.refs_3_ = bf16[32,7296]{1,0:T(8,128)(2,1)S(1)} collective-permute-done((bf16[32,7296]{1,0:T(8,128)(2,1)S(1)}, bf16[32,7296]{1,0:T(8,128)(2,1)S(1)}, u32[]{:S(2)}, u32[]{:S(2)}) %collective-permute-start.6) | collective-permute-done | bytes 466976 | tf_op jit(solution)/shard_map/ppermute | solution.py:35
  27.8 23.0 %shard_map.71 = (bf16[64,7168]{1,0:T(8,128)(2,1)S(1)}, bf16[64,7168]{1,0:T(8,128)(2,1)S(1)}) custom-call(bf16[32,7296]{1,0:T(8,128)(2,1)S(1)} %shard_map.68.refs_2_.refs_0_, bf16[32,7296]{1,0:T(8,128)(2,1)S(1)} %shard_map.70.refs_1_, bf16[32,7296]{1,0:T(8,128)(2,1)S(1)} %collective-permute-done.5.refs_2_, ...), custom_call_target="tpu_custom_call" | custom-call | flops 11274289152 | bytes 58720256 | tf_op jit(solution)/shard_map/pallas_call | solution.py:250
  50.8 0.2 collective-permute-start.7
  51.0 2.3 %collective-permute-done.7.refs_1_ = bf16[64,7168]{1,0:T(8,128)(2,1)S(1)} collective-permute-done((bf16[64,7168]{1,0:T(8,128)(2,1)S(1)}, bf16[64,7168]{1,0:T(8,128)(2,1)S(1)}, u32[]{:S(2)}, u32[]{:S(2)}) %collective-permute-start.7) | collective-permute-done | bytes 917536 | tf_op jit(solution)/shard_map/ppermute | solution.py:35
  53.3 0.2 shard_map.72
  53.5 1.7 %collective-permute-start.8 = (bf16[32,7168]{1,0:T(8,128)(2,1)S(1)}, bf16[32,7168]{1,0:T(8,128)(2,1)S(1)}, u32[]{:S(2)}, u32[]{:S(2)}) collective-permute-start(bf16[32,7168]{1,0:T(8,128)(2,1)S(1)} %get-tuple-element.32), channel_id=1, source_target_pairs={{0,16},{1,9},{2,18},{3,11},{4,20},{5,13},{6,22},{7,15},{8,24},{9,1... | collective-permute-start | bytes 1376264 | tf_op jit(solution)/shard_map/ppermute | solution.py:43
  55.2 6.9 %collective-permute-done.8.refs_1_ = bf16[32,7168]{1,0:T(8,128)(2,1)S(1)} collective-permute-done((bf16[32,7168]{1,0:T(8,128)(2,1)S(1)}, bf16[32,7168]{1,0:T(8,128)(2,1)S(1)}, u32[]{:S(2)}, u32[]{:S(2)}) %collective-permute-start.8) | collective-permute-done | bytes 458784 | tf_op jit(solution)/shard_map/ppermute | solution.py:43
  62.1 0.1 shard_map.73
  62.2 1.6 %collective-permute-start.9 = (bf16[16,7168]{1,0:T(8,128)(2,1)S(1)}, bf16[16,7168]{1,0:T(8,128)(2,1)S(1)}, u32[]{:S(2)}, u32[]{:S(2)}) collective-permute-start(bf16[16,7168]{1,0:T(8,128)(2,1)S(1)} %get-tuple-element.34), channel_id=1, source_target_pairs={{0,8},{1,17},{2,10},{3,19},{4,12},{5,21},{6,14},{7,23},{8,0},{9,25... | collective-permute-start | bytes 688136 | tf_op jit(solution)/shard_map/ppermute | solution.py:43
  63.8 4.4 %collective-permute-done.9.refs_1_ = bf16[16,7168]{1,0:T(8,128)(2,1)S(1)} collective-permute-done((bf16[16,7168]{1,0:T(8,128)(2,1)S(1)}, bf16[16,7168]{1,0:T(8,128)(2,1)S(1)}, u32[]{:S(2)}, u32[]{:S(2)}) %collective-permute-start.9) | collective-permute-done | bytes 229408 | tf_op jit(solution)/shard_map/ppermute | solution.py:43
  68.3 0.1 shard_map.74
  68.4 1.3 %collective-permute-start.10 = (bf16[4,7168]{1,0:T(4,128)(2,1)S(1)}, bf16[4,7168]{1,0:T(4,128)(2,1)S(1)}, u32[]{:S(2)}, u32[]{:S(2)}) collective-permute-start(bf16[4,7168]{1,0:T(4,128)(2,1)S(1)} %get-tuple-element.36), channel_id=1, source_target_pairs={{0,2},{1,3},{2,0},{3,1},{4,6},{5,7},{6,4},{7,5},{8,10},{9,11},{10,... | collective-permute-start | bytes 172040 | tf_op jit(solution)/shard_map/ppermute | solution.py:35
  69.7 2.9 %collective-permute-start.11 = (bf16[4,7168]{1,0:T(4,128)(2,1)S(1)}, bf16[4,7168]{1,0:T(4,128)(2,1)S(1)}, u32[]{:S(2)}, u32[]{:S(2)}) collective-permute-start(bf16[4,7168]{1,0:T(4,128)(2,1)S(1)} %get-tuple-element.37), channel_id=1, source_target_pairs={{0,4},{1,5},{2,6},{3,7},{4,0},{5,1},{6,2},{7,3},{8,12},{9,13},{10,... | collective-permute-start | bytes 172040 | tf_op jit(solution)/shard_map/ppermute | solution.py:35
  72.6 0.2 collective-permute-start.12
  72.8 0.0 collective-permute-done.10
  72.8 3.2 %collective-permute-done.11 = bf16[4,7168]{1,0:T(4,128)(2,1)S(1)} collective-permute-done((bf16[4,7168]{1,0:T(4,128)(2,1)S(1)}, bf16[4,7168]{1,0:T(4,128)(2,1)S(1)}, u32[]{:S(2)}, u32[]{:S(2)}) %collective-permute-start.11) | collective-permute-done | bytes 57376 | tf_op jit(solution)/shard_map/ppermute | solution.py:35
  76.0 2.6 %collective-permute-done.12 = bf16[4,7168]{1,0:T(4,128)(2,1)S(1)} collective-permute-done((bf16[4,7168]{1,0:T(4,128)(2,1)S(1)}, bf16[4,7168]{1,0:T(4,128)(2,1)S(1)}, u32[]{:S(2)}, u32[]{:S(2)}) %collective-permute-start.12) | collective-permute-done | bytes 57376 | tf_op jit(solution)/shard_map/ppermute | solution.py:35
  78.6 0.7 add_convert_fusion
  (2 shorter events, 0.0 us)
Async XLA Ops:
  0.9 10.1 %collective-permute-start.2 = (bf16[4,7296]{1,0:T(4,128)(2,1)S(1)}, bf16[4,7296]{1,0:T(4,128)(2,1)S(1)}, u32[]{:S(2)}, u32[]{:S(2)}) collective-permute-start(bf16[4,7296]{1,0:T(4,128)(2,1)S(1)} %shard_map.64.refs_1_.refs_0_), channel_id=1, source_target_pairs={{0,6},{1,7},{2,4},{3,5},{4,2},{5,3},{6,0},{7,1},{8,14},{9,15},{10,... | collective-permute-start | bytes 175112 | tf_op jit(solution)/shard_map/ppermute | solution.py:35
  6.0 5.1 %collective-permute-start.1 = (bf16[4,7296]{1,0:T(4,128)(2,1)S(1)}, bf16[4,7296]{1,0:T(4,128)(2,1)S(1)}, u32[]{:S(2)}, u32[]{:S(2)}) collective-permute-start(bf16[4,7296]{1,0:T(4,128)(2,1)S(1)} %shard_map.64.refs_1_.refs_0_), channel_id=1, source_target_pairs={{0,4},{1,5},{2,6},{3,7},{4,0},{5,1},{6,2},{7,3},{8,12},{9,13},{10,... | collective-permute-start | bytes 175112 | tf_op jit(solution)/shard_map/ppermute | solution.py:35
  6.1 5.1 %collective-permute-start = (bf16[4,7296]{1,0:T(4,128)(2,1)S(1)}, bf16[4,7296]{1,0:T(4,128)(2,1)S(1)}, u32[]{:S(2)}, u32[]{:S(2)}) collective-permute-start(bf16[4,7296]{1,0:T(4,128)(2,1)S(1)} %shard_map.64.refs_1_.refs_0_), channel_id=1, source_target_pairs={{0,2},{1,3},{2,0},{3,1},{4,6},{5,7},{6,4},{7,5},{8,10},{9,11},{10,... | collective-permute-start | bytes 175112 | tf_op jit(solution)/shard_map/ppermute | solution.py:35
  11.2 6.1 %collective-permute-start.3 = (bf16[16,7296]{1,0:T(8,128)(2,1)S(1)}, bf16[16,7296]{1,0:T(8,128)(2,1)S(1)}, u32[]{:S(2)}, u32[]{:S(2)}) collective-permute-start(bf16[16,7296]{1,0:T(8,128)(2,1)S(1)} %shard_map.66.refs_1_.refs_0_), channel_id=1, source_target_pairs={{0,8},{1,17},{2,10},{3,19},{4,12},{5,21},{6,14},{7,23},{8,0},{9,25... | collective-permute-start | bytes 700424 | tf_op jit(solution)/shard_map/ppermute | solution.py:43
  17.4 8.6 %collective-permute-start.4 = (bf16[32,7296]{1,0:T(8,128)(2,1)S(1)}, bf16[32,7296]{1,0:T(8,128)(2,1)S(1)}, u32[]{:S(2)}, u32[]{:S(2)}) collective-permute-start(bf16[32,7296]{1,0:T(8,128)(2,1)S(1)} %shard_map.68.refs_2_.refs_0_), channel_id=1, source_target_pairs={{0,16},{1,9},{2,18},{3,11},{4,20},{5,13},{6,22},{7,15},{8,24},{9,1... | collective-permute-start | bytes 1400840 | tf_op jit(solution)/shard_map/ppermute | solution.py:43
  19.0 7.0 %collective-permute-start.5 = (bf16[32,7296]{1,0:T(8,128)(2,1)S(1)}, bf16[32,7296]{1,0:T(8,128)(2,1)S(1)}, u32[]{:S(2)}, u32[]{:S(2)}) collective-permute-start(bf16[32,7296]{1,0:T(8,128)(2,1)S(1)} %shard_map.68.refs_2_.refs_0_), channel_id=1, source_target_pairs={{0,1},{1,0},{2,3},{3,2},{4,5},{5,4},{6,7},{7,6},{8,9},{9,8},{10,11... | collective-permute-start | bytes 1400840 | tf_op jit(solution)/shard_map/ppermute | solution.py:35
  26.0 1.8 %collective-permute-start.6 = (bf16[32,7296]{1,0:T(8,128)(2,1)S(1)}, bf16[32,7296]{1,0:T(8,128)(2,1)S(1)}, u32[]{:S(2)}, u32[]{:S(2)}) collective-permute-start(bf16[32,7296]{1,0:T(8,128)(2,1)S(1)} %shard_map.70.refs_1_), channel_id=1, source_target_pairs={{0,1},{1,0},{2,3},{3,2},{4,5},{5,4},{6,7},{7,6},{8,9},{9,8},{10,11... | collective-permute-start | bytes 1400840 | tf_op jit(solution)/shard_map/ppermute | solution.py:35
  50.8 2.5 %collective-permute-start.7 = (bf16[64,7168]{1,0:T(8,128)(2,1)S(1)}, bf16[64,7168]{1,0:T(8,128)(2,1)S(1)}, u32[]{:S(2)}, u32[]{:S(2)}) collective-permute-start(bf16[64,7168]{1,0:T(8,128)(2,1)S(1)} %get-tuple-element.30), channel_id=1, source_target_pairs={{0,1},{1,0},{2,3},{3,2},{4,5},{5,4},{6,7},{7,6},{8,9},{9,8},{10,11... | collective-permute-start | bytes 2752520 | tf_op jit(solution)/shard_map/ppermute | solution.py:35
  53.5 8.5 %collective-permute-start.8 = (bf16[32,7168]{1,0:T(8,128)(2,1)S(1)}, bf16[32,7168]{1,0:T(8,128)(2,1)S(1)}, u32[]{:S(2)}, u32[]{:S(2)}) collective-permute-start(bf16[32,7168]{1,0:T(8,128)(2,1)S(1)} %get-tuple-element.32), channel_id=1, source_target_pairs={{0,16},{1,9},{2,18},{3,11},{4,20},{5,13},{6,22},{7,15},{8,24},{9,1... | collective-permute-start | bytes 1376264 | tf_op jit(solution)/shard_map/ppermute | solution.py:43
  62.2 6.1 %collective-permute-start.9 = (bf16[16,7168]{1,0:T(8,128)(2,1)S(1)}, bf16[16,7168]{1,0:T(8,128)(2,1)S(1)}, u32[]{:S(2)}, u32[]{:S(2)}) collective-permute-start(bf16[16,7168]{1,0:T(8,128)(2,1)S(1)} %get-tuple-element.34), channel_id=1, source_target_pairs={{0,8},{1,17},{2,10},{3,19},{4,12},{5,21},{6,14},{7,23},{8,0},{9,25... | collective-permute-start | bytes 688136 | tf_op jit(solution)/shard_map/ppermute | solution.py:43
  68.4 4.5 %collective-permute-start.10 = (bf16[4,7168]{1,0:T(4,128)(2,1)S(1)}, bf16[4,7168]{1,0:T(4,128)(2,1)S(1)}, u32[]{:S(2)}, u32[]{:S(2)}) collective-permute-start(bf16[4,7168]{1,0:T(4,128)(2,1)S(1)} %get-tuple-element.36), channel_id=1, source_target_pairs={{0,2},{1,3},{2,0},{3,1},{4,6},{5,7},{6,4},{7,5},{8,10},{9,11},{10,... | collective-permute-start | bytes 172040 | tf_op jit(solution)/shard_map/ppermute | solution.py:35
  69.7 6.3 %collective-permute-start.11 = (bf16[4,7168]{1,0:T(4,128)(2,1)S(1)}, bf16[4,7168]{1,0:T(4,128)(2,1)S(1)}, u32[]{:S(2)}, u32[]{:S(2)}) collective-permute-start(bf16[4,7168]{1,0:T(4,128)(2,1)S(1)} %get-tuple-element.37), channel_id=1, source_target_pairs={{0,4},{1,5},{2,6},{3,7},{4,0},{5,1},{6,2},{7,3},{8,12},{9,13},{10,... | collective-permute-start | bytes 172040 | tf_op jit(solution)/shard_map/ppermute | solution.py:35
  72.6 6.0 %collective-permute-start.12 = (bf16[4,7168]{1,0:T(4,128)(2,1)S(1)}, bf16[4,7168]{1,0:T(4,128)(2,1)S(1)}, u32[]{:S(2)}, u32[]{:S(2)}) collective-permute-start(bf16[4,7168]{1,0:T(4,128)(2,1)S(1)} %get-tuple-element.38), channel_id=1, source_target_pairs={{0,6},{1,7},{2,4},{3,5},{4,2},{5,3},{6,0},{7,1},{8,14},{9,15},{10,... | collective-permute-start | bytes 172040 | tf_op jit(solution)/shard_map/ppermute | solution.py:35

commit v8 on v7

--- a/solution.py
+++ b/solution.py
@@ -13,7 +13,7 @@
 VMEM = pltpu.VMEM
 UNIT_BLOCK = 256
 DOWN_BLOCK = 512
-UP_RING = 2
+RING = 4
 DOWN_RING = 5
 FOLD_BLOCK = 1024
 DEPTH_CUT = 1024
@@ -117,22 +117,23 @@
     return out, mark
 
 
-def join_kernel(start, *refs):
-    *in_refs, after_ref, out_ref = refs
-    columns = slice(start, start + out_ref.shape[1])
-    pieces = [r[:, columns].astype(jnp.float32) for r in in_refs]
-    out_ref[...] = jnp.concatenate(pieces, axis=0).astype(out_ref.dtype)
-
-
-def join(values, after, start=0, width=None):
+def join_kernel(cuts, *refs):
+    in_refs, out_refs = refs[: -len(cuts) - 1], refs[-len(cuts) :]
+    for (start, size), out_ref in zip(cuts, out_refs):
+        pieces = [r[:, start : start + size].astype(jnp.float32) for r in in_refs]
+        out_ref[...] = jnp.concatenate(pieces, axis=0).astype(out_ref.dtype)
+
+
+def join(values, after, cuts=None):
     rows = sum(v.shape[0] for v in values)
-    width = width or values[0].shape[1]
+    width = values[0].shape[1]
+    cuts = cuts or [(0, width)]
     after = values[0] if after is None else after
     return pl.pallas_call(
-        functools.partial(join_kernel, start),
+        functools.partial(join_kernel, cuts),
         in_specs=whole_vmem(len(values)) + [pl.BlockSpec(memory_space=pl.ANY)],
-        out_specs=whole_vmem(1)[0],
-        out_shape=VMEM((rows, width), values[0].dtype),
+        out_specs=whole_vmem(len(cuts)),
+        out_shape=[VMEM((rows, size), values[0].dtype) for _, size in cuts],
         compiler_params=limit(1024 * 1024 + 8 * rows * width),
     )(*[in_vmem(v) for v in values], after)
 
@@ -141,17 +142,17 @@
     pass
 
 
-def hold(value, after):
+def hold(values, after):
     if after is None:
-        return value
+        return values
     return pl.pallas_call(
         hold_kernel,
-        in_specs=[pl.BlockSpec(memory_space=pl.ANY)] * 2,
-        out_specs=pl.BlockSpec(memory_space=pl.ANY),
-        out_shape=jax.ShapeDtypeStruct(value.shape, value.dtype),
-        input_output_aliases={0: 0},
+        in_specs=[pl.BlockSpec(memory_space=pl.ANY)] * (len(values) + 1),
+        out_specs=[pl.BlockSpec(memory_space=pl.ANY)] * len(values),
+        out_shape=[jax.ShapeDtypeStruct(v.shape, v.dtype) for v in values],
+        input_output_aliases={i: i for i in range(len(values))},
         compiler_params=limit(256 * 1024),
-    )(value, after)
+    )(*values, after)
 
 
 def times(left_ref, right_ref):
@@ -164,94 +165,107 @@
     return total
 
 
-def expert_kernel(gate_at, up_at, streamed, held, *refs):
-    x_refs, w_refs, refs = refs[:4], refs[4 : 4 + held], refs[4 + held :]
-    up_hbm, down_hbm, me_ref, own_ref, far_ref = refs[:5]
-    x, hidden, scale_ref, up_ring, down_ring, up_sem, down_sem = refs[5:]
+def expert_kernel(place, order, streams, held, *refs):
+    x_refs, w_refs, refs = refs[:8], refs[8 : 8 + held], refs[8 + held :]
+    hbm, down_hbm, me_ref = refs[:2], refs[2], refs[3]
+    own_refs, far_refs = refs[4:6], refs[6:8]
+    x, hidden, scale_ref, ring, down_ring, sems, down_sem = refs[8:]
     depth, units = x.shape[1], hidden.shape[1]
     blocks = units // UNIT_BLOCK
     downs = depth // DOWN_BLOCK
 
-    def up_copy(n):
+    def copy(n):
+        m, b = streams[n]
         return pltpu.make_async_copy(
-            up_hbm.at[0, :, pl.ds(streamed[n] * UNIT_BLOCK, UNIT_BLOCK)],
-            up_ring.at[n % UP_RING],
-            up_sem.at[n % UP_RING],
+            hbm[m].at[0, :, pl.ds(b * UNIT_BLOCK, UNIT_BLOCK)], ring.at[n % RING], sems.at[n % RING]
         )
 
     def down_copy(d, slot):
-        first = d * DOWN_BLOCK
-        if not isinstance(d, int):
-            first = pl.multiple_of(first, DOWN_BLOCK)
         return pltpu.make_async_copy(
-            down_hbm.at[0, :, pl.ds(first, DOWN_BLOCK)], down_ring.at[slot], down_sem.at[slot]
+            down_hbm.at[0, :, pl.ds(d * DOWN_BLOCK, DOWN_BLOCK)],
+            down_ring.at[slot],
+            down_sem.at[slot],
         )
 
     later = {}
     for n in range(min(DOWN_RING, downs)):
-        later.setdefault(min(blocks - 1, 1 + n), []).append(down_copy(n, n))
-    for n in range(min(UP_RING, len(streamed))):
-        up_copy(n).start()
+        later.setdefault(min(blocks - 1, 3 + n), []).append(down_copy(n, n))
+    for n in range(min(RING, len(streams))):
+        copy(n).start()
 
     part = x_refs[0].shape[0]
-    for n, x_ref in enumerate(x_refs):
-        x[n * part : (n + 1) * part, :] = x_ref[:, :depth]
-        route = x_ref[:, depth:].astype(jnp.float32)
+    width = depth // 2
+    for n in range(4):
+        rows = slice(n * part, (n + 1) * part)
+        x[rows, :width] = x_refs[n][...]
+        x[rows, width:] = x_refs[4 + n][:, :width]
+        route = x_refs[4 + n][:, width:].astype(jnp.float32)
         lane = lax.broadcasted_iota(jnp.int32, route.shape, 1)
         scale = jnp.sum(jnp.where(lane == me_ref[0], route, 0.0), axis=1, keepdims=True)
-        scale_ref[n * part : (n + 1) * part, :] = jnp.broadcast_to(scale, route.shape)
-
-    for b in range(blocks):
-        where, first = gate_at[b]
-        gate = times(x, w_refs[where].at[:, first : first + UNIT_BLOCK])
-        if up_at[b] is None:
-            n = streamed.index(b)
-            up_copy(n).wait()
-            up = times(x, up_ring.at[n % UP_RING])
-            if n + UP_RING < len(streamed):
-                up_copy(n + UP_RING).start()
-        else:
-            where, first = up_at[b]
-            up = times(x, w_refs[where].at[:, first : first + UNIT_BLOCK])
-        for copy in later.get(b, []):
-            copy.start()
+        scale_ref[rows, :] = jnp.broadcast_to(scale, route.shape)
+
+    def finish(b, gate, up):
         hidden[:, b * UNIT_BLOCK : (b + 1) * UNIT_BLOCK] = (jax.nn.silu(gate) * up).astype(
             jnp.bfloat16
         )
 
-    @pl.loop(0, downs)
-    def _(d):
-        slot = lax.rem(d, DOWN_RING)
-        columns = pl.ds(pl.multiple_of(d * DOWN_BLOCK, DOWN_BLOCK), DOWN_BLOCK)
-        down_copy(d, slot).wait()
-        value = (times(hidden, down_ring.at[slot]) * scale_ref[:, :1]).astype(jnp.bfloat16)
-
-        @pl.when(d + DOWN_RING < downs)
-        def _():
-            down_copy(d + DOWN_RING, slot).start()
-
-        own_ref[:, columns] = value[: 2 * part]
-        far_ref[:, columns] = value[2 * part :]
-
-
-def run_expert(parts, held, gate_at, up_at, streamed, w_up, w_down, me):
-    rows = sum(p.shape[0] for p in parts)
+    waiting = None
+    for turn, b in enumerate(order):
+        weights, used = [], []
+        for m in range(2):
+            if (m, b) in place:
+                where, first = place[m, b]
+                weights.append(w_refs[where].at[:, first : first + UNIT_BLOCK])
+            else:
+                n = streams.index((m, b))
+                copy(n).wait()
+                weights.append(ring.at[n % RING])
+                used.append(n)
+        gate, up = [times(x, w) for w in weights]
+        if waiting:
+            finish(*waiting)
+        waiting = (b, gate, up)
+        for n in used:
+            if n + RING < len(streams):
+                copy(n + RING).start()
+        for piece in later.get(turn, []):
+            piece.start()
+    finish(*waiting)
+
+    for first in range(0, downs, 2):
+        pair = range(first, min(first + 2, downs))
+        for d in pair:
+            down_copy(d, d % DOWN_RING).wait()
+        for d in pair:
+            value = times(hidden, down_ring.at[d % DOWN_RING]) * scale_ref[:, :1]
+            value = value.astype(jnp.bfloat16)
+            half, at = divmod(d * DOWN_BLOCK, width)
+            own_refs[half][:, at : at + DOWN_BLOCK] = value[: 2 * part]
+            far_refs[half][:, at : at + DOWN_BLOCK] = value[2 * part :]
+        for d in pair:
+            if d + DOWN_RING < downs:
+                down_copy(d + DOWN_RING, d % DOWN_RING).start()
+
+
+def run_expert(a_parts, b_parts, held, place, order, w_gate, w_up, w_down, me):
+    rows = sum(p.shape[0] for p in a_parts)
     depth, units = w_up.shape[1], w_up.shape[2]
-    half = VMEM((rows // 2, depth), jnp.bfloat16)
+    half = VMEM((rows // 2, depth // 2), jnp.bfloat16)
     hbm = pl.BlockSpec(memory_space=pltpu.HBM)
-    ring = max(1, min(UP_RING, len(streamed)))
+    streams = [(m, b) for b in order for m in range(2) if (m, b) not in place]
+    ring = max(1, min(RING, len(streams)))
     scratch = 2 * (
         rows * (depth + units + 2 * LANES)
         + ring * depth * UNIT_BLOCK
         + DOWN_RING * units * DOWN_BLOCK
     )
     work = 2560 * 1024 + 12 * rows * UNIT_BLOCK + 4 * rows * DOWN_BLOCK
-    args = [in_vmem(v) for v in [*parts, *held]]
-    return pl.pallas_call(
-        functools.partial(expert_kernel, gate_at, up_at, streamed, len(held)),
-        in_specs=whole_vmem(len(args)) + [hbm, hbm, pl.BlockSpec(memory_space=pltpu.SMEM)],
-        out_specs=whole_vmem(2),
-        out_shape=(half, half),
+    args = [in_vmem(v) for v in [*a_parts, *b_parts, *held]]
+    return pl.pallas_call(
+        functools.partial(expert_kernel, place, order, streams, len(held)),
+        in_specs=whole_vmem(len(args)) + [hbm] * 3 + [pl.BlockSpec(memory_space=pltpu.SMEM)],
+        out_specs=whole_vmem(4),
+        out_shape=(half,) * 4,
         scratch_shapes=[
             VMEM((rows, depth), jnp.bfloat16),
             VMEM((rows, units), jnp.bfloat16),
@@ -263,7 +277,7 @@
         ],
         compiler_params=limit(scratch + work),
         cost_estimate=cost(6 * rows * depth * units, 4 * depth * units),
-    )(*args, in_hbm(w_up), in_hbm(w_down), me)
+    )(*args, in_hbm(w_gate), in_hbm(w_up), in_hbm(w_down), me)
 
 
 def fold_kernel(count, *refs):
@@ -319,41 +333,49 @@
     me = lax.axis_index("group") * EXP_GRP + lax.axis_index("expert") // split
     me = me.astype(jnp.int32).reshape(1)
     blocks = w_gate.shape[2] // UNIT_BLOCK
-    ups = max(1, blocks // 4)
-    order = [(0, n) for n in range(blocks)] + [(1, n) for n in range(ups)]
-    cuts = [len(order) * 3 // 10, len(order) * 6 // 10, len(order)]
-    jobs, place = [], {}
-    for start, stop in zip([0] + cuts, cuts):
+    gates, ups = max(1, blocks // 2), max(1, blocks * 3 // 8)
+    cuts = [0, max(1, gates // 2), max(1, gates * 3 // 4), gates]
+    jobs, place, count = [], {}, 0
+    for n in range(3):
+        pieces = [(0, list(range(cuts[n], cuts[n + 1]))), (1, list(range(ups)) if n == 2 else [])]
         job = []
-        for m in range(2):
-            inside = [n for k, n in order[start:stop] if k == m]
-            for i, n in enumerate(inside):
-                place[m, n] = (sum(map(len, jobs)) + len(job), i * UNIT_BLOCK)
+        for m, inside in pieces:
             if inside:
-                weight = (w_gate, w_up)[m]
-                job.append((weight, inside[0] * UNIT_BLOCK, len(inside) * UNIT_BLOCK))
+                job.append(((w_gate, w_up)[m], inside[0] * UNIT_BLOCK, len(inside) * UNIT_BLOCK))
+                for i, b in enumerate(inside):
+                    place[m, b] = (count, i * UNIT_BLOCK)
+                count += 1
         jobs.append(job)
-    gate_at = [place[0, n] for n in range(blocks)]
-    up_at = [place.get((1, n)) for n in range(blocks)]
-    streamed = list(range(ups, blocks))
+    order = list(range(min(2, ups)))
+    fixed, loose = list(range(len(order), gates)), list(range(gates, blocks))
+    while fixed or loose:
+        order += loose[:1] + fixed[:1]
+        fixed, loose = fixed[1:], loose[1:]
 
     value = pack(me, tokens, expert_ids, gate_weights)
+    width = tokens.shape[1] // 2
+    halves = [(0, width), (width, width + LANES)]
     held, mark = fetch(jobs[0], value)
-    for masks in line_steps(members // 2):
+    steps = line_steps(members // 2)
+    for n, masks in enumerate(steps):
         line = [value] + [swap(value, "expert", members, m) for m in masks]
-        value = join(line, mark)
-    got = swap_group(value, groups, members, (1, 2))
-    more, mark = fetch(jobs[1], value)
+        value, *other = join(line, mark, halves if n == len(steps) - 1 else None)
+    a, b = value, other[0]
+    a_got, b_got = [swap_group(v, groups, members, (1, 2)) for v in (a, b)]
+    more, mark = fetch(jobs[1], a)
     held += more
-    value = join([value, got], mark)
-    got = swap_group(value, groups, members, (2, 1))
-    core = swap(value, "expert", members, 1)
-    more, mark = fetch(jobs[2], value)
+    (a,) = join([a, a_got], mark)
+    (b,) = join([b, b_got], mark)
+    a_got, b_got = [swap_group(v, groups, members, (2, 1)) for v in (a, b)]
+    a_core, b_core = swap(a, "expert", members, 1), swap(b, "expert", members, 1)
+    more, mark = fetch(jobs[2], a)
     held += more
-    got = hold(got, mark)
-    parts = [value, got, core, swap(got, "expert", members, 1)]
-    own, far = run_expert(parts, held, gate_at, up_at, streamed, w_up, w_down, me)
-    return give_back(own, far, groups, members)
+    (a_got,), (b_got,) = hold([a_got], mark), hold([b_got], mark)
+    a_parts = [a, a_got, a_core, swap(a_got, "expert", members, 1)]
+    b_parts = [b, b_got, b_core, swap(b_got, "expert", members, 1)]
+    sums = run_expert(a_parts, b_parts, held, place, order, w_gate, w_up, w_down, me)
+    out = [give_back(own, far, groups, members) for own, far in zip(sums[:2], sums[2:])]
+    return jnp.concatenate(out, axis=1)
 
 
 def solution(mesh):

time: 79.4 us -> 78.9 us (level)
  starting transfers between devices: 17 us -> 25.7 us
  waiting for transfers between devices: 23 us -> 16.7 us
  Pallas kernels: 38.4 us -> 35.4 us
    ppermute x9 -> x15, starting transfers between devices: 10.4 us -> 16.3 us  [swap(): return lax.ppermute(value, axis, [(i, i ^ mask) for i in range(size)])]
    ppermute x4 -> x8, waiting for transfers between devices: 13 us -> 8.11 us  [swap_group(): return lax.ppermute(value, AXES, pairs)]
    pallas_call x3, Pallas kernels: 14.1 us -> 10.7 us  [fetch(): pl.pallas_call(functools.partial(fetch_kernel, jobs), in_specs=[hbm] * le...]
    ppermute x4 -> x8, starting transfers between devices: 6.62 us -> 9.37 us  [swap_group(): return lax.ppermute(value, AXES, pairs)]
    ppermute x9 -> x15, waiting for transfers between devices: 10.1 us -> 8.64 us  [swap(): return lax.ppermute(value, axis, [(i, i ^ mask) for i in range(size)])]
    pallas_call x3 -> x4, Pallas kernels: 23 us -> 23.4 us  [the longest x1 23.3 us: run_expert(): pl.pallas_call(functools.partial(expert_kernel, place, order, streams, le...]
  transfers between devices with their start and end apart: 13 -> 23, of which waited for: 9 -> 12; matrix products, arithmetic and copies ran while one was open for 0% -> 0% of each run, Pallas kernels for 18% -> 14%
where the time goes in v8:
time: 78.9 us; the launch traced here: 78.7 us
  Pallas kernels  35.4 us (45%)
  starting transfers between devices  25.7 us (33%)
  waiting for transfers between devices  16.7 us (21%)
    pallas_call x1, Pallas kernels, run_expert(): pl.pallas_call(functools.partial(expert_kernel, place, order, streams, le...  23.3 us
    ppermute x15, starting transfers between devices, swap(): return lax.ppermute(value, axis, [(i, i ^ mask) for i in range(size)])  16.3 us
    pallas_call x3, Pallas kernels, fetch(): pl.pallas_call(functools.partial(fetch_kernel, jobs), in_specs=[hbm] * le...  10.7 us
    ppermute x8, starting transfers between devices, swap_group(): return lax.ppermute(value, AXES, pairs)  9.37 us
    ppermute x15, waiting for transfers between devices, swap(): return lax.ppermute(value, axis, [(i, i ^ mask) for i in range(size)])  8.64 us
    ppermute x8, waiting for transfers between devices, swap_group(): return lax.ppermute(value, AXES, pairs)  8.11 us
  transfers between devices with their start and end apart: 23, of which 12 were waited for; matrix products, arithmetic and copies ran while one was open for 0% of the time, Pallas kernels for 14%

profile of v8, /device:TPU:0, one launch (start us, length us, event | category | flops | bytes accessed | tf_op | source)
XLA Modules:
  0.0 78.7 jit_solution(161566041399105283)
XLA Ops:
  0.0 0.9 %shard_map.64.refs_1_.refs_0_ = bf16[4,7296]{1,0:T(4,128)(2,1)S(1)} custom-call(s32[1]{0:T(128)} %bitcast.me_ref.refs_15_, bf16[4,7168]{1,0:T(4,128)(2,1)} %tokens_ref.1, s32[4,8]{1,0:T(4,128)} %ids_ref.1, bf16[4,8]{1,0:T(4,128)(2,1)} %weights_ref.1), custom_call_target="tpu_custom_call" | custom-call | tf_op jit(solution)/shard_map/pallas_call | solution.py:69
  0.9 5.1 %collective-permute-start.2 = (bf16[4,7296]{1,0:T(4,128)(2,1)S(1)}, bf16[4,7296]{1,0:T(4,128)(2,1)S(1)}, u32[]{:S(2)}, u32[]{:S(2)}) collective-permute-start(bf16[4,7296]{1,0:T(4,128)(2,1)S(1)} %shard_map.64.refs_1_.refs_0_), channel_id=1, source_target_pairs={{0,6},{1,7},{2,4},{3,5},{4,2},{5,3},{6,0},{7,1},{8,14},{9,15},{10,... | collective-permute-start | bytes 175112 | tf_op jit(solution)/shard_map/ppermute | solution.py:35
  6.1 0.6 collective-permute-start
  6.7 3.2 %shard_map.65 = (bf16[7168,512]{1,0:T(8,128)(2,1)S(1)}, f32[8,128]{1,0:T(8,128)S(1)}) custom-call(bf16[1,7168,2048]{2,1,0:T(8,128)(2,1)} %refs_12_.1, bf16[4,7296]{1,0:T(4,128)(2,1)S(1)} %shard_map.64.refs_1_.refs_0_), custom_call_target="tpu_custom_call" | custom-call | bytes 7340032 | tf_op jit(solution)/shard_map/pallas_call | solution.py:107
  9.9 0.0 collective-permute-done.2.refs_3_
  9.9 1.2 %collective-permute-done.1.refs_2_ = bf16[4,7296]{1,0:T(4,128)(2,1)S(1)} collective-permute-done((bf16[4,7296]{1,0:T(4,128)(2,1)S(1)}, bf16[4,7296]{1,0:T(4,128)(2,1)S(1)}, u32[]{:S(2)}, u32[]{:S(2)}) %collective-permute-start.1) | collective-permute-done | bytes 58400 | tf_op jit(solution)/shard_map/ppermute | solution.py:35
  11.1 0.0 collective-permute-done.refs_1_
  11.1 0.1 shard_map.66
  11.2 1.6 %collective-permute-start.7 = (bf16[16,3712]{1,0:T(8,128)(2,1)S(1)}, bf16[16,3712]{1,0:T(8,128)(2,1)S(1)}, u32[]{:S(2)}, u32[]{:S(2)}) collective-permute-start(bf16[16,3712]{1,0:T(8,128)(2,1)S(1)} %get-tuple-element.38.refs_0_), channel_id=1, source_target_pairs={{0,8},{1,17},{2,10},{3,19},{4,12},{5,21},{6,14},{7,23},{8,0},{9,25... | collective-permute-start | bytes 356360 | tf_op jit(solution)/shard_map/ppermute | solution.py:43
  12.8 0.4 collective-permute-start.3
  13.3 2.1 %shard_map.67 = (bf16[7168,256]{1,0:T(8,128)(2,1)S(1)}, f32[8,128]{1,0:T(8,128)S(1)}) custom-call(bf16[1,7168,2048]{2,1,0:T(8,128)(2,1)} %refs_12_.1, bf16[16,3584]{1,0:T(8,128)(2,1)S(1)} %get-tuple-element.35.refs_1_.refs_0_), custom_call_target="tpu_custom_call" | custom-call | bytes 3670016 | tf_op jit(solution)/shard_map/pallas_call | solution.py:107
  15.4 0.7 collective-permute-done.7.refs_1_
  16.1 1.7 %collective-permute-start.8 = (bf16[32,3712]{1,0:T(8,128)(2,1)S(1)}, bf16[32,3712]{1,0:T(8,128)(2,1)S(1)}, u32[]{:S(2)}, u32[]{:S(2)}) collective-permute-start(bf16[32,3712]{1,0:T(8,128)(2,1)S(1)} %shard_map.71.refs_4_), channel_id=1, source_target_pairs={{0,16},{1,9},{2,18},{3,11},{4,20},{5,13},{6,22},{7,15},{8,24},{9,1... | collective-permute-start | bytes 712712 | tf_op jit(solution)/shard_map/ppermute | solution.py:43
  17.8 0.7 collective-permute-done.3.refs_1_
  18.6 1.5 %collective-permute-start.4 = (bf16[32,3584]{1,0:T(8,128)(2,1)S(1)}, bf16[32,3584]{1,0:T(8,128)(2,1)S(1)}, u32[]{:S(2)}, u32[]{:S(2)}) collective-permute-start(bf16[32,3584]{1,0:T(8,128)(2,1)S(1)} %shard_map.68.refs_2_.refs_0_), channel_id=1, source_target_pairs={{0,16},{1,9},{2,18},{3,11},{4,20},{5,13},{6,22},{7,15},{8,24},{9,1... | collective-permute-start | bytes 688136 | tf_op jit(solution)/shard_map/ppermute | solution.py:43
  20.0 5.4 %shard_map.69 = (bf16[7168,256]{1,0:T(8,128)(2,1)S(1)}, bf16[7168,768]{1,0:T(8,128)(2,1)S(1)}, f32[8,128]{1,0:T(8,128)S(1)}) custom-call(bf16[1,7168,2048]{2,1,0:T(8,128)(2,1)} %refs_12_.1, bf16[1,7168,2048]{2,1,0:T(8,128)(2,1)} %refs_13_.1, bf16[32,3584]{1,0:T(8,128)(2,1)S(1)} %shard_map.68.refs_2_.refs_0_), custom_call_target="tpu_custom_call" | custom-call | bytes 14680064 | tf_op jit(solution)/shard_map/pallas_call | solution.py:107
  25.5 0.1 collective-permute-start.9
  25.6 0.5 collective-permute-start.10
  26.1 0.1 collective-permute-start.5
  26.2 0.4 collective-permute-start.6
  26.6 1.1 %collective-permute-done.5.refs_2_ = bf16[32,3584]{1,0:T(8,128)(2,1)S(1)} collective-permute-done((bf16[32,3584]{1,0:T(8,128)(2,1)S(1)}, bf16[32,3584]{1,0:T(8,128)(2,1)S(1)}, u32[]{:S(2)}, u32[]{:S(2)}) %collective-permute-start.5) | collective-permute-done | bytes 229408 | tf_op jit(solution)/shard_map/ppermute | solution.py:35
  27.7 0.3 collective-permute-done.6.refs_3_
  28.0 0.0 collective-permute-done.10.refs_7_
  28.0 23.3 %shard_map.73 = (bf16[64,3584]{1,0:T(8,128)(2,1)S(1)}, bf16[64,3584]{1,0:T(8,128)(2,1)S(1)}, bf16[64,3584]{1,0:T(8,128)(2,1)S(1)}, bf16[64,3584]{1,0:T(8,128)(2,1)S(1)}) custom-call(bf16[32,3584]{1,0:T(8,128)(2,1)S(1)} %shard_map.68.refs_2_.refs_0_, bf16[32,3584]{1,0:T(8,128)(2,1)S(1)} %shard_map.70.refs_1_, ...), custom_call_target="tpu_custom_call" | custom-call | flops 11274289152 | bytes 58720256 | tf_op jit(solution)/shard_map/pallas_call | solution.py:264
  51.3 0.2 collective-permute-start.11
  51.6 0.3 collective-permute-start.17
  51.9 1.3 %collective-permute-done.11.refs_1_ = bf16[64,3584]{1,0:T(8,128)(2,1)S(1)} collective-permute-done((bf16[64,3584]{1,0:T(8,128)(2,1)S(1)}, bf16[64,3584]{1,0:T(8,128)(2,1)S(1)}, u32[]{:S(2)}, u32[]{:S(2)}) %collective-permute-start.11) | collective-permute-done | bytes 458784 | tf_op jit(solution)/shard_map/ppermute | solution.py:35
  53.2 0.1 shard_map.74
  53.3 0.7 collective-permute-start.12
  54.0 0.1 shard_map.77
  54.1 1.5 %collective-permute-start.18 = (bf16[32,3584]{1,0:T(8,128)(2,1)S(1)}, bf16[32,3584]{1,0:T(8,128)(2,1)S(1)}, u32[]{:S(2)}, u32[]{:S(2)}) collective-permute-start(bf16[32,3584]{1,0:T(8,128)(2,1)S(1)} %get-tuple-element.56), channel_id=1, source_target_pairs={{0,16},{1,9},{2,18},{3,11},{4,20},{5,13},{6,22},{7,15},{8,24},{9,1... | collective-permute-start | bytes 688136 | tf_op jit(solution)/shard_map/ppermute | solution.py:43
  55.6 3.8 %collective-permute-done.12.refs_1_ = bf16[32,3584]{1,0:T(8,128)(2,1)S(1)} collective-permute-done((bf16[32,3584]{1,0:T(8,128)(2,1)S(1)}, bf16[32,3584]{1,0:T(8,128)(2,1)S(1)}, u32[]{:S(2)}, u32[]{:S(2)}) %collective-permute-start.12) | collective-permute-done | bytes 229408 | tf_op jit(solution)/shard_map/ppermute | solution.py:43
  59.4 0.1 shard_map.75
  59.5 1.0 %collective-permute-start.13 = (bf16[16,3584]{1,0:T(8,128)(2,1)S(1)}, bf16[16,3584]{1,0:T(8,128)(2,1)S(1)}, u32[]{:S(2)}, u32[]{:S(2)}) collective-permute-start(bf16[16,3584]{1,0:T(8,128)(2,1)S(1)} %get-tuple-element.48), channel_id=1, source_target_pairs={{0,8},{1,17},{2,10},{3,19},{4,12},{5,21},{6,14},{7,23},{8,0},{9,25... | collective-permute-start | bytes 344072 | tf_op jit(solution)/shard_map/ppermute | solution.py:43
  60.4 1.8 %collective-permute-done.18.refs_1_ = bf16[32,3584]{1,0:T(8,128)(2,1)S(1)} collective-permute-done((bf16[32,3584]{1,0:T(8,128)(2,1)S(1)}, bf16[32,3584]{1,0:T(8,128)(2,1)S(1)}, u32[]{:S(2)}, u32[]{:S(2)}) %collective-permute-start.18) | collective-permute-done | bytes 229408 | tf_op jit(solution)/shard_map/ppermute | solution.py:43
  62.2 0.1 shard_map.78
  62.3 1.0 %collective-permute-start.19 = (bf16[16,3584]{1,0:T(8,128)(2,1)S(1)}, bf16[16,3584]{1,0:T(8,128)(2,1)S(1)}, u32[]{:S(2)}, u32[]{:S(2)}) collective-permute-start(bf16[16,3584]{1,0:T(8,128)(2,1)S(1)} %get-tuple-element.58), channel_id=1, source_target_pairs={{0,8},{1,17},{2,10},{3,19},{4,12},{5,21},{6,14},{7,23},{8,0},{9,25... | collective-permute-start | bytes 344072 | tf_op jit(solution)/shard_map/ppermute | solution.py:43
  63.3 1.1 %collective-permute-done.13.refs_1_ = bf16[16,3584]{1,0:T(8,128)(2,1)S(1)} collective-permute-done((bf16[16,3584]{1,0:T(8,128)(2,1)S(1)}, bf16[16,3584]{1,0:T(8,128)(2,1)S(1)}, u32[]{:S(2)}, u32[]{:S(2)}) %collective-permute-start.13) | collective-permute-done | bytes 114720 | tf_op jit(solution)/shard_map/ppermute | solution.py:43
  64.4 1.5 %collective-permute-start.14 = (bf16[4,3584]{1,0:T(4,128)(2,1)S(1)}, bf16[4,3584]{1,0:T(4,128)(2,1)S(1)}, u32[]{:S(2)}, u32[]{:S(2)}) collective-permute-start(bf16[4,3584]{1,0:T(4,128)(2,1)S(1)} %get-tuple-element.50), channel_id=1, source_target_pairs={{0,2},{1,3},{2,0},{3,1},{4,6},{5,7},{6,4},{7,5},{8,10},{9,11},{10,... | collective-permute-start | bytes 86024 | tf_op jit(solution)/shard_map/ppermute | solution.py:35
  65.9 2.0 %collective-permute-start.15 = (bf16[4,3584]{1,0:T(4,128)(2,1)S(1)}, bf16[4,3584]{1,0:T(4,128)(2,1)S(1)}, u32[]{:S(2)}, u32[]{:S(2)}) collective-permute-start(bf16[4,3584]{1,0:T(4,128)(2,1)S(1)} %get-tuple-element.51), channel_id=1, source_target_pairs={{0,4},{1,5},{2,6},{3,7},{4,0},{5,1},{6,2},{7,3},{8,12},{9,13},{10,... | collective-permute-start | bytes 86024 | tf_op jit(solution)/shard_map/ppermute | solution.py:35
  67.8 1.0 %collective-permute-start.16 = (bf16[4,3584]{1,0:T(4,128)(2,1)S(1)}, bf16[4,3584]{1,0:T(4,128)(2,1)S(1)}, u32[]{:S(2)}, u32[]{:S(2)}) collective-permute-start(bf16[4,3584]{1,0:T(4,128)(2,1)S(1)} %get-tuple-element.52), channel_id=1, source_target_pairs={{0,6},{1,7},{2,4},{3,5},{4,2},{5,3},{6,0},{7,1},{8,14},{9,15},{10,... | collective-permute-start | bytes 86024 | tf_op jit(solution)/shard_map/ppermute | solution.py:35
  68.9 0.6 collective-permute-start.20
  69.5 2.9 %collective-permute-start.21 = (bf16[4,3584]{1,0:T(4,128)(2,1)S(1)}, bf16[4,3584]{1,0:T(4,128)(2,1)S(1)}, u32[]{:S(2)}, u32[]{:S(2)}) collective-permute-start(bf16[4,3584]{1,0:T(4,128)(2,1)S(1)} %get-tuple-element.61), channel_id=1, source_target_pairs={{0,4},{1,5},{2,6},{3,7},{4,0},{5,1},{6,2},{7,3},{8,12},{9,13},{10,... | collective-permute-start | bytes 86024 | tf_op jit(solution)/shard_map/ppermute | solution.py:35
  72.4 1.0 %collective-permute-start.22 = (bf16[4,3584]{1,0:T(4,128)(2,1)S(1)}, bf16[4,3584]{1,0:T(4,128)(2,1)S(1)}, u32[]{:S(2)}, u32[]{:S(2)}) collective-permute-start(bf16[4,3584]{1,0:T(4,128)(2,1)S(1)} %get-tuple-element.62), channel_id=1, source_target_pairs={{0,6},{1,7},{2,4},{3,5},{4,2},{5,3},{6,0},{7,1},{8,14},{9,15},{10,... | collective-permute-start | bytes 86024 | tf_op jit(solution)/shard_map/ppermute | solution.py:35
  73.3 0.2 collective-permute-done.16
  73.6 1.0 %collective-permute-done.21 = bf16[4,3584]{1,0:T(4,128)(2,1)S(1)} collective-permute-done((bf16[4,3584]{1,0:T(4,128)(2,1)S(1)}, bf16[4,3584]{1,0:T(4,128)(2,1)S(1)}, u32[]{:S(2)}, u32[]{:S(2)}) %collective-permute-start.21) | collective-permute-done | bytes 28704 | tf_op jit(solution)/shard_map/ppermute | solution.py:35
  74.6 3.5 %collective-permute-done.22 = bf16[4,3584]{1,0:T(4,128)(2,1)S(1)} collective-permute-done((bf16[4,3584]{1,0:T(4,128)(2,1)S(1)}, bf16[4,3584]{1,0:T(4,128)(2,1)S(1)}, u32[]{:S(2)}, u32[]{:S(2)}) %collective-permute-start.22) | collective-permute-done | bytes 28704 | tf_op jit(solution)/shard_map/ppermute | solution.py:35
  78.1 0.7 pad_maximum_fusion
  (17 shorter events, 0.2 us)
Async XLA Ops:
  0.9 9.0 %collective-permute-start.2 = (bf16[4,7296]{1,0:T(4,128)(2,1)S(1)}, bf16[4,7296]{1,0:T(4,128)(2,1)S(1)}, u32[]{:S(2)}, u32[]{:S(2)}) collective-permute-start(bf16[4,7296]{1,0:T(4,128)(2,1)S(1)} %shard_map.64.refs_1_.refs_0_), channel_id=1, source_target_pairs={{0,6},{1,7},{2,4},{3,5},{4,2},{5,3},{6,0},{7,1},{8,14},{9,15},{10,... | collective-permute-start | bytes 175112 | tf_op jit(solution)/shard_map/ppermute | solution.py:35
  6.0 5.1 %collective-permute-start.1 = (bf16[4,7296]{1,0:T(4,128)(2,1)S(1)}, bf16[4,7296]{1,0:T(4,128)(2,1)S(1)}, u32[]{:S(2)}, u32[]{:S(2)}) collective-permute-start(bf16[4,7296]{1,0:T(4,128)(2,1)S(1)} %shard_map.64.refs_1_.refs_0_), channel_id=1, source_target_pairs={{0,4},{1,5},{2,6},{3,7},{4,0},{5,1},{6,2},{7,3},{8,12},{9,13},{10,... | collective-permute-start | bytes 175112 | tf_op jit(solution)/shard_map/ppermute | solution.py:35
  6.1 5.1 %collective-permute-start = (bf16[4,7296]{1,0:T(4,128)(2,1)S(1)}, bf16[4,7296]{1,0:T(4,128)(2,1)S(1)}, u32[]{:S(2)}, u32[]{:S(2)}) collective-permute-start(bf16[4,7296]{1,0:T(4,128)(2,1)S(1)} %shard_map.64.refs_1_.refs_0_), channel_id=1, source_target_pairs={{0,2},{1,3},{2,0},{3,1},{4,6},{5,7},{6,4},{7,5},{8,10},{9,11},{10,... | collective-permute-start | bytes 175112 | tf_op jit(solution)/shard_map/ppermute | solution.py:35
  11.2 4.9 %collective-permute-start.7 = (bf16[16,3712]{1,0:T(8,128)(2,1)S(1)}, bf16[16,3712]{1,0:T(8,128)(2,1)S(1)}, u32[]{:S(2)}, u32[]{:S(2)}) collective-permute-start(bf16[16,3712]{1,0:T(8,128)(2,1)S(1)} %get-tuple-element.38.refs_0_), channel_id=1, source_target_pairs={{0,8},{1,17},{2,10},{3,19},{4,12},{5,21},{6,14},{7,23},{8,0},{9,25... | collective-permute-start | bytes 356360 | tf_op jit(solution)/shard_map/ppermute | solution.py:43
  12.8 5.7 %collective-permute-start.3 = (bf16[16,3584]{1,0:T(8,128)(2,1)S(1)}, bf16[16,3584]{1,0:T(8,128)(2,1)S(1)}, u32[]{:S(2)}, u32[]{:S(2)}) collective-permute-start(bf16[16,3584]{1,0:T(8,128)(2,1)S(1)} %get-tuple-element.35.refs_1_.refs_0_), channel_id=1, source_target_pairs={{0,8},{1,17},{2,10},{3,19},{4,12},{5,21},{6,14},{7,23},{8,0},{9,25... | collective-permute-start | bytes 344072 | tf_op jit(solution)/shard_map/ppermute | solution.py:43
  16.1 9.4 %collective-permute-start.8 = (bf16[32,3712]{1,0:T(8,128)(2,1)S(1)}, bf16[32,3712]{1,0:T(8,128)(2,1)S(1)}, u32[]{:S(2)}, u32[]{:S(2)}) collective-permute-start(bf16[32,3712]{1,0:T(8,128)(2,1)S(1)} %shard_map.71.refs_4_), channel_id=1, source_target_pairs={{0,16},{1,9},{2,18},{3,11},{4,20},{5,13},{6,22},{7,15},{8,24},{9,1... | collective-permute-start | bytes 712712 | tf_op jit(solution)/shard_map/ppermute | solution.py:43
  18.6 7.6 %collective-permute-start.4 = (bf16[32,3584]{1,0:T(8,128)(2,1)S(1)}, bf16[32,3584]{1,0:T(8,128)(2,1)S(1)}, u32[]{:S(2)}, u32[]{:S(2)}) collective-permute-start(bf16[32,3584]{1,0:T(8,128)(2,1)S(1)} %shard_map.68.refs_2_.refs_0_), channel_id=1, source_target_pairs={{0,16},{1,9},{2,18},{3,11},{4,20},{5,13},{6,22},{7,15},{8,24},{9,1... | collective-permute-start | bytes 688136 | tf_op jit(solution)/shard_map/ppermute | solution.py:43
  25.5 2.2 %collective-permute-start.9 = (bf16[32,3712]{1,0:T(8,128)(2,1)S(1)}, bf16[32,3712]{1,0:T(8,128)(2,1)S(1)}, u32[]{:S(2)}, u32[]{:S(2)}) collective-permute-start(bf16[32,3712]{1,0:T(8,128)(2,1)S(1)} %shard_map.71.refs_4_), channel_id=1, source_target_pairs={{0,1},{1,0},{2,3},{3,2},{4,5},{5,4},{6,7},{7,6},{8,9},{9,8},{10,11... | collective-permute-start | bytes 712712 | tf_op jit(solution)/shard_map/ppermute | solution.py:35
  25.6 2.5 %collective-permute-start.10 = (bf16[32,3712]{1,0:T(8,128)(2,1)S(1)}, bf16[32,3712]{1,0:T(8,128)(2,1)S(1)}, u32[]{:S(2)}, u32[]{:S(2)}) collective-permute-start(bf16[32,3712]{1,0:T(8,128)(2,1)S(1)} %shard_map.72.refs_5_), channel_id=1, source_target_pairs={{0,1},{1,0},{2,3},{3,2},{4,5},{5,4},{6,7},{7,6},{8,9},{9,8},{10,11... | collective-permute-start | bytes 712712 | tf_op jit(solution)/shard_map/ppermute | solution.py:35
  26.1 1.7 %collective-permute-start.5 = (bf16[32,3584]{1,0:T(8,128)(2,1)S(1)}, bf16[32,3584]{1,0:T(8,128)(2,1)S(1)}, u32[]{:S(2)}, u32[]{:S(2)}) collective-permute-start(bf16[32,3584]{1,0:T(8,128)(2,1)S(1)} %shard_map.68.refs_2_.refs_0_), channel_id=1, source_target_pairs={{0,1},{1,0},{2,3},{3,2},{4,5},{5,4},{6,7},{7,6},{8,9},{9,8},{10,11... | collective-permute-start | bytes 688136 | tf_op jit(solution)/shard_map/ppermute | solution.py:35
  26.2 1.9 %collective-permute-start.6 = (bf16[32,3584]{1,0:T(8,128)(2,1)S(1)}, bf16[32,3584]{1,0:T(8,128)(2,1)S(1)}, u32[]{:S(2)}, u32[]{:S(2)}) collective-permute-start(bf16[32,3584]{1,0:T(8,128)(2,1)S(1)} %shard_map.70.refs_1_), channel_id=1, source_target_pairs={{0,1},{1,0},{2,3},{3,2},{4,5},{5,4},{6,7},{7,6},{8,9},{9,8},{10,11... | collective-permute-start | bytes 688136 | tf_op jit(solution)/shard_map/ppermute | solution.py:35
  51.3 1.9 %collective-permute-start.11 = (bf16[64,3584]{1,0:T(8,128)(2,1)S(1)}, bf16[64,3584]{1,0:T(8,128)(2,1)S(1)}, u32[]{:S(2)}, u32[]{:S(2)}) collective-permute-start(bf16[64,3584]{1,0:T(8,128)(2,1)S(1)} %get-tuple-element.44), channel_id=1, source_target_pairs={{0,1},{1,0},{2,3},{3,2},{4,5},{5,4},{6,7},{7,6},{8,9},{9,8},{10,11... | collective-permute-start | bytes 1376264 | tf_op jit(solution)/shard_map/ppermute | solution.py:35
  51.6 2.4 %collective-permute-start.17 = (bf16[64,3584]{1,0:T(8,128)(2,1)S(1)}, bf16[64,3584]{1,0:T(8,128)(2,1)S(1)}, u32[]{:S(2)}, u32[]{:S(2)}) collective-permute-start(bf16[64,3584]{1,0:T(8,128)(2,1)S(1)} %get-tuple-element.54), channel_id=1, source_target_pairs={{0,1},{1,0},{2,3},{3,2},{4,5},{5,4},{6,7},{7,6},{8,9},{9,8},{10,11... | collective-permute-start | bytes 1376264 | tf_op jit(solution)/shard_map/ppermute | solution.py:35
  53.3 6.1 %collective-permute-start.12 = (bf16[32,3584]{1,0:T(8,128)(2,1)S(1)}, bf16[32,3584]{1,0:T(8,128)(2,1)S(1)}, u32[]{:S(2)}, u32[]{:S(2)}) collective-permute-start(bf16[32,3584]{1,0:T(8,128)(2,1)S(1)} %get-tuple-element.46), channel_id=1, source_target_pairs={{0,16},{1,9},{2,18},{3,11},{4,20},{5,13},{6,22},{7,15},{8,24},{9,1... | collective-permute-start | bytes 688136 | tf_op jit(solution)/shard_map/ppermute | solution.py:43
  54.1 8.1 %collective-permute-start.18 = (bf16[32,3584]{1,0:T(8,128)(2,1)S(1)}, bf16[32,3584]{1,0:T(8,128)(2,1)S(1)}, u32[]{:S(2)}, u32[]{:S(2)}) collective-permute-start(bf16[32,3584]{1,0:T(8,128)(2,1)S(1)} %get-tuple-element.56), channel_id=1, source_target_pairs={{0,16},{1,9},{2,18},{3,11},{4,20},{5,13},{6,22},{7,15},{8,24},{9,1... | collective-permute-start | bytes 688136 | tf_op jit(solution)/shard_map/ppermute | solution.py:43
  59.5 4.9 %collective-permute-start.13 = (bf16[16,3584]{1,0:T(8,128)(2,1)S(1)}, bf16[16,3584]{1,0:T(8,128)(2,1)S(1)}, u32[]{:S(2)}, u32[]{:S(2)}) collective-permute-start(bf16[16,3584]{1,0:T(8,128)(2,1)S(1)} %get-tuple-element.48), channel_id=1, source_target_pairs={{0,8},{1,17},{2,10},{3,19},{4,12},{5,21},{6,14},{7,23},{8,0},{9,25... | collective-permute-start | bytes 344072 | tf_op jit(solution)/shard_map/ppermute | solution.py:43
  62.3 6.5 %collective-permute-start.19 = (bf16[16,3584]{1,0:T(8,128)(2,1)S(1)}, bf16[16,3584]{1,0:T(8,128)(2,1)S(1)}, u32[]{:S(2)}, u32[]{:S(2)}) collective-permute-start(bf16[16,3584]{1,0:T(8,128)(2,1)S(1)} %get-tuple-element.58), channel_id=1, source_target_pairs={{0,8},{1,17},{2,10},{3,19},{4,12},{5,21},{6,14},{7,23},{8,0},{9,25... | collective-permute-start | bytes 344072 | tf_op jit(solution)/shard_map/ppermute | solution.py:43
  64.4 8.0 %collective-permute-start.14 = (bf16[4,3584]{1,0:T(4,128)(2,1)S(1)}, bf16[4,3584]{1,0:T(4,128)(2,1)S(1)}, u32[]{:S(2)}, u32[]{:S(2)}) collective-permute-start(bf16[4,3584]{1,0:T(4,128)(2,1)S(1)} %get-tuple-element.50), channel_id=1, source_target_pairs={{0,2},{1,3},{2,0},{3,1},{4,6},{5,7},{6,4},{7,5},{8,10},{9,11},{10,... | collective-permute-start | bytes 86024 | tf_op jit(solution)/shard_map/ppermute | solution.py:35
  65.9 7.4 %collective-permute-start.15 = (bf16[4,3584]{1,0:T(4,128)(2,1)S(1)}, bf16[4,3584]{1,0:T(4,128)(2,1)S(1)}, u32[]{:S(2)}, u32[]{:S(2)}) collective-permute-start(bf16[4,3584]{1,0:T(4,128)(2,1)S(1)} %get-tuple-element.51), channel_id=1, source_target_pairs={{0,4},{1,5},{2,6},{3,7},{4,0},{5,1},{6,2},{7,3},{8,12},{9,13},{10,... | collective-permute-start | bytes 86024 | tf_op jit(solution)/shard_map/ppermute | solution.py:35
  67.8 5.7 %collective-permute-start.16 = (bf16[4,3584]{1,0:T(4,128)(2,1)S(1)}, bf16[4,3584]{1,0:T(4,128)(2,1)S(1)}, u32[]{:S(2)}, u32[]{:S(2)}) collective-permute-start(bf16[4,3584]{1,0:T(4,128)(2,1)S(1)} %get-tuple-element.52), channel_id=1, source_target_pairs={{0,6},{1,7},{2,4},{3,5},{4,2},{5,3},{6,0},{7,1},{8,14},{9,15},{10,... | collective-permute-start | bytes 86024 | tf_op jit(solution)/shard_map/ppermute | solution.py:35
  68.9 4.7 %collective-permute-start.20 = (bf16[4,3584]{1,0:T(4,128)(2,1)S(1)}, bf16[4,3584]{1,0:T(4,128)(2,1)S(1)}, u32[]{:S(2)}, u32[]{:S(2)}) collective-permute-start(bf16[4,3584]{1,0:T(4,128)(2,1)S(1)} %get-tuple-element.60), channel_id=1, source_target_pairs={{0,2},{1,3},{2,0},{3,1},{4,6},{5,7},{6,4},{7,5},{8,10},{9,11},{10,... | collective-permute-start | bytes 86024 | tf_op jit(solution)/shard_map/ppermute | solution.py:35
  69.5 5.1 %collective-permute-start.21 = (bf16[4,3584]{1,0:T(4,128)(2,1)S(1)}, bf16[4,3584]{1,0:T(4,128)(2,1)S(1)}, u32[]{:S(2)}, u32[]{:S(2)}) collective-permute-start(bf16[4,3584]{1,0:T(4,128)(2,1)S(1)} %get-tuple-element.61), channel_id=1, source_target_pairs={{0,4},{1,5},{2,6},{3,7},{4,0},{5,1},{6,2},{7,3},{8,12},{9,13},{10,... | collective-permute-start | bytes 86024 | tf_op jit(solution)/shard_map/ppermute | solution.py:35
  72.4 5.7 %collective-permute-start.22 = (bf16[4,3584]{1,0:T(4,128)(2,1)S(1)}, bf16[4,3584]{1,0:T(4,128)(2,1)S(1)}, u32[]{:S(2)}, u32[]{:S(2)}) collective-permute-start(bf16[4,3584]{1,0:T(4,128)(2,1)S(1)} %get-tuple-element.62), channel_id=1, source_target_pairs={{0,6},{1,7},{2,4},{3,5},{4,2},{5,3},{6,0},{7,1},{8,14},{9,15},{10,... | collective-permute-start | bytes 86024 | tf_op jit(solution)/shard_map/ppermute | solution.py:35

commit v9 on v6

--- a/solution.py
+++ b/solution.py
@@ -11,11 +11,12 @@
 LANES = 128
 AXES = ("group", "expert")
 VMEM = pltpu.VMEM
-FIRST_BLOCK = 512
 UNIT_BLOCK = 256
 DOWN_BLOCK = 512
-EARLY = 2
-RING = 6
+FIRST_BLOCK = 512
+EARLY = 5
+EARLY_DOWN = 3
+RING = 4
 DOWN_RING = 4
 FOLD_BLOCK = 1024
 DEPTH_CUT = 1024
@@ -102,6 +103,8 @@
 
 
 def fetch(jobs, rows, after):
+    if not jobs:
+        return [], None
     hbm = pl.BlockSpec(memory_space=pltpu.HBM)
     *out, mark = pl.pallas_call(
         functools.partial(fetch_kernel, jobs),
@@ -116,22 +119,23 @@
     return out, mark
 
 
-def join_kernel(start, *refs):
-    *in_refs, after_ref, out_ref = refs
-    columns = slice(start, start + out_ref.shape[1])
-    pieces = [r[:, columns].astype(jnp.float32) for r in in_refs]
-    out_ref[...] = jnp.concatenate(pieces, axis=0).astype(out_ref.dtype)
-
-
-def join(values, after, start=0, width=None):
+def join_kernel(cuts, *refs):
+    in_refs, out_refs = refs[: -len(cuts) - 1], refs[-len(cuts) :]
+    for (start, size), out_ref in zip(cuts, out_refs):
+        pieces = [r[:, start : start + size].astype(jnp.float32) for r in in_refs]
+        out_ref[...] = jnp.concatenate(pieces, axis=0).astype(out_ref.dtype)
+
+
+def join(values, after, cuts=None):
     rows = sum(v.shape[0] for v in values)
-    width = width or values[0].shape[1]
+    width = values[0].shape[1]
+    cuts = cuts or [(0, width)]
     after = values[0] if after is None else after
     return pl.pallas_call(
-        functools.partial(join_kernel, start),
+        functools.partial(join_kernel, cuts),
         in_specs=whole_vmem(len(values)) + [pl.BlockSpec(memory_space=pl.ANY)],
-        out_specs=whole_vmem(1)[0],
-        out_shape=VMEM((rows, width), values[0].dtype),
+        out_specs=whole_vmem(len(cuts)),
+        out_shape=[VMEM((rows, size), values[0].dtype) for _, size in cuts],
         compiler_params=limit(1024 * 1024 + 8 * rows * width),
     )(*[in_vmem(v) for v in values], after)
 
@@ -140,15 +144,17 @@
     pass
 
 
-def hold(value, after):
+def hold(values, after):
+    if after is None:
+        return values
     return pl.pallas_call(
         hold_kernel,
-        in_specs=[pl.BlockSpec(memory_space=pl.ANY)] * 2,
-        out_specs=pl.BlockSpec(memory_space=pl.ANY),
-        out_shape=jax.ShapeDtypeStruct(value.shape, value.dtype),
-        input_output_aliases={0: 0},
+        in_specs=[pl.BlockSpec(memory_space=pl.ANY)] * (len(values) + 1),
+        out_specs=[pl.BlockSpec(memory_space=pl.ANY)] * len(values),
+        out_shape=[jax.ShapeDtypeStruct(v.shape, v.dtype) for v in values],
+        input_output_aliases={i: i for i in range(len(values))},
         compiler_params=limit(256 * 1024),
-    )(value, after)
+    )(*values, after)
 
 
 def times(left_ref, right_ref):
@@ -164,11 +170,12 @@
 def first_kernel(held, streams, early, *refs):
     x_refs, refs = refs[:4], refs[4:]
     held_refs, refs = refs[:held], refs[held:]
-    hbm, after_ref, gate_ref, up_ref = refs[:2], *refs[2:5]
-    early_refs, refs = refs[5 : 5 + len(early)], refs[5 + len(early) :]
+    hbm, refs = refs[:2], refs[3:]
+    gate_ref, up_ref, refs = refs[0], refs[1], refs[2:]
+    early_refs, refs = refs[: len(early)], refs[len(early) :]
     x, slots, stream_sem, early_sem = refs
     depth = x.shape[1]
-    block = held_refs[0].shape[1]
+    block = slots.shape[2]
     count = gate_ref.shape[1] // block
 
     copies = [
@@ -187,6 +194,8 @@
     ]
     for copy in copies:
         copy.start()
+    for copy in later[: len(later) // 2]:
+        copy.start()
     part = x_refs[0].shape[0]
     for n, x_ref in enumerate(x_refs):
         x[n * part : (n + 1) * part, :] = x_ref[...]
@@ -197,10 +206,11 @@
             copies[n - held].wait()
             weight = slots.at[n - held]
         out_ref = gate_ref if n < count else up_ref
-        at = n % count * block
-        out_ref[:, at : at + block] = times(x, weight)
-        if n == min(1, 2 * count - 1):
-            for copy in later:
+        for at in range(0, block, UNIT_BLOCK):
+            first = n % count * block + at
+            out_ref[:, first : first + UNIT_BLOCK] = times(x, weight.at[:, at : at + UNIT_BLOCK])
+        if n == min(2, 2 * count - 1):
+            for copy in later[len(later) // 2 :]:
                 copy.start()
     for copy in later:
         copy.wait()
@@ -212,7 +222,7 @@
     units = w_gate.shape[2]
     block = held[0].shape[1]
     count = units // block
-    order = [(0, b) for b in range(count)] + [(1, b) for b in range(count)]
+    order = [(m, b) for m in range(2) for b in range(count)]
     streams = order[len(held) :]
     early = [(m, b) for b in range(min(EARLY, units // UNIT_BLOCK)) for m in range(2)]
     hbm = pl.BlockSpec(memory_space=pltpu.HBM)
@@ -231,20 +241,45 @@
             pltpu.SemaphoreType.DMA((slots,)),
             pltpu.SemaphoreType.DMA((len(early),)),
         ],
-        compiler_params=limit(scratch + 4 * 1024 * 1024 + 16 * rows * block),
+        compiler_params=limit(scratch + 2 * 1024 * 1024 + 16 * rows * UNIT_BLOCK),
         cost_estimate=cost(4 * rows * depth * units, 2 * depth * units),
     )(*args, in_hbm(w_gate), in_hbm(w_up), after)
+
+
+def down_copier(down_hbm, ring, sems):
+    def copy(d):
+        return pltpu.make_async_copy(
+            down_hbm.at[0, :, pl.ds(d * DOWN_BLOCK, DOWN_BLOCK)],
+            ring.at[d % DOWN_RING],
+            sems.at[d % DOWN_RING],
+        )
+
+    return copy
+
+
+def down_blocks(hidden, scale_ref, weight_of, first, stop, own_ref, far_ref, after):
+    half = own_ref.shape[0]
+    for start in range(first, stop, 2):
+        pair = range(start, min(start + 2, stop))
+        weights = [weight_of(d) for d in pair]
+        for d, weight in zip(pair, weights):
+            value = (times(hidden, weight) * scale_ref[:, :1]).astype(jnp.bfloat16)
+            at = (d - first) * DOWN_BLOCK
+            own_ref[:, at : at + DOWN_BLOCK] = value[:half]
+            far_ref[:, at : at + DOWN_BLOCK] = value[half:]
+        for d in pair:
+            after(d)
 
 
 def second_kernel(start, early, streams, *refs):
     x_refs, refs = refs[:4], refs[4:]
     gate_ref, up_ref, refs = refs[0], refs[1], refs[2:]
     early_refs, refs = refs[: len(early)], refs[len(early) :]
-    hbm, down_hbm, me_ref, own_ref, far_ref = refs[:2], *refs[2:6]
-    x, hidden, scale_ref, ring, down_ring, sems, down_sem = refs[6:]
-    depth, units = x.shape[1], hidden.shape[1]
-    blocks = units // UNIT_BLOCK
-    downs = down_hbm.shape[2] // DOWN_BLOCK
+    hbm, down_hbm, me_ref, refs = refs[:2], refs[2], refs[3], refs[4:]
+    own_ref, far_ref, hidden, scale_ref, next_ref = refs[:5]
+    x, ring, down_ring, sems, down_sem, next_sem = refs[5:]
+    depth, units, width = x.shape[1], hidden.shape[1], own_ref.shape[1]
+    blocks, downs = units // UNIT_BLOCK, width // DOWN_BLOCK
 
     def copy(n):
         m, b = streams[n]
@@ -254,95 +289,135 @@
             sems.at[n % RING],
         )
 
-    def down_copy(d, slot):
-        first = d * DOWN_BLOCK
-        if not isinstance(d, int):
-            first = pl.multiple_of(first, DOWN_BLOCK)
-        return pltpu.make_async_copy(
-            down_hbm.at[0, :, pl.ds(first, DOWN_BLOCK)], down_ring.at[slot], down_sem.at[slot]
-        )
-
+    down_copy = down_copier(down_hbm, down_ring, down_sem)
+    next_copy = pltpu.make_async_copy(
+        down_hbm.at[0, :, pl.ds(width, next_ref.shape[1])], next_ref, next_sem
+    )
     for n in range(min(RING, len(streams))):
         copy(n).start()
     later = {}
     for n in range(min(DOWN_RING, downs)):
-        later.setdefault(min(blocks - 1, 3 + n), []).append(down_copy(n, n))
+        later.setdefault(min(blocks - 1, 1 + n), []).append(down_copy(n))
 
     part = x_refs[0].shape[0]
     for n, x_ref in enumerate(x_refs):
-        x[n * part : (n + 1) * part, :] = x_ref[:, :depth]
+        rows = slice(n * part, (n + 1) * part)
+        x[rows, :] = x_ref[:, :depth]
         route = x_ref[:, depth:].astype(jnp.float32)
         lane = lax.broadcasted_iota(jnp.int32, route.shape, 1)
         scale = jnp.sum(jnp.where(lane == me_ref[0], route, 0.0), axis=1, keepdims=True)
-        scale_ref[n * part : (n + 1) * part, :] = jnp.broadcast_to(scale, route.shape)
-
-    def product(m, b):
-        if (m, b) in early:
-            return times(x, early_refs[early.index((m, b))])
-        n = streams.index((m, b))
-        copy(n).wait()
-        value = times(x, ring.at[n % RING])
-        if n + RING < len(streams):
-            copy(n + RING).start()
-        return value
+        scale_ref[rows, :] = jnp.broadcast_to(scale, route.shape)
 
     for b in range(blocks):
         columns = slice(b * UNIT_BLOCK, (b + 1) * UNIT_BLOCK)
-        gate = gate_ref[:, columns] + product(0, b)
-        up = up_ref[:, columns] + product(1, b)
+        weights, used = [], []
+        for m in range(2):
+            if (m, b) in early:
+                weights.append(early_refs[early.index((m, b))])
+            else:
+                n = streams.index((m, b))
+                copy(n).wait()
+                weights.append(ring.at[n % RING])
+                used.append(n)
+        gate = gate_ref[:, columns] + times(x, weights[0])
+        up = up_ref[:, columns] + times(x, weights[1])
+        for n in used:
+            if n + RING < len(streams):
+                copy(n + RING).start()
         for piece in later.get(b, []):
             piece.start()
         hidden[:, columns] = (jax.nn.silu(gate) * up).astype(jnp.bfloat16)
 
-    @pl.loop(0, downs)
-    def _(d):
-        slot = lax.rem(d, DOWN_RING)
-        columns = pl.ds(pl.multiple_of(d * DOWN_BLOCK, DOWN_BLOCK), DOWN_BLOCK)
-        down_copy(d, slot).wait()
-        value = (times(hidden, down_ring.at[slot]) * scale_ref[:, :1]).astype(jnp.bfloat16)
-
-        @pl.when(d + DOWN_RING < downs)
-        def _():
-            down_copy(d + DOWN_RING, slot).start()
-
-        own_ref[:, columns] = value[: 2 * part]
-        far_ref[:, columns] = value[2 * part :]
+    def weight_of(d):
+        down_copy(d).wait()
+        return down_ring.at[d % DOWN_RING]
+
+    def after(d):
+        if d + DOWN_RING < downs:
+            down_copy(d + DOWN_RING).start()
+        if d == max(0, downs - DOWN_RING - 1):
+            next_copy.start()
+
+    down_blocks(hidden, scale_ref, weight_of, 0, downs, own_ref, far_ref, after)
+    next_copy.wait()
 
 
 def run_second(parts, gate, up, early_values, w_gate, w_up, w_down, me):
     rows = sum(p.shape[0] for p in parts)
     units, width = w_down.shape[1], w_down.shape[2]
     depth = parts[0].shape[1] - LANES
-    blocks = units // UNIT_BLOCK
-    order = [(m, b) for b in range(blocks) for m in range(2)]
-    early = order[: len(early_values)]
-    streams = order[len(early_values) :]
-    half = VMEM((rows // 2, width), jnp.bfloat16)
+    order = [(m, b) for b in range(units // UNIT_BLOCK) for m in range(2)]
+    early, streams = order[: len(early_values)], order[len(early_values) :]
+    half = VMEM((rows // 2, width // 2), jnp.bfloat16)
     hbm = pl.BlockSpec(memory_space=pltpu.HBM)
     ring = max(1, min(RING, len(streams)))
     scratch = 2 * (
-        rows * (depth + units + 2 * LANES)
-        + ring * depth * UNIT_BLOCK
-        + DOWN_RING * units * DOWN_BLOCK
+        rows * depth + ring * depth * UNIT_BLOCK + DOWN_RING * units * DOWN_BLOCK
     )
     args = [in_vmem(v) for v in [*parts, gate, up, *early_values]]
     return pl.pallas_call(
         functools.partial(second_kernel, width - depth, early, streams),
         in_specs=whole_vmem(len(args)) + [hbm] * 3 + [pl.BlockSpec(memory_space=pltpu.SMEM)],
-        out_specs=whole_vmem(2),
-        out_shape=(half, half),
+        out_specs=whole_vmem(5),
+        out_shape=(
+            half,
+            half,
+            VMEM((rows, units), jnp.bfloat16),
+            VMEM((rows, LANES), jnp.float32),
+            VMEM((units, EARLY_DOWN * DOWN_BLOCK), w_down.dtype),
+        ),
         scratch_shapes=[
             VMEM((rows, depth), jnp.bfloat16),
-            VMEM((rows, units), jnp.bfloat16),
-            VMEM((rows, LANES), jnp.float32),
             VMEM((ring, depth, UNIT_BLOCK), jnp.bfloat16),
             VMEM((DOWN_RING, units, DOWN_BLOCK), jnp.bfloat16),
             pltpu.SemaphoreType.DMA((ring,)),
             pltpu.SemaphoreType.DMA((DOWN_RING,)),
+            pltpu.SemaphoreType.DMA,
         ],
-        compiler_params=limit(scratch + 4 * 1024 * 1024 + 16 * rows * DOWN_BLOCK),
-        cost_estimate=cost(2 * rows * units * (2 * depth + width), 2 * depth * units),
+        compiler_params=limit(scratch + 2 * 1024 * 1024 + 16 * rows * DOWN_BLOCK),
+        cost_estimate=cost(2 * rows * units * (2 * depth + width // 2), 2 * depth * units),
     )(*args, in_hbm(w_gate), in_hbm(w_up), in_hbm(w_down), me)
+
+
+def third_kernel(hidden, scale_ref, next_ref, down_hbm, after_ref, own_ref, far_ref, ring, sems):
+    downs = own_ref.shape[1] // DOWN_BLOCK
+    copy = down_copier(down_hbm, ring, sems)
+    resident = downs + EARLY_DOWN
+    for d in range(resident, min(resident + DOWN_RING, 2 * downs)):
+        copy(d).start()
+
+    def weight_of(d):
+        if d < resident:
+            at = (d - downs) * DOWN_BLOCK
+            return next_ref.at[:, at : at + DOWN_BLOCK]
+        copy(d).wait()
+        return ring.at[d % DOWN_RING]
+
+    def after(d):
+        if d >= resident and d + DOWN_RING < 2 * downs:
+            copy(d + DOWN_RING).start()
+
+    down_blocks(hidden, scale_ref, weight_of, downs, 2 * downs, own_ref, far_ref, after)
+
+
+def run_third(hidden, scale, early, w_down, after):
+    rows, units = hidden.shape
+    width = w_down.shape[2] // 2
+    half = VMEM((rows // 2, width), jnp.bfloat16)
+    scratch = 2 * DOWN_RING * units * DOWN_BLOCK
+    return pl.pallas_call(
+        third_kernel,
+        in_specs=whole_vmem(3)
+        + [pl.BlockSpec(memory_space=pltpu.HBM), pl.BlockSpec(memory_space=pl.ANY)],
+        out_specs=whole_vmem(2),
+        out_shape=(half, half),
+        scratch_shapes=[
+            VMEM((DOWN_RING, units, DOWN_BLOCK), jnp.bfloat16),
+            pltpu.SemaphoreType.DMA((DOWN_RING,)),
+        ],
+        compiler_params=limit(scratch + 2 * 1024 * 1024 + 16 * rows * DOWN_BLOCK),
+        cost_estimate=cost(2 * rows * width * units, 2 * width * units),
+    )(in_vmem(hidden), in_vmem(scale), in_vmem(early), in_hbm(w_down), after)
 
 
 def fold_kernel(count, *refs):
@@ -377,11 +452,13 @@
     return steps
 
 
-def give_back(own, far, groups, members):
-    values = [own, swap(far, "expert", members, 1)]
-    for masks in [(2, 1), (1, 2)]:
-        keep, send = fold(values, 2)
-        values = [keep, swap_group(send, groups, members, masks)]
+def chip_sum(own, far, members):
+    return fold([own, swap(far, "expert", members, 1)], 2)
+
+
+def give_back(keep, got, groups, members):
+    keep, send = fold([keep, got], 2)
+    values = [keep, swap_group(send, groups, members, (1, 2))]
     for masks in reversed(line_steps(members // 2)):
         keep, *sends = fold(values, len(masks) + 1)
         values = [keep] + [swap(v, "expert", members, m) for v, m in zip(sends, masks)]
@@ -397,36 +474,40 @@
     split = members // EXP_GRP
     me = lax.axis_index("group") * EXP_GRP + lax.axis_index("expert") // split
     me = me.astype(jnp.int32).reshape(1)
-    depth, units = w_gate.shape[1], w_gate.shape[2]
-    first = depth // DOWN_BLOCK * 3 // 8 * DOWN_BLOCK
+    width, units = w_gate.shape[1] // 2, w_gate.shape[2]
     block = min(FIRST_BLOCK, units)
     jobs = [(w, at, block) for w in (w_gate, w_up) for at in range(0, units, block)]
-    one = max(1, len(jobs) * 3 // 8)
-    two = one + max(1, len(jobs) // 4)
+    cuts = [max(1, len(jobs) * 3 // 8), len(jobs) * 5 // 8, len(jobs) * 7 // 8]
 
     value = pack(me, tokens, expert_ids, gate_weights)
-    held, mark = fetch(jobs[:one], first, value)
+    held, mark = fetch(jobs[: cuts[0]], width, value)
     for masks in line_steps(members // 2):
         line = [value] + [swap(value, "expert", members, m) for m in masks]
-        if masks[0] > 2:
-            value = join(line, mark)
-    a = join(line, mark, 0, first)
-    b = join(line, a, first, depth - first + LANES)
-
-    a_got = swap_group(a, groups, members, (1, 2))
-    b_got = swap_group(b, groups, members, (1, 2))
-    a = join([a, a_got], b)
-    b = join([b, b_got], a)
-    a_got = swap_group(a, groups, members, (2, 1))
-    b_got = swap_group(b, groups, members, (2, 1))
-    more, mark = fetch(jobs[one:two], first, a)
-    a_got = hold(a_got, mark)
-    parts = [a, a_got, swap(a, "expert", members, 1), swap(a_got, "expert", members, 1)]
-    gate, up, *early = run_first(parts, held + more, w_gate, w_up, b)
-    b_got = hold(b_got, gate)
-    parts = [b, b_got, swap(b, "expert", members, 1), swap(b_got, "expert", members, 1)]
-    own, far = run_second(parts, gate, up, early, w_gate, w_up, w_down, me)
-    return give_back(own, far, groups, members)
+        (value,) = join(line, mark)
+    got = swap_group(value, groups, members, (1, 2))
+    more, mark = fetch(jobs[cuts[0] : cuts[1]], width, value)
+    held += more
+    a, b = join([value, got], mark, [(0, width), (width, width + LANES)])
+    a_got, b_got = [swap_group(v, groups, members, (2, 1)) for v in (a, b)]
+    a_core, b_core = swap(a, "expert", members, 1), swap(b, "expert", members, 1)
+    more, mark = fetch(jobs[cuts[1] : cuts[2]], width, a)
+    held += more
+    (a_got,) = hold([a_got], mark)
+    parts = [a, a_got, a_core, swap(a_got, "expert", members, 1)]
+    gate, up, *early = run_first(parts, held, w_gate, w_up, b)
+    (b_got,) = hold([b_got], gate)
+    parts = [b, b_got, b_core, swap(b_got, "expert", members, 1)]
+    own, far, hidden, scale, early = run_second(
+        parts, gate, up, early, w_gate, w_up, w_down, me
+    )
+    keep, send = chip_sum(own, far, members)
+    got = swap_group(send, groups, members, (2, 1))
+    own, far = run_third(hidden, scale, early, w_down, keep)
+    (far,) = hold([far], got)
+    left = give_back(keep, got, groups, members)
+    keep, send = chip_sum(own, far, members)
+    right = give_back(keep, swap_group(send, groups, members, (2, 1)), groups, members)
+    return jnp.concatenate([left, right], axis=1)
 
 
 def solution(mesh):

time: 81.8 us -> 98.3 us (1.20)
  local copies, waits for them, and re-layouts: 0 us -> 11 us
  waiting for transfers between devices: 24.4 us -> 17.4 us
  Pallas kernels: 36.4 us -> 43 us
  starting transfers between devices: 20 us -> 25.8 us
    unnamed x0 -> x16, local copies, waits for them, and re-layouts: none -> 11 us
    ppermute x6 -> x7, waiting for transfers between devices: 15.2 us -> 7.35 us  [swap_group(): return lax.ppermute(value, AXES, pairs)]
    pallas_call x1, Pallas kernels: 21.1 us -> 15.7 us  [run_second(): pl.pallas_call(functools.partial(second_kernel, width - depth, early, str...]
    pallas_call x2 -> x3, Pallas kernels: 5.97 us -> 10.8 us  [fetch(): pl.pallas_call(functools.partial(fetch_kernel, jobs), in_specs=[hbm] * le...]
    pallas_call x4 -> x3, Pallas kernels: 0.09 us -> 4.26 us  [the longest x1 4.17 us: run_third(): pl.pallas_call(third_kernel, in_specs=whole_vmem(3) + [pl.BlockSpec(memor...]
    ppermute x11 -> x15, starting transfers between devices: 11.7 us -> 15.5 us  [swap(): return lax.ppermute(value, axis, [(i, i ^ mask) for i in range(size)])]
    pallas_call x1, Pallas kernels: 7.94 us -> 10.9 us  [run_first(): pl.pallas_call(functools.partial(first_kernel, len(held), streams, early)...]
    ppermute x6 -> x7, starting transfers between devices: 8.33 us -> 10.2 us  [swap_group(): return lax.ppermute(value, AXES, pairs)]
  transfers between devices with their start and end apart: 17 -> 22, of which waited for: 10 -> 10; matrix products, arithmetic and copies ran while one was open for 0% -> 0% of each run, Pallas kernels for 17% -> 27%
where the time goes in v9:
time: 98.3 us; the launch traced here: 98 us
  Pallas kernels  43 us (44%)
  starting transfers between devices  25.8 us (26%)
  waiting for transfers between devices  17.4 us (18%)
  local copies, waits for them, and re-layouts  11 us (11%)
    pallas_call x1, Pallas kernels, run_second(): pl.pallas_call(functools.partial(second_kernel, width - depth, early, str...  15.7 us
    ppermute x15, starting transfers between devices, swap(): return lax.ppermute(value, axis, [(i, i ^ mask) for i in range(size)])  15.5 us
    unnamed x16, local copies, waits for them, and re-layouts  11 us
    pallas_call x1, Pallas kernels, run_first(): pl.pallas_call(functools.partial(first_kernel, len(held), streams, early)...  10.9 us
    pallas_call x3, Pallas kernels, fetch(): pl.pallas_call(functools.partial(fetch_kernel, jobs), in_specs=[hbm] * le...  10.8 us
    ppermute x7, starting transfers between devices, swap_group(): return lax.ppermute(value, AXES, pairs)  10.2 us
    ppermute x15, waiting for transfers between devices, swap(): return lax.ppermute(value, axis, [(i, i ^ mask) for i in range(size)])  10 us
    ppermute x7, waiting for transfers between devices, swap_group(): return lax.ppermute(value, AXES, pairs)  7.35 us
  transfers between devices with their start and end apart: 22, of which 10 were waited for; matrix products, arithmetic and copies ran while one was open for 0% of the time, Pallas kernels for 27%

profile of v9, /device:TPU:0, one launch (start us, length us, event | category | flops | bytes accessed | tf_op | source)
XLA Modules:
  0.0 98.0 jit_solution(16896450928106637825)
XLA Ops:
  0.0 0.9 shard_map.64.refs_3_.refs_0_
  0.9 3.1 %collective-permute-start = (bf16[4,7296]{1,0:T(4,128)(2,1)S(1)}, bf16[4,7296]{1,0:T(4,128)(2,1)S(1)}, u32[]{:S(2)}, u32[]{:S(2)}) collective-permute-start(bf16[4,7296]{1,0:T(4,128)(2,1)S(1)} %shard_map.64.refs_3_.refs_0_), channel_id=1, source_target_pairs={{0,2},{1,3},{2,0},{3,1},{4,6},{5,7},{6,4},{7,5},{8,10},{9,11},{10,... | collective-permute-start | bytes 175112 | tf_op jit(solution)/shard_map/ppermute | solution.py:38
  4.0 2.6 %collective-permute-start.1 = (bf16[4,7296]{1,0:T(4,128)(2,1)S(1)}, bf16[4,7296]{1,0:T(4,128)(2,1)S(1)}, u32[]{:S(2)}, u32[]{:S(2)}) collective-permute-start(bf16[4,7296]{1,0:T(4,128)(2,1)S(1)} %shard_map.64.refs_3_.refs_0_), channel_id=1, source_target_pairs={{0,4},{1,5},{2,6},{3,7},{4,0},{5,1},{6,2},{7,3},{8,12},{9,13},{10,... | collective-permute-start | bytes 175112 | tf_op jit(solution)/shard_map/ppermute | solution.py:38
  6.6 4.3 %shard_map.65 = (bf16[3584,512]{1,0:T(8,128)(2,1)S(1)}, bf16[3584,512]{1,0:T(8,128)(2,1)S(1)}, bf16[3584,512]{1,0:T(8,128)(2,1)S(1)}, f32[8,128]{1,0:T(8,128)S(1)}) custom-call(bf16[1,7168,2048]{2,1,0:T(8,128)(2,1)} %refs_16_.1, bf16[1,7168,2048]{2,1,0:T(8,128)(2,1)} %refs_16_.1, bf16[1,7168,2048]{2,1,0:T(8,128)(2,1)} %refs_16_.1, ...), custom_call_target="tpu_custom_call" | custom-call | bytes 11010048 | tf_op jit(solution)/shard_map/pallas_call | solution.py:109
  11.0 1.6 %collective-permute-done.2.refs_3_ = bf16[4,7296]{1,0:T(4,128)(2,1)S(1)} collective-permute-done((bf16[4,7296]{1,0:T(4,128)(2,1)S(1)}, bf16[4,7296]{1,0:T(4,128)(2,1)S(1)}, u32[]{:S(2)}, u32[]{:S(2)}) %collective-permute-start.2) | collective-permute-done | bytes 58400 | tf_op jit(solution)/shard_map/ppermute | solution.py:38
  12.6 0.1 shard_map.66.refs_2_.refs_0_
  12.7 1.6 %collective-permute-start.3 = (bf16[16,7296]{1,0:T(8,128)(2,1)S(1)}, bf16[16,7296]{1,0:T(8,128)(2,1)S(1)}, u32[]{:S(2)}, u32[]{:S(2)}) collective-permute-start(bf16[16,7296]{1,0:T(8,128)(2,1)S(1)} %shard_map.66.refs_2_.refs_0_), channel_id=1, source_target_pairs={{0,8},{1,17},{2,10},{3,19},{4,12},{5,21},{6,14},{7,23},{8,0},{9,25... | collective-permute-start | bytes 700424 | tf_op jit(solution)/shard_map/ppermute | solution.py:46
  14.2 3.3 %shard_map.67 = (bf16[3584,512]{1,0:T(8,128)(2,1)S(1)}, bf16[3584,512]{1,0:T(8,128)(2,1)S(1)}, f32[8,128]{1,0:T(8,128)S(1)}) custom-call(bf16[1,7168,2048]{2,1,0:T(8,128)(2,1)} %refs_16_.1, bf16[1,7168,2048]{2,1,0:T(8,128)(2,1)} %refs_17_.1, bf16[16,7296]{1,0:T(8,128)(2,1)S(1)} %shard_map.66.refs_2_.refs_0_), custom_call_target="tpu_custom_call" | custom-call | bytes 7340032 | tf_op jit(solution)/shard_map/pallas_call | solution.py:109
  17.5 1.5 %collective-permute-done.3.refs_1_ = bf16[16,7296]{1,0:T(8,128)(2,1)S(1)} collective-permute-done((bf16[16,7296]{1,0:T(8,128)(2,1)S(1)}, bf16[16,7296]{1,0:T(8,128)(2,1)S(1)}, u32[]{:S(2)}, u32[]{:S(2)}) %collective-permute-start.3) | collective-permute-done | bytes 233504 | tf_op jit(solution)/shard_map/ppermute | solution.py:46
  19.0 1.6 %collective-permute-start.5 = (bf16[32,3584]{1,0:T(8,128)(2,1)S(1)}, bf16[32,3584]{1,0:T(8,128)(2,1)S(1)}, u32[]{:S(2)}, u32[]{:S(2)}) collective-permute-start(bf16[32,3584]{1,0:T(8,128)(2,1)S(1)} %get-tuple-element.55.refs_2_.refs_0_), channel_id=1, source_target_pairs={{0,16},{1,9},{2,18},{3,11},{4,20},{5,13},{6,22},{7,15},{8,24},{9,1... | collective-permute-start | bytes 688136 | tf_op jit(solution)/shard_map/ppermute | solution.py:46
  20.6 3.2 %shard_map.69 = (bf16[3584,512]{1,0:T(8,128)(2,1)S(1)}, bf16[3584,512]{1,0:T(8,128)(2,1)S(1)}, f32[8,128]{1,0:T(8,128)S(1)}) custom-call(bf16[1,7168,2048]{2,1,0:T(8,128)(2,1)} %refs_17_.1, bf16[1,7168,2048]{2,1,0:T(8,128)(2,1)} %refs_17_.1, bf16[32,3584]{1,0:T(8,128)(2,1)S(1)} %get-tuple-element.55.refs_2_.refs_0_), custom_call_target="tpu_custom_call" | custom-call | bytes 7340032 | tf_op jit(solution)/shard_map/pallas_call | solution.py:109
  23.8 0.1 collective-permute-start.6
  23.9 1.2 %collective-permute-done.5.refs_0_ = bf16[32,3584]{1,0:T(8,128)(2,1)S(1)} collective-permute-done((bf16[32,3584]{1,0:T(8,128)(2,1)S(1)}, bf16[32,3584]{1,0:T(8,128)(2,1)S(1)}, u32[]{:S(2)}, u32[]{:S(2)}) %collective-permute-start.5) | collective-permute-done | bytes 229408 | tf_op jit(solution)/shard_map/ppermute | solution.py:46
  25.1 1.5 %collective-permute-start.4 = (bf16[32,3712]{1,0:T(8,128)(2,1)S(1)}, bf16[32,3712]{1,0:T(8,128)(2,1)S(1)}, u32[]{:S(2)}, u32[]{:S(2)}) collective-permute-start(bf16[32,3712]{1,0:T(8,128)(2,1)S(1)} %get-tuple-element.54.refs_13_.refs_0_), channel_id=1, source_target_pairs={{0,16},{1,9},{2,18},{3,11},{4,20},{5,13},{6,22},{7,15},{8,24},{9,1... | collective-permute-start | bytes 712712 | tf_op jit(solution)/shard_map/ppermute | solution.py:46
  26.6 0.2 collective-permute-start.8
  26.8 10.9 %shard_map.71 = (f32[128,2048]{1,0:T(8,128)S(1)}, f32[128,2048]{1,0:T(8,128)S(1)}, bf16[3584,256]{1,0:T(8,128)(2,1)S(1)}, bf16[3584,256]{1,0:T(8,128)(2,1)S(1)},...) custom-call(bf16[32,3584]{1,0:T(8,128)(2,1)S(1)} %get-tuple-element., ...), custom_call_target="tpu_custom_call" | custom-call | flops 3758096384 | bytes 14680064 | tf_op jit(solution)/shard_map/pallas_call | solution.py:232
  37.7 1.2 %copy-done = bf16[3584,256]{1,0:T(8,128)(2,1)} copy-done((bf16[3584,256]{1,0:T(8,128)(2,1)}, bf16[3584,256]{1,0:T(8,128)(2,1)S(1)}, u32[]{:S(2)}) %copy-start) | copy-done | bytes 1835032
  39.0 1.2 %copy-done.2 = bf16[3584,256]{1,0:T(8,128)(2,1)} copy-done((bf16[3584,256]{1,0:T(8,128)(2,1)}, bf16[3584,256]{1,0:T(8,128)(2,1)S(1)}, u32[]{:S(2)}) %copy-start.2) | copy-done | bytes 1835032
  40.2 1.3 %copy-done.4 = bf16[3584,256]{1,0:T(8,128)(2,1)} copy-done((bf16[3584,256]{1,0:T(8,128)(2,1)}, bf16[3584,256]{1,0:T(8,128)(2,1)S(1)}, u32[]{:S(2)}) %copy-start.4) | copy-done | bytes 1835032
  41.5 1.2 %copy-done.6 = bf16[3584,256]{1,0:T(8,128)(2,1)} copy-done((bf16[3584,256]{1,0:T(8,128)(2,1)}, bf16[3584,256]{1,0:T(8,128)(2,1)S(1)}, u32[]{:S(2)}) %copy-start.6) | copy-done | bytes 1835032
  42.7 0.3 collective-permute-start.9
  43.1 1.2 %collective-permute-done.9.refs_3_ = bf16[32,3712]{1,0:T(8,128)(2,1)S(1)} collective-permute-done((bf16[32,3712]{1,0:T(8,128)(2,1)S(1)}, bf16[32,3712]{1,0:T(8,128)(2,1)S(1)}, u32[]{:S(2)}, u32[]{:S(2)}) %collective-permute-start.9) | collective-permute-done | bytes 237600 | tf_op jit(solution)/shard_map/ppermute | solution.py:38
  44.2 1.5 %copy-done.1 = bf16[3584,256]{1,0:T(8,128)(2,1)S(1)} copy-done((bf16[3584,256]{1,0:T(8,128)(2,1)S(1)}, bf16[3584,256]{1,0:T(8,128)(2,1)}, u32[]{:S(2)}) %copy-start.1) | copy-done | bytes 1835032
  45.7 1.5 %copy-done.3 = bf16[3584,256]{1,0:T(8,128)(2,1)S(1)} copy-done((bf16[3584,256]{1,0:T(8,128)(2,1)S(1)}, bf16[3584,256]{1,0:T(8,128)(2,1)}, u32[]{:S(2)}) %copy-start.3) | copy-done | bytes 1835032
  47.2 1.5 %copy-done.5 = bf16[3584,256]{1,0:T(8,128)(2,1)S(1)} copy-done((bf16[3584,256]{1,0:T(8,128)(2,1)S(1)}, bf16[3584,256]{1,0:T(8,128)(2,1)}, u32[]{:S(2)}) %copy-start.5) | copy-done | bytes 1835032
  48.7 1.5 %copy-done.7 = bf16[3584,256]{1,0:T(8,128)(2,1)S(1)} copy-done((bf16[3584,256]{1,0:T(8,128)(2,1)S(1)}, bf16[3584,256]{1,0:T(8,128)(2,1)}, u32[]{:S(2)}) %copy-start.7) | copy-done | bytes 1835032
  50.2 15.7 %shard_map.73 = (bf16[64,3584]{1,0:T(8,128)(2,1)S(1)}, bf16[64,3584]{1,0:T(8,128)(2,1)S(1)}, bf16[128,2048]{1,0:T(8,128)(2,1)S(1)}, f32[128,128]{1,0:T(8,128)S(1)}, bf16[2048,1536]{1,0:T(8,128)(2,1)S(1)}) custom-call(bf16[32,3712]{1,0:T(8,128)(2,1)S(1)} %get-tuple-element.54.refs_13_.refs_0_, bf16[32,3712]{1,0:T(8,128)(2,1)S(1)} %shard_map.72.refs_1_, ...), custom_call_target="tpu_custom_call" | custom-call | flops 5637144576 | bytes 14680064 | tf_op jit(solution)/shard_map/pallas_call | solution.py:358
  66.0 0.4 collective-permute-start.10
  66.3 1.5 %collective-permute-done.10.refs_1_ = bf16[64,3584]{1,0:T(8,128)(2,1)S(1)} collective-permute-done((bf16[64,3584]{1,0:T(8,128)(2,1)S(1)}, bf16[64,3584]{1,0:T(8,128)(2,1)S(1)}, u32[]{:S(2)}, u32[]{:S(2)}) %collective-permute-start.10) | collective-permute-done | bytes 458784 | tf_op jit(solution)/shard_map/ppermute | solution.py:38
  67.8 0.1 shard_map.74
  68.0 1.6 %collective-permute-start.11 = (bf16[32,3584]{1,0:T(8,128)(2,1)S(1)}, bf16[32,3584]{1,0:T(8,128)(2,1)S(1)}, u32[]{:S(2)}, u32[]{:S(2)}) collective-permute-start(bf16[32,3584]{1,0:T(8,128)(2,1)S(1)} %get-tuple-element.79), channel_id=1, source_target_pairs={{0,16},{1,9},{2,18},{3,11},{4,20},{5,13},{6,22},{7,15},{8,24},{9,1... | collective-permute-start | bytes 688136 | tf_op jit(solution)/shard_map/ppermute | solution.py:46
  69.5 4.2 %shard_map.77 = (bf16[64,3584]{1,0:T(8,128)(2,1)S(1)}, bf16[64,3584]{1,0:T(8,128)(2,1)S(1)}) custom-call(bf16[128,2048]{1,0:T(8,128)(2,1)S(1)} %get-tuple-element.86.hidden, f32[128,128]{1,0:T(8,128)S(1)} %get-tuple-element.87.scale_ref, bf16[2048,1536]{1,0:T(8,128)(2,1)S(1)} %get-tuple-element.88.next_ref, bf16[1,2048,7168]{2,1,0:T(8,128)(2,1)} %down_hbm.1, ...), custom_call_target="tpu_custom_call" | custom-call | flops 1879048192 | bytes 14680064 | tf_op jit(solution)/shard_map/pallas_call | solution.py:408
  73.7 0.3 collective-permute-done.11.refs_1_
  74.0 1.8 %collective-permute-done.16.refs_1_ = bf16[64,3584]{1,0:T(8,128)(2,1)S(1)} collective-permute-done((bf16[64,3584]{1,0:T(8,128)(2,1)S(1)}, bf16[64,3584]{1,0:T(8,128)(2,1)S(1)}, u32[]{:S(2)}, u32[]{:S(2)}) %collective-permute-start.16) | collective-permute-done | bytes 458784 | tf_op jit(solution)/shard_map/ppermute | solution.py:38
  75.9 0.1 shard_map.79
  76.0 1.6 %collective-permute-start.17 = (bf16[32,3584]{1,0:T(8,128)(2,1)S(1)}, bf16[32,3584]{1,0:T(8,128)(2,1)S(1)}, u32[]{:S(2)}, u32[]{:S(2)}) collective-permute-start(bf16[32,3584]{1,0:T(8,128)(2,1)S(1)} %get-tuple-element.92), channel_id=1, source_target_pairs={{0,16},{1,9},{2,18},{3,11},{4,20},{5,13},{6,22},{7,15},{8,24},{9,1... | collective-permute-start | bytes 688136 | tf_op jit(solution)/shard_map/ppermute | solution.py:46
  77.6 1.3 %collective-permute-start.12 = (bf16[16,3584]{1,0:T(8,128)(2,1)S(1)}, bf16[16,3584]{1,0:T(8,128)(2,1)S(1)}, u32[]{:S(2)}, u32[]{:S(2)}) collective-permute-start(bf16[16,3584]{1,0:T(8,128)(2,1)S(1)} %get-tuple-element.81), channel_id=1, source_target_pairs={{0,8},{1,17},{2,10},{3,19},{4,12},{5,21},{6,14},{7,23},{8,0},{9,25... | collective-permute-start | bytes 344072 | tf_op jit(solution)/shard_map/ppermute | solution.py:46
  78.9 4.4 %collective-permute-done.17.refs_1_ = bf16[32,3584]{1,0:T(8,128)(2,1)S(1)} collective-permute-done((bf16[32,3584]{1,0:T(8,128)(2,1)S(1)}, bf16[32,3584]{1,0:T(8,128)(2,1)S(1)}, u32[]{:S(2)}, u32[]{:S(2)}) %collective-permute-start.17) | collective-permute-done | bytes 229408 | tf_op jit(solution)/shard_map/ppermute | solution.py:46
  83.3 1.1 %collective-permute-start.18 = (bf16[16,3584]{1,0:T(8,128)(2,1)S(1)}, bf16[16,3584]{1,0:T(8,128)(2,1)S(1)}, u32[]{:S(2)}, u32[]{:S(2)}) collective-permute-start(bf16[16,3584]{1,0:T(8,128)(2,1)S(1)} %get-tuple-element.94), channel_id=1, source_target_pairs={{0,8},{1,17},{2,10},{3,19},{4,12},{5,21},{6,14},{7,23},{8,0},{9,25... | collective-permute-start | bytes 344072 | tf_op jit(solution)/shard_map/ppermute | solution.py:46
  84.5 0.1 collective-permute-start.13
  84.6 2.6 %collective-permute-start.14 = (bf16[4,3584]{1,0:T(4,128)(2,1)S(1)}, bf16[4,3584]{1,0:T(4,128)(2,1)S(1)}, u32[]{:S(2)}, u32[]{:S(2)}) collective-permute-start(bf16[4,3584]{1,0:T(4,128)(2,1)S(1)} %get-tuple-element.84), channel_id=1, source_target_pairs={{0,4},{1,5},{2,6},{3,7},{4,0},{5,1},{6,2},{7,3},{8,12},{9,13},{10,... | collective-permute-start | bytes 86024 | tf_op jit(solution)/shard_map/ppermute | solution.py:38
  87.2 1.8 %collective-permute-start.15 = (bf16[4,3584]{1,0:T(4,128)(2,1)S(1)}, bf16[4,3584]{1,0:T(4,128)(2,1)S(1)}, u32[]{:S(2)}, u32[]{:S(2)}) collective-permute-start(bf16[4,3584]{1,0:T(4,128)(2,1)S(1)} %get-tuple-element.85), channel_id=1, source_target_pairs={{0,6},{1,7},{2,4},{3,5},{4,2},{5,3},{6,0},{7,1},{8,14},{9,15},{10,... | collective-permute-start | bytes 86024 | tf_op jit(solution)/shard_map/ppermute | solution.py:38
  89.0 0.1 collective-permute-start.19
  89.1 2.6 %collective-permute-start.20 = (bf16[4,3584]{1,0:T(4,128)(2,1)S(1)}, bf16[4,3584]{1,0:T(4,128)(2,1)S(1)}, u32[]{:S(2)}, u32[]{:S(2)}) collective-permute-start(bf16[4,3584]{1,0:T(4,128)(2,1)S(1)} %get-tuple-element.97), channel_id=1, source_target_pairs={{0,4},{1,5},{2,6},{3,7},{4,0},{5,1},{6,2},{7,3},{8,12},{9,13},{10,... | collective-permute-start | bytes 86024 | tf_op jit(solution)/shard_map/ppermute | solution.py:38
  91.7 1.8 %collective-permute-start.21 = (bf16[4,3584]{1,0:T(4,128)(2,1)S(1)}, bf16[4,3584]{1,0:T(4,128)(2,1)S(1)}, u32[]{:S(2)}, u32[]{:S(2)}) collective-permute-start(bf16[4,3584]{1,0:T(4,128)(2,1)S(1)} %get-tuple-element.98), channel_id=1, source_target_pairs={{0,6},{1,7},{2,4},{3,5},{4,2},{5,3},{6,0},{7,1},{8,14},{9,15},{10,... | collective-permute-start | bytes 86024 | tf_op jit(solution)/shard_map/ppermute | solution.py:38
  93.5 0.4 collective-permute-done.20
  93.9 3.4 %collective-permute-done.21 = bf16[4,3584]{1,0:T(4,128)(2,1)S(1)} collective-permute-done((bf16[4,3584]{1,0:T(4,128)(2,1)S(1)}, bf16[4,3584]{1,0:T(4,128)(2,1)S(1)}, u32[]{:S(2)}, u32[]{:S(2)}) %collective-permute-start.21) | collective-permute-done | bytes 28704 | tf_op jit(solution)/shard_map/ppermute | solution.py:38
  97.4 0.7 pad_maximum_fusion
  (33 shorter events, 0.3 us)
Async XLA Ops:
  0.9 10.0 %collective-permute-start = (bf16[4,7296]{1,0:T(4,128)(2,1)S(1)}, bf16[4,7296]{1,0:T(4,128)(2,1)S(1)}, u32[]{:S(2)}, u32[]{:S(2)}) collective-permute-start(bf16[4,7296]{1,0:T(4,128)(2,1)S(1)} %shard_map.64.refs_3_.refs_0_), channel_id=1, source_target_pairs={{0,2},{1,3},{2,0},{3,1},{4,6},{5,7},{6,4},{7,5},{8,10},{9,11},{10,... | collective-permute-start | bytes 175112 | tf_op jit(solution)/shard_map/ppermute | solution.py:38
  4.0 6.9 %collective-permute-start.1 = (bf16[4,7296]{1,0:T(4,128)(2,1)S(1)}, bf16[4,7296]{1,0:T(4,128)(2,1)S(1)}, u32[]{:S(2)}, u32[]{:S(2)}) collective-permute-start(bf16[4,7296]{1,0:T(4,128)(2,1)S(1)} %shard_map.64.refs_3_.refs_0_), channel_id=1, source_target_pairs={{0,4},{1,5},{2,6},{3,7},{4,0},{5,1},{6,2},{7,3},{8,12},{9,13},{10,... | collective-permute-start | bytes 175112 | tf_op jit(solution)/shard_map/ppermute | solution.py:38
  6.6 6.0 %collective-permute-start.2 = (bf16[4,7296]{1,0:T(4,128)(2,1)S(1)}, bf16[4,7296]{1,0:T(4,128)(2,1)S(1)}, u32[]{:S(2)}, u32[]{:S(2)}) collective-permute-start(bf16[4,7296]{1,0:T(4,128)(2,1)S(1)} %shard_map.64.refs_3_.refs_0_), channel_id=1, source_target_pairs={{0,6},{1,7},{2,4},{3,5},{4,2},{5,3},{6,0},{7,1},{8,14},{9,15},{10,... | collective-permute-start | bytes 175112 | tf_op jit(solution)/shard_map/ppermute | solution.py:38
  12.7 6.3 %collective-permute-start.3 = (bf16[16,7296]{1,0:T(8,128)(2,1)S(1)}, bf16[16,7296]{1,0:T(8,128)(2,1)S(1)}, u32[]{:S(2)}, u32[]{:S(2)}) collective-permute-start(bf16[16,7296]{1,0:T(8,128)(2,1)S(1)} %shard_map.66.refs_2_.refs_0_), channel_id=1, source_target_pairs={{0,8},{1,17},{2,10},{3,19},{4,12},{5,21},{6,14},{7,23},{8,0},{9,25... | collective-permute-start | bytes 700424 | tf_op jit(solution)/shard_map/ppermute | solution.py:46
  19.0 6.1 %collective-permute-start.5 = (bf16[32,3584]{1,0:T(8,128)(2,1)S(1)}, bf16[32,3584]{1,0:T(8,128)(2,1)S(1)}, u32[]{:S(2)}, u32[]{:S(2)}) collective-permute-start(bf16[32,3584]{1,0:T(8,128)(2,1)S(1)} %get-tuple-element.55.refs_2_.refs_0_), channel_id=1, source_target_pairs={{0,16},{1,9},{2,18},{3,11},{4,20},{5,13},{6,22},{7,15},{8,24},{9,1... | collective-permute-start | bytes 688136 | tf_op jit(solution)/shard_map/ppermute | solution.py:46
  23.8 3.0 %collective-permute-start.6 = (bf16[32,3584]{1,0:T(8,128)(2,1)S(1)}, bf16[32,3584]{1,0:T(8,128)(2,1)S(1)}, u32[]{:S(2)}, u32[]{:S(2)}) collective-permute-start(bf16[32,3584]{1,0:T(8,128)(2,1)S(1)} %get-tuple-element.55.refs_2_.refs_0_), channel_id=1, source_target_pairs={{0,1},{1,0},{2,3},{3,2},{4,5},{5,4},{6,7},{7,6},{8,9},{9,8},{10,11... | collective-permute-start | bytes 688136 | tf_op jit(solution)/shard_map/ppermute | solution.py:38
  25.1 1.7 %collective-permute-start.7 = (bf16[32,3584]{1,0:T(8,128)(2,1)S(1)}, bf16[32,3584]{1,0:T(8,128)(2,1)S(1)}, u32[]{:S(2)}, u32[]{:S(2)}) collective-permute-start(bf16[32,3584]{1,0:T(8,128)(2,1)S(1)} %shard_map.70.refs_1_), channel_id=1, source_target_pairs={{0,1},{1,0},{2,3},{3,2},{4,5},{5,4},{6,7},{7,6},{8,9},{9,8},{10,11... | collective-permute-start | bytes 688136 | tf_op jit(solution)/shard_map/ppermute | solution.py:38
  25.1 17.7 %collective-permute-start.4 = (bf16[32,3712]{1,0:T(8,128)(2,1)S(1)}, bf16[32,3712]{1,0:T(8,128)(2,1)S(1)}, u32[]{:S(2)}, u32[]{:S(2)}) collective-permute-start(bf16[32,3712]{1,0:T(8,128)(2,1)S(1)} %get-tuple-element.54.refs_13_.refs_0_), channel_id=1, source_target_pairs={{0,16},{1,9},{2,18},{3,11},{4,20},{5,13},{6,22},{7,15},{8,24},{9,1... | collective-permute-start | bytes 712712 | tf_op jit(solution)/shard_map/ppermute | solution.py:46
  26.6 16.5 %collective-permute-start.8 = (bf16[32,3712]{1,0:T(8,128)(2,1)S(1)}, bf16[32,3712]{1,0:T(8,128)(2,1)S(1)}, u32[]{:S(2)}, u32[]{:S(2)}) collective-permute-start(bf16[32,3712]{1,0:T(8,128)(2,1)S(1)} %get-tuple-element.54.refs_13_.refs_0_), channel_id=1, source_target_pairs={{0,1},{1,0},{2,3},{3,2},{4,5},{5,4},{6,7},{7,6},{8,9},{9,8},{10,11... | collective-permute-start | bytes 712712 | tf_op jit(solution)/shard_map/ppermute | solution.py:38
  37.7 1.3 %copy-start = (bf16[3584,256]{1,0:T(8,128)(2,1)}, bf16[3584,256]{1,0:T(8,128)(2,1)S(1)}, u32[]{:S(2)}) copy-start(bf16[3584,256]{1,0:T(8,128)(2,1)S(1)} %get-tuple-element.69.refs_9_) | copy-start | bytes 5505028
  39.0 1.2 %copy-start.2 = (bf16[3584,256]{1,0:T(8,128)(2,1)}, bf16[3584,256]{1,0:T(8,128)(2,1)S(1)}, u32[]{:S(2)}) copy-start(bf16[3584,256]{1,0:T(8,128)(2,1)S(1)} %get-tuple-element.70.refs_10_) | copy-start | bytes 5505028
  40.2 1.3 %copy-start.4 = (bf16[3584,256]{1,0:T(8,128)(2,1)}, bf16[3584,256]{1,0:T(8,128)(2,1)S(1)}, u32[]{:S(2)}) copy-start(bf16[3584,256]{1,0:T(8,128)(2,1)S(1)} %get-tuple-element.71.refs_11_) | copy-start | bytes 5505028
  41.5 1.2 %copy-start.6 = (bf16[3584,256]{1,0:T(8,128)(2,1)}, bf16[3584,256]{1,0:T(8,128)(2,1)S(1)}, u32[]{:S(2)}) copy-start(bf16[3584,256]{1,0:T(8,128)(2,1)S(1)} %get-tuple-element.72.refs_12_) | copy-start | bytes 5505028
  42.7 1.5 %collective-permute-start.9 = (bf16[32,3712]{1,0:T(8,128)(2,1)S(1)}, bf16[32,3712]{1,0:T(8,128)(2,1)S(1)}, u32[]{:S(2)}, u32[]{:S(2)}) collective-permute-start(bf16[32,3712]{1,0:T(8,128)(2,1)S(1)} %shard_map.72.refs_1_), channel_id=1, source_target_pairs={{0,1},{1,0},{2,3},{3,2},{4,5},{5,4},{6,7},{7,6},{8,9},{9,8},{10,11... | collective-permute-start | bytes 712712 | tf_op jit(solution)/shard_map/ppermute | solution.py:38
  44.2 1.5 %copy-start.1 = (bf16[3584,256]{1,0:T(8,128)(2,1)S(1)}, bf16[3584,256]{1,0:T(8,128)(2,1)}, u32[]{:S(2)}) copy-start(bf16[3584,256]{1,0:T(8,128)(2,1)} %copy-done) | copy-start | bytes 5505028
  45.7 1.5 %copy-start.3 = (bf16[3584,256]{1,0:T(8,128)(2,1)S(1)}, bf16[3584,256]{1,0:T(8,128)(2,1)}, u32[]{:S(2)}) copy-start(bf16[3584,256]{1,0:T(8,128)(2,1)} %copy-done.2) | copy-start | bytes 5505028
  47.2 1.5 %copy-start.5 = (bf16[3584,256]{1,0:T(8,128)(2,1)S(1)}, bf16[3584,256]{1,0:T(8,128)(2,1)}, u32[]{:S(2)}) copy-start(bf16[3584,256]{1,0:T(8,128)(2,1)} %copy-done.4) | copy-start | bytes 5505028
  48.7 1.5 %copy-start.7 = (bf16[3584,256]{1,0:T(8,128)(2,1)S(1)}, bf16[3584,256]{1,0:T(8,128)(2,1)}, u32[]{:S(2)}) copy-start(bf16[3584,256]{1,0:T(8,128)(2,1)} %copy-done.6) | copy-start | bytes 5505028
  66.0 1.9 %collective-permute-start.10 = (bf16[64,3584]{1,0:T(8,128)(2,1)S(1)}, bf16[64,3584]{1,0:T(8,128)(2,1)S(1)}, u32[]{:S(2)}, u32[]{:S(2)}) collective-permute-start(bf16[64,3584]{1,0:T(8,128)(2,1)S(1)} %get-tuple-element.77), channel_id=1, source_target_pairs={{0,1},{1,0},{2,3},{3,2},{4,5},{5,4},{6,7},{7,6},{8,9},{9,8},{10,11... | collective-permute-start | bytes 1376264 | tf_op jit(solution)/shard_map/ppermute | solution.py:38
  68.0 6.1 %collective-permute-start.11 = (bf16[32,3584]{1,0:T(8,128)(2,1)S(1)}, bf16[32,3584]{1,0:T(8,128)(2,1)S(1)}, u32[]{:S(2)}, u32[]{:S(2)}) collective-permute-start(bf16[32,3584]{1,0:T(8,128)(2,1)S(1)} %get-tuple-element.79), channel_id=1, source_target_pairs={{0,16},{1,9},{2,18},{3,11},{4,20},{5,13},{6,22},{7,15},{8,24},{9,1... | collective-permute-start | bytes 688136 | tf_op jit(solution)/shard_map/ppermute | solution.py:46
  74.0 1.8 %collective-permute-start.16 = (bf16[64,3584]{1,0:T(8,128)(2,1)S(1)}, bf16[64,3584]{1,0:T(8,128)(2,1)S(1)}, u32[]{:S(2)}, u32[]{:S(2)}) collective-permute-start(bf16[64,3584]{1,0:T(8,128)(2,1)S(1)} %shard_map.78), channel_id=1, source_target_pairs={{0,1},{1,0},{2,3},{3,2},{4,5},{5,4},{6,7},{7,6},{8,9},{9,8},{10,11... | collective-permute-start | bytes 1376264 | tf_op jit(solution)/shard_map/ppermute | solution.py:38
  76.0 7.3 %collective-permute-start.17 = (bf16[32,3584]{1,0:T(8,128)(2,1)S(1)}, bf16[32,3584]{1,0:T(8,128)(2,1)S(1)}, u32[]{:S(2)}, u32[]{:S(2)}) collective-permute-start(bf16[32,3584]{1,0:T(8,128)(2,1)S(1)} %get-tuple-element.92), channel_id=1, source_target_pairs={{0,16},{1,9},{2,18},{3,11},{4,20},{5,13},{6,22},{7,15},{8,24},{9,1... | collective-permute-start | bytes 688136 | tf_op jit(solution)/shard_map/ppermute | solution.py:46
  77.6 6.8 %collective-permute-start.12 = (bf16[16,3584]{1,0:T(8,128)(2,1)S(1)}, bf16[16,3584]{1,0:T(8,128)(2,1)S(1)}, u32[]{:S(2)}, u32[]{:S(2)}) collective-permute-start(bf16[16,3584]{1,0:T(8,128)(2,1)S(1)} %get-tuple-element.81), channel_id=1, source_target_pairs={{0,8},{1,17},{2,10},{3,19},{4,12},{5,21},{6,14},{7,23},{8,0},{9,25... | collective-permute-start | bytes 344072 | tf_op jit(solution)/shard_map/ppermute | solution.py:46
  83.3 5.6 %collective-permute-start.18 = (bf16[16,3584]{1,0:T(8,128)(2,1)S(1)}, bf16[16,3584]{1,0:T(8,128)(2,1)S(1)}, u32[]{:S(2)}, u32[]{:S(2)}) collective-permute-start(bf16[16,3584]{1,0:T(8,128)(2,1)S(1)} %get-tuple-element.94), channel_id=1, source_target_pairs={{0,8},{1,17},{2,10},{3,19},{4,12},{5,21},{6,14},{7,23},{8,0},{9,25... | collective-permute-start | bytes 344072 | tf_op jit(solution)/shard_map/ppermute | solution.py:46
  84.5 7.2 %collective-permute-start.13 = (bf16[4,3584]{1,0:T(4,128)(2,1)S(1)}, bf16[4,3584]{1,0:T(4,128)(2,1)S(1)}, u32[]{:S(2)}, u32[]{:S(2)}) collective-permute-start(bf16[4,3584]{1,0:T(4,128)(2,1)S(1)} %get-tuple-element.83), channel_id=1, source_target_pairs={{0,2},{1,3},{2,0},{3,1},{4,6},{5,7},{6,4},{7,5},{8,10},{9,11},{10,... | collective-permute-start | bytes 86024 | tf_op jit(solution)/shard_map/ppermute | solution.py:38
  84.6 8.9 %collective-permute-start.14 = (bf16[4,3584]{1,0:T(4,128)(2,1)S(1)}, bf16[4,3584]{1,0:T(4,128)(2,1)S(1)}, u32[]{:S(2)}, u32[]{:S(2)}) collective-permute-start(bf16[4,3584]{1,0:T(4,128)(2,1)S(1)} %get-tuple-element.84), channel_id=1, source_target_pairs={{0,4},{1,5},{2,6},{3,7},{4,0},{5,1},{6,2},{7,3},{8,12},{9,13},{10,... | collective-permute-start | bytes 86024 | tf_op jit(solution)/shard_map/ppermute | solution.py:38
  87.2 6.3 %collective-permute-start.15 = (bf16[4,3584]{1,0:T(4,128)(2,1)S(1)}, bf16[4,3584]{1,0:T(4,128)(2,1)S(1)}, u32[]{:S(2)}, u32[]{:S(2)}) collective-permute-start(bf16[4,3584]{1,0:T(4,128)(2,1)S(1)} %get-tuple-element.85), channel_id=1, source_target_pairs={{0,6},{1,7},{2,4},{3,5},{4,2},{5,3},{6,0},{7,1},{8,14},{9,15},{10,... | collective-permute-start | bytes 86024 | tf_op jit(solution)/shard_map/ppermute | solution.py:38
  89.0 4.5 %collective-permute-start.19 = (bf16[4,3584]{1,0:T(4,128)(2,1)S(1)}, bf16[4,3584]{1,0:T(4,128)(2,1)S(1)}, u32[]{:S(2)}, u32[]{:S(2)}) collective-permute-start(bf16[4,3584]{1,0:T(4,128)(2,1)S(1)} %get-tuple-element.96), channel_id=1, source_target_pairs={{0,2},{1,3},{2,0},{3,1},{4,6},{5,7},{6,4},{7,5},{8,10},{9,11},{10,... | collective-permute-start | bytes 86024 | tf_op jit(solution)/shard_map/ppermute | solution.py:38
  89.1 4.8 %collective-permute-start.20 = (bf16[4,3584]{1,0:T(4,128)(2,1)S(1)}, bf16[4,3584]{1,0:T(4,128)(2,1)S(1)}, u32[]{:S(2)}, u32[]{:S(2)}) collective-permute-start(bf16[4,3584]{1,0:T(4,128)(2,1)S(1)} %get-tuple-element.97), channel_id=1, source_target_pairs={{0,4},{1,5},{2,6},{3,7},{4,0},{5,1},{6,2},{7,3},{8,12},{9,13},{10,... | collective-permute-start | bytes 86024 | tf_op jit(solution)/shard_map/ppermute | solution.py:38
  91.7 5.7 %collective-permute-start.21 = (bf16[4,3584]{1,0:T(4,128)(2,1)S(1)}, bf16[4,3584]{1,0:T(4,128)(2,1)S(1)}, u32[]{:S(2)}, u32[]{:S(2)}) collective-permute-start(bf16[4,3584]{1,0:T(4,128)(2,1)S(1)} %get-tuple-element.98), channel_id=1, source_target_pairs={{0,6},{1,7},{2,4},{3,5},{4,2},{5,3},{6,0},{7,1},{8,14},{9,15},{10,... | collective-permute-start | bytes 86024 | tf_op jit(solution)/shard_map/ppermute | solution.py:38

commit v10 on v8

--- a/solution.py
+++ b/solution.py
@@ -13,10 +13,9 @@
 VMEM = pltpu.VMEM
 UNIT_BLOCK = 256
 DOWN_BLOCK = 512
-RING = 4
+RING = 5
 DOWN_RING = 5
 FOLD_BLOCK = 1024
-DEPTH_CUT = 1024
 
 
 def in_vmem(value):
@@ -156,13 +155,7 @@
 
 
 def times(left_ref, right_ref):
-    depth = left_ref.shape[1]
-    total = None
-    for k in range(0, depth, DEPTH_CUT):
-        inner = slice(k, min(depth, k + DEPTH_CUT))
-        value = jnp.dot(left_ref[:, inner], right_ref[inner, :], preferred_element_type=jnp.float32)
-        total = value if total is None else total + value
-    return total
+    return jnp.dot(left_ref[...], right_ref[...], preferred_element_type=jnp.float32)
 
 
 def expert_kernel(place, order, streams, held, *refs):
@@ -259,7 +252,7 @@
         + ring * depth * UNIT_BLOCK
         + DOWN_RING * units * DOWN_BLOCK
     )
-    work = 2560 * 1024 + 12 * rows * UNIT_BLOCK + 4 * rows * DOWN_BLOCK
+    work = 1024 * 1024 + 12 * rows * UNIT_BLOCK + 4 * rows * DOWN_BLOCK
     args = [in_vmem(v) for v in [*a_parts, *b_parts, *held]]
     return pl.pallas_call(
         functools.partial(expert_kernel, place, order, streams, len(held)),
@@ -333,8 +326,8 @@
     me = lax.axis_index("group") * EXP_GRP + lax.axis_index("expert") // split
     me = me.astype(jnp.int32).reshape(1)
     blocks = w_gate.shape[2] // UNIT_BLOCK
-    gates, ups = max(1, blocks // 2), max(1, blocks * 3 // 8)
-    cuts = [0, max(1, gates // 2), max(1, gates * 3 // 4), gates]
+    gates, ups = max(1, blocks // 2), max(1, blocks // 4)
+    cuts = [0, max(1, gates * 3 // 4), gates, gates]
     jobs, place, count = [], {}, 0
     for n in range(3):
         pieces = [(0, list(range(cuts[n], cuts[n + 1]))), (1, list(range(ups)) if n == 2 else [])]

time: 78.9 us -> 78.9 us (level)
  starting transfers between devices: 25.7 us -> 26.6 us
  waiting for transfers between devices: 16.7 us -> 15.9 us
    ppermute x8, starting transfers between devices: 9.37 us -> 10.8 us  [swap_group(): return lax.ppermute(value, AXES, pairs)]
    pallas_call x3, Pallas kernels: 10.7 us -> 9.6 us  [fetch(): pl.pallas_call(functools.partial(fetch_kernel, jobs), in_specs=[hbm] * le...]
    pallas_call x1, Pallas kernels: 23.3 us -> 24.3 us  [run_expert(): pl.pallas_call(functools.partial(expert_kernel, place, order, streams, le...]
  transfers between devices with their start and end apart: 23 -> 23, of which waited for: 12 -> 13; matrix products, arithmetic and copies ran while one was open for 0% -> 0% of each run, Pallas kernels for 14% -> 13%
where the time goes in v10:
time: 78.9 us; the launch traced here: 78.7 us
  Pallas kernels  35.3 us (45%)
  starting transfers between devices  26.6 us (34%)
  waiting for transfers between devices  15.9 us (20%)
    pallas_call x1, Pallas kernels, run_expert(): pl.pallas_call(functools.partial(expert_kernel, place, order, streams, le...  24.3 us
    ppermute x15, starting transfers between devices, swap(): return lax.ppermute(value, axis, [(i, i ^ mask) for i in range(size)])  15.9 us
    ppermute x8, starting transfers between devices, swap_group(): return lax.ppermute(value, AXES, pairs)  10.8 us
    pallas_call x3, Pallas kernels, fetch(): pl.pallas_call(functools.partial(fetch_kernel, jobs), in_specs=[hbm] * le...  9.6 us
    ppermute x15, waiting for transfers between devices, swap(): return lax.ppermute(value, axis, [(i, i ^ mask) for i in range(size)])  8.36 us
    ppermute x8, waiting for transfers between devices, swap_group(): return lax.ppermute(value, AXES, pairs)  7.52 us
  transfers between devices with their start and end apart: 23, of which 13 were waited for; matrix products, arithmetic and copies ran while one was open for 0% of the time, Pallas kernels for 13%

profile of v10, /device:TPU:0, one launch (start us, length us, event | category | flops | bytes accessed | tf_op | source)
XLA Modules:
  0.0 78.7 jit_solution(10223814982435269347)
XLA Ops:
  0.0 0.9 %shard_map.64.refs_1_.refs_0_ = bf16[4,7296]{1,0:T(4,128)(2,1)S(1)} custom-call(s32[1]{0:T(128)} %bitcast.me_ref.refs_14_, bf16[4,7168]{1,0:T(4,128)(2,1)} %tokens_ref.1, s32[4,8]{1,0:T(4,128)} %ids_ref.1, bf16[4,8]{1,0:T(4,128)(2,1)} %weights_ref.1), custom_call_target="tpu_custom_call" | custom-call | tf_op jit(solution)/shard_map/pallas_call | solution.py:68
  0.9 5.1 %collective-permute-start.2 = (bf16[4,7296]{1,0:T(4,128)(2,1)S(1)}, bf16[4,7296]{1,0:T(4,128)(2,1)S(1)}, u32[]{:S(2)}, u32[]{:S(2)}) collective-permute-start(bf16[4,7296]{1,0:T(4,128)(2,1)S(1)} %shard_map.64.refs_1_.refs_0_), channel_id=1, source_target_pairs={{0,6},{1,7},{2,4},{3,5},{4,2},{5,3},{6,0},{7,1},{8,14},{9,15},{10,... | collective-permute-start | bytes 175112 | tf_op jit(solution)/shard_map/ppermute | solution.py:34
  6.1 0.6 collective-permute-start
  6.7 4.3 %shard_map.65 = (bf16[7168,768]{1,0:T(8,128)(2,1)S(1)}, f32[8,128]{1,0:T(8,128)S(1)}) custom-call(bf16[1,7168,2048]{2,1,0:T(8,128)(2,1)} %refs_11_.1, bf16[4,7296]{1,0:T(4,128)(2,1)S(1)} %shard_map.64.refs_1_.refs_0_), custom_call_target="tpu_custom_call" | custom-call | bytes 11010048 | tf_op jit(solution)/shard_map/pallas_call | solution.py:106
  11.0 0.0 collective-permute-done.2.refs_3_
  11.0 0.1 collective-permute-done.1.refs_2_
  11.1 0.1 shard_map.66
  11.2 1.6 %collective-permute-start.7 = (bf16[16,3712]{1,0:T(8,128)(2,1)S(1)}, bf16[16,3712]{1,0:T(8,128)(2,1)S(1)}, u32[]{:S(2)}, u32[]{:S(2)}) collective-permute-start(bf16[16,3712]{1,0:T(8,128)(2,1)S(1)} %get-tuple-element.37.refs_0_), channel_id=1, source_target_pairs={{0,8},{1,17},{2,10},{3,19},{4,12},{5,21},{6,14},{7,23},{8,0},{9,25... | collective-permute-start | bytes 356360 | tf_op jit(solution)/shard_map/ppermute | solution.py:42
  12.8 0.4 collective-permute-start.3
  13.3 2.1 %shard_map.67 = (bf16[7168,256]{1,0:T(8,128)(2,1)S(1)}, f32[8,128]{1,0:T(8,128)S(1)}) custom-call(bf16[1,7168,2048]{2,1,0:T(8,128)(2,1)} %refs_11_.1, bf16[16,3584]{1,0:T(8,128)(2,1)S(1)} %get-tuple-element.34.refs_1_.refs_0_), custom_call_target="tpu_custom_call" | custom-call | bytes 3670016 | tf_op jit(solution)/shard_map/pallas_call | solution.py:106
  15.4 0.7 collective-permute-done.7.refs_1_
  16.1 1.7 %collective-permute-start.8 = (bf16[32,3712]{1,0:T(8,128)(2,1)S(1)}, bf16[32,3712]{1,0:T(8,128)(2,1)S(1)}, u32[]{:S(2)}, u32[]{:S(2)}) collective-permute-start(bf16[32,3712]{1,0:T(8,128)(2,1)S(1)} %shard_map.71.refs_4_), channel_id=1, source_target_pairs={{0,16},{1,9},{2,18},{3,11},{4,20},{5,13},{6,22},{7,15},{8,24},{9,1... | collective-permute-start | bytes 712712 | tf_op jit(solution)/shard_map/ppermute | solution.py:42
  17.8 0.7 collective-permute-done.3.refs_1_
  18.6 1.5 %collective-permute-start.4 = (bf16[32,3584]{1,0:T(8,128)(2,1)S(1)}, bf16[32,3584]{1,0:T(8,128)(2,1)S(1)}, u32[]{:S(2)}, u32[]{:S(2)}) collective-permute-start(bf16[32,3584]{1,0:T(8,128)(2,1)S(1)} %shard_map.68.refs_1_.refs_0_), channel_id=1, source_target_pairs={{0,16},{1,9},{2,18},{3,11},{4,20},{5,13},{6,22},{7,15},{8,24},{9,1... | collective-permute-start | bytes 688136 | tf_op jit(solution)/shard_map/ppermute | solution.py:42
  20.0 3.2 %shard_map.69 = (bf16[7168,512]{1,0:T(8,128)(2,1)S(1)}, f32[8,128]{1,0:T(8,128)S(1)}) custom-call(bf16[1,7168,2048]{2,1,0:T(8,128)(2,1)} %refs_12_.1, bf16[32,3584]{1,0:T(8,128)(2,1)S(1)} %shard_map.68.refs_1_.refs_0_), custom_call_target="tpu_custom_call" | custom-call | bytes 7340032 | tf_op jit(solution)/shard_map/pallas_call | solution.py:106
  23.3 0.1 collective-permute-start.9
  23.4 0.0 collective-permute-done.8.refs_0_
  23.4 0.5 collective-permute-start.10
  23.9 0.1 collective-permute-start.5
  24.0 0.8 %collective-permute-done.4.refs_0_ = bf16[32,3584]{1,0:T(8,128)(2,1)S(1)} collective-permute-done((bf16[32,3584]{1,0:T(8,128)(2,1)S(1)}, bf16[32,3584]{1,0:T(8,128)(2,1)S(1)}, u32[]{:S(2)}, u32[]{:S(2)}) %collective-permute-start.4) | collective-permute-done | bytes 229408 | tf_op jit(solution)/shard_map/ppermute | solution.py:42
  24.8 0.7 collective-permute-done.5.refs_2_
  25.5 0.7 collective-permute-done.6.refs_3_
  26.3 24.3 %shard_map.73 = (bf16[64,3584]{1,0:T(8,128)(2,1)S(1)}, bf16[64,3584]{1,0:T(8,128)(2,1)S(1)}, bf16[64,3584]{1,0:T(8,128)(2,1)S(1)}, bf16[64,3584]{1,0:T(8,128)(2,1)S(1)}) custom-call(bf16[32,3584]{1,0:T(8,128)(2,1)S(1)} %shard_map.68.refs_1_.refs_0_, bf16[32,3584]{1,0:T(8,128)(2,1)S(1)} %shard_map.70.refs_1_, ...), custom_call_target="tpu_custom_call" | custom-call | flops 11274289152 | bytes 58720256 | tf_op jit(solution)/shard_map/pallas_call | solution.py:257
  50.6 0.2 collective-permute-start.11
  50.8 0.4 collective-permute-start.17
  51.1 1.3 %collective-permute-done.11.refs_1_ = bf16[64,3584]{1,0:T(8,128)(2,1)S(1)} collective-permute-done((bf16[64,3584]{1,0:T(8,128)(2,1)S(1)}, bf16[64,3584]{1,0:T(8,128)(2,1)S(1)}, u32[]{:S(2)}, u32[]{:S(2)}) %collective-permute-start.11) | collective-permute-done | bytes 458784 | tf_op jit(solution)/shard_map/ppermute | solution.py:34
  52.5 0.1 shard_map.74
  52.6 1.7 %collective-permute-start.12 = (bf16[32,3584]{1,0:T(8,128)(2,1)S(1)}, bf16[32,3584]{1,0:T(8,128)(2,1)S(1)}, u32[]{:S(2)}, u32[]{:S(2)}) collective-permute-start(bf16[32,3584]{1,0:T(8,128)(2,1)S(1)} %get-tuple-element.44), channel_id=1, source_target_pairs={{0,16},{1,9},{2,18},{3,11},{4,20},{5,13},{6,22},{7,15},{8,24},{9,1... | collective-permute-start | bytes 688136 | tf_op jit(solution)/shard_map/ppermute | solution.py:42
  54.2 0.0 collective-permute-done.17.refs_1_
  54.2 0.1 shard_map.77
  54.4 0.5 collective-permute-start.18
  54.9 3.8 %collective-permute-done.12.refs_1_ = bf16[32,3584]{1,0:T(8,128)(2,1)S(1)} collective-permute-done((bf16[32,3584]{1,0:T(8,128)(2,1)S(1)}, bf16[32,3584]{1,0:T(8,128)(2,1)S(1)}, u32[]{:S(2)}, u32[]{:S(2)}) %collective-permute-start.12) | collective-permute-done | bytes 229408 | tf_op jit(solution)/shard_map/ppermute | solution.py:42
  58.7 0.1 shard_map.75
  58.7 1.6 %collective-permute-start.13 = (bf16[16,3584]{1,0:T(8,128)(2,1)S(1)}, bf16[16,3584]{1,0:T(8,128)(2,1)S(1)}, u32[]{:S(2)}, u32[]{:S(2)}) collective-permute-start(bf16[16,3584]{1,0:T(8,128)(2,1)S(1)} %get-tuple-element.46), channel_id=1, source_target_pairs={{0,8},{1,17},{2,10},{3,19},{4,12},{5,21},{6,14},{7,23},{8,0},{9,25... | collective-permute-start | bytes 344072 | tf_op jit(solution)/shard_map/ppermute | solution.py:42
  60.4 1.1 %collective-permute-done.18.refs_1_ = bf16[32,3584]{1,0:T(8,128)(2,1)S(1)} collective-permute-done((bf16[32,3584]{1,0:T(8,128)(2,1)S(1)}, bf16[32,3584]{1,0:T(8,128)(2,1)S(1)}, u32[]{:S(2)}, u32[]{:S(2)}) %collective-permute-start.18) | collective-permute-done | bytes 229408 | tf_op jit(solution)/shard_map/ppermute | solution.py:42
  61.5 0.1 shard_map.78
  61.6 1.6 %collective-permute-start.19 = (bf16[16,3584]{1,0:T(8,128)(2,1)S(1)}, bf16[16,3584]{1,0:T(8,128)(2,1)S(1)}, u32[]{:S(2)}, u32[]{:S(2)}) collective-permute-start(bf16[16,3584]{1,0:T(8,128)(2,1)S(1)} %get-tuple-element.56), channel_id=1, source_target_pairs={{0,8},{1,17},{2,10},{3,19},{4,12},{5,21},{6,14},{7,23},{8,0},{9,25... | collective-permute-start | bytes 344072 | tf_op jit(solution)/shard_map/ppermute | solution.py:42
  63.2 0.4 collective-permute-done.13.refs_1_
  63.6 1.3 %collective-permute-start.14 = (bf16[4,3584]{1,0:T(4,128)(2,1)S(1)}, bf16[4,3584]{1,0:T(4,128)(2,1)S(1)}, u32[]{:S(2)}, u32[]{:S(2)}) collective-permute-start(bf16[4,3584]{1,0:T(4,128)(2,1)S(1)} %get-tuple-element.48), channel_id=1, source_target_pairs={{0,2},{1,3},{2,0},{3,1},{4,6},{5,7},{6,4},{7,5},{8,10},{9,11},{10,... | collective-permute-start | bytes 86024 | tf_op jit(solution)/shard_map/ppermute | solution.py:34
  64.9 2.9 %collective-permute-start.15 = (bf16[4,3584]{1,0:T(4,128)(2,1)S(1)}, bf16[4,3584]{1,0:T(4,128)(2,1)S(1)}, u32[]{:S(2)}, u32[]{:S(2)}) collective-permute-start(bf16[4,3584]{1,0:T(4,128)(2,1)S(1)} %get-tuple-element.49), channel_id=1, source_target_pairs={{0,4},{1,5},{2,6},{3,7},{4,0},{5,1},{6,2},{7,3},{8,12},{9,13},{10,... | collective-permute-start | bytes 86024 | tf_op jit(solution)/shard_map/ppermute | solution.py:34
  67.9 0.2 collective-permute-start.16
  68.1 0.4 collective-permute-start.20
  68.5 3.8 %collective-permute-start.21 = (bf16[4,3584]{1,0:T(4,128)(2,1)S(1)}, bf16[4,3584]{1,0:T(4,128)(2,1)S(1)}, u32[]{:S(2)}, u32[]{:S(2)}) collective-permute-start(bf16[4,3584]{1,0:T(4,128)(2,1)S(1)} %get-tuple-element.59), channel_id=1, source_target_pairs={{0,4},{1,5},{2,6},{3,7},{4,0},{5,1},{6,2},{7,3},{8,12},{9,13},{10,... | collective-permute-start | bytes 86024 | tf_op jit(solution)/shard_map/ppermute | solution.py:34
  72.4 0.2 collective-permute-start.22
  72.6 1.0 %collective-permute-done.16 = bf16[4,3584]{1,0:T(4,128)(2,1)S(1)} collective-permute-done((bf16[4,3584]{1,0:T(4,128)(2,1)S(1)}, bf16[4,3584]{1,0:T(4,128)(2,1)S(1)}, u32[]{:S(2)}, u32[]{:S(2)}) %collective-permute-start.16) | collective-permute-done | bytes 28704 | tf_op jit(solution)/shard_map/ppermute | solution.py:34
  73.6 1.2 %collective-permute-done.21 = bf16[4,3584]{1,0:T(4,128)(2,1)S(1)} collective-permute-done((bf16[4,3584]{1,0:T(4,128)(2,1)S(1)}, bf16[4,3584]{1,0:T(4,128)(2,1)S(1)}, u32[]{:S(2)}, u32[]{:S(2)}) %collective-permute-start.21) | collective-permute-done | bytes 28704 | tf_op jit(solution)/shard_map/ppermute | solution.py:34
  74.8 3.2 %collective-permute-done.22 = bf16[4,3584]{1,0:T(4,128)(2,1)S(1)} collective-permute-done((bf16[4,3584]{1,0:T(4,128)(2,1)S(1)}, bf16[4,3584]{1,0:T(4,128)(2,1)S(1)}, u32[]{:S(2)}, u32[]{:S(2)}) %collective-permute-start.22) | collective-permute-done | bytes 28704 | tf_op jit(solution)/shard_map/ppermute | solution.py:34
  78.1 0.7 pad_maximum_fusion
  (17 shorter events, 0.2 us)
Async XLA Ops:
  0.9 10.1 %collective-permute-start.2 = (bf16[4,7296]{1,0:T(4,128)(2,1)S(1)}, bf16[4,7296]{1,0:T(4,128)(2,1)S(1)}, u32[]{:S(2)}, u32[]{:S(2)}) collective-permute-start(bf16[4,7296]{1,0:T(4,128)(2,1)S(1)} %shard_map.64.refs_1_.refs_0_), channel_id=1, source_target_pairs={{0,6},{1,7},{2,4},{3,5},{4,2},{5,3},{6,0},{7,1},{8,14},{9,15},{10,... | collective-permute-start | bytes 175112 | tf_op jit(solution)/shard_map/ppermute | solution.py:34
  6.0 5.1 %collective-permute-start.1 = (bf16[4,7296]{1,0:T(4,128)(2,1)S(1)}, bf16[4,7296]{1,0:T(4,128)(2,1)S(1)}, u32[]{:S(2)}, u32[]{:S(2)}) collective-permute-start(bf16[4,7296]{1,0:T(4,128)(2,1)S(1)} %shard_map.64.refs_1_.refs_0_), channel_id=1, source_target_pairs={{0,4},{1,5},{2,6},{3,7},{4,0},{5,1},{6,2},{7,3},{8,12},{9,13},{10,... | collective-permute-start | bytes 175112 | tf_op jit(solution)/shard_map/ppermute | solution.py:34
  6.1 5.1 %collective-permute-start = (bf16[4,7296]{1,0:T(4,128)(2,1)S(1)}, bf16[4,7296]{1,0:T(4,128)(2,1)S(1)}, u32[]{:S(2)}, u32[]{:S(2)}) collective-permute-start(bf16[4,7296]{1,0:T(4,128)(2,1)S(1)} %shard_map.64.refs_1_.refs_0_), channel_id=1, source_target_pairs={{0,2},{1,3},{2,0},{3,1},{4,6},{5,7},{6,4},{7,5},{8,10},{9,11},{10,... | collective-permute-start | bytes 175112 | tf_op jit(solution)/shard_map/ppermute | solution.py:34
  11.2 4.9 %collective-permute-start.7 = (bf16[16,3712]{1,0:T(8,128)(2,1)S(1)}, bf16[16,3712]{1,0:T(8,128)(2,1)S(1)}, u32[]{:S(2)}, u32[]{:S(2)}) collective-permute-start(bf16[16,3712]{1,0:T(8,128)(2,1)S(1)} %get-tuple-element.37.refs_0_), channel_id=1, source_target_pairs={{0,8},{1,17},{2,10},{3,19},{4,12},{5,21},{6,14},{7,23},{8,0},{9,25... | collective-permute-start | bytes 356360 | tf_op jit(solution)/shard_map/ppermute | solution.py:42
  12.8 5.7 %collective-permute-start.3 = (bf16[16,3584]{1,0:T(8,128)(2,1)S(1)}, bf16[16,3584]{1,0:T(8,128)(2,1)S(1)}, u32[]{:S(2)}, u32[]{:S(2)}) collective-permute-start(bf16[16,3584]{1,0:T(8,128)(2,1)S(1)} %get-tuple-element.34.refs_1_.refs_0_), channel_id=1, source_target_pairs={{0,8},{1,17},{2,10},{3,19},{4,12},{5,21},{6,14},{7,23},{8,0},{9,25... | collective-permute-start | bytes 344072 | tf_op jit(solution)/shard_map/ppermute | solution.py:42
  16.1 7.2 %collective-permute-start.8 = (bf16[32,3712]{1,0:T(8,128)(2,1)S(1)}, bf16[32,3712]{1,0:T(8,128)(2,1)S(1)}, u32[]{:S(2)}, u32[]{:S(2)}) collective-permute-start(bf16[32,3712]{1,0:T(8,128)(2,1)S(1)} %shard_map.71.refs_4_), channel_id=1, source_target_pairs={{0,16},{1,9},{2,18},{3,11},{4,20},{5,13},{6,22},{7,15},{8,24},{9,1... | collective-permute-start | bytes 712712 | tf_op jit(solution)/shard_map/ppermute | solution.py:42
  18.6 6.2 %collective-permute-start.4 = (bf16[32,3584]{1,0:T(8,128)(2,1)S(1)}, bf16[32,3584]{1,0:T(8,128)(2,1)S(1)}, u32[]{:S(2)}, u32[]{:S(2)}) collective-permute-start(bf16[32,3584]{1,0:T(8,128)(2,1)S(1)} %shard_map.68.refs_1_.refs_0_), channel_id=1, source_target_pairs={{0,16},{1,9},{2,18},{3,11},{4,20},{5,13},{6,22},{7,15},{8,24},{9,1... | collective-permute-start | bytes 688136 | tf_op jit(solution)/shard_map/ppermute | solution.py:42
  23.3 2.2 %collective-permute-start.9 = (bf16[32,3712]{1,0:T(8,128)(2,1)S(1)}, bf16[32,3712]{1,0:T(8,128)(2,1)S(1)}, u32[]{:S(2)}, u32[]{:S(2)}) collective-permute-start(bf16[32,3712]{1,0:T(8,128)(2,1)S(1)} %shard_map.71.refs_4_), channel_id=1, source_target_pairs={{0,1},{1,0},{2,3},{3,2},{4,5},{5,4},{6,7},{7,6},{8,9},{9,8},{10,11... | collective-permute-start | bytes 712712 | tf_op jit(solution)/shard_map/ppermute | solution.py:34
  23.4 2.9 %collective-permute-start.10 = (bf16[32,3712]{1,0:T(8,128)(2,1)S(1)}, bf16[32,3712]{1,0:T(8,128)(2,1)S(1)}, u32[]{:S(2)}, u32[]{:S(2)}) collective-permute-start(bf16[32,3712]{1,0:T(8,128)(2,1)S(1)} %shard_map.72.refs_5_), channel_id=1, source_target_pairs={{0,1},{1,0},{2,3},{3,2},{4,5},{5,4},{6,7},{7,6},{8,9},{9,8},{10,11... | collective-permute-start | bytes 712712 | tf_op jit(solution)/shard_map/ppermute | solution.py:34
  23.9 1.7 %collective-permute-start.5 = (bf16[32,3584]{1,0:T(8,128)(2,1)S(1)}, bf16[32,3584]{1,0:T(8,128)(2,1)S(1)}, u32[]{:S(2)}, u32[]{:S(2)}) collective-permute-start(bf16[32,3584]{1,0:T(8,128)(2,1)S(1)} %shard_map.68.refs_1_.refs_0_), channel_id=1, source_target_pairs={{0,1},{1,0},{2,3},{3,2},{4,5},{5,4},{6,7},{7,6},{8,9},{9,8},{10,11... | collective-permute-start | bytes 688136 | tf_op jit(solution)/shard_map/ppermute | solution.py:34
  24.8 1.5 %collective-permute-start.6 = (bf16[32,3584]{1,0:T(8,128)(2,1)S(1)}, bf16[32,3584]{1,0:T(8,128)(2,1)S(1)}, u32[]{:S(2)}, u32[]{:S(2)}) collective-permute-start(bf16[32,3584]{1,0:T(8,128)(2,1)S(1)} %shard_map.70.refs_1_), channel_id=1, source_target_pairs={{0,1},{1,0},{2,3},{3,2},{4,5},{5,4},{6,7},{7,6},{8,9},{9,8},{10,11... | collective-permute-start | bytes 688136 | tf_op jit(solution)/shard_map/ppermute | solution.py:34
  50.6 1.9 %collective-permute-start.11 = (bf16[64,3584]{1,0:T(8,128)(2,1)S(1)}, bf16[64,3584]{1,0:T(8,128)(2,1)S(1)}, u32[]{:S(2)}, u32[]{:S(2)}) collective-permute-start(bf16[64,3584]{1,0:T(8,128)(2,1)S(1)} %get-tuple-element.42), channel_id=1, source_target_pairs={{0,1},{1,0},{2,3},{3,2},{4,5},{5,4},{6,7},{7,6},{8,9},{9,8},{10,11... | collective-permute-start | bytes 1376264 | tf_op jit(solution)/shard_map/ppermute | solution.py:34
  50.8 3.5 %collective-permute-start.17 = (bf16[64,3584]{1,0:T(8,128)(2,1)S(1)}, bf16[64,3584]{1,0:T(8,128)(2,1)S(1)}, u32[]{:S(2)}, u32[]{:S(2)}) collective-permute-start(bf16[64,3584]{1,0:T(8,128)(2,1)S(1)} %get-tuple-element.52), channel_id=1, source_target_pairs={{0,1},{1,0},{2,3},{3,2},{4,5},{5,4},{6,7},{7,6},{8,9},{9,8},{10,11... | collective-permute-start | bytes 1376264 | tf_op jit(solution)/shard_map/ppermute | solution.py:34
  52.6 6.1 %collective-permute-start.12 = (bf16[32,3584]{1,0:T(8,128)(2,1)S(1)}, bf16[32,3584]{1,0:T(8,128)(2,1)S(1)}, u32[]{:S(2)}, u32[]{:S(2)}) collective-permute-start(bf16[32,3584]{1,0:T(8,128)(2,1)S(1)} %get-tuple-element.44), channel_id=1, source_target_pairs={{0,16},{1,9},{2,18},{3,11},{4,20},{5,13},{6,22},{7,15},{8,24},{9,1... | collective-permute-start | bytes 688136 | tf_op jit(solution)/shard_map/ppermute | solution.py:42
  54.4 7.1 %collective-permute-start.18 = (bf16[32,3584]{1,0:T(8,128)(2,1)S(1)}, bf16[32,3584]{1,0:T(8,128)(2,1)S(1)}, u32[]{:S(2)}, u32[]{:S(2)}) collective-permute-start(bf16[32,3584]{1,0:T(8,128)(2,1)S(1)} %get-tuple-element.54), channel_id=1, source_target_pairs={{0,16},{1,9},{2,18},{3,11},{4,20},{5,13},{6,22},{7,15},{8,24},{9,1... | collective-permute-start | bytes 688136 | tf_op jit(solution)/shard_map/ppermute | solution.py:42
  58.7 4.9 %collective-permute-start.13 = (bf16[16,3584]{1,0:T(8,128)(2,1)S(1)}, bf16[16,3584]{1,0:T(8,128)(2,1)S(1)}, u32[]{:S(2)}, u32[]{:S(2)}) collective-permute-start(bf16[16,3584]{1,0:T(8,128)(2,1)S(1)} %get-tuple-element.46), channel_id=1, source_target_pairs={{0,8},{1,17},{2,10},{3,19},{4,12},{5,21},{6,14},{7,23},{8,0},{9,25... | collective-permute-start | bytes 344072 | tf_op jit(solution)/shard_map/ppermute | solution.py:42
  61.6 6.5 %collective-permute-start.19 = (bf16[16,3584]{1,0:T(8,128)(2,1)S(1)}, bf16[16,3584]{1,0:T(8,128)(2,1)S(1)}, u32[]{:S(2)}, u32[]{:S(2)}) collective-permute-start(bf16[16,3584]{1,0:T(8,128)(2,1)S(1)} %get-tuple-element.56), channel_id=1, source_target_pairs={{0,8},{1,17},{2,10},{3,19},{4,12},{5,21},{6,14},{7,23},{8,0},{9,25... | collective-permute-start | bytes 344072 | tf_op jit(solution)/shard_map/ppermute | solution.py:42
  63.6 8.8 %collective-permute-start.14 = (bf16[4,3584]{1,0:T(4,128)(2,1)S(1)}, bf16[4,3584]{1,0:T(4,128)(2,1)S(1)}, u32[]{:S(2)}, u32[]{:S(2)}) collective-permute-start(bf16[4,3584]{1,0:T(4,128)(2,1)S(1)} %get-tuple-element.48), channel_id=1, source_target_pairs={{0,2},{1,3},{2,0},{3,1},{4,6},{5,7},{6,4},{7,5},{8,10},{9,11},{10,... | collective-permute-start | bytes 86024 | tf_op jit(solution)/shard_map/ppermute | solution.py:34
  64.9 7.6 %collective-permute-start.15 = (bf16[4,3584]{1,0:T(4,128)(2,1)S(1)}, bf16[4,3584]{1,0:T(4,128)(2,1)S(1)}, u32[]{:S(2)}, u32[]{:S(2)}) collective-permute-start(bf16[4,3584]{1,0:T(4,128)(2,1)S(1)} %get-tuple-element.49), channel_id=1, source_target_pairs={{0,4},{1,5},{2,6},{3,7},{4,0},{5,1},{6,2},{7,3},{8,12},{9,13},{10,... | collective-permute-start | bytes 86024 | tf_op jit(solution)/shard_map/ppermute | solution.py:34
  67.9 5.7 %collective-permute-start.16 = (bf16[4,3584]{1,0:T(4,128)(2,1)S(1)}, bf16[4,3584]{1,0:T(4,128)(2,1)S(1)}, u32[]{:S(2)}, u32[]{:S(2)}) collective-permute-start(bf16[4,3584]{1,0:T(4,128)(2,1)S(1)} %get-tuple-element.50), channel_id=1, source_target_pairs={{0,6},{1,7},{2,4},{3,5},{4,2},{5,3},{6,0},{7,1},{8,14},{9,15},{10,... | collective-permute-start | bytes 86024 | tf_op jit(solution)/shard_map/ppermute | solution.py:34
  68.1 5.5 %collective-permute-start.20 = (bf16[4,3584]{1,0:T(4,128)(2,1)S(1)}, bf16[4,3584]{1,0:T(4,128)(2,1)S(1)}, u32[]{:S(2)}, u32[]{:S(2)}) collective-permute-start(bf16[4,3584]{1,0:T(4,128)(2,1)S(1)} %get-tuple-element.58), channel_id=1, source_target_pairs={{0,2},{1,3},{2,0},{3,1},{4,6},{5,7},{6,4},{7,5},{8,10},{9,11},{10,... | collective-permute-start | bytes 86024 | tf_op jit(solution)/shard_map/ppermute | solution.py:34
  68.5 6.3 %collective-permute-start.21 = (bf16[4,3584]{1,0:T(4,128)(2,1)S(1)}, bf16[4,3584]{1,0:T(4,128)(2,1)S(1)}, u32[]{:S(2)}, u32[]{:S(2)}) collective-permute-start(bf16[4,3584]{1,0:T(4,128)(2,1)S(1)} %get-tuple-element.59), channel_id=1, source_target_pairs={{0,4},{1,5},{2,6},{3,7},{4,0},{5,1},{6,2},{7,3},{8,12},{9,13},{10,... | collective-permute-start | bytes 86024 | tf_op jit(solution)/shard_map/ppermute | solution.py:34
  72.4 5.7 %collective-permute-start.22 = (bf16[4,3584]{1,0:T(4,128)(2,1)S(1)}, bf16[4,3584]{1,0:T(4,128)(2,1)S(1)}, u32[]{:S(2)}, u32[]{:S(2)}) collective-permute-start(bf16[4,3584]{1,0:T(4,128)(2,1)S(1)} %get-tuple-element.60), channel_id=1, source_target_pairs={{0,6},{1,7},{2,4},{3,5},{4,2},{5,3},{6,0},{7,1},{8,14},{9,15},{10,... | collective-permute-start | bytes 86024 | tf_op jit(solution)/shard_map/ppermute | solution.py:34

commit v11 on v10

--- a/solution.py
+++ b/solution.py
@@ -13,7 +13,7 @@
 VMEM = pltpu.VMEM
 UNIT_BLOCK = 256
 DOWN_BLOCK = 512
-RING = 5
+RING = 3
 DOWN_RING = 5
 FOLD_BLOCK = 1024
 
@@ -30,8 +30,9 @@
     return [pl.BlockSpec(memory_space=VMEM)] * count
 
 
-def swap(value, axis, size, mask):
-    return lax.ppermute(value, axis, [(i, i ^ mask) for i in range(size)])
+def swap(value, axis, size, masks):
+    masks = masks if isinstance(masks, tuple) else (masks, masks)
+    return lax.ppermute(value, axis, [(i, i ^ masks[i % 2]) for i in range(size)])
 
 
 def swap_group(value, groups, members, masks):
@@ -301,7 +302,12 @@
     while lines > 1:
         radix = min(4, lines)
         lines //= radix
-        steps.append([2 * lines * m for m in range(1, radix)])
+        near, wide = 2 * lines, 4 * lines
+        if radix == 4:
+            out = [(wide, near), (near, wide), (near + wide, near + wide)]
+            steps.append((out, [(near, wide), (wide, near)]))
+        else:
+            steps.append(([(near, near)], [(near, near)]))
     return steps
 
 
@@ -310,12 +316,11 @@
     for masks in [(2, 1), (1, 2)]:
         keep, send = fold(values, 2)
         values = [keep, swap_group(send, groups, members, masks)]
-    for masks in reversed(line_steps(members // 2)):
-        keep, *sends = fold(values, len(masks) + 1)
-        values = [keep] + [swap(v, "expert", members, m) for v, m in zip(sends, masks)]
-    total = values[0].astype(jnp.float32)
-    for value in values[1:]:
-        total = total + value.astype(jnp.float32)
+    for _, back in reversed(line_steps(members // 2)):
+        for masks in back:
+            keep, send = fold(values, 2)
+            values = [keep, swap(send, "expert", members, masks)]
+    total = values[0].astype(jnp.float32) + values[1].astype(jnp.float32)
     return total.astype(jnp.bfloat16)
 
 
@@ -326,11 +331,14 @@
     me = lax.axis_index("group") * EXP_GRP + lax.axis_index("expert") // split
     me = me.astype(jnp.int32).reshape(1)
     blocks = w_gate.shape[2] // UNIT_BLOCK
-    gates, ups = max(1, blocks // 2), max(1, blocks // 4)
-    cuts = [0, max(1, gates * 3 // 4), gates, gates]
+    gates, ups = max(1, blocks * 5 // 8), max(1, blocks // 2)
+    gate_cuts = [0, max(1, gates * 3 // 5), gates, gates]
+    up_cuts = [0, 0, ups // 4, ups]
     jobs, place, count = [], {}, 0
     for n in range(3):
-        pieces = [(0, list(range(cuts[n], cuts[n + 1]))), (1, list(range(ups)) if n == 2 else [])]
+        pieces = [
+            (m, list(range(cuts[n], cuts[n + 1]))) for m, cuts in enumerate([gate_cuts, up_cuts])
+        ]
         job = []
         for m, inside in pieces:
             if inside:
@@ -349,16 +357,13 @@
     width = tokens.shape[1] // 2
     halves = [(0, width), (width, width + LANES)]
     held, mark = fetch(jobs[0], value)
-    steps = line_steps(members // 2)
-    for n, masks in enumerate(steps):
+    for masks, _ in line_steps(members // 2):
         line = [value] + [swap(value, "expert", members, m) for m in masks]
-        value, *other = join(line, mark, halves if n == len(steps) - 1 else None)
-    a, b = value, other[0]
-    a_got, b_got = [swap_group(v, groups, members, (1, 2)) for v in (a, b)]
-    more, mark = fetch(jobs[1], a)
+        (value,) = join(line, mark)
+    got = swap_group(value, groups, members, (1, 2))
+    more, mark = fetch(jobs[1], value)
     held += more
-    (a,) = join([a, a_got], mark)
-    (b,) = join([b, b_got], mark)
+    a, b = join([value, got], mark, halves)
     a_got, b_got = [swap_group(v, groups, members, (2, 1)) for v in (a, b)]
     a_core, b_core = swap(a, "expert", members, 1), swap(b, "expert", members, 1)
     more, mark = fetch(jobs[2], a)

time: 78.9 us -> 75.1 us (0.952)
  waiting for transfers between devices: 15.9 us -> 13.6 us
  starting transfers between devices: 26.6 us -> 24.5 us
    pallas_call x3, Pallas kernels: 9.6 us -> 12.9 us  [fetch(): pl.pallas_call(functools.partial(fetch_kernel, jobs), in_specs=[hbm] * le...]
    ppermute x15 -> x13, waiting for transfers between devices: 8.36 us -> 5.63 us  [swap(): lax.ppermute(value, axis, [(i, i ^ masks[i % 2]) for i in range(size)])]
    pallas_call x1, Pallas kernels: 24.3 us -> 21.7 us  [run_expert(): pl.pallas_call(functools.partial(expert_kernel, place, order, streams, le...]
    ppermute x8 -> x7, starting transfers between devices: 10.8 us -> 9.01 us  [swap_group(): return lax.ppermute(value, AXES, pairs)]
    ppermute x8 -> x7, waiting for transfers between devices: 7.52 us -> 7.96 us  [swap_group(): return lax.ppermute(value, AXES, pairs)]
    ppermute x15 -> x13, starting transfers between devices: 15.9 us -> 15.5 us  [swap(): lax.ppermute(value, axis, [(i, i ^ masks[i % 2]) for i in range(size)])]
  transfers between devices with their start and end apart: 23 -> 20, of which waited for: 13 -> 11; matrix products, arithmetic and copies ran while one was open for 0% -> 0% of each run, Pallas kernels for 13% -> 18%
where the time goes in v11:
time: 75.1 us; the launch traced here: 74.9 us
  Pallas kernels  36 us (48%)
  starting transfers between devices  24.5 us (33%)
  waiting for transfers between devices  13.6 us (18%)
    pallas_call x1, Pallas kernels, run_expert(): pl.pallas_call(functools.partial(expert_kernel, place, order, streams, le...  21.7 us
    ppermute x13, starting transfers between devices, swap(): lax.ppermute(value, axis, [(i, i ^ masks[i % 2]) for i in range(size)])  15.5 us
    pallas_call x3, Pallas kernels, fetch(): pl.pallas_call(functools.partial(fetch_kernel, jobs), in_specs=[hbm] * le...  12.9 us
    ppermute x7, starting transfers between devices, swap_group(): return lax.ppermute(value, AXES, pairs)  9.01 us
    ppermute x7, waiting for transfers between devices, swap_group(): return lax.ppermute(value, AXES, pairs)  7.96 us
    ppermute x13, waiting for transfers between devices, swap(): lax.ppermute(value, axis, [(i, i ^ masks[i % 2]) for i in range(size)])  5.63 us
  transfers between devices with their start and end apart: 20, of which 11 were waited for; matrix products, arithmetic and copies ran while one was open for 0% of the time, Pallas kernels for 18%

profile of v11, /device:TPU:0, one launch (start us, length us, event | category | flops | bytes accessed | tf_op | source)
XLA Modules:
  0.0 74.9 jit_solution(16942026148440965033)
XLA Ops:
  0.0 0.9 %shard_map.64.refs_1_.refs_0_ = bf16[4,7296]{1,0:T(4,128)(2,1)S(1)} custom-call(s32[1]{0:T(128)} %bitcast.me_ref.refs_15_, bf16[4,7168]{1,0:T(4,128)(2,1)} %tokens_ref.1, s32[4,8]{1,0:T(4,128)} %ids_ref.1, bf16[4,8]{1,0:T(4,128)(2,1)} %weights_ref.1), custom_call_target="tpu_custom_call" | custom-call | tf_op jit(solution)/shard_map/pallas_call | solution.py:69
  0.9 5.1 %collective-permute-start.2 = (bf16[4,7296]{1,0:T(4,128)(2,1)S(1)}, bf16[4,7296]{1,0:T(4,128)(2,1)S(1)}, u32[]{:S(2)}, u32[]{:S(2)}) collective-permute-start(bf16[4,7296]{1,0:T(4,128)(2,1)S(1)} %shard_map.64.refs_1_.refs_0_), channel_id=1, source_target_pairs={{0,6},{1,7},{2,4},{3,5},{4,2},{5,3},{6,0},{7,1},{8,14},{9,15},{10,... | collective-permute-start | bytes 175112 | tf_op jit(solution)/shard_map/ppermute | solution.py:35
  6.0 0.0 collective-permute-start.1
  6.1 0.6 collective-permute-start
  6.7 4.3 %shard_map.65 = (bf16[7168,768]{1,0:T(8,128)(2,1)S(1)}, f32[8,128]{1,0:T(8,128)S(1)}) custom-call(bf16[1,7168,2048]{2,1,0:T(8,128)(2,1)} %refs_12_.1, bf16[4,7296]{1,0:T(4,128)(2,1)S(1)} %shard_map.64.refs_1_.refs_0_), custom_call_target="tpu_custom_call" | custom-call | bytes 11010048 | tf_op jit(solution)/shard_map/pallas_call | solution.py:107
  11.0 0.0 collective-permute-done.2.refs_3_
  11.0 0.0 collective-permute-done.1.refs_2_
  11.0 0.1 collective-permute-done.refs_1_
  11.1 0.1 shard_map.66.refs_2_.refs_0_
  11.2 1.6 %collective-permute-start.3 = (bf16[16,7296]{1,0:T(8,128)(2,1)S(1)}, bf16[16,7296]{1,0:T(8,128)(2,1)S(1)}, u32[]{:S(2)}, u32[]{:S(2)}) collective-permute-start(bf16[16,7296]{1,0:T(8,128)(2,1)S(1)} %shard_map.66.refs_2_.refs_0_), channel_id=1, source_target_pairs={{0,8},{1,17},{2,10},{3,19},{4,12},{5,21},{6,14},{7,23},{8,0},{9,25... | collective-permute-start | bytes 700424 | tf_op jit(solution)/shard_map/ppermute | solution.py:43
  12.8 4.3 %shard_map.67 = (bf16[7168,512]{1,0:T(8,128)(2,1)S(1)}, bf16[7168,256]{1,0:T(8,128)(2,1)S(1)}, f32[8,128]{1,0:T(8,128)S(1)}) custom-call(bf16[1,7168,2048]{2,1,0:T(8,128)(2,1)} %refs_12_.1, bf16[1,7168,2048]{2,1,0:T(8,128)(2,1)} %refs_13_.1, bf16[16,7296]{1,0:T(8,128)(2,1)S(1)} %shard_map.66.refs_2_.refs_0_), custom_call_target="tpu_custom_call" | custom-call | bytes 11010048 | tf_op jit(solution)/shard_map/pallas_call | solution.py:107
  17.1 0.2 collective-permute-done.3.refs_1_
  17.4 1.6 %collective-permute-start.7 = (bf16[32,3712]{1,0:T(8,128)(2,1)S(1)}, bf16[32,3712]{1,0:T(8,128)(2,1)S(1)}, u32[]{:S(2)}, u32[]{:S(2)}) collective-permute-start(bf16[32,3712]{1,0:T(8,128)(2,1)S(1)} %get-tuple-element.38.refs_4_), channel_id=1, source_target_pairs={{0,16},{1,9},{2,18},{3,11},{4,20},{5,13},{6,22},{7,15},{8,24},{9,1... | collective-permute-start | bytes 712712 | tf_op jit(solution)/shard_map/ppermute | solution.py:43
  19.0 0.5 collective-permute-start.4
  19.5 0.0 collective-permute-start.8
  19.5 4.3 %shard_map.69 = (bf16[7168,768]{1,0:T(8,128)(2,1)S(1)}, f32[8,128]{1,0:T(8,128)S(1)}) custom-call(bf16[1,7168,2048]{2,1,0:T(8,128)(2,1)} %refs_13_.1, bf16[32,3584]{1,0:T(8,128)(2,1)S(1)} %get-tuple-element.36.refs_1_.refs_0_), custom_call_target="tpu_custom_call" | custom-call | bytes 11010048 | tf_op jit(solution)/shard_map/pallas_call | solution.py:107
  23.8 0.0 collective-permute-done.7.refs_0_
  23.8 0.6 collective-permute-start.9
  24.3 0.1 collective-permute-start.5
  24.4 1.6 %collective-permute-done.4.refs_0_ = bf16[32,3584]{1,0:T(8,128)(2,1)S(1)} collective-permute-done((bf16[32,3584]{1,0:T(8,128)(2,1)S(1)}, bf16[32,3584]{1,0:T(8,128)(2,1)S(1)}, u32[]{:S(2)}, u32[]{:S(2)}) %collective-permute-start.4) | collective-permute-done | bytes 229408 | tf_op jit(solution)/shard_map/ppermute | solution.py:43
  26.0 0.0 collective-permute-start.6
  26.0 0.0 collective-permute-done.5.refs_2_
  26.0 0.0 collective-permute-done.8.refs_6_
  26.0 1.5 %collective-permute-done.6.refs_3_ = bf16[32,3584]{1,0:T(8,128)(2,1)S(1)} collective-permute-done((bf16[32,3584]{1,0:T(8,128)(2,1)S(1)}, bf16[32,3584]{1,0:T(8,128)(2,1)S(1)}, u32[]{:S(2)}, u32[]{:S(2)}) %collective-permute-start.6) | collective-permute-done | bytes 229408 | tf_op jit(solution)/shard_map/ppermute | solution.py:35
  27.5 0.0 collective-permute-done.9.refs_7_
  27.5 21.7 %shard_map.72 = (bf16[64,3584]{1,0:T(8,128)(2,1)S(1)}, bf16[64,3584]{1,0:T(8,128)(2,1)S(1)}, bf16[64,3584]{1,0:T(8,128)(2,1)S(1)}, bf16[64,3584]{1,0:T(8,128)(2,1)S(1)}) custom-call(bf16[32,3584]{1,0:T(8,128)(2,1)S(1)} %get-tuple-element.36.refs_1_.refs_0_, bf16[32,3584]{1,0:T(8,128)(2,1)S(1)} %shard_map.70.refs_1_, ...), custom_call_target="tpu_custom_call" | custom-call | flops 11274289152 | bytes 58720256 | tf_op jit(solution)/shard_map/pallas_call | solution.py:258
  49.2 0.2 collective-permute-start.10
  49.4 0.4 collective-permute-start.15
  49.7 1.3 %collective-permute-done.10.refs_1_ = bf16[64,3584]{1,0:T(8,128)(2,1)S(1)} collective-permute-done((bf16[64,3584]{1,0:T(8,128)(2,1)S(1)}, bf16[64,3584]{1,0:T(8,128)(2,1)S(1)}, u32[]{:S(2)}, u32[]{:S(2)}) %collective-permute-start.10) | collective-permute-done | bytes 458784 | tf_op jit(solution)/shard_map/ppermute | solution.py:35
  51.1 0.1 shard_map.73
  51.2 1.6 %collective-permute-start.11 = (bf16[32,3584]{1,0:T(8,128)(2,1)S(1)}, bf16[32,3584]{1,0:T(8,128)(2,1)S(1)}, u32[]{:S(2)}, u32[]{:S(2)}) collective-permute-start(bf16[32,3584]{1,0:T(8,128)(2,1)S(1)} %get-tuple-element.46), channel_id=1, source_target_pairs={{0,16},{1,9},{2,18},{3,11},{4,20},{5,13},{6,22},{7,15},{8,24},{9,1... | collective-permute-start | bytes 688136 | tf_op jit(solution)/shard_map/ppermute | solution.py:43
  52.8 0.1 shard_map.77
  52.9 0.5 collective-permute-start.16
  53.4 3.8 %collective-permute-done.11.refs_1_ = bf16[32,3584]{1,0:T(8,128)(2,1)S(1)} collective-permute-done((bf16[32,3584]{1,0:T(8,128)(2,1)S(1)}, bf16[32,3584]{1,0:T(8,128)(2,1)S(1)}, u32[]{:S(2)}, u32[]{:S(2)}) %collective-permute-start.11) | collective-permute-done | bytes 229408 | tf_op jit(solution)/shard_map/ppermute | solution.py:43
  57.3 0.1 shard_map.74
  57.3 1.6 %collective-permute-start.12 = (bf16[16,3584]{1,0:T(8,128)(2,1)S(1)}, bf16[16,3584]{1,0:T(8,128)(2,1)S(1)}, u32[]{:S(2)}, u32[]{:S(2)}) collective-permute-start(bf16[16,3584]{1,0:T(8,128)(2,1)S(1)} %get-tuple-element.48), channel_id=1, source_target_pairs={{0,8},{1,17},{2,10},{3,19},{4,12},{5,21},{6,14},{7,23},{8,0},{9,25... | collective-permute-start | bytes 344072 | tf_op jit(solution)/shard_map/ppermute | solution.py:43
  58.9 1.2 %collective-permute-done.16.refs_1_ = bf16[32,3584]{1,0:T(8,128)(2,1)S(1)} collective-permute-done((bf16[32,3584]{1,0:T(8,128)(2,1)S(1)}, bf16[32,3584]{1,0:T(8,128)(2,1)S(1)}, u32[]{:S(2)}, u32[]{:S(2)}) %collective-permute-start.16) | collective-permute-done | bytes 229408 | tf_op jit(solution)/shard_map/ppermute | solution.py:43
  60.1 0.1 shard_map.78
  60.2 1.6 %collective-permute-start.17 = (bf16[16,3584]{1,0:T(8,128)(2,1)S(1)}, bf16[16,3584]{1,0:T(8,128)(2,1)S(1)}, u32[]{:S(2)}, u32[]{:S(2)}) collective-permute-start(bf16[16,3584]{1,0:T(8,128)(2,1)S(1)} %get-tuple-element.58), channel_id=1, source_target_pairs={{0,8},{1,17},{2,10},{3,19},{4,12},{5,21},{6,14},{7,23},{8,0},{9,25... | collective-permute-start | bytes 344072 | tf_op jit(solution)/shard_map/ppermute | solution.py:43
  61.7 0.4 collective-permute-done.12.refs_1_
  62.2 2.1 %collective-permute-start.13 = (bf16[8,3584]{1,0:T(8,128)(2,1)S(1)}, bf16[8,3584]{1,0:T(8,128)(2,1)S(1)}, u32[]{:S(2)}, u32[]{:S(2)}) collective-permute-start(bf16[8,3584]{1,0:T(8,128)(2,1)S(1)} %get-tuple-element.50), channel_id=1, source_target_pairs={{0,2},{1,5},{2,0},{3,7},{4,6},{5,1},{6,4},{7,3},{8,10},{9,13},{10,... | collective-permute-start | bytes 172040 | tf_op jit(solution)/shard_map/ppermute | solution.py:35
  64.3 0.7 collective-permute-done.17.refs_1_
  65.0 2.1 %collective-permute-start.18 = (bf16[8,3584]{1,0:T(8,128)(2,1)S(1)}, bf16[8,3584]{1,0:T(8,128)(2,1)S(1)}, u32[]{:S(2)}, u32[]{:S(2)}) collective-permute-start(bf16[8,3584]{1,0:T(8,128)(2,1)S(1)} %get-tuple-element.60), channel_id=1, source_target_pairs={{0,2},{1,5},{2,0},{3,7},{4,6},{5,1},{6,4},{7,3},{8,10},{9,13},{10,... | collective-permute-start | bytes 172040 | tf_op jit(solution)/shard_map/ppermute | solution.py:35
  67.2 2.2 %collective-permute-start.14 = (bf16[4,3584]{1,0:T(4,128)(2,1)S(1)}, bf16[4,3584]{1,0:T(4,128)(2,1)S(1)}, u32[]{:S(2)}, u32[]{:S(2)}) collective-permute-start(bf16[4,3584]{1,0:T(4,128)(2,1)S(1)} %get-tuple-element.52), channel_id=1, source_target_pairs={{0,4},{1,3},{2,6},{3,1},{4,0},{5,7},{6,2},{7,5},{8,12},{9,11},{10,... | collective-permute-start | bytes 86024 | tf_op jit(solution)/shard_map/ppermute | solution.py:35
  69.4 2.1 %collective-permute-start.19 = (bf16[4,3584]{1,0:T(4,128)(2,1)S(1)}, bf16[4,3584]{1,0:T(4,128)(2,1)S(1)}, u32[]{:S(2)}, u32[]{:S(2)}) collective-permute-start(bf16[4,3584]{1,0:T(4,128)(2,1)S(1)} %get-tuple-element.62), channel_id=1, source_target_pairs={{0,4},{1,3},{2,6},{3,1},{4,0},{5,7},{6,2},{7,5},{8,12},{9,11},{10,... | collective-permute-start | bytes 86024 | tf_op jit(solution)/shard_map/ppermute | solution.py:35
  71.6 0.4 collective-permute-done.14
  72.0 2.2 %collective-permute-done.19 = bf16[4,3584]{1,0:T(4,128)(2,1)S(1)} collective-permute-done((bf16[4,3584]{1,0:T(4,128)(2,1)S(1)}, bf16[4,3584]{1,0:T(4,128)(2,1)S(1)}, u32[]{:S(2)}, u32[]{:S(2)}) %collective-permute-start.19) | collective-permute-done | bytes 28704 | tf_op jit(solution)/shard_map/ppermute | solution.py:35
  74.3 0.7 pad_maximum_fusion
  (12 shorter events, 0.2 us)
Async XLA Ops:
  0.9 10.1 %collective-permute-start.2 = (bf16[4,7296]{1,0:T(4,128)(2,1)S(1)}, bf16[4,7296]{1,0:T(4,128)(2,1)S(1)}, u32[]{:S(2)}, u32[]{:S(2)}) collective-permute-start(bf16[4,7296]{1,0:T(4,128)(2,1)S(1)} %shard_map.64.refs_1_.refs_0_), channel_id=1, source_target_pairs={{0,6},{1,7},{2,4},{3,5},{4,2},{5,3},{6,0},{7,1},{8,14},{9,15},{10,... | collective-permute-start | bytes 175112 | tf_op jit(solution)/shard_map/ppermute | solution.py:35
  6.0 4.9 %collective-permute-start.1 = (bf16[4,7296]{1,0:T(4,128)(2,1)S(1)}, bf16[4,7296]{1,0:T(4,128)(2,1)S(1)}, u32[]{:S(2)}, u32[]{:S(2)}) collective-permute-start(bf16[4,7296]{1,0:T(4,128)(2,1)S(1)} %shard_map.64.refs_1_.refs_0_), channel_id=1, source_target_pairs={{0,2},{1,5},{2,0},{3,7},{4,6},{5,1},{6,4},{7,3},{8,10},{9,13},{10,... | collective-permute-start | bytes 175112 | tf_op jit(solution)/shard_map/ppermute | solution.py:35
  6.1 5.1 %collective-permute-start = (bf16[4,7296]{1,0:T(4,128)(2,1)S(1)}, bf16[4,7296]{1,0:T(4,128)(2,1)S(1)}, u32[]{:S(2)}, u32[]{:S(2)}) collective-permute-start(bf16[4,7296]{1,0:T(4,128)(2,1)S(1)} %shard_map.64.refs_1_.refs_0_), channel_id=1, source_target_pairs={{0,4},{1,3},{2,6},{3,1},{4,0},{5,7},{6,2},{7,5},{8,12},{9,11},{10,... | collective-permute-start | bytes 175112 | tf_op jit(solution)/shard_map/ppermute | solution.py:35
  11.2 6.1 %collective-permute-start.3 = (bf16[16,7296]{1,0:T(8,128)(2,1)S(1)}, bf16[16,7296]{1,0:T(8,128)(2,1)S(1)}, u32[]{:S(2)}, u32[]{:S(2)}) collective-permute-start(bf16[16,7296]{1,0:T(8,128)(2,1)S(1)} %shard_map.66.refs_2_.refs_0_), channel_id=1, source_target_pairs={{0,8},{1,17},{2,10},{3,19},{4,12},{5,21},{6,14},{7,23},{8,0},{9,25... | collective-permute-start | bytes 700424 | tf_op jit(solution)/shard_map/ppermute | solution.py:43
  17.4 6.4 %collective-permute-start.7 = (bf16[32,3712]{1,0:T(8,128)(2,1)S(1)}, bf16[32,3712]{1,0:T(8,128)(2,1)S(1)}, u32[]{:S(2)}, u32[]{:S(2)}) collective-permute-start(bf16[32,3712]{1,0:T(8,128)(2,1)S(1)} %get-tuple-element.38.refs_4_), channel_id=1, source_target_pairs={{0,16},{1,9},{2,18},{3,11},{4,20},{5,13},{6,22},{7,15},{8,24},{9,1... | collective-permute-start | bytes 712712 | tf_op jit(solution)/shard_map/ppermute | solution.py:43
  19.0 7.0 %collective-permute-start.4 = (bf16[32,3584]{1,0:T(8,128)(2,1)S(1)}, bf16[32,3584]{1,0:T(8,128)(2,1)S(1)}, u32[]{:S(2)}, u32[]{:S(2)}) collective-permute-start(bf16[32,3584]{1,0:T(8,128)(2,1)S(1)} %get-tuple-element.36.refs_1_.refs_0_), channel_id=1, source_target_pairs={{0,16},{1,9},{2,18},{3,11},{4,20},{5,13},{6,22},{7,15},{8,24},{9,1... | collective-permute-start | bytes 688136 | tf_op jit(solution)/shard_map/ppermute | solution.py:43
  19.5 6.6 %collective-permute-start.8 = (bf16[32,3712]{1,0:T(8,128)(2,1)S(1)}, bf16[32,3712]{1,0:T(8,128)(2,1)S(1)}, u32[]{:S(2)}, u32[]{:S(2)}) collective-permute-start(bf16[32,3712]{1,0:T(8,128)(2,1)S(1)} %get-tuple-element.38.refs_4_), channel_id=1, source_target_pairs={{0,1},{1,0},{2,3},{3,2},{4,5},{5,4},{6,7},{7,6},{8,9},{9,8},{10,11... | collective-permute-start | bytes 712712 | tf_op jit(solution)/shard_map/ppermute | solution.py:35
  23.8 3.7 %collective-permute-start.9 = (bf16[32,3712]{1,0:T(8,128)(2,1)S(1)}, bf16[32,3712]{1,0:T(8,128)(2,1)S(1)}, u32[]{:S(2)}, u32[]{:S(2)}) collective-permute-start(bf16[32,3712]{1,0:T(8,128)(2,1)S(1)} %shard_map.71.refs_5_), channel_id=1, source_target_pairs={{0,1},{1,0},{2,3},{3,2},{4,5},{5,4},{6,7},{7,6},{8,9},{9,8},{10,11... | collective-permute-start | bytes 712712 | tf_op jit(solution)/shard_map/ppermute | solution.py:35
  24.3 1.7 %collective-permute-start.5 = (bf16[32,3584]{1,0:T(8,128)(2,1)S(1)}, bf16[32,3584]{1,0:T(8,128)(2,1)S(1)}, u32[]{:S(2)}, u32[]{:S(2)}) collective-permute-start(bf16[32,3584]{1,0:T(8,128)(2,1)S(1)} %get-tuple-element.36.refs_1_.refs_0_), channel_id=1, source_target_pairs={{0,1},{1,0},{2,3},{3,2},{4,5},{5,4},{6,7},{7,6},{8,9},{9,8},{10,11... | collective-permute-start | bytes 688136 | tf_op jit(solution)/shard_map/ppermute | solution.py:35
  26.0 1.5 %collective-permute-start.6 = (bf16[32,3584]{1,0:T(8,128)(2,1)S(1)}, bf16[32,3584]{1,0:T(8,128)(2,1)S(1)}, u32[]{:S(2)}, u32[]{:S(2)}) collective-permute-start(bf16[32,3584]{1,0:T(8,128)(2,1)S(1)} %shard_map.70.refs_1_), channel_id=1, source_target_pairs={{0,1},{1,0},{2,3},{3,2},{4,5},{5,4},{6,7},{7,6},{8,9},{9,8},{10,11... | collective-permute-start | bytes 688136 | tf_op jit(solution)/shard_map/ppermute | solution.py:35
  49.2 1.9 %collective-permute-start.10 = (bf16[64,3584]{1,0:T(8,128)(2,1)S(1)}, bf16[64,3584]{1,0:T(8,128)(2,1)S(1)}, u32[]{:S(2)}, u32[]{:S(2)}) collective-permute-start(bf16[64,3584]{1,0:T(8,128)(2,1)S(1)} %get-tuple-element.44), channel_id=1, source_target_pairs={{0,1},{1,0},{2,3},{3,2},{4,5},{5,4},{6,7},{7,6},{8,9},{9,8},{10,11... | collective-permute-start | bytes 1376264 | tf_op jit(solution)/shard_map/ppermute | solution.py:35
  49.4 3.4 %collective-permute-start.15 = (bf16[64,3584]{1,0:T(8,128)(2,1)S(1)}, bf16[64,3584]{1,0:T(8,128)(2,1)S(1)}, u32[]{:S(2)}, u32[]{:S(2)}) collective-permute-start(bf16[64,3584]{1,0:T(8,128)(2,1)S(1)} %get-tuple-element.54), channel_id=1, source_target_pairs={{0,1},{1,0},{2,3},{3,2},{4,5},{5,4},{6,7},{7,6},{8,9},{9,8},{10,11... | collective-permute-start | bytes 1376264 | tf_op jit(solution)/shard_map/ppermute | solution.py:35
  51.2 6.1 %collective-permute-start.11 = (bf16[32,3584]{1,0:T(8,128)(2,1)S(1)}, bf16[32,3584]{1,0:T(8,128)(2,1)S(1)}, u32[]{:S(2)}, u32[]{:S(2)}) collective-permute-start(bf16[32,3584]{1,0:T(8,128)(2,1)S(1)} %get-tuple-element.46), channel_id=1, source_target_pairs={{0,16},{1,9},{2,18},{3,11},{4,20},{5,13},{6,22},{7,15},{8,24},{9,1... | collective-permute-start | bytes 688136 | tf_op jit(solution)/shard_map/ppermute | solution.py:43
  52.9 7.2 %collective-permute-start.16 = (bf16[32,3584]{1,0:T(8,128)(2,1)S(1)}, bf16[32,3584]{1,0:T(8,128)(2,1)S(1)}, u32[]{:S(2)}, u32[]{:S(2)}) collective-permute-start(bf16[32,3584]{1,0:T(8,128)(2,1)S(1)} %get-tuple-element.56), channel_id=1, source_target_pairs={{0,16},{1,9},{2,18},{3,11},{4,20},{5,13},{6,22},{7,15},{8,24},{9,1... | collective-permute-start | bytes 688136 | tf_op jit(solution)/shard_map/ppermute | solution.py:43
  57.3 4.9 %collective-permute-start.12 = (bf16[16,3584]{1,0:T(8,128)(2,1)S(1)}, bf16[16,3584]{1,0:T(8,128)(2,1)S(1)}, u32[]{:S(2)}, u32[]{:S(2)}) collective-permute-start(bf16[16,3584]{1,0:T(8,128)(2,1)S(1)} %get-tuple-element.48), channel_id=1, source_target_pairs={{0,8},{1,17},{2,10},{3,19},{4,12},{5,21},{6,14},{7,23},{8,0},{9,25... | collective-permute-start | bytes 344072 | tf_op jit(solution)/shard_map/ppermute | solution.py:43
  60.2 4.9 %collective-permute-start.17 = (bf16[16,3584]{1,0:T(8,128)(2,1)S(1)}, bf16[16,3584]{1,0:T(8,128)(2,1)S(1)}, u32[]{:S(2)}, u32[]{:S(2)}) collective-permute-start(bf16[16,3584]{1,0:T(8,128)(2,1)S(1)} %get-tuple-element.58), channel_id=1, source_target_pairs={{0,8},{1,17},{2,10},{3,19},{4,12},{5,21},{6,14},{7,23},{8,0},{9,25... | collective-permute-start | bytes 344072 | tf_op jit(solution)/shard_map/ppermute | solution.py:43
  62.2 4.9 %collective-permute-start.13 = (bf16[8,3584]{1,0:T(8,128)(2,1)S(1)}, bf16[8,3584]{1,0:T(8,128)(2,1)S(1)}, u32[]{:S(2)}, u32[]{:S(2)}) collective-permute-start(bf16[8,3584]{1,0:T(8,128)(2,1)S(1)} %get-tuple-element.50), channel_id=1, source_target_pairs={{0,2},{1,5},{2,0},{3,7},{4,6},{5,1},{6,4},{7,3},{8,10},{9,13},{10,... | collective-permute-start | bytes 172040 | tf_op jit(solution)/shard_map/ppermute | solution.py:35
  65.0 4.4 %collective-permute-start.18 = (bf16[8,3584]{1,0:T(8,128)(2,1)S(1)}, bf16[8,3584]{1,0:T(8,128)(2,1)S(1)}, u32[]{:S(2)}, u32[]{:S(2)}) collective-permute-start(bf16[8,3584]{1,0:T(8,128)(2,1)S(1)} %get-tuple-element.60), channel_id=1, source_target_pairs={{0,2},{1,5},{2,0},{3,7},{4,6},{5,1},{6,4},{7,3},{8,10},{9,13},{10,... | collective-permute-start | bytes 172040 | tf_op jit(solution)/shard_map/ppermute | solution.py:35
  67.2 4.8 %collective-permute-start.14 = (bf16[4,3584]{1,0:T(4,128)(2,1)S(1)}, bf16[4,3584]{1,0:T(4,128)(2,1)S(1)}, u32[]{:S(2)}, u32[]{:S(2)}) collective-permute-start(bf16[4,3584]{1,0:T(4,128)(2,1)S(1)} %get-tuple-element.52), channel_id=1, source_target_pairs={{0,4},{1,3},{2,6},{3,1},{4,0},{5,7},{6,2},{7,5},{8,12},{9,11},{10,... | collective-permute-start | bytes 86024 | tf_op jit(solution)/shard_map/ppermute | solution.py:35
  69.4 4.8 %collective-permute-start.19 = (bf16[4,3584]{1,0:T(4,128)(2,1)S(1)}, bf16[4,3584]{1,0:T(4,128)(2,1)S(1)}, u32[]{:S(2)}, u32[]{:S(2)}) collective-permute-start(bf16[4,3584]{1,0:T(4,128)(2,1)S(1)} %get-tuple-element.62), channel_id=1, source_target_pairs={{0,4},{1,3},{2,6},{3,1},{4,0},{5,7},{6,2},{7,5},{8,12},{9,11},{10,... | collective-permute-start | bytes 86024 | tf_op jit(solution)/shard_map/ppermute | solution.py:35

commit v12 on v11

--- a/solution.py
+++ b/solution.py
@@ -30,9 +30,8 @@
     return [pl.BlockSpec(memory_space=VMEM)] * count
 
 
-def swap(value, axis, size, masks):
-    masks = masks if isinstance(masks, tuple) else (masks, masks)
-    return lax.ppermute(value, axis, [(i, i ^ masks[i % 2]) for i in range(size)])
+def swap(value, axis, size, mask):
+    return lax.ppermute(value, axis, [(i, i ^ mask) for i in range(size)])
 
 
 def swap_group(value, groups, members, masks):
@@ -304,10 +303,9 @@
         lines //= radix
         near, wide = 2 * lines, 4 * lines
         if radix == 4:
-            out = [(wide, near), (near, wide), (near + wide, near + wide)]
-            steps.append((out, [(near, wide), (wide, near)]))
+            steps.append(([near, wide, near + wide], [wide, near]))
         else:
-            steps.append(([(near, near)], [(near, near)]))
+            steps.append(([near], [near]))
     return steps
 
 
@@ -317,9 +315,9 @@
         keep, send = fold(values, 2)
         values = [keep, swap_group(send, groups, members, masks)]
     for _, back in reversed(line_steps(members // 2)):
-        for masks in back:
+        for mask in back:
             keep, send = fold(values, 2)
-            values = [keep, swap(send, "expert", members, masks)]
+            values = [keep, swap(send, "expert", members, mask)]
     total = values[0].astype(jnp.float32) + values[1].astype(jnp.float32)
     return total.astype(jnp.bfloat16)
 
@@ -365,12 +363,12 @@
     held += more
     a, b = join([value, got], mark, halves)
     a_got, b_got = [swap_group(v, groups, members, (2, 1)) for v in (a, b)]
-    a_core, b_core = swap(a, "expert", members, 1), swap(b, "expert", members, 1)
     more, mark = fetch(jobs[2], a)
     held += more
     (a_got,), (b_got,) = hold([a_got], mark), hold([b_got], mark)
-    a_parts = [a, a_got, a_core, swap(a_got, "expert", members, 1)]
-    b_parts = [b, b_got, b_core, swap(b_got, "expert", members, 1)]
+    (a_late,), (b_late,) = join([a], mark), join([b], mark)
+    a_parts = [a, a_got] + [swap(v, "expert", members, 1) for v in (a_late, a_got)]
+    b_parts = [b, b_got] + [swap(v, "expert", members, 1) for v in (b_late, b_got)]
     sums = run_expert(a_parts, b_parts, held, place, order, w_gate, w_up, w_down, me)
     out = [give_back(own, far, groups, members) for own, far in zip(sums[:2], sums[2:])]
     return jnp.concatenate(out, axis=1)

time: 75.1 us -> 75 us (level)
  starting transfers between devices: 24.5 us -> 22.8 us
  waiting for transfers between devices: 13.6 us -> 15.2 us
    ppermute x13, waiting for transfers between devices: 5.63 us -> 7.66 us  [swap(): return lax.ppermute(value, axis, [(i, i ^ mask) for i in range(size)])]
    ppermute x13, starting transfers between devices: 15.5 us -> 13.6 us  [swap(): return lax.ppermute(value, axis, [(i, i ^ mask) for i in range(size)])]
  transfers between devices with their start and end apart: 20 -> 20, of which waited for: 11 -> 13; matrix products, arithmetic and copies ran while one was open for 0% -> 0% of each run, Pallas kernels for 18% -> 18%
where the time goes in v12:
time: 75 us; the launch traced here: 74.8 us
  Pallas kernels  36 us (48%)
  starting transfers between devices  22.8 us (30%)
  waiting for transfers between devices  15.2 us (20%)
    pallas_call x1, Pallas kernels, run_expert(): pl.pallas_call(functools.partial(expert_kernel, place, order, streams, le...  21.7 us
    ppermute x13, starting transfers between devices, swap(): return lax.ppermute(value, axis, [(i, i ^ mask) for i in range(size)])  13.6 us
    pallas_call x3, Pallas kernels, fetch(): pl.pallas_call(functools.partial(fetch_kernel, jobs), in_specs=[hbm] * le...  12.9 us
    ppermute x7, starting transfers between devices, swap_group(): return lax.ppermute(value, AXES, pairs)  9.24 us
    ppermute x13, waiting for transfers between devices, swap(): return lax.ppermute(value, axis, [(i, i ^ mask) for i in range(size)])  7.66 us
    ppermute x7, waiting for transfers between devices, swap_group(): return lax.ppermute(value, AXES, pairs)  7.49 us
  transfers between devices with their start and end apart: 20, of which 13 were waited for; matrix products, arithmetic and copies ran while one was open for 0% of the time, Pallas kernels for 18%

profile of v12, /device:TPU:0, one launch (start us, length us, event | category | flops | bytes accessed | tf_op | source)
XLA Modules:
  0.0 74.8 jit_solution(16756386959120002243)
XLA Ops:
  0.0 0.9 %shard_map.64.refs_1_.refs_0_ = bf16[4,7296]{1,0:T(4,128)(2,1)S(1)} custom-call(s32[1]{0:T(128)} %bitcast.me_ref.refs_15_, bf16[4,7168]{1,0:T(4,128)(2,1)} %tokens_ref.1, s32[4,8]{1,0:T(4,128)} %ids_ref.1, bf16[4,8]{1,0:T(4,128)(2,1)} %weights_ref.1), custom_call_target="tpu_custom_call" | custom-call | tf_op jit(solution)/shard_map/pallas_call | solution.py:68
  0.9 5.1 %collective-permute-start.2 = (bf16[4,7296]{1,0:T(4,128)(2,1)S(1)}, bf16[4,7296]{1,0:T(4,128)(2,1)S(1)}, u32[]{:S(2)}, u32[]{:S(2)}) collective-permute-start(bf16[4,7296]{1,0:T(4,128)(2,1)S(1)} %shard_map.64.refs_1_.refs_0_), channel_id=1, source_target_pairs={{0,6},{1,7},{2,4},{3,5},{4,2},{5,3},{6,0},{7,1},{8,14},{9,15},{10,... | collective-permute-start | bytes 175112 | tf_op jit(solution)/shard_map/ppermute | solution.py:34
  6.0 0.0 collective-permute-start.1
  6.1 0.6 collective-permute-start
  6.7 4.3 %shard_map.65 = (bf16[7168,768]{1,0:T(8,128)(2,1)S(1)}, f32[8,128]{1,0:T(8,128)S(1)}) custom-call(bf16[1,7168,2048]{2,1,0:T(8,128)(2,1)} %refs_12_.1, bf16[4,7296]{1,0:T(4,128)(2,1)S(1)} %shard_map.64.refs_1_.refs_0_), custom_call_target="tpu_custom_call" | custom-call | bytes 11010048 | tf_op jit(solution)/shard_map/pallas_call | solution.py:106
  11.0 0.1 collective-permute-done.1.refs_2_
  11.1 0.0 collective-permute-done.refs_1_
  11.1 0.1 shard_map.66.refs_2_.refs_0_
  11.2 1.6 %collective-permute-start.3 = (bf16[16,7296]{1,0:T(8,128)(2,1)S(1)}, bf16[16,7296]{1,0:T(8,128)(2,1)S(1)}, u32[]{:S(2)}, u32[]{:S(2)}) collective-permute-start(bf16[16,7296]{1,0:T(8,128)(2,1)S(1)} %shard_map.66.refs_2_.refs_0_), channel_id=1, source_target_pairs={{0,8},{1,17},{2,10},{3,19},{4,12},{5,21},{6,14},{7,23},{8,0},{9,25... | collective-permute-start | bytes 700424 | tf_op jit(solution)/shard_map/ppermute | solution.py:42
  12.8 4.3 %shard_map.67 = (bf16[7168,512]{1,0:T(8,128)(2,1)S(1)}, bf16[7168,256]{1,0:T(8,128)(2,1)S(1)}, f32[8,128]{1,0:T(8,128)S(1)}) custom-call(bf16[1,7168,2048]{2,1,0:T(8,128)(2,1)} %refs_12_.1, bf16[1,7168,2048]{2,1,0:T(8,128)(2,1)} %refs_13_.1, bf16[16,7296]{1,0:T(8,128)(2,1)S(1)} %shard_map.66.refs_2_.refs_0_), custom_call_target="tpu_custom_call" | custom-call | bytes 11010048 | tf_op jit(solution)/shard_map/pallas_call | solution.py:106
  17.2 0.2 collective-permute-done.3.refs_1_
  17.4 1.7 %collective-permute-start.7 = (bf16[32,3712]{1,0:T(8,128)(2,1)S(1)}, bf16[32,3712]{1,0:T(8,128)(2,1)S(1)}, u32[]{:S(2)}, u32[]{:S(2)}) collective-permute-start(bf16[32,3712]{1,0:T(8,128)(2,1)S(1)} %get-tuple-element.38.refs_0_.refs_4_), channel_id=1, source_target_pairs={{0,16},{1,9},{2,18},{3,11},{4,20},{5,13},{6,22},{7,15},{8,24},{9,1... | collective-permute-start | bytes 712712 | tf_op jit(solution)/shard_map/ppermute | solution.py:42
  19.0 0.4 collective-permute-start.4
  19.5 4.3 %shard_map.69 = (bf16[7168,768]{1,0:T(8,128)(2,1)S(1)}, f32[8,128]{1,0:T(8,128)S(1)}) custom-call(bf16[1,7168,2048]{2,1,0:T(8,128)(2,1)} %refs_13_.1, bf16[32,3584]{1,0:T(8,128)(2,1)S(1)} %get-tuple-element.36.refs_1_.refs_0_), custom_call_target="tpu_custom_call" | custom-call | bytes 11010048 | tf_op jit(solution)/shard_map/pallas_call | solution.py:106
  23.8 0.1 collective-permute-start.8
  23.9 0.0 collective-permute-done.7.refs_0_
  23.9 0.5 collective-permute-start.9
  24.4 0.2 collective-permute-start.5
  24.5 1.5 %collective-permute-done.4.refs_0_ = bf16[32,3584]{1,0:T(8,128)(2,1)S(1)} collective-permute-done((bf16[32,3584]{1,0:T(8,128)(2,1)S(1)}, bf16[32,3584]{1,0:T(8,128)(2,1)S(1)}, u32[]{:S(2)}, u32[]{:S(2)}) %collective-permute-start.4) | collective-permute-done | bytes 229408 | tf_op jit(solution)/shard_map/ppermute | solution.py:42
  26.0 0.0 collective-permute-start.6
  26.0 0.0 collective-permute-done.5.refs_2_
  26.0 1.5 %collective-permute-done.6.refs_3_ = bf16[32,3584]{1,0:T(8,128)(2,1)S(1)} collective-permute-done((bf16[32,3584]{1,0:T(8,128)(2,1)S(1)}, bf16[32,3584]{1,0:T(8,128)(2,1)S(1)}, u32[]{:S(2)}, u32[]{:S(2)}) %collective-permute-start.6) | collective-permute-done | bytes 229408 | tf_op jit(solution)/shard_map/ppermute | solution.py:34
  27.5 0.0 collective-permute-done.9.refs_7_
  27.5 21.7 %shard_map.74 = (bf16[64,3584]{1,0:T(8,128)(2,1)S(1)}, bf16[64,3584]{1,0:T(8,128)(2,1)S(1)}, bf16[64,3584]{1,0:T(8,128)(2,1)S(1)}, bf16[64,3584]{1,0:T(8,128)(2,1)S(1)}) custom-call(bf16[32,3584]{1,0:T(8,128)(2,1)S(1)} %get-tuple-element.36.refs_1_.refs_0_, bf16[32,3584]{1,0:T(8,128)(2,1)S(1)} %shard_map.70.refs_1_, ...), custom_call_target="tpu_custom_call" | custom-call | flops 11274289152 | bytes 58720256 | tf_op jit(solution)/shard_map/pallas_call | solution.py:257
  49.2 0.2 collective-permute-start.10
  49.4 0.4 collective-permute-start.15
  49.7 1.3 %collective-permute-done.10.refs_1_ = bf16[64,3584]{1,0:T(8,128)(2,1)S(1)} collective-permute-done((bf16[64,3584]{1,0:T(8,128)(2,1)S(1)}, bf16[64,3584]{1,0:T(8,128)(2,1)S(1)}, u32[]{:S(2)}, u32[]{:S(2)}) %collective-permute-start.10) | collective-permute-done | bytes 458784 | tf_op jit(solution)/shard_map/ppermute | solution.py:34
  51.1 0.1 shard_map.75
  51.2 1.7 %collective-permute-start.11 = (bf16[32,3584]{1,0:T(8,128)(2,1)S(1)}, bf16[32,3584]{1,0:T(8,128)(2,1)S(1)}, u32[]{:S(2)}, u32[]{:S(2)}) collective-permute-start(bf16[32,3584]{1,0:T(8,128)(2,1)S(1)} %get-tuple-element.46), channel_id=1, source_target_pairs={{0,16},{1,9},{2,18},{3,11},{4,20},{5,13},{6,22},{7,15},{8,24},{9,1... | collective-permute-start | bytes 688136 | tf_op jit(solution)/shard_map/ppermute | solution.py:42
  52.9 0.1 shard_map.79
  53.0 0.5 collective-permute-start.16
  53.5 3.7 %collective-permute-done.11.refs_1_ = bf16[32,3584]{1,0:T(8,128)(2,1)S(1)} collective-permute-done((bf16[32,3584]{1,0:T(8,128)(2,1)S(1)}, bf16[32,3584]{1,0:T(8,128)(2,1)S(1)}, u32[]{:S(2)}, u32[]{:S(2)}) %collective-permute-start.11) | collective-permute-done | bytes 229408 | tf_op jit(solution)/shard_map/ppermute | solution.py:42
  57.3 0.1 shard_map.76
  57.3 1.6 %collective-permute-start.12 = (bf16[16,3584]{1,0:T(8,128)(2,1)S(1)}, bf16[16,3584]{1,0:T(8,128)(2,1)S(1)}, u32[]{:S(2)}, u32[]{:S(2)}) collective-permute-start(bf16[16,3584]{1,0:T(8,128)(2,1)S(1)} %get-tuple-element.48), channel_id=1, source_target_pairs={{0,8},{1,17},{2,10},{3,19},{4,12},{5,21},{6,14},{7,23},{8,0},{9,25... | collective-permute-start | bytes 344072 | tf_op jit(solution)/shard_map/ppermute | solution.py:42
  59.0 1.1 %collective-permute-done.16.refs_1_ = bf16[32,3584]{1,0:T(8,128)(2,1)S(1)} collective-permute-done((bf16[32,3584]{1,0:T(8,128)(2,1)S(1)}, bf16[32,3584]{1,0:T(8,128)(2,1)S(1)}, u32[]{:S(2)}, u32[]{:S(2)}) %collective-permute-start.16) | collective-permute-done | bytes 229408 | tf_op jit(solution)/shard_map/ppermute | solution.py:42
  60.1 0.1 shard_map.80
  60.2 1.6 %collective-permute-start.17 = (bf16[16,3584]{1,0:T(8,128)(2,1)S(1)}, bf16[16,3584]{1,0:T(8,128)(2,1)S(1)}, u32[]{:S(2)}, u32[]{:S(2)}) collective-permute-start(bf16[16,3584]{1,0:T(8,128)(2,1)S(1)} %get-tuple-element.58), channel_id=1, source_target_pairs={{0,8},{1,17},{2,10},{3,19},{4,12},{5,21},{6,14},{7,23},{8,0},{9,25... | collective-permute-start | bytes 344072 | tf_op jit(solution)/shard_map/ppermute | solution.py:42
  61.8 0.4 collective-permute-done.12.refs_1_
  62.2 2.2 %collective-permute-start.13 = (bf16[8,3584]{1,0:T(8,128)(2,1)S(1)}, bf16[8,3584]{1,0:T(8,128)(2,1)S(1)}, u32[]{:S(2)}, u32[]{:S(2)}) collective-permute-start(bf16[8,3584]{1,0:T(8,128)(2,1)S(1)} %get-tuple-element.50), channel_id=1, source_target_pairs={{0,4},{1,5},{2,6},{3,7},{4,0},{5,1},{6,2},{7,3},{8,12},{9,13},{10,... | collective-permute-start | bytes 172040 | tf_op jit(solution)/shard_map/ppermute | solution.py:34
  64.4 0.6 collective-permute-done.17.refs_1_
  65.0 2.2 %collective-permute-start.18 = (bf16[8,3584]{1,0:T(8,128)(2,1)S(1)}, bf16[8,3584]{1,0:T(8,128)(2,1)S(1)}, u32[]{:S(2)}, u32[]{:S(2)}) collective-permute-start(bf16[8,3584]{1,0:T(8,128)(2,1)S(1)} %get-tuple-element.60), channel_id=1, source_target_pairs={{0,4},{1,5},{2,6},{3,7},{4,0},{5,1},{6,2},{7,3},{8,12},{9,13},{10,... | collective-permute-start | bytes 172040 | tf_op jit(solution)/shard_map/ppermute | solution.py:34
  67.3 1.5 %collective-permute-done.13.refs_1_ = bf16[8,3584]{1,0:T(8,128)(2,1)S(1)} collective-permute-done((bf16[8,3584]{1,0:T(8,128)(2,1)S(1)}, bf16[8,3584]{1,0:T(8,128)(2,1)S(1)}, u32[]{:S(2)}, u32[]{:S(2)}) %collective-permute-start.13) | collective-permute-done | bytes 57376 | tf_op jit(solution)/shard_map/ppermute | solution.py:34
  68.8 0.6 collective-permute-start.14
  69.4 0.8 %collective-permute-done.18.refs_1_ = bf16[8,3584]{1,0:T(8,128)(2,1)S(1)} collective-permute-done((bf16[8,3584]{1,0:T(8,128)(2,1)S(1)}, bf16[8,3584]{1,0:T(8,128)(2,1)S(1)}, u32[]{:S(2)}, u32[]{:S(2)}) %collective-permute-start.18) | collective-permute-done | bytes 57376 | tf_op jit(solution)/shard_map/ppermute | solution.py:34
  70.2 1.5 %collective-permute-start.19 = (bf16[4,3584]{1,0:T(4,128)(2,1)S(1)}, bf16[4,3584]{1,0:T(4,128)(2,1)S(1)}, u32[]{:S(2)}, u32[]{:S(2)}) collective-permute-start(bf16[4,3584]{1,0:T(4,128)(2,1)S(1)} %get-tuple-element.62), channel_id=1, source_target_pairs={{0,2},{1,3},{2,0},{3,1},{4,6},{5,7},{6,4},{7,5},{8,10},{9,11},{10,... | collective-permute-start | bytes 86024 | tf_op jit(solution)/shard_map/ppermute | solution.py:34
  71.7 1.0 %collective-permute-done.14 = bf16[4,3584]{1,0:T(4,128)(2,1)S(1)} collective-permute-done((bf16[4,3584]{1,0:T(4,128)(2,1)S(1)}, bf16[4,3584]{1,0:T(4,128)(2,1)S(1)}, u32[]{:S(2)}, u32[]{:S(2)}) %collective-permute-start.14) | collective-permute-done | bytes 28704 | tf_op jit(solution)/shard_map/ppermute | solution.py:34
  72.8 1.4 %collective-permute-done.19 = bf16[4,3584]{1,0:T(4,128)(2,1)S(1)} collective-permute-done((bf16[4,3584]{1,0:T(4,128)(2,1)S(1)}, bf16[4,3584]{1,0:T(4,128)(2,1)S(1)}, u32[]{:S(2)}, u32[]{:S(2)}) %collective-permute-start.19) | collective-permute-done | bytes 28704 | tf_op jit(solution)/shard_map/ppermute | solution.py:34
  74.2 0.7 pad_maximum_fusion
  (14 shorter events, 0.2 us)
Async XLA Ops:
  0.9 10.1 %collective-permute-start.2 = (bf16[4,7296]{1,0:T(4,128)(2,1)S(1)}, bf16[4,7296]{1,0:T(4,128)(2,1)S(1)}, u32[]{:S(2)}, u32[]{:S(2)}) collective-permute-start(bf16[4,7296]{1,0:T(4,128)(2,1)S(1)} %shard_map.64.refs_1_.refs_0_), channel_id=1, source_target_pairs={{0,6},{1,7},{2,4},{3,5},{4,2},{5,3},{6,0},{7,1},{8,14},{9,15},{10,... | collective-permute-start | bytes 175112 | tf_op jit(solution)/shard_map/ppermute | solution.py:34
  6.0 5.1 %collective-permute-start.1 = (bf16[4,7296]{1,0:T(4,128)(2,1)S(1)}, bf16[4,7296]{1,0:T(4,128)(2,1)S(1)}, u32[]{:S(2)}, u32[]{:S(2)}) collective-permute-start(bf16[4,7296]{1,0:T(4,128)(2,1)S(1)} %shard_map.64.refs_1_.refs_0_), channel_id=1, source_target_pairs={{0,4},{1,5},{2,6},{3,7},{4,0},{5,1},{6,2},{7,3},{8,12},{9,13},{10,... | collective-permute-start | bytes 175112 | tf_op jit(solution)/shard_map/ppermute | solution.py:34
  6.1 5.1 %collective-permute-start = (bf16[4,7296]{1,0:T(4,128)(2,1)S(1)}, bf16[4,7296]{1,0:T(4,128)(2,1)S(1)}, u32[]{:S(2)}, u32[]{:S(2)}) collective-permute-start(bf16[4,7296]{1,0:T(4,128)(2,1)S(1)} %shard_map.64.refs_1_.refs_0_), channel_id=1, source_target_pairs={{0,2},{1,3},{2,0},{3,1},{4,6},{5,7},{6,4},{7,5},{8,10},{9,11},{10,... | collective-permute-start | bytes 175112 | tf_op jit(solution)/shard_map/ppermute | solution.py:34
  11.2 6.1 %collective-permute-start.3 = (bf16[16,7296]{1,0:T(8,128)(2,1)S(1)}, bf16[16,7296]{1,0:T(8,128)(2,1)S(1)}, u32[]{:S(2)}, u32[]{:S(2)}) collective-permute-start(bf16[16,7296]{1,0:T(8,128)(2,1)S(1)} %shard_map.66.refs_2_.refs_0_), channel_id=1, source_target_pairs={{0,8},{1,17},{2,10},{3,19},{4,12},{5,21},{6,14},{7,23},{8,0},{9,25... | collective-permute-start | bytes 700424 | tf_op jit(solution)/shard_map/ppermute | solution.py:42
  17.4 6.5 %collective-permute-start.7 = (bf16[32,3712]{1,0:T(8,128)(2,1)S(1)}, bf16[32,3712]{1,0:T(8,128)(2,1)S(1)}, u32[]{:S(2)}, u32[]{:S(2)}) collective-permute-start(bf16[32,3712]{1,0:T(8,128)(2,1)S(1)} %get-tuple-element.38.refs_0_.refs_4_), channel_id=1, source_target_pairs={{0,16},{1,9},{2,18},{3,11},{4,20},{5,13},{6,22},{7,15},{8,24},{9,1... | collective-permute-start | bytes 712712 | tf_op jit(solution)/shard_map/ppermute | solution.py:42
  19.0 7.0 %collective-permute-start.4 = (bf16[32,3584]{1,0:T(8,128)(2,1)S(1)}, bf16[32,3584]{1,0:T(8,128)(2,1)S(1)}, u32[]{:S(2)}, u32[]{:S(2)}) collective-permute-start(bf16[32,3584]{1,0:T(8,128)(2,1)S(1)} %get-tuple-element.36.refs_1_.refs_0_), channel_id=1, source_target_pairs={{0,16},{1,9},{2,18},{3,11},{4,20},{5,13},{6,22},{7,15},{8,24},{9,1... | collective-permute-start | bytes 688136 | tf_op jit(solution)/shard_map/ppermute | solution.py:42
  23.8 2.2 %collective-permute-start.8 = (bf16[32,3712]{1,0:T(8,128)(2,1)S(1)}, bf16[32,3712]{1,0:T(8,128)(2,1)S(1)}, u32[]{:S(2)}, u32[]{:S(2)}) collective-permute-start(bf16[32,3712]{1,0:T(8,128)(2,1)S(1)} %shard_map.73), channel_id=1, source_target_pairs={{0,1},{1,0},{2,3},{3,2},{4,5},{5,4},{6,7},{7,6},{8,9},{9,8},{10,11... | collective-permute-start | bytes 712712 | tf_op jit(solution)/shard_map/ppermute | solution.py:34
  23.9 3.6 %collective-permute-start.9 = (bf16[32,3712]{1,0:T(8,128)(2,1)S(1)}, bf16[32,3712]{1,0:T(8,128)(2,1)S(1)}, u32[]{:S(2)}, u32[]{:S(2)}) collective-permute-start(bf16[32,3712]{1,0:T(8,128)(2,1)S(1)} %shard_map.72.refs_5_), channel_id=1, source_target_pairs={{0,1},{1,0},{2,3},{3,2},{4,5},{5,4},{6,7},{7,6},{8,9},{9,8},{10,11... | collective-permute-start | bytes 712712 | tf_op jit(solution)/shard_map/ppermute | solution.py:34
  24.4 1.6 %collective-permute-start.5 = (bf16[32,3584]{1,0:T(8,128)(2,1)S(1)}, bf16[32,3584]{1,0:T(8,128)(2,1)S(1)}, u32[]{:S(2)}, u32[]{:S(2)}) collective-permute-start(bf16[32,3584]{1,0:T(8,128)(2,1)S(1)} %shard_map.71), channel_id=1, source_target_pairs={{0,1},{1,0},{2,3},{3,2},{4,5},{5,4},{6,7},{7,6},{8,9},{9,8},{10,11... | collective-permute-start | bytes 688136 | tf_op jit(solution)/shard_map/ppermute | solution.py:34
  26.0 1.5 %collective-permute-start.6 = (bf16[32,3584]{1,0:T(8,128)(2,1)S(1)}, bf16[32,3584]{1,0:T(8,128)(2,1)S(1)}, u32[]{:S(2)}, u32[]{:S(2)}) collective-permute-start(bf16[32,3584]{1,0:T(8,128)(2,1)S(1)} %shard_map.70.refs_1_), channel_id=1, source_target_pairs={{0,1},{1,0},{2,3},{3,2},{4,5},{5,4},{6,7},{7,6},{8,9},{9,8},{10,11... | collective-permute-start | bytes 688136 | tf_op jit(solution)/shard_map/ppermute | solution.py:34
  49.2 1.9 %collective-permute-start.10 = (bf16[64,3584]{1,0:T(8,128)(2,1)S(1)}, bf16[64,3584]{1,0:T(8,128)(2,1)S(1)}, u32[]{:S(2)}, u32[]{:S(2)}) collective-permute-start(bf16[64,3584]{1,0:T(8,128)(2,1)S(1)} %get-tuple-element.44), channel_id=1, source_target_pairs={{0,1},{1,0},{2,3},{3,2},{4,5},{5,4},{6,7},{7,6},{8,9},{9,8},{10,11... | collective-permute-start | bytes 1376264 | tf_op jit(solution)/shard_map/ppermute | solution.py:34
  49.4 3.5 %collective-permute-start.15 = (bf16[64,3584]{1,0:T(8,128)(2,1)S(1)}, bf16[64,3584]{1,0:T(8,128)(2,1)S(1)}, u32[]{:S(2)}, u32[]{:S(2)}) collective-permute-start(bf16[64,3584]{1,0:T(8,128)(2,1)S(1)} %get-tuple-element.54), channel_id=1, source_target_pairs={{0,1},{1,0},{2,3},{3,2},{4,5},{5,4},{6,7},{7,6},{8,9},{9,8},{10,11... | collective-permute-start | bytes 1376264 | tf_op jit(solution)/shard_map/ppermute | solution.py:34
  51.2 6.1 %collective-permute-start.11 = (bf16[32,3584]{1,0:T(8,128)(2,1)S(1)}, bf16[32,3584]{1,0:T(8,128)(2,1)S(1)}, u32[]{:S(2)}, u32[]{:S(2)}) collective-permute-start(bf16[32,3584]{1,0:T(8,128)(2,1)S(1)} %get-tuple-element.46), channel_id=1, source_target_pairs={{0,16},{1,9},{2,18},{3,11},{4,20},{5,13},{6,22},{7,15},{8,24},{9,1... | collective-permute-start | bytes 688136 | tf_op jit(solution)/shard_map/ppermute | solution.py:42
  53.0 7.1 %collective-permute-start.16 = (bf16[32,3584]{1,0:T(8,128)(2,1)S(1)}, bf16[32,3584]{1,0:T(8,128)(2,1)S(1)}, u32[]{:S(2)}, u32[]{:S(2)}) collective-permute-start(bf16[32,3584]{1,0:T(8,128)(2,1)S(1)} %get-tuple-element.56), channel_id=1, source_target_pairs={{0,16},{1,9},{2,18},{3,11},{4,20},{5,13},{6,22},{7,15},{8,24},{9,1... | collective-permute-start | bytes 688136 | tf_op jit(solution)/shard_map/ppermute | solution.py:42
  57.3 4.9 %collective-permute-start.12 = (bf16[16,3584]{1,0:T(8,128)(2,1)S(1)}, bf16[16,3584]{1,0:T(8,128)(2,1)S(1)}, u32[]{:S(2)}, u32[]{:S(2)}) collective-permute-start(bf16[16,3584]{1,0:T(8,128)(2,1)S(1)} %get-tuple-element.48), channel_id=1, source_target_pairs={{0,8},{1,17},{2,10},{3,19},{4,12},{5,21},{6,14},{7,23},{8,0},{9,25... | collective-permute-start | bytes 344072 | tf_op jit(solution)/shard_map/ppermute | solution.py:42
  60.2 4.9 %collective-permute-start.17 = (bf16[16,3584]{1,0:T(8,128)(2,1)S(1)}, bf16[16,3584]{1,0:T(8,128)(2,1)S(1)}, u32[]{:S(2)}, u32[]{:S(2)}) collective-permute-start(bf16[16,3584]{1,0:T(8,128)(2,1)S(1)} %get-tuple-element.58), channel_id=1, source_target_pairs={{0,8},{1,17},{2,10},{3,19},{4,12},{5,21},{6,14},{7,23},{8,0},{9,25... | collective-permute-start | bytes 344072 | tf_op jit(solution)/shard_map/ppermute | solution.py:42
  62.2 6.6 %collective-permute-start.13 = (bf16[8,3584]{1,0:T(8,128)(2,1)S(1)}, bf16[8,3584]{1,0:T(8,128)(2,1)S(1)}, u32[]{:S(2)}, u32[]{:S(2)}) collective-permute-start(bf16[8,3584]{1,0:T(8,128)(2,1)S(1)} %get-tuple-element.50), channel_id=1, source_target_pairs={{0,4},{1,5},{2,6},{3,7},{4,0},{5,1},{6,2},{7,3},{8,12},{9,13},{10,... | collective-permute-start | bytes 172040 | tf_op jit(solution)/shard_map/ppermute | solution.py:34
  65.0 5.1 %collective-permute-start.18 = (bf16[8,3584]{1,0:T(8,128)(2,1)S(1)}, bf16[8,3584]{1,0:T(8,128)(2,1)S(1)}, u32[]{:S(2)}, u32[]{:S(2)}) collective-permute-start(bf16[8,3584]{1,0:T(8,128)(2,1)S(1)} %get-tuple-element.60), channel_id=1, source_target_pairs={{0,4},{1,5},{2,6},{3,7},{4,0},{5,1},{6,2},{7,3},{8,12},{9,13},{10,... | collective-permute-start | bytes 172040 | tf_op jit(solution)/shard_map/ppermute | solution.py:34
  68.8 3.9 %collective-permute-start.14 = (bf16[4,3584]{1,0:T(4,128)(2,1)S(1)}, bf16[4,3584]{1,0:T(4,128)(2,1)S(1)}, u32[]{:S(2)}, u32[]{:S(2)}) collective-permute-start(bf16[4,3584]{1,0:T(4,128)(2,1)S(1)} %get-tuple-element.52), channel_id=1, source_target_pairs={{0,2},{1,3},{2,0},{3,1},{4,6},{5,7},{6,4},{7,5},{8,10},{9,11},{10,... | collective-permute-start | bytes 86024 | tf_op jit(solution)/shard_map/ppermute | solution.py:34
  70.2 3.9 %collective-permute-start.19 = (bf16[4,3584]{1,0:T(4,128)(2,1)S(1)}, bf16[4,3584]{1,0:T(4,128)(2,1)S(1)}, u32[]{:S(2)}, u32[]{:S(2)}) collective-permute-start(bf16[4,3584]{1,0:T(4,128)(2,1)S(1)} %get-tuple-element.62), channel_id=1, source_target_pairs={{0,2},{1,3},{2,0},{3,1},{4,6},{5,7},{6,4},{7,5},{8,10},{9,11},{10,... | collective-permute-start | bytes 86024 | tf_op jit(solution)/shard_map/ppermute | solution.py:34
